TPU v7x, 256 devices: a whole 4x4x8 slice. The times are simulated.
256 devices in a mesh: layer: 4 (over x), latent: 64 (over y, z, core).
Axes of the slice: x: 4, y: 4, z: 8, core: 2. Of those that a mesh axis runs over, the one named last changes fastest.
Arguments:
- residual: bfloat16 [4, 512, 1792], P('layer', 'latent'), may hold values from -6 to 6
- target: bfloat16 [4, 512, 1792], P('layer', 'latent'), may hold values from -6 to 6
- enc_weight: bfloat16 [4, 1792, 16384], P('layer', None, 'latent'), may hold values from -0.125 to 0.125
- enc_bias: float32 [4, 16384], P('layer', 'latent'), may hold values from -3 to 3
- dec_weight: bfloat16 [4, 4, 16384, 1792], P(None, 'layer', 'latent'), may hold values from -0.0625 to 0.0625
- active: int32 [4, 8, 32], replicated, may hold values from 0 to 63, all different within a row; in each aligned block of 8 rows (0 to 7, 8 to 15, ..., all dimensions but the last counted through in order) at most 6 rows name the same one
Outputs:
- loss: float32 [], replicated
- enc_grad: bfloat16 [4, 1792, 16384], P('layer', None, 'latent')
- bias_grad: float32 [4, 16384], P('layer', 'latent')
- dec_grad: bfloat16 [4, 4, 16384, 1792], P(None, 'layer', 'latent')
Inputs may be any that keep to these rules, and one draw needn't show every extreme that they name: `active`: each row lists 32 different blocks of its layer; within one layer no block is listed on more than 6 token tiles, and in every draw some block of some layer is listed on exactly 6.
All inputs are finite; a program needn't handle non-finite values.
Results may differ from a plain program's by a relative error of at most 0.023.
Values may be sent and summed in bfloat16 or wider, within the bound.
No kernel may reach another device: no remote copies, remote signals or barrier semaphores. Data moves between devices by JAX's collectives and lax.ppermute only.
A program may use at most 128 MiB of HBM per device.

v0:
```python
import jax
import jax.numpy as jnp
from jax import lax
from jax.sharding import PartitionSpec as P

D = 1792
BLOCK = 256
TILE = 64
NTILE = 8
CAP = 6


def shifted(value, axis, steps):
    count = lax.axis_size(axis)
    leading, last = (max(0, -steps), min(count, count - steps))
    return lax.ppermute(value, axis, [(source, source + steps) for source in range(leading, last)])


def slot_list(active, layer, my_block, slot_count):
    block_ids = lax.dynamic_index_in_dim(active, layer, 0, keepdims=False)
    hit = jnp.any(block_ids == my_block, axis=1).astype(jnp.int32)
    every = jnp.arange(NTILE, dtype=jnp.int32)
    place = jnp.cumsum(hit) - 1
    chosen = (hit[None, :] == 1) & (
        place[None, :] == jnp.arange(slot_count, dtype=jnp.int32)[:, None]
    )
    tile_ids = jnp.sum(jnp.where(chosen, every[None, :], 0), axis=1)
    filled = jnp.sum(chosen.astype(jnp.float32), axis=1)
    return (tile_ids, filled)


def shards(residual, target, enc_weight, enc_bias, dec_weight, active):
    layers = dec_weight.shape[0]
    feat_dev = enc_weight.shape[2]
    layer_index = lax.axis_index("layer")
    my_block = lax.axis_index("latent") * feat_dev // BLOCK
    slot_count = CAP
    slot_rows = slot_count * TILE
    full_inputs = lax.all_gather(residual[0], "latent", axis=0, tiled=True).reshape(NTILE, TILE, D)
    own_tiles, own_filled = slot_list(active, layer_index, my_block, slot_count)
    rows = jnp.take(full_inputs, own_tiles, axis=0).reshape(slot_rows, D)
    preact = jnp.dot(rows, enc_weight[0], preferred_element_type=jnp.float32) + enc_bias[0][None, :]
    live = jnp.repeat(own_filled, TILE)[:, None]
    sparse_codes = (jnp.maximum(preact, 0.0) * live).astype(jnp.bfloat16)
    dec_all = dec_weight[:, 0]

    def take_source(carry, portion, source):
        writes, kept = carry
        usable = (source >= 0) & (source <= layer_index)
        source_idx = jnp.clip(source, 0, layers - 1)
        portion = jnp.where(usable, portion, jnp.zeros_like(portion))
        tile_ids, _ = slot_list(active, source_idx, my_block, slot_count)
        weight = lax.dynamic_index_in_dim(dec_all, source_idx, 0, keepdims=False)
        product = jnp.dot(portion, weight, preferred_element_type=jnp.float32).reshape(
            slot_count, TILE, D
        )
        writes = writes.at[tile_ids].add(product)
        kept = jnp.where(usable, kept.at[source_idx].set(portion), kept)
        return (writes, kept)

    start_state = (
        jnp.zeros((NTILE, TILE, D), jnp.float32),
        jnp.zeros((layers, slot_rows, feat_dev), jnp.bfloat16),
    )
    state = take_source(start_state, sparse_codes, layer_index)
    moving = sparse_codes
    for hop in range(1, layers):
        moving = shifted(moving, "layer", 1)
        state = take_source(state, moving, layer_index - hop)
    writes, kept = state
    recon = lax.psum_scatter(
        writes.reshape(NTILE * TILE, D), "latent", scatter_dimension=0, tiled=True
    )
    errors = recon - target[0].astype(jnp.float32)
    total = lax.psum(jnp.sum(errors * errors), ("layer", "latent"))
    loss = 0.5 * total / (layers * NTILE * TILE * D)
    full_errors = lax.all_gather(errors.astype(jnp.bfloat16), "latent", axis=0, tiled=True).reshape(
        NTILE, TILE, D
    )
    dec_grads = []
    code_grads = []
    for source in range(layers):
        tile_ids, _ = slot_list(active, source, my_block, slot_count)
        error_part = jnp.take(full_errors, tile_ids, axis=0).reshape(slot_rows, D)
        grad = lax.dot_general(
            kept[source], error_part, (((0,), (0,)), ((), ())), preferred_element_type=jnp.float32
        )
        dec_grads.append((grad / TILE).astype(jnp.bfloat16))
        back = lax.dot_general(
            error_part,
            dec_all[source],
            (((1,), (1,)), ((), ())),
            preferred_element_type=jnp.float32,
        )
        code_grads.append(jnp.where(source <= layer_index, back, jnp.zeros_like(back)))
    dec_grad = jnp.stack(dec_grads)[:, None]
    code_grad = jnp.stack(code_grads)
    running = code_grad
    for hop in range(1, layers):
        running = code_grad + shifted(running, "layer", -1)
    mine = lax.dynamic_index_in_dim(running, layer_index, 0, keepdims=False)
    pre_grad = jnp.where(preact > 0, mine, jnp.zeros_like(mine)) * live
    bias_grad = (jnp.sum(pre_grad, axis=0) / TILE)[None]
    enc_term = lax.dot_general(
        rows,
        pre_grad.astype(jnp.bfloat16),
        (((0,), (0,)), ((), ())),
        preferred_element_type=jnp.float32,
    )
    enc_grad = (enc_term / TILE).astype(jnp.bfloat16)[None]
    return (loss, enc_grad, bias_grad, dec_grad)


def solution(mesh):
    in_specs = (
        P("layer", "latent", None),
        P("layer", "latent", None),
        P("layer", None, "latent"),
        P("layer", "latent"),
        P(None, "layer", "latent", None),
        P(),
    )
    out_specs = (
        P(),
        P("layer", None, "latent"),
        P("layer", "latent"),
        P(None, "layer", "latent", None),
    )
    return jax.shard_map(shards, mesh=mesh, in_specs=in_specs, out_specs=out_specs, check_vma=False)
```

profile of v0, /device:TPU:1, one launch (start us, length us, event | category | flops | bytes accessed | tf_op | source)
XLA Modules:
  0.0 591.4 jit_solution(5166759479777857975)
XLA Ops:
  7.2 0.7 all-gather.6.cloned.1.call-update
  8.0 1.2 fusion.57
  11.0 1.5 and_reduce_fusion
  12.5 79.5 %all-gather.6.cloned.1.call-done = bf16[1,512,1792]{2,1,0:T(8,128)(2,1)} async-done(((bf16[1,8,1792]{2,1,0:T(8,128)(2,1)}), bf16[1,512,1792]{2,1,0:T(8,128)(2,1)}) %all-gather.6.cloned.1.call-update) | async-done | bytes 1835024 | tf_op jit(solution)/shard_map/all_gather | solution.py:39
  92.0 2.1 gather_fusion
  94.8 1.9 bitcast_dynamic-update-slice_fusion
  96.8 3.1 collective-permute-start
  99.9 3.3 fusion.20
  103.2 2.1 broadcast_in_dim.129
  105.3 8.1 %scatter_fusion = f32[8,64,1792]{2,1,0:T(8,128)} fusion(f32[8,64,1792]{2,1,0:T(8,128)} %broadcast_in_dim.129, s32[6]{0:T(128)S(1)} %get-tuple-element.105, f32[6,64,1792]{2,1,0:T(8,128)} %fusion.20), kind=kCustom, calls=%fused_computation.5 | custom fusion | flops 688128 | bytes 8257560 | tf_op jit(solution)/shard_map/scatter-add | solution.py:57
  113.4 3.0 collective-permute-start.1
  116.5 3.3 fusion.18
  119.8 8.1 %scatter_fusion.1 = f32[8,64,1792]{2,1,0:T(8,128)} fusion(f32[8,64,1792]{2,1,0:T(8,128)} %scatter_fusion, s32[6]{0:T(128)S(1)} %fusion.71, f32[6,64,1792]{2,1,0:T(8,128)} %fusion.18), kind=kCustom, calls=%fused_computation.6 | custom fusion | flops 688128 | bytes 8257560 | tf_op jit(solution)/shard_map/scatter-add | solution.py:57
  127.8 2.8 collective-permute-start.2
  130.6 3.3 fusion.16
  133.9 8.1 %scatter_fusion.2 = f32[8,64,1792]{2,1,0:T(8,128)} fusion(f32[8,64,1792]{2,1,0:T(8,128)} %scatter_fusion.1, s32[6]{0:T(128)S(1)} %fusion.72, f32[6,64,1792]{2,1,0:T(8,128)} %fusion.16), kind=kCustom, calls=%fused_computation.7 | custom fusion | flops 688128 | bytes 8257560 | tf_op jit(solution)/shard_map/scatter-add | solution.py:57
  142.0 3.3 fusion.14
  145.3 8.1 %scatter_fusion.3 = f32[8,64,1792]{2,1,0:T(8,128)} fusion(f32[8,64,1792]{2,1,0:T(8,128)} %scatter_fusion.2, s32[6]{0:T(128)S(1)} %get-tuple-element.106, f32[6,64,1792]{2,1,0:T(8,128)} %fusion.14), kind=kCustom, calls=%fused_computation.8 | custom fusion | flops 688128 | bytes 8257560 | tf_op jit(solution)/shard_map/scatter-add | solution.py:57
  153.5 133.9 %reduce-scatter.2.cloned.1.call-done = f32[8,1792]{1,0:T(8,128)} async-done(((f32[512,1792]{1,0:T(8,128)}), f32[8,1792]{1,0:T(8,128)}) %reduce-scatter.2.cloned.1.call-update) | async-done | bytes 57360 | tf_op jit(solution)/shard_map/reduce_scatter | solution.py:71
  287.4 2.1 fusion.42
  293.6 78.3 %all-gather.4.cloned.1.call-done = bf16[512,1792]{1,0:T(8,128)(2,1)} async-done(((bf16[8,1792]{1,0:T(8,128)(2,1)}), bf16[512,1792]{1,0:T(8,128)(2,1)}) %all-gather.4.cloned.1.call-update) | async-done | bytes 1835024 | tf_op jit(solution)/shard_map/all_gather | solution.py:77
  372.0 3.4 gather_fusion.1
  375.4 1.8 gather_fusion.2
  377.1 1.8 gather_fusion.3
  378.9 2.0 gather_fusion.4
  380.9 1.5 broadcast_select_fusion.3
  382.5 1.8 fusion.13
  384.6 1.1 copy-done.9
  385.9 1.6 copy-done.8
  387.7 1.3 copy-done.11
  390.8 1.1 copy-done.12
  392.0 1.4 collective-permute-start.3
  393.4 36.4 %collective-permute-done.3 = f32[4,384,256]{2,1,0:T(8,128)S(1)} collective-permute-done((f32[4,384,256]{2,1,0:T(8,128)S(1)}, f32[4,384,256]{2,1,0:T(8,128)S(1)}, u32[]{:S(2)}, u32[]{:S(2)}) %collective-permute-start.3) | collective-permute-done | bytes 1572896 | tf_op jit(solution)/shard_map/ppermute | solution.py:16
  430.0 1.3 collective-permute-start.4
  431.3 0.7 fusion.38
  432.0 34.7 %collective-permute-done.4 = f32[4,384,256]{2,1,0:T(8,128)S(1)} collective-permute-done((f32[4,384,256]{2,1,0:T(8,128)S(1)}, f32[4,384,256]{2,1,0:T(8,128)S(1)}, u32[]{:S(2)}, u32[]{:S(2)}) %collective-permute-start.4) | collective-permute-done | bytes 1572896 | tf_op jit(solution)/shard_map/ppermute | solution.py:16
  466.7 1.3 fusion.74
  468.0 1.3 collective-permute-start.5
  469.3 0.8 fusion.39
  470.1 0.7 fusion.40
  470.8 102.0 %psum.7 = f32[]{:T(128)} all-reduce(f32[]{:T(128)} %get-tuple-element.79), channel_id=1, replica_groups=mesh['layer'=4,'latent'=64] {'layer','latent'}, use_global_device_ids=true, to_apply=%region_22.24 | all-reduce | flops 1 | bytes 8 | tf_op jit(solution)/shard_map/psum | solution.py:75
  573.5 0.7 fusion.8
  574.1 0.7 copy-done.3
  575.5 0.7 copy-done.5
  576.8 0.7 copy-done.7
  578.2 2.1 maximum_bitcast_fusion
  580.3 1.3 fusion.76
  581.5 1.6 fusion.9
  (130 shorter events, 11.9 us)
Async XLA Ops:
  7.2 87.3 %copy-start = (bf16[1,1792,256]{2,1,0:T(8,128)(2,1)S(1)}, bf16[1,1792,256]{2,1,0:T(8,128)(2,1)}, u32[]{:S(2)}) copy-start(bf16[1,1792,256]{2,1,0:T(8,128)(2,1)} %param.18) | copy-start | bytes 2752516
  7.2 84.8 %all-gather.6.cloned.1.call-start = ((), (), s32[]{:S(2)}) async-start(), calls=%async_computation.3 | async-start | bytes 1863680 | tf_op jit(solution)/shard_map/all_gather | solution.py:39
  7.9 279.5 %reduce-scatter.2.cloned.1.call-start = ((), (), s32[]{:S(2)}) async-start(), calls=%async_computation.1 | async-start | bytes 3727360 | tf_op jit(solution)/shard_map/reduce_scatter | solution.py:71
  94.2 0.7 copy-start.27
  94.4 2.4 copy-start.13
  96.8 16.6 %collective-permute-start = (bf16[384,256]{1,0:T(8,128)(2,1)S(1)}, bf16[384,256]{1,0:T(8,128)(2,1)S(1)}, u32[]{:S(2)}, u32[]{:S(2)}) collective-permute-start(bf16[384,256]{1,0:T(8,128)(2,1)S(1)} %get-tuple-element.75), channel_id=1, source_target_pairs={{0,64},{64,128},{128,192},{1,65},{65,129},{129,193},{2,66},{66,130... | collective-permute-start | bytes 589832 | tf_op jit(solution)/shard_map/ppermute | solution.py:16
  113.4 6.4 %copy-start.17 = (bf16[384,256]{1,0:T(8,128)(2,1)}, bf16[384,256]{1,0:T(8,128)(2,1)S(1)}, u32[]{:S(2)}) copy-start(bf16[384,256]{1,0:T(8,128)(2,1)S(1)} %collective-permute-done) | copy-start | bytes 589828
  113.4 14.4 %collective-permute-start.1 = (bf16[384,256]{1,0:T(8,128)(2,1)S(1)}, bf16[384,256]{1,0:T(8,128)(2,1)S(1)}, u32[]{:S(2)}, u32[]{:S(2)}) collective-permute-start(bf16[384,256]{1,0:T(8,128)(2,1)S(1)} %collective-permute-done), channel_id=1, source_target_pairs={{0,64},{64,128},{128,192},{1,65},{65,129},{129,193},{2,66},{66,130... | collective-permute-start | bytes 589832 | tf_op jit(solution)/shard_map/ppermute | solution.py:16
  127.8 6.1 %copy-start.15 = (bf16[384,256]{1,0:T(8,128)(2,1)}, bf16[384,256]{1,0:T(8,128)(2,1)S(1)}, u32[]{:S(2)}) copy-start(bf16[384,256]{1,0:T(8,128)(2,1)S(1)} %collective-permute-done.1) | copy-start | bytes 589828
  127.8 14.1 %collective-permute-start.2 = (bf16[384,256]{1,0:T(8,128)(2,1)S(1)}, bf16[384,256]{1,0:T(8,128)(2,1)S(1)}, u32[]{:S(2)}, u32[]{:S(2)}) collective-permute-start(bf16[384,256]{1,0:T(8,128)(2,1)S(1)} %collective-permute-done.1), channel_id=1, source_target_pairs={{0,64},{64,128},{128,192},{1,65},{65,129},{129,193},{2,66},{66,130... | collective-permute-start | bytes 589832 | tf_op jit(solution)/shard_map/ppermute | solution.py:16
  142.0 3.4 copy-start.19
  153.4 134.0 %copy-start.22 = (bf16[1,8,1792]{2,1,0:T(8,128)(2,1)S(1)}, bf16[1,8,1792]{2,1,0:T(8,128)(2,1)}, u32[]{:S(2)}) copy-start(bf16[1,8,1792]{2,1,0:T(8,128)(2,1)} %param.17) | copy-start | bytes 86020
  153.4 218.5 %all-gather.4.cloned.1.call-start = ((), (), s32[]{:S(2)}) async-start(), calls=%async_computation.2 | async-start | bytes 1863680 | tf_op jit(solution)/shard_map/all_gather | solution.py:77
  371.9 3.4 copy-start.1
  378.9 2.0 copy-start.26
  382.4 1.9 copy-start.10
  382.4 1.9 copy-start.25
  384.3 1.3 copy-start.9
  384.3 1.3 copy-start.24
  384.3 1.5 copy-start.23
  385.7 3.9 copy-start.2
  385.7 1.8 copy-start.8
  385.7 3.3 copy-start.11
  387.5 2.1 copy-start.4
  387.7 2.4 copy-start.6
  390.8 1.2 copy-start.12
  392.0 39.3 %copy-start.18 = (bf16[384,256]{1,0:T(8,128)(2,1)S(1)}, bf16[384,256]{1,0:T(8,128)(2,1)}, u32[]{:S(2)}) copy-start(bf16[384,256]{1,0:T(8,128)(2,1)} %copy-done.17) | copy-start | bytes 589828
  392.0 37.8 %collective-permute-start.3 = (f32[4,384,256]{2,1,0:T(8,128)S(1)}, f32[4,384,256]{2,1,0:T(8,128)S(1)}, u32[]{:S(2)}, u32[]{:S(2)}) collective-permute-start(f32[4,384,256]{2,1,0:T(8,128)S(1)} %pad_maximum_fusion), channel_id=1, source_target_pairs={{64,0},{128,64},{192,128},{65,1},{129,65},{193,129},{66,2},{130,66... | collective-permute-start | bytes 4718600 | tf_op jit(solution)/shard_map/ppermute | solution.py:16
  430.0 36.7 %collective-permute-start.4 = (f32[4,384,256]{2,1,0:T(8,128)S(1)}, f32[4,384,256]{2,1,0:T(8,128)S(1)}, u32[]{:S(2)}, u32[]{:S(2)}) collective-permute-start(f32[4,384,256]{2,1,0:T(8,128)S(1)} %fusion.75), channel_id=1, source_target_pairs={{64,0},{128,64},{192,128},{65,1},{129,65},{193,129},{66,2},{130,66... | collective-permute-start | bytes 4718600 | tf_op jit(solution)/shard_map/ppermute | solution.py:16
  432.0 37.3 %copy-start.16 = (bf16[384,256]{1,0:T(8,128)(2,1)S(1)}, bf16[384,256]{1,0:T(8,128)(2,1)}, u32[]{:S(2)}) copy-start(bf16[384,256]{1,0:T(8,128)(2,1)} %copy-done.15) | copy-start | bytes 589828
  432.0 38.1 %copy-start.20 = (bf16[384,256]{1,0:T(8,128)(2,1)S(1)}, bf16[384,256]{1,0:T(8,128)(2,1)}, u32[]{:S(2)}) copy-start(bf16[384,256]{1,0:T(8,128)(2,1)} %copy-done.19) | copy-start | bytes 589828
  468.0 112.2 %collective-permute-start.5 = (f32[4,384,256]{2,1,0:T(8,128)}, f32[4,384,256]{2,1,0:T(8,128)}, u32[]{:S(2)}, u32[]{:S(2)}) collective-permute-start(f32[4,384,256]{2,1,0:T(8,128)} %fusion.74), channel_id=1, source_target_pairs={{64,0},{128,64},{192,128},{65,1},{129,65},{193,129},{66,2},{130,66... | collective-permute-start | bytes 4718600 | tf_op jit(solution)/shard_map/ppermute | solution.py:16
  573.5 1.3 copy-start.3
  574.8 1.3 copy-start.5
  576.1 1.3 copy-start.7
  578.1 2.1 copy-start.21
  578.2 3.4 copy-start.14
Sparse Core Ops, SparseCore 0:
  10.7 81.2 all-gather.5
  153.6 133.8 reduce-scatter.1
  291.1 80.8 all-gather.3
where the time goes:
time: 592 us; the launch traced here: 591 us
  waiting for transfers between devices  364 us (61%)
  blocking collectives  102 us (17%)
  other arithmetic  52.8 us (9%)
  matrix products  22.8 us (4%)
  local copies, waits for them, and re-layouts  21.1 us (4%)
  between operations  16.1 us (3%)
  starting transfers between devices  13 us (2%)
    reduce_scatter x1, waiting for transfers between devices, shards(): lax.psum_scatter(writes.reshape(NTILE * TILE, D), 'latent', scatter_dimen...  134 us
    psum x1, blocking collectives, shards(): total = lax.psum(jnp.sum(errors * errors), ('layer', 'latent'))  102 us
    all_gather x1, waiting for transfers between devices, shards(): lax.all_gather(residual[0], 'latent', axis=0, tiled=True)  79.5 us
    all_gather x1, waiting for transfers between devices, shards(): lax.all_gather(errors.astype(jnp.bfloat16), 'latent', axis=0, tiled=True)  78.3 us
    ppermute x6, waiting for transfers between devices, shifted(): lax.ppermute(value, axis, [(source, source + steps) for source in range(l...  71.1 us
    scatter-add x4, other arithmetic, take_source(): writes = writes.at[tile_ids].add(product)  32.3 us
    dot_general x4, matrix products, take_source(): jnp.dot(portion, weight, preferred_element_type=jnp.float32)  13.2 us
    ppermute x6, starting transfers between devices, shifted(): lax.ppermute(value, axis, [(source, source + steps) for source in range(l...  12.9 us
  transfers between devices with their start and end apart: 9, of which 5 were waited for; matrix products, arithmetic and copies ran while one was open for 9% of the time, Pallas kernels for 0%

commit v1 on v0

v1 whole, which is shorter than its diff:
```python
import jax
import jax.numpy as jnp
from jax import lax
from jax.sharding import PartitionSpec as P

TILE = 64
NTILE = 8
Y, Z, C = 4, 8, 2
BF = jnp.bfloat16
F32 = jnp.float32


def index_of(y, z, c):
    return ((y % Y) * Z + z % Z) * C + c


def pairs(move, cores=(0, 1)):
    return [
        (index_of(y, z, c), index_of(*move(y, z, c)))
        for y in range(Y)
        for z in range(Z)
        for c in cores
    ]


def send(value, move, cores=(0, 1)):
    return lax.ppermute(value, "latent", pairs(move, cores))


def swap(value):
    return send(value, lambda y, z, c: (y, z, 1 - c))


def send_layer(value, steps):
    count = lax.axis_size("layer")
    sources = [s for s in range(count) if 0 <= s + steps < count]
    return lax.ppermute(value, "layer", [(s, s + steps) for s in sources])


def chip_rows(value, core):
    other = swap(value)
    return jnp.where(core == 0, jnp.concatenate([value, other]), jnp.concatenate([other, value]))


def spread(chip, core):
    near = [
        send(chip, lambda y, z, c, k=k: (y, z + k if c == 0 else z - k, c)) for k in (1, 2, 3)
    ]
    far = send(chip, lambda y, z, c: (y, z + 4, c), (1,))
    first = jnp.where(core == 0, chip, far)
    row = jnp.concatenate([first] + near)
    parts = [row] + [send(row, lambda y, z, c, k=k: (y + k, z, c)) for k in (1, 2, 3)]
    return jnp.concatenate(parts + [swap(part) for part in parts])


def collect(partial, core):
    width = partial.shape[-1]
    halves = partial.reshape(2, Y, 4 * 2 * 8, width)
    own = [
        (halves[0, k].astype(F32) + swap(halves[1, k]).astype(F32)).astype(BF) for k in range(Y)
    ]
    row = own[0].astype(F32)
    for k in (1, 2, 3):
        row = row + send(own[k], lambda y, z, c, k=k: (y - k, z, c)).astype(F32)
    row = row.astype(BF).reshape(4, 16, width)
    total = jnp.where(core == 0, row[0], send(row[0], lambda y, z, c: (y, z + 4, c), (1,)))
    total = total.astype(F32)
    for k in (1, 2, 3):
        piece = send(row[k], lambda y, z, c, k=k: (y, z - k if c == 0 else z + k, c))
        total = total + piece.astype(F32)
    total = total.astype(BF)
    return total.astype(F32) + swap(total).astype(F32)


def shard_chips(latent):
    y, z, c = latent // (Z * C), latent // C % Z, latent % C
    p = jnp.arange(Y * Z, dtype=jnp.int32)
    half, step, j = p // 16, p // 4 % 4, p % 4
    side = (half + c) % 2
    from_z = jnp.where(side == 0, z - j, jnp.where(j == 0, z + 4, z + j)) % Z
    return (y - step) % Y * Z + from_z


def shards(residual, target, enc_weight, enc_bias, dec_weight, active):
    layers = dec_weight.shape[0]
    width = residual.shape[-1]
    layer = lax.axis_index("layer")
    latent = lax.axis_index("latent")
    core = latent % C
    chips = shard_chips(latent)
    names = lax.dynamic_index_in_dim(active, layer, 0, keepdims=False)
    hit = jnp.any(names == latent, axis=1)
    tile = chips // 4
    live = jnp.any((tile[:, None] == jnp.arange(NTILE)[None, :]) & hit[None, :], axis=1)
    live = jnp.repeat(live, 16)[:, None]

    rows = spread(chip_rows(residual[0], core), core)
    goal = chip_rows(target[0], core)
    preact = jnp.dot(rows, enc_weight[0], preferred_element_type=F32) + enc_bias[0][None, :]
    on = live & (preact > 0)
    codes = jnp.where(on, preact, 0.0).astype(BF)
    dec = dec_weight[:, 0]
    sources = [codes] + [send_layer(codes, k) for k in range(1, layers)]
    weights = [
        lax.dynamic_index_in_dim(dec, (layer - k) % layers, 0, keepdims=False)
        for k in range(layers)
    ]
    partial = jnp.dot(
        jnp.concatenate(sources, axis=1), jnp.concatenate(weights), preferred_element_type=F32
    ).astype(BF)
    errors = collect(partial, core) - goal.astype(F32)
    full = spread(errors.astype(BF), core)

    backs = [
        lax.dot_general(full, weight, (((1,), (1,)), ((), ())), preferred_element_type=F32)
        for weight in weights
    ]
    mine = backs[0]
    for k in range(1, layers):
        mine = mine + send_layer(backs[k].astype(BF), -k).astype(F32)

    square = full.astype(F32).reshape(Y * Z, 16, width)
    square = jnp.sum(square * square, axis=(1, 2))
    place = chips[None, :] == jnp.arange(Y * Z)[:, None]
    square = jnp.sum(jnp.sum(jnp.where(place, square[None, :], 0.0), axis=1))
    square = jnp.full((8, 128), square)
    ring = [(s, (s + 1) % layers) for s in range(layers)]
    loss = jnp.zeros((layers, 8, 128), F32)
    moving = square
    for k in range(layers):
        loss = lax.dynamic_update_index_in_dim(loss, moving, (layer - k) % layers, 0)
        if k < layers - 1:
            moving = lax.ppermute(moving, "layer", ring)
    loss = loss[:, 0, 0]
    total = loss[0]
    for s in range(1, layers):
        total = total + loss[s]
    total = 0.5 * total / (layers * NTILE * TILE * width)

    placed = jnp.stack(
        [
            sum(
                jnp.where((layer - k) % layers == s, sources[k], jnp.zeros_like(codes))
                for k in range(layers)
            )
            for s in range(layers)
        ]
    )
    dec_grad = jnp.stack(
        [
            lax.dot_general(
                placed[s], full, (((0,), (0,)), ((), ())), preferred_element_type=F32
            )
            for s in range(layers)
        ]
    )
    dec_grad = (dec_grad / TILE).astype(BF)[:, None]
    pre_grad = jnp.where(on, mine, 0.0)
    bias_grad = (jnp.sum(pre_grad, axis=0) / TILE)[None]
    enc_grad = lax.dot_general(
        rows, pre_grad.astype(BF), (((0,), (0,)), ((), ())), preferred_element_type=F32
    )
    enc_grad = (enc_grad / TILE).astype(BF)[None]
    return (total, enc_grad, bias_grad, dec_grad)


def solution(mesh):
    in_specs = (
        P("layer", "latent", None),
        P("layer", "latent", None),
        P("layer", None, "latent"),
        P("layer", "latent"),
        P(None, "layer", "latent", None),
        P(),
    )
    out_specs = (
        P(),
        P("layer", None, "latent"),
        P("layer", "latent"),
        P(None, "layer", "latent", None),
    )
    return jax.shard_map(shards, mesh=mesh, in_specs=in_specs, out_specs=out_specs, check_vma=False)
```

time: 592 us -> 161 us (0.27)
  waiting for transfers between devices: 364 us -> 51.4 us
  blocking collectives: 102 us -> 0 us
  starting transfers between devices: 13 us -> 74.2 us
  other arithmetic: 52.8 us -> 10.6 us
  local copies, waits for them, and re-layouts: 21.1 us -> 4.1 us
  between operations: 16.1 us -> 5.08 us
  matrix products: 22.8 us -> 13.7 us
    all_gather x2 -> x0, waiting for transfers between devices: 158 us -> none  [the longest x1 79.5 us: shards(): lax.all_gather(residual[0], 'latent', axis=0, tiled=True)]
    reduce_scatter x1 -> x0, waiting for transfers between devices: 134 us -> none  [shards(): lax.psum_scatter(writes.reshape(NTILE * TILE, D), 'latent', scatter_dimen...]
    psum x1 -> x0, blocking collectives: 102 us -> none  [shards(): total = lax.psum(jnp.sum(errors * errors), ('layer', 'latent'))]
    ppermute x6 -> x45, starting transfers between devices: 12.9 us -> 74.2 us  [the longest x36 58.6 us: send(): return lax.ppermute(value, 'latent', pairs(move, cores))]
    scatter-add x4 -> x0, other arithmetic: 32.3 us -> none  [take_source(): writes = writes.at[tile_ids].add(product)]
    ppermute x6 -> x45, waiting for transfers between devices: 71.1 us -> 51.4 us  [the longest x36 34.6 us: send(): return lax.ppermute(value, 'latent', pairs(move, cores))]
    gather x5 -> x0, local copies, waits for them, and re-layouts: 11.1 us -> none  [the longest x4 8.94 us: shards(): error_part = jnp.take(full_errors, tile_ids, axis=0).reshape(slot_rows, D)]
    dot_general x14 -> x11, matrix products: 22.8 us -> 13.7 us  [the longest x4 4.91 us: shards(): lax.dot_general(full, weight, (((1,), (1,)), ((), ())), preferred_element...]
  transfers between devices with their start and end apart: 9 -> 45, of which waited for: 5 -> 21; matrix products, arithmetic and copies ran while one was open for 9% -> 7% of each run, Pallas kernels for 0% -> 0%
where the time goes in v1:
time: 161 us; the launch traced here: 159 us
  starting transfers between devices  74.2 us (46%)
  waiting for transfers between devices  51.4 us (32%)
  matrix products  13.7 us (9%)
  other arithmetic  10.6 us (7%)
  between operations  5.08 us (3%)
  local copies, waits for them, and re-layouts  4.1 us (3%)
    ppermute x36, starting transfers between devices, send(): return lax.ppermute(value, 'latent', pairs(move, cores))  58.6 us
    ppermute x36, waiting for transfers between devices, send(): return lax.ppermute(value, 'latent', pairs(move, cores))  34.6 us
    ppermute x6, starting transfers between devices, send_layer(): return lax.ppermute(value, 'layer', [(s, s + steps) for s in sources])  12.2 us
    ppermute x3, waiting for transfers between devices, shards(): moving = lax.ppermute(moving, 'layer', ring)  8.51 us
    ppermute x6, waiting for transfers between devices, send_layer(): return lax.ppermute(value, 'layer', [(s, s + steps) for s in sources])  8.21 us
    dot_general x4, matrix products, shards(): lax.dot_general(full, weight, (((1,), (1,)), ((), ())), preferred_element...  4.91 us
    dot_general x4, matrix products, shards(): lax.dot_general(placed[s], full, (((0,), (0,)), ((), ())), preferred_elem...  3.71 us
    ppermute x3, starting transfers between devices, shards(): moving = lax.ppermute(moving, 'layer', ring)  3.5 us
  transfers between devices with their start and end apart: 45, of which 21 were waited for; matrix products, arithmetic and copies ran while one was open for 7% of the time, Pallas kernels for 0%

profile of v1, /device:TPU:1, one launch (start us, length us, event | category | flops | bytes accessed | tf_op | source)
XLA Modules:
  0.0 159.1 jit_solution(6604315913161557554)
XLA Ops:
  0.6 3.3 %collective-permute-start = (bf16[8,1792]{1,0:T(8,128)(2,1)}, bf16[8,1792]{1,0:T(8,128)(2,1)S(1)}, u32[]{:S(2)}, u32[]{:S(2)}) collective-permute-start(bf16[8,1792]{1,0:T(8,128)(2,1)} %bitcast.81), channel_id=1, source_target_pairs={{0,1},{1,0},{2,3},{3,2},{4,5},{5,4},{6,7},{7,6},{8,9},{9,8},{10,11... | collective-permute-start | bytes 86024 | tf_op jit(solution)/shard_map/ppermute | solution.py:27
  6.2 7.1 %collective-permute-start.1 = (bf16[16,1792]{1,0:T(8,128)(2,1)S(1)}, bf16[16,1792]{1,0:T(8,128)(2,1)S(1)}, u32[]{:S(2)}, u32[]{:S(2)}) collective-permute-start(bf16[16,1792]{1,0:T(8,128)(2,1)S(1)} %maximum_select_fusion), channel_id=1, source_target_pairs={{1,9},{3,11},{5,13},{7,15},{9,1},{11,3},{13,5},{15,7},{17,25},{19,... | collective-permute-start | bytes 172040 | tf_op jit(solution)/shard_map/ppermute | solution.py:27
  13.7 4.7 %collective-permute-start.4 = (bf16[16,1792]{1,0:T(8,128)(2,1)S(1)}, bf16[16,1792]{1,0:T(8,128)(2,1)S(1)}, u32[]{:S(2)}, u32[]{:S(2)}) collective-permute-start(bf16[16,1792]{1,0:T(8,128)(2,1)S(1)} %maximum_select_fusion), channel_id=1, source_target_pairs={{0,6},{1,11},{2,8},{3,13},{4,10},{5,15},{6,12},{7,1},{8,14},{9,3},... | collective-permute-start | bytes 172040 | tf_op jit(solution)/shard_map/ppermute | solution.py:27
  19.7 1.4 collective-permute-start.5
  21.0 2.6 %collective-permute-start.6 = (bf16[64,1792]{1,0:T(8,128)(2,1)S(1)}, bf16[64,1792]{1,0:T(8,128)(2,1)S(1)}, u32[]{:S(2)}, u32[]{:S(2)}) collective-permute-start(bf16[64,1792]{1,0:T(8,128)(2,1)S(1)} %pad_maximum_fusion), channel_id=1, source_target_pairs={{0,32},{1,33},{2,34},{3,35},{4,36},{5,37},{6,38},{7,39},{8,40},{9,... | collective-permute-start | bytes 688136 | tf_op jit(solution)/shard_map/ppermute | solution.py:27
  24.8 2.9 %collective-permute-done.5 = bf16[64,1792]{1,0:T(8,128)(2,1)S(1)} collective-permute-done((bf16[64,1792]{1,0:T(8,128)(2,1)S(1)}, bf16[64,1792]{1,0:T(8,128)(2,1)S(1)}, u32[]{:S(2)}, u32[]{:S(2)}) %collective-permute-start.5) | collective-permute-done | bytes 229408 | tf_op jit(solution)/shard_map/ppermute | solution.py:27
  27.8 6.0 %collective-permute-done.6 = bf16[64,1792]{1,0:T(8,128)(2,1)S(1)} collective-permute-done((bf16[64,1792]{1,0:T(8,128)(2,1)S(1)}, bf16[64,1792]{1,0:T(8,128)(2,1)S(1)}, u32[]{:S(2)}, u32[]{:S(2)}) %collective-permute-start.6) | collective-permute-done | bytes 229408 | tf_op jit(solution)/shard_map/ppermute | solution.py:27
  35.7 1.4 select_convert_fusion
  37.2 4.5 %collective-permute-start.14 = (bf16[512,256]{1,0:T(8,128)(2,1)S(1)}, bf16[512,256]{1,0:T(8,128)(2,1)S(1)}, u32[]{:S(2)}, u32[]{:S(2)}) collective-permute-start(bf16[512,256]{1,0:T(8,128)(2,1)S(1)} %get-tuple-element.29), channel_id=1, source_target_pairs={{0,192},{1,193},{2,194},{3,195},{4,196},{5,197},{6,198},{7,199},{8... | collective-permute-start | bytes 786440 | tf_op jit(solution)/shard_map/ppermute | solution.py:37
  41.7 1.3 collective-permute-start.13
  43.0 2.5 %collective-permute-start.12 = (bf16[512,256]{1,0:T(8,128)(2,1)S(1)}, bf16[512,256]{1,0:T(8,128)(2,1)S(1)}, u32[]{:S(2)}, u32[]{:S(2)}) collective-permute-start(bf16[512,256]{1,0:T(8,128)(2,1)S(1)} %get-tuple-element.29), channel_id=1, source_target_pairs={{0,64},{64,128},{128,192},{1,65},{65,129},{129,193},{2,66},{66,130... | collective-permute-start | bytes 786440 | tf_op jit(solution)/shard_map/ppermute | solution.py:37
  45.9 6.8 %collective-permute-done.14 = bf16[512,256]{1,0:T(8,128)(2,1)S(1)} collective-permute-done((bf16[512,256]{1,0:T(8,128)(2,1)S(1)}, bf16[512,256]{1,0:T(8,128)(2,1)S(1)}, u32[]{:S(2)}, u32[]{:S(2)}) %collective-permute-start.14) | collective-permute-done | bytes 262176 | tf_op jit(solution)/shard_map/ppermute | solution.py:37
  52.7 1.4 collective-permute-done.12
  54.1 2.1 %fusion.9 = bf16[512,1792]{1,0:T(8,128)(2,1)S(1)} fusion(bf16[256,1792]{1,0:T(8,128)(2,1)S(1)} %get-tuple-element.12, bf16[256,1792]{1,0:T(8,128)(2,1)S(1)} %get-tuple-element.13, bf16[256,1792]{1,0:T(8,128)(2,1)S(1)} %get-tuple-element.11, bf16[256,1792]{1,0:T(8,128)(2,1)S(1)} %get-tuple-element.10, bf16[512,256]{1,0:T(8,128)(2,1)S(1)} %collective-permute-done.14, ...), kind=kOutput, calls=%fused_computation.11 | convolution fusion | flops 1898840064 | bytes 6553600 | tf_op jit(solution)/shard_map/dot_general | solution.py:108
  56.3 1.2 collective-permute-start.16
  59.4 1.2 collective-permute-start.21
  60.7 2.0 %collective-permute-start.19 = (bf16[64,1792]{1,0:T(8,128)(2,1)S(1)}, bf16[64,1792]{1,0:T(8,128)(2,1)S(1)}, u32[]{:S(2)}, u32[]{:S(2)}) collective-permute-start(bf16[64,1792]{1,0:T(8,128)(2,1)S(1)} %get-tuple-element.20), channel_id=1, source_target_pairs={{0,32},{1,33},{2,34},{3,35},{4,36},{5,37},{6,38},{7,39},{8,40},{9,... | collective-permute-start | bytes 688136 | tf_op jit(solution)/shard_map/ppermute | solution.py:27
  62.7 1.2 collective-permute-start.17
  63.9 3.7 %collective-permute-done.21 = bf16[64,1792]{1,0:T(8,128)(2,1)S(1)} collective-permute-done((bf16[64,1792]{1,0:T(8,128)(2,1)S(1)}, bf16[64,1792]{1,0:T(8,128)(2,1)S(1)}, u32[]{:S(2)}, u32[]{:S(2)}) %collective-permute-start.21) | collective-permute-done | bytes 229408 | tf_op jit(solution)/shard_map/ppermute | solution.py:27
  67.6 5.4 %collective-permute-done.19 = bf16[64,1792]{1,0:T(8,128)(2,1)S(1)} collective-permute-done((bf16[64,1792]{1,0:T(8,128)(2,1)S(1)}, bf16[64,1792]{1,0:T(8,128)(2,1)S(1)}, u32[]{:S(2)}, u32[]{:S(2)}) %collective-permute-start.19) | collective-permute-done | bytes 229408 | tf_op jit(solution)/shard_map/ppermute | solution.py:27
  73.2 1.8 %collective-permute-start.25 = (bf16[16,1792]{1,0:T(8,128)(2,1)S(1)}, bf16[16,1792]{1,0:T(8,128)(2,1)S(1)}, u32[]{:S(2)}, u32[]{:S(2)}) collective-permute-start(bf16[16,1792]{1,0:T(8,128)(2,1)S(1)} %get-tuple-element.22), channel_id=1, source_target_pairs={{0,10},{1,7},{2,12},{3,9},{4,14},{5,11},{6,0},{7,13},{8,2},{9,15},... | collective-permute-start | bytes 172040 | tf_op jit(solution)/shard_map/ppermute | solution.py:27
  75.0 4.2 %collective-permute-start.24 = (bf16[16,1792]{1,0:T(8,128)(2,1)S(1)}, bf16[16,1792]{1,0:T(8,128)(2,1)S(1)}, u32[]{:S(2)}, u32[]{:S(2)}) collective-permute-start(bf16[16,1792]{1,0:T(8,128)(2,1)S(1)} %get-tuple-element.23), channel_id=1, source_target_pairs={{0,12},{1,5},{2,14},{3,7},{4,0},{5,9},{6,2},{7,11},{8,4},{9,13},{1... | collective-permute-start | bytes 172040 | tf_op jit(solution)/shard_map/ppermute | solution.py:27
  79.2 5.2 %collective-permute-start.22 = (bf16[16,1792]{1,0:T(8,128)(2,1)S(1)}, bf16[16,1792]{1,0:T(8,128)(2,1)S(1)}, u32[]{:S(2)}, u32[]{:S(2)}) collective-permute-start(bf16[16,1792]{1,0:T(8,128)(2,1)S(1)} %get-tuple-element.21), channel_id=1, source_target_pairs={{1,9},{3,11},{5,13},{7,15},{9,1},{11,3},{13,5},{15,7},{17,25},{19,... | collective-permute-start | bytes 172040 | tf_op jit(solution)/shard_map/ppermute | solution.py:27
  84.4 3.6 %collective-permute-done.22 = bf16[16,1792]{1,0:T(8,128)(2,1)S(1)} collective-permute-done((bf16[16,1792]{1,0:T(8,128)(2,1)S(1)}, bf16[16,1792]{1,0:T(8,128)(2,1)S(1)}, u32[]{:S(2)}, u32[]{:S(2)}) %collective-permute-start.22) | collective-permute-done | bytes 57376 | tf_op jit(solution)/shard_map/ppermute | solution.py:27
  90.2 5.8 %collective-permute-start.28 = (bf16[16,1792]{1,0:T(8,128)(2,1)}, bf16[16,1792]{1,0:T(8,128)(2,1)}, u32[]{:S(2)}, u32[]{:S(2)}) collective-permute-start(bf16[16,1792]{1,0:T(8,128)(2,1)} %subtract_convert_fusion), channel_id=1, source_target_pairs={{1,9},{3,11},{5,13},{7,15},{9,1},{11,3},{13,5},{15,7},{17,25},{19,... | collective-permute-start | bytes 172040 | tf_op jit(solution)/shard_map/ppermute | solution.py:27
  97.0 3.7 %collective-permute-start.31 = (bf16[16,1792]{1,0:T(8,128)(2,1)}, bf16[16,1792]{1,0:T(8,128)(2,1)S(1)}, u32[]{:S(2)}, u32[]{:S(2)}) collective-permute-start(bf16[16,1792]{1,0:T(8,128)(2,1)} %subtract_convert_fusion), channel_id=1, source_target_pairs={{0,6},{1,11},{2,8},{3,13},{4,10},{5,15},{6,12},{7,1},{8,14},{9,3},... | collective-permute-start | bytes 172040 | tf_op jit(solution)/shard_map/ppermute | solution.py:27
  101.6 1.1 collective-permute-done.31
  102.7 2.2 %collective-permute-start.32 = (bf16[64,1792]{1,0:T(8,128)(2,1)S(1)}, bf16[64,1792]{1,0:T(8,128)(2,1)S(1)}, u32[]{:S(2)}, u32[]{:S(2)}) collective-permute-start(bf16[64,1792]{1,0:T(8,128)(2,1)S(1)} %pad_maximum_fusion.1), channel_id=1, source_target_pairs={{0,16},{1,17},{2,18},{3,19},{4,20},{5,21},{6,22},{7,23},{8,24},{9,... | collective-permute-start | bytes 688136 | tf_op jit(solution)/shard_map/ppermute | solution.py:27
  104.9 2.3 %collective-permute-start.33 = (bf16[64,1792]{1,0:T(8,128)(2,1)S(1)}, bf16[64,1792]{1,0:T(8,128)(2,1)S(1)}, u32[]{:S(2)}, u32[]{:S(2)}) collective-permute-start(bf16[64,1792]{1,0:T(8,128)(2,1)S(1)} %pad_maximum_fusion.1), channel_id=1, source_target_pairs={{0,32},{1,33},{2,34},{3,35},{4,36},{5,37},{6,38},{7,39},{8,40},{9,... | collective-permute-start | bytes 688136 | tf_op jit(solution)/shard_map/ppermute | solution.py:27
  107.4 1.7 %collective-permute-start.35 = (bf16[64,1792]{1,0:T(8,128)(2,1)S(1)}, bf16[64,1792]{1,0:T(8,128)(2,1)S(1)}, u32[]{:S(2)}, u32[]{:S(2)}) collective-permute-start(bf16[64,1792]{1,0:T(8,128)(2,1)S(1)} %pad_maximum_fusion.1), channel_id=1, source_target_pairs={{0,1},{1,0},{2,3},{3,2},{4,5},{5,4},{6,7},{7,6},{8,9},{9,8},{10,11... | collective-permute-start | bytes 688136 | tf_op jit(solution)/shard_map/ppermute | solution.py:27
  109.1 1.9 %collective-permute-done.32 = bf16[64,1792]{1,0:T(8,128)(2,1)S(1)} collective-permute-done((bf16[64,1792]{1,0:T(8,128)(2,1)S(1)}, bf16[64,1792]{1,0:T(8,128)(2,1)S(1)}, u32[]{:S(2)}, u32[]{:S(2)}) %collective-permute-start.32) | collective-permute-done | bytes 229408 | tf_op jit(solution)/shard_map/ppermute | solution.py:27
  111.1 1.5 collective-permute-start.36
  112.6 4.9 %collective-permute-done.33 = bf16[64,1792]{1,0:T(8,128)(2,1)S(1)} collective-permute-done((bf16[64,1792]{1,0:T(8,128)(2,1)S(1)}, bf16[64,1792]{1,0:T(8,128)(2,1)S(1)}, u32[]{:S(2)}, u32[]{:S(2)}) %collective-permute-start.33) | collective-permute-done | bytes 229408 | tf_op jit(solution)/shard_map/ppermute | solution.py:27
  117.5 1.1 collective-permute-start.37
  121.3 1.4 convolution_convert_fusion
  122.7 1.4 convolution_convert_fusion.1
  124.1 1.4 convolution_convert_fusion.2
  126.9 1.3 select_reduce_fusion
  128.7 2.3 %collective-permute-start.39 = (f32[8,128]{1,0:T(8,128)S(1)}, f32[8,128]{1,0:T(8,128)S(1)}, u32[]{:S(2)}, u32[]{:S(2)}) collective-permute-start(f32[8,128]{1,0:T(8,128)S(1)} %broadcast_in_dim.58), channel_id=1, source_target_pairs={{0,64},{64,128},{128,192},{192,0},{1,65},{65,129},{129,193},{193,1... | collective-permute-start | bytes 12296 | tf_op jit(solution)/shard_map/ppermute | solution.py:133
  131.0 1.3 collective-permute-start.44
  132.3 1.3 collective-permute-start.43
  133.6 1.3 collective-permute-start.42
  134.9 1.6 %convolution_bitcast_fusion = f32[1,1,256,1792]{3,2,1,0:T(8,128)S(1)} fusion(bf16[512,1792]{1,0:T(8,128)(2,1)S(1)} %constant_dynamic-update-slice_fusion.11, bf16[512,256]{1,0:T(8,128)(2,1)S(1)} %collective-permute-done.14, bf16[512,256]{1,0:T(8,128)(2,1)S(1)} %collective-permute-done.13, bf16[512,256]{1,0:T(8,128)(2,1)} %copy-done.1, ...), kind=kOutput, calls=%fused_computation.13 | convolution fusion | flops 470679552 | bytes 4718596 | tf_op jit(solution)/shard_map/dot_general | solution.py:151
  138.6 2.1 %fusion = bf16[4,1,256,1792]{3,2,1,0:T(8,128)(2,1)} fusion(f32[1,1,256,1792]{3,2,1,0:T(8,128)S(1)} %convolution_bitcast_fusion, f32[1,1,256,1792]{3,2,1,0:T(8,128)S(1)} %convolution_bitcast_fusion.1, f32[1,1,256,1792]{3,2,1,0:T(8,128)S(1)} %convolution_bitcast_fusion.2, f32[1,1,256,1792]{3,2,1,0:T(8,128)S(1)} %convolution_bitcast_fusion.3), kind=kLoop, calls=%fused_computation.1 | loop fusion | flops 9175040 | bytes 11010048 | tf_op jit(solution)/shard_map/convert_element_type | solution.py:157
  141.3 1.2 collective-permute-start.40
  142.5 4.8 %collective-permute-done.40 = f32[8,128]{1,0:T(8,128)S(1)} collective-permute-done((f32[8,128]{1,0:T(8,128)S(1)}, f32[8,128]{1,0:T(8,128)S(1)}, u32[]{:S(2)}, u32[]{:S(2)}) %collective-permute-start.40) | collective-permute-done | bytes 4128 | tf_op jit(solution)/shard_map/ppermute | solution.py:133
  147.4 3.7 %collective-permute-done.41 = f32[8,128]{1,0:T(8,128)S(1)} collective-permute-done((f32[8,128]{1,0:T(8,128)S(1)}, f32[8,128]{1,0:T(8,128)S(1)}, u32[]{:S(2)}, u32[]{:S(2)}) %collective-permute-start.41) | collective-permute-done | bytes 4128 | tf_op jit(solution)/shard_map/ppermute | solution.py:133
  155.8 1.6 %fusion.13 = bf16[1,1792,256]{2,1,0:T(8,128)(2,1)} fusion(bf16[512,1792]{1,0:T(8,128)(2,1)S(1)} %copy-done.14, bf16[512,256]{1,0:T(8,128)(2,1)S(1)} %get-tuple-element.32), kind=kOutput, calls=%fused_computation.18 | convolution fusion | flops 470679552 | bytes 3014656 | tf_op jit(solution)/shard_map/dot_general | solution.py:160
  (141 shorter events, 23.5 us)
Async XLA Ops:
  0.6 35.1 %copy-start = (bf16[1,1792,256]{2,1,0:T(8,128)(2,1)S(1)}, bf16[1,1792,256]{2,1,0:T(8,128)(2,1)}, u32[]{:S(2)}) copy-start(bf16[1,1792,256]{2,1,0:T(8,128)(2,1)} %param.8) | copy-start | bytes 2752516
  0.6 4.7 %collective-permute-start = (bf16[8,1792]{1,0:T(8,128)(2,1)}, bf16[8,1792]{1,0:T(8,128)(2,1)S(1)}, u32[]{:S(2)}, u32[]{:S(2)}) collective-permute-start(bf16[8,1792]{1,0:T(8,128)(2,1)} %bitcast.81), channel_id=1, source_target_pairs={{0,1},{1,0},{2,3},{3,2},{4,5},{5,4},{6,7},{7,6},{8,9},{9,8},{10,11... | collective-permute-start | bytes 86024 | tf_op jit(solution)/shard_map/ppermute | solution.py:27
  6.2 12.2 %collective-permute-start.1 = (bf16[16,1792]{1,0:T(8,128)(2,1)S(1)}, bf16[16,1792]{1,0:T(8,128)(2,1)S(1)}, u32[]{:S(2)}, u32[]{:S(2)}) collective-permute-start(bf16[16,1792]{1,0:T(8,128)(2,1)S(1)} %maximum_select_fusion), channel_id=1, source_target_pairs={{1,9},{3,11},{5,13},{7,15},{9,1},{11,3},{13,5},{15,7},{17,25},{19,... | collective-permute-start | bytes 172040 | tf_op jit(solution)/shard_map/ppermute | solution.py:27
  13.5 22.2 %copy-start.15 = (pred[512]{0:T(512)(128)(4,1)}, pred[512]{0:T(512)(128)(4,1)S(1)}, u32[]{:S(2)}) copy-start(pred[512]{0:T(512)(128)(4,1)S(1)} %and.242) | copy-start | bytes 1540
  13.5 5.7 %collective-permute-start.2 = (bf16[16,1792]{1,0:T(8,128)(2,1)S(1)}, bf16[16,1792]{1,0:T(8,128)(2,1)S(1)}, u32[]{:S(2)}, u32[]{:S(2)}) collective-permute-start(bf16[16,1792]{1,0:T(8,128)(2,1)S(1)} %maximum_select_fusion), channel_id=1, source_target_pairs={{0,2},{1,15},{2,4},{3,1},{4,6},{5,3},{6,8},{7,5},{8,10},{9,7},{10,... | collective-permute-start | bytes 172040 | tf_op jit(solution)/shard_map/ppermute | solution.py:27
  13.6 5.6 %collective-permute-start.3 = (bf16[16,1792]{1,0:T(8,128)(2,1)S(1)}, bf16[16,1792]{1,0:T(8,128)(2,1)S(1)}, u32[]{:S(2)}, u32[]{:S(2)}) collective-permute-start(bf16[16,1792]{1,0:T(8,128)(2,1)S(1)} %maximum_select_fusion), channel_id=1, source_target_pairs={{0,4},{1,13},{2,6},{3,15},{4,8},{5,1},{6,10},{7,3},{8,12},{9,5},{1... | collective-permute-start | bytes 172040 | tf_op jit(solution)/shard_map/ppermute | solution.py:27
  13.7 5.9 %collective-permute-start.4 = (bf16[16,1792]{1,0:T(8,128)(2,1)S(1)}, bf16[16,1792]{1,0:T(8,128)(2,1)S(1)}, u32[]{:S(2)}, u32[]{:S(2)}) collective-permute-start(bf16[16,1792]{1,0:T(8,128)(2,1)S(1)} %maximum_select_fusion), channel_id=1, source_target_pairs={{0,6},{1,11},{2,8},{3,13},{4,10},{5,15},{6,12},{7,1},{8,14},{9,3},... | collective-permute-start | bytes 172040 | tf_op jit(solution)/shard_map/ppermute | solution.py:27
  19.7 8.0 %collective-permute-start.5 = (bf16[64,1792]{1,0:T(8,128)(2,1)S(1)}, bf16[64,1792]{1,0:T(8,128)(2,1)S(1)}, u32[]{:S(2)}, u32[]{:S(2)}) collective-permute-start(bf16[64,1792]{1,0:T(8,128)(2,1)S(1)} %pad_maximum_fusion), channel_id=1, source_target_pairs={{0,16},{1,17},{2,18},{3,19},{4,20},{5,21},{6,22},{7,23},{8,24},{9,... | collective-permute-start | bytes 688136 | tf_op jit(solution)/shard_map/ppermute | solution.py:27
  21.0 12.8 %collective-permute-start.6 = (bf16[64,1792]{1,0:T(8,128)(2,1)S(1)}, bf16[64,1792]{1,0:T(8,128)(2,1)S(1)}, u32[]{:S(2)}, u32[]{:S(2)}) collective-permute-start(bf16[64,1792]{1,0:T(8,128)(2,1)S(1)} %pad_maximum_fusion), channel_id=1, source_target_pairs={{0,32},{1,33},{2,34},{3,35},{4,36},{5,37},{6,38},{7,39},{8,40},{9,... | collective-permute-start | bytes 688136 | tf_op jit(solution)/shard_map/ppermute | solution.py:27
  23.7 10.4 %collective-permute-start.7 = (bf16[64,1792]{1,0:T(8,128)(2,1)S(1)}, bf16[64,1792]{1,0:T(8,128)(2,1)S(1)}, u32[]{:S(2)}, u32[]{:S(2)}) collective-permute-start(bf16[64,1792]{1,0:T(8,128)(2,1)S(1)} %pad_maximum_fusion), channel_id=1, source_target_pairs={{0,48},{1,49},{2,50},{3,51},{4,52},{5,53},{6,54},{7,55},{8,56},{9,... | collective-permute-start | bytes 688136 | tf_op jit(solution)/shard_map/ppermute | solution.py:27
  24.7 9.8 %collective-permute-start.8 = (bf16[64,1792]{1,0:T(8,128)(2,1)S(1)}, bf16[64,1792]{1,0:T(8,128)(2,1)S(1)}, u32[]{:S(2)}, u32[]{:S(2)}) collective-permute-start(bf16[64,1792]{1,0:T(8,128)(2,1)S(1)} %pad_maximum_fusion), channel_id=1, source_target_pairs={{0,1},{1,0},{2,3},{3,2},{4,5},{5,4},{6,7},{7,6},{8,9},{9,8},{10,11... | collective-permute-start | bytes 688136 | tf_op jit(solution)/shard_map/ppermute | solution.py:27
  27.7 6.8 %collective-permute-start.9 = (bf16[64,1792]{1,0:T(8,128)(2,1)S(1)}, bf16[64,1792]{1,0:T(8,128)(2,1)S(1)}, u32[]{:S(2)}, u32[]{:S(2)}) collective-permute-start(bf16[64,1792]{1,0:T(8,128)(2,1)S(1)} %collective-permute-done.5), channel_id=1, source_target_pairs={{0,1},{1,0},{2,3},{3,2},{4,5},{5,4},{6,7},{7,6},{8,9},{9,8},{10,11... | collective-permute-start | bytes 688136 | tf_op jit(solution)/shard_map/ppermute | solution.py:27
  33.9 1.5 collective-permute-start.10
  34.1 1.6 %collective-permute-start.11 = (bf16[64,1792]{1,0:T(8,128)(2,1)S(1)}, bf16[64,1792]{1,0:T(8,128)(2,1)S(1)}, u32[]{:S(2)}, u32[]{:S(2)}) collective-permute-start(bf16[64,1792]{1,0:T(8,128)(2,1)S(1)} %collective-permute-done.7), channel_id=1, source_target_pairs={{0,1},{1,0},{2,3},{3,2},{4,5},{5,4},{6,7},{7,6},{8,9},{9,8},{10,11... | collective-permute-start | bytes 688136 | tf_op jit(solution)/shard_map/ppermute | solution.py:27
  37.2 15.5 %collective-permute-start.14 = (bf16[512,256]{1,0:T(8,128)(2,1)S(1)}, bf16[512,256]{1,0:T(8,128)(2,1)S(1)}, u32[]{:S(2)}, u32[]{:S(2)}) collective-permute-start(bf16[512,256]{1,0:T(8,128)(2,1)S(1)} %get-tuple-element.29), channel_id=1, source_target_pairs={{0,192},{1,193},{2,194},{3,195},{4,196},{5,197},{6,198},{7,199},{8... | collective-permute-start | bytes 786440 | tf_op jit(solution)/shard_map/ppermute | solution.py:37
  41.7 11.0 %collective-permute-start.13 = (bf16[512,256]{1,0:T(8,128)(2,1)S(1)}, bf16[512,256]{1,0:T(8,128)(2,1)S(1)}, u32[]{:S(2)}, u32[]{:S(2)}) collective-permute-start(bf16[512,256]{1,0:T(8,128)(2,1)S(1)} %get-tuple-element.29), channel_id=1, source_target_pairs={{0,128},{64,192},{1,129},{65,193},{2,130},{66,194},{3,131},{67,195... | collective-permute-start | bytes 786440 | tf_op jit(solution)/shard_map/ppermute | solution.py:37
  43.0 11.0 %collective-permute-start.12 = (bf16[512,256]{1,0:T(8,128)(2,1)S(1)}, bf16[512,256]{1,0:T(8,128)(2,1)S(1)}, u32[]{:S(2)}, u32[]{:S(2)}) collective-permute-start(bf16[512,256]{1,0:T(8,128)(2,1)S(1)} %get-tuple-element.29), channel_id=1, source_target_pairs={{0,64},{64,128},{128,192},{1,65},{65,129},{129,193},{2,66},{66,130... | collective-permute-start | bytes 786440 | tf_op jit(solution)/shard_map/ppermute | solution.py:37
  56.3 2.3 %collective-permute-start.16 = (bf16[64,1792]{1,0:T(8,128)(2,1)S(1)}, bf16[64,1792]{1,0:T(8,128)(2,1)S(1)}, u32[]{:S(2)}, u32[]{:S(2)}) collective-permute-start(bf16[64,1792]{1,0:T(8,128)(2,1)S(1)} %get-tuple-element.17), channel_id=1, source_target_pairs={{0,1},{1,0},{2,3},{3,2},{4,5},{5,4},{6,7},{7,6},{8,9},{9,8},{10,11... | collective-permute-start | bytes 688136 | tf_op jit(solution)/shard_map/ppermute | solution.py:27
  57.5 1.5 collective-permute-start.20
  57.6 1.7 %collective-permute-start.18 = (bf16[64,1792]{1,0:T(8,128)(2,1)S(1)}, bf16[64,1792]{1,0:T(8,128)(2,1)S(1)}, u32[]{:S(2)}, u32[]{:S(2)}) collective-permute-start(bf16[64,1792]{1,0:T(8,128)(2,1)S(1)} %get-tuple-element.16), channel_id=1, source_target_pairs={{0,1},{1,0},{2,3},{3,2},{4,5},{5,4},{6,7},{7,6},{8,9},{9,8},{10,11... | collective-permute-start | bytes 688136 | tf_op jit(solution)/shard_map/ppermute | solution.py:27
  58.0 30.2 %copy-start.12 = (bf16[1,8,1792]{2,1,0:T(8,128)(2,1)S(1)}, bf16[1,8,1792]{2,1,0:T(8,128)(2,1)}, u32[]{:S(2)}) copy-start(bf16[1,8,1792]{2,1,0:T(8,128)(2,1)} %param.7) | copy-start | bytes 86020
  58.0 5.9 %collective-permute-start.15 = (bf16[64,1792]{1,0:T(8,128)(2,1)S(1)}, bf16[64,1792]{1,0:T(8,128)(2,1)S(1)}, u32[]{:S(2)}, u32[]{:S(2)}) collective-permute-start(bf16[64,1792]{1,0:T(8,128)(2,1)S(1)} %get-tuple-element.14), channel_id=1, source_target_pairs={{0,1},{1,0},{2,3},{3,2},{4,5},{5,4},{6,7},{7,6},{8,9},{9,8},{10,11... | collective-permute-start | bytes 688136 | tf_op jit(solution)/shard_map/ppermute | solution.py:27
  59.4 8.2 %collective-permute-start.21 = (bf16[64,1792]{1,0:T(8,128)(2,1)S(1)}, bf16[64,1792]{1,0:T(8,128)(2,1)S(1)}, u32[]{:S(2)}, u32[]{:S(2)}) collective-permute-start(bf16[64,1792]{1,0:T(8,128)(2,1)S(1)} %get-tuple-element.19), channel_id=1, source_target_pairs={{0,16},{1,17},{2,18},{3,19},{4,20},{5,21},{6,22},{7,23},{8,24},{9,... | collective-permute-start | bytes 688136 | tf_op jit(solution)/shard_map/ppermute | solution.py:27
  60.7 12.3 %collective-permute-start.19 = (bf16[64,1792]{1,0:T(8,128)(2,1)S(1)}, bf16[64,1792]{1,0:T(8,128)(2,1)S(1)}, u32[]{:S(2)}, u32[]{:S(2)}) collective-permute-start(bf16[64,1792]{1,0:T(8,128)(2,1)S(1)} %get-tuple-element.20), channel_id=1, source_target_pairs={{0,32},{1,33},{2,34},{3,35},{4,36},{5,37},{6,38},{7,39},{8,40},{9,... | collective-permute-start | bytes 688136 | tf_op jit(solution)/shard_map/ppermute | solution.py:27
  62.7 10.3 %collective-permute-start.17 = (bf16[64,1792]{1,0:T(8,128)(2,1)S(1)}, bf16[64,1792]{1,0:T(8,128)(2,1)S(1)}, u32[]{:S(2)}, u32[]{:S(2)}) collective-permute-start(bf16[64,1792]{1,0:T(8,128)(2,1)S(1)} %get-tuple-element.18), channel_id=1, source_target_pairs={{0,48},{1,49},{2,50},{3,51},{4,52},{5,53},{6,54},{7,55},{8,56},{9,... | collective-permute-start | bytes 688136 | tf_op jit(solution)/shard_map/ppermute | solution.py:27
  73.2 11.2 %collective-permute-start.25 = (bf16[16,1792]{1,0:T(8,128)(2,1)S(1)}, bf16[16,1792]{1,0:T(8,128)(2,1)S(1)}, u32[]{:S(2)}, u32[]{:S(2)}) collective-permute-start(bf16[16,1792]{1,0:T(8,128)(2,1)S(1)} %get-tuple-element.22), channel_id=1, source_target_pairs={{0,10},{1,7},{2,12},{3,9},{4,14},{5,11},{6,0},{7,13},{8,2},{9,15},... | collective-permute-start | bytes 172040 | tf_op jit(solution)/shard_map/ppermute | solution.py:27
  75.0 9.4 %collective-permute-start.24 = (bf16[16,1792]{1,0:T(8,128)(2,1)S(1)}, bf16[16,1792]{1,0:T(8,128)(2,1)S(1)}, u32[]{:S(2)}, u32[]{:S(2)}) collective-permute-start(bf16[16,1792]{1,0:T(8,128)(2,1)S(1)} %get-tuple-element.23), channel_id=1, source_target_pairs={{0,12},{1,5},{2,14},{3,7},{4,0},{5,9},{6,2},{7,11},{8,4},{9,13},{1... | collective-permute-start | bytes 172040 | tf_op jit(solution)/shard_map/ppermute | solution.py:27
  79.2 5.2 %collective-permute-start.23 = (bf16[16,1792]{1,0:T(8,128)(2,1)S(1)}, bf16[16,1792]{1,0:T(8,128)(2,1)S(1)}, u32[]{:S(2)}, u32[]{:S(2)}) collective-permute-start(bf16[16,1792]{1,0:T(8,128)(2,1)S(1)} %get-tuple-element.24), channel_id=1, source_target_pairs={{0,14},{1,3},{2,0},{3,5},{4,2},{5,7},{6,4},{7,9},{8,6},{9,11},{10,... | collective-permute-start | bytes 172040 | tf_op jit(solution)/shard_map/ppermute | solution.py:27
  79.2 8.8 %collective-permute-start.22 = (bf16[16,1792]{1,0:T(8,128)(2,1)S(1)}, bf16[16,1792]{1,0:T(8,128)(2,1)S(1)}, u32[]{:S(2)}, u32[]{:S(2)}) collective-permute-start(bf16[16,1792]{1,0:T(8,128)(2,1)S(1)} %get-tuple-element.21), channel_id=1, source_target_pairs={{1,9},{3,11},{5,13},{7,15},{9,1},{11,3},{13,5},{15,7},{17,25},{19,... | collective-permute-start | bytes 172040 | tf_op jit(solution)/shard_map/ppermute | solution.py:27
  88.1 1.5 collective-permute-start.26
  88.2 1.3 collective-permute-start.27
  90.2 10.5 %collective-permute-start.28 = (bf16[16,1792]{1,0:T(8,128)(2,1)}, bf16[16,1792]{1,0:T(8,128)(2,1)}, u32[]{:S(2)}, u32[]{:S(2)}) collective-permute-start(bf16[16,1792]{1,0:T(8,128)(2,1)} %subtract_convert_fusion), channel_id=1, source_target_pairs={{1,9},{3,11},{5,13},{7,15},{9,1},{11,3},{13,5},{15,7},{17,25},{19,... | collective-permute-start | bytes 172040 | tf_op jit(solution)/shard_map/ppermute | solution.py:27
  96.0 5.5 %collective-permute-start.29 = (bf16[16,1792]{1,0:T(8,128)(2,1)}, bf16[16,1792]{1,0:T(8,128)(2,1)S(1)}, u32[]{:S(2)}, u32[]{:S(2)}) collective-permute-start(bf16[16,1792]{1,0:T(8,128)(2,1)} %subtract_convert_fusion), channel_id=1, source_target_pairs={{0,2},{1,15},{2,4},{3,1},{4,6},{5,3},{6,8},{7,5},{8,10},{9,7},{10,... | collective-permute-start | bytes 172040 | tf_op jit(solution)/shard_map/ppermute | solution.py:27
  96.4 5.2 %collective-permute-start.30 = (bf16[16,1792]{1,0:T(8,128)(2,1)}, bf16[16,1792]{1,0:T(8,128)(2,1)S(1)}, u32[]{:S(2)}, u32[]{:S(2)}) collective-permute-start(bf16[16,1792]{1,0:T(8,128)(2,1)} %subtract_convert_fusion), channel_id=1, source_target_pairs={{0,4},{1,13},{2,6},{3,15},{4,8},{5,1},{6,10},{7,3},{8,12},{9,5},{1... | collective-permute-start | bytes 172040 | tf_op jit(solution)/shard_map/ppermute | solution.py:27
  97.0 5.7 %collective-permute-start.31 = (bf16[16,1792]{1,0:T(8,128)(2,1)}, bf16[16,1792]{1,0:T(8,128)(2,1)S(1)}, u32[]{:S(2)}, u32[]{:S(2)}) collective-permute-start(bf16[16,1792]{1,0:T(8,128)(2,1)} %subtract_convert_fusion), channel_id=1, source_target_pairs={{0,6},{1,11},{2,8},{3,13},{4,10},{5,15},{6,12},{7,1},{8,14},{9,3},... | collective-permute-start | bytes 172040 | tf_op jit(solution)/shard_map/ppermute | solution.py:27
  102.7 8.3 %collective-permute-start.32 = (bf16[64,1792]{1,0:T(8,128)(2,1)S(1)}, bf16[64,1792]{1,0:T(8,128)(2,1)S(1)}, u32[]{:S(2)}, u32[]{:S(2)}) collective-permute-start(bf16[64,1792]{1,0:T(8,128)(2,1)S(1)} %pad_maximum_fusion.1), channel_id=1, source_target_pairs={{0,16},{1,17},{2,18},{3,19},{4,20},{5,21},{6,22},{7,23},{8,24},{9,... | collective-permute-start | bytes 688136 | tf_op jit(solution)/shard_map/ppermute | solution.py:27
  104.9 12.6 %collective-permute-start.33 = (bf16[64,1792]{1,0:T(8,128)(2,1)S(1)}, bf16[64,1792]{1,0:T(8,128)(2,1)S(1)}, u32[]{:S(2)}, u32[]{:S(2)}) collective-permute-start(bf16[64,1792]{1,0:T(8,128)(2,1)S(1)} %pad_maximum_fusion.1), channel_id=1, source_target_pairs={{0,32},{1,33},{2,34},{3,35},{4,36},{5,37},{6,38},{7,39},{8,40},{9,... | collective-permute-start | bytes 688136 | tf_op jit(solution)/shard_map/ppermute | solution.py:27
  107.2 11.5 %collective-permute-start.34 = (bf16[64,1792]{1,0:T(8,128)(2,1)S(1)}, bf16[64,1792]{1,0:T(8,128)(2,1)S(1)}, u32[]{:S(2)}, u32[]{:S(2)}) collective-permute-start(bf16[64,1792]{1,0:T(8,128)(2,1)S(1)} %pad_maximum_fusion.1), channel_id=1, source_target_pairs={{0,48},{1,49},{2,50},{3,51},{4,52},{5,53},{6,54},{7,55},{8,56},{9,... | collective-permute-start | bytes 688136 | tf_op jit(solution)/shard_map/ppermute | solution.py:27
  107.4 11.4 %collective-permute-start.35 = (bf16[64,1792]{1,0:T(8,128)(2,1)S(1)}, bf16[64,1792]{1,0:T(8,128)(2,1)S(1)}, u32[]{:S(2)}, u32[]{:S(2)}) collective-permute-start(bf16[64,1792]{1,0:T(8,128)(2,1)S(1)} %pad_maximum_fusion.1), channel_id=1, source_target_pairs={{0,1},{1,0},{2,3},{3,2},{4,5},{5,4},{6,7},{7,6},{8,9},{9,8},{10,11... | collective-permute-start | bytes 688136 | tf_op jit(solution)/shard_map/ppermute | solution.py:27
  111.1 7.8 %collective-permute-start.36 = (bf16[64,1792]{1,0:T(8,128)(2,1)S(1)}, bf16[64,1792]{1,0:T(8,128)(2,1)S(1)}, u32[]{:S(2)}, u32[]{:S(2)}) collective-permute-start(bf16[64,1792]{1,0:T(8,128)(2,1)S(1)} %collective-permute-done.32), channel_id=1, source_target_pairs={{0,1},{1,0},{2,3},{3,2},{4,5},{5,4},{6,7},{7,6},{8,9},{9,8},{10,11... | collective-permute-start | bytes 688136 | tf_op jit(solution)/shard_map/ppermute | solution.py:27
  117.5 2.3 %collective-permute-start.37 = (bf16[64,1792]{1,0:T(8,128)(2,1)S(1)}, bf16[64,1792]{1,0:T(8,128)(2,1)S(1)}, u32[]{:S(2)}, u32[]{:S(2)}) collective-permute-start(bf16[64,1792]{1,0:T(8,128)(2,1)S(1)} %collective-permute-done.33), channel_id=1, source_target_pairs={{0,1},{1,0},{2,3},{3,2},{4,5},{5,4},{6,7},{7,6},{8,9},{9,8},{10,11... | collective-permute-start | bytes 688136 | tf_op jit(solution)/shard_map/ppermute | solution.py:27
  118.7 1.6 collective-permute-start.38
  128.7 12.6 %collective-permute-start.39 = (f32[8,128]{1,0:T(8,128)S(1)}, f32[8,128]{1,0:T(8,128)S(1)}, u32[]{:S(2)}, u32[]{:S(2)}) collective-permute-start(f32[8,128]{1,0:T(8,128)S(1)} %broadcast_in_dim.58), channel_id=1, source_target_pairs={{0,64},{64,128},{128,192},{192,0},{1,65},{65,129},{129,193},{193,1... | collective-permute-start | bytes 12296 | tf_op jit(solution)/shard_map/ppermute | solution.py:133
  131.0 23.2 %collective-permute-start.44 = (bf16[512,256]{1,0:T(8,128)(2,1)}, bf16[512,256]{1,0:T(8,128)(2,1)S(1)}, u32[]{:S(2)}, u32[]{:S(2)}) collective-permute-start(bf16[512,256]{1,0:T(8,128)(2,1)} %convolution_convert_fusion), channel_id=1, source_target_pairs={{192,0},{193,1},{194,2},{195,3},{196,4},{197,5},{198,6},{199,7},{2... | collective-permute-start | bytes 786440 | tf_op jit(solution)/shard_map/ppermute | solution.py:37
  132.3 22.0 %collective-permute-start.43 = (bf16[512,256]{1,0:T(8,128)(2,1)}, bf16[512,256]{1,0:T(8,128)(2,1)S(1)}, u32[]{:S(2)}, u32[]{:S(2)}) collective-permute-start(bf16[512,256]{1,0:T(8,128)(2,1)} %convolution_convert_fusion.1), channel_id=1, source_target_pairs={{128,0},{192,64},{129,1},{193,65},{130,2},{194,66},{131,3},{195,67... | collective-permute-start | bytes 786440 | tf_op jit(solution)/shard_map/ppermute | solution.py:37
  133.6 20.7 %collective-permute-start.42 = (bf16[512,256]{1,0:T(8,128)(2,1)}, bf16[512,256]{1,0:T(8,128)(2,1)S(1)}, u32[]{:S(2)}, u32[]{:S(2)}) collective-permute-start(bf16[512,256]{1,0:T(8,128)(2,1)} %convolution_convert_fusion.2), channel_id=1, source_target_pairs={{64,0},{128,64},{192,128},{65,1},{129,65},{193,129},{66,2},{130,66... | collective-permute-start | bytes 786440 | tf_op jit(solution)/shard_map/ppermute | solution.py:37
  141.3 6.1 %collective-permute-start.40 = (f32[8,128]{1,0:T(8,128)S(1)}, f32[8,128]{1,0:T(8,128)S(1)}, u32[]{:S(2)}, u32[]{:S(2)}) collective-permute-start(f32[8,128]{1,0:T(8,128)S(1)} %collective-permute-done.39), channel_id=1, source_target_pairs={{0,64},{64,128},{128,192},{192,0},{1,65},{65,129},{129,193},{193,1... | collective-permute-start | bytes 12296 | tf_op jit(solution)/shard_map/ppermute | solution.py:133
  147.4 3.7 %collective-permute-start.41 = (f32[8,128]{1,0:T(8,128)S(1)}, f32[8,128]{1,0:T(8,128)S(1)}, u32[]{:S(2)}, u32[]{:S(2)}) collective-permute-start(f32[8,128]{1,0:T(8,128)S(1)} %collective-permute-done.40), channel_id=1, source_target_pairs={{0,64},{64,128},{128,192},{192,0},{1,65},{65,129},{129,193},{193,1... | collective-permute-start | bytes 12296 | tf_op jit(solution)/shard_map/ppermute | solution.py:133
  (16 other events, 132.4 us)

commit v2 on v1

v2 whole, which is shorter than its diff:
```python
import jax
import jax.numpy as jnp
from jax import lax
from jax.sharding import PartitionSpec as P

TILE = 64
NTILE = 8
Y, Z, C = 4, 8, 2
BF = jnp.bfloat16
F32 = jnp.float32


def index_of(y, z, c):
    return ((y % Y) * Z + z % Z) * C + c


def pairs(move, cores=(0, 1)):
    return [
        (index_of(y, z, c), index_of(*move(y, z, c)))
        for y in range(Y)
        for z in range(Z)
        for c in cores
    ]


def send(value, move, cores=(0, 1)):
    return lax.ppermute(value, "latent", pairs(move, cores))


def swap(value):
    return send(value, lambda y, z, c: (y, z, 1 - c))


def send_layer(value, steps):
    count = lax.axis_size("layer")
    sources = [s for s in range(count) if 0 <= s + steps < count]
    return lax.ppermute(value, "layer", [(s, s + steps) for s in sources])


def chip_rows(value, core):
    other = swap(value)
    return jnp.where(core == 0, jnp.concatenate([value, other]), jnp.concatenate([other, value]))


def spread(chip, core):
    near = [
        send(chip, lambda y, z, c, k=k: (y, z + k if c == 0 else z - k, c)) for k in (1, 2, 3)
    ]
    far = send(chip, lambda y, z, c: (y, z + 4, c), (1,))
    half = jnp.concatenate([jnp.where(core == 0, chip, far)] + near)
    across = send(half, lambda y, z, c: (y + 2, z, c))
    row = jnp.concatenate([half, swap(half)])
    beside = send(row, lambda y, z, c: (y + 1 if c == 0 else y - 1, z, c))
    beside = jnp.concatenate([beside, swap(beside)])
    across = jnp.concatenate([across, swap(across)])
    return [row, beside, across]


def collect(partial, core):
    row, beside, across = partial
    count, width = row.shape
    half = count // 2
    beside = (beside[:count].astype(F32) + swap(beside[count:]).astype(F32)).astype(BF)
    beside = send(beside, lambda y, z, c: (y - 1 if c == 0 else y + 1, z, c))
    across = (across[:half].astype(F32) + swap(across[half:]).astype(F32)).astype(BF)
    across = send(across, lambda y, z, c: (y + 2, z, c))
    row = row.astype(F32) + beside.astype(F32)
    row = row[:half] + swap(row[half:].astype(BF)).astype(F32) + across.astype(F32)
    row = row.astype(BF).reshape(4, half // 4, width)
    far = send(row[0], lambda y, z, c: (y, z + 4, c), (1,))
    total = jnp.where(core == 0, row[0], far).astype(F32)
    for k in (1, 2, 3):
        piece = send(row[k], lambda y, z, c, k=k: (y, z - k if c == 0 else z + k, c))
        total = total + piece.astype(F32)
    total = total.astype(BF)
    return total.astype(F32) + swap(total).astype(F32)


def shard_chips(latent):
    y, z, c = latent // (Z * C), latent // C % Z, latent % C
    p = jnp.arange(Y * Z, dtype=jnp.int32)
    chunk, half, j = p // 8, p // 4 % 2, p % 4
    side = (half + c + (chunk == 2)) % 2
    step = 1 - 2 * c
    from_y = y + jnp.where(chunk == 1, -step, jnp.where(chunk == 2, step, jnp.where(chunk == 3, 2, 0)))
    from_z = jnp.where(side == 0, z - j, jnp.where(j == 0, z + 4, z + j)) % Z
    return from_y % Y * Z + from_z


def shards(residual, target, enc_weight, enc_bias, dec_weight, active):
    layers = dec_weight.shape[0]
    width = residual.shape[-1]
    layer = lax.axis_index("layer")
    latent = lax.axis_index("latent")
    core = latent % C
    chips = shard_chips(latent)
    names = lax.dynamic_index_in_dim(active, layer, 0, keepdims=False)
    hit = jnp.any(names == latent, axis=1)
    live = jnp.any((chips[:, None] // 4 == jnp.arange(NTILE)[None, :]) & hit[None, :], axis=1)
    live = jnp.repeat(live, 16)[:, None]
    dec = dec_weight[:, 0]
    weights = [
        lax.dynamic_index_in_dim(dec, (layer - k) % layers, 0, keepdims=False)
        for k in range(layers)
    ]

    inputs = spread(chip_rows(residual[0], core), core)
    goal = chip_rows(target[0], core)
    codes, on, partial = [], [], []
    start = 0
    for rows in inputs:
        preact = jnp.dot(rows, enc_weight[0], preferred_element_type=F32) + enc_bias[0][None, :]
        on.append(live[start : start + rows.shape[0]] & (preact > 0))
        start += rows.shape[0]
        own = jnp.where(on[-1], preact, 0.0).astype(BF)
        codes.append([own] + [send_layer(own, k) for k in range(1, layers)])
        partial.append(
            jnp.dot(
                jnp.concatenate(codes[-1], axis=1),
                jnp.concatenate(weights),
                preferred_element_type=F32,
            ).astype(BF)
        )
    errors = (collect(partial, core) - goal.astype(F32)).astype(BF)
    errors = spread(errors, core)

    mine = []
    for part in errors:
        backs = [
            lax.dot_general(part, weight, (((1,), (1,)), ((), ())), preferred_element_type=F32)
            for weight in weights
        ]
        total = backs[0]
        for k in range(1, layers):
            total = total + send_layer(backs[k].astype(BF), -k).astype(F32)
        mine.append(total)

    full = jnp.concatenate(errors)
    sources = [jnp.concatenate([part[k] for part in codes]) for k in range(layers)]
    placed = [
        sum(
            jnp.where((layer - k) % layers == s, sources[k], jnp.zeros_like(sources[k]))
            for k in range(layers)
        )
        for s in range(layers)
    ]
    dec_grad = lax.dot_general(
        jnp.concatenate(placed, axis=1),
        full,
        (((0,), (0,)), ((), ())),
        preferred_element_type=F32,
    )
    dec_grad = (dec_grad / TILE).astype(BF).reshape(layers, 1, -1, width)

    square = full.astype(F32).reshape(Y * Z, 16, width)
    square = jnp.sum(square * square, axis=(1, 2))
    place = chips[None, :] == jnp.arange(Y * Z)[:, None]
    square = jnp.sum(jnp.sum(jnp.where(place, square[None, :], 0.0), axis=1))
    square = jnp.full((8, 128), square)
    loss = jnp.zeros((layers, 8, 128), F32)
    for k in range(layers):
        ring = [(s, (s + k) % layers) for s in range(layers)]
        moved = lax.ppermute(square, "layer", ring) if k else square
        loss = lax.dynamic_update_index_in_dim(loss, moved, (layer - k) % layers, 0)
    total = loss[0]
    for s in range(1, layers):
        total = total + loss[s]
    total = 0.5 * total[0, 0] / (layers * NTILE * TILE * width)

    pre_grad = jnp.where(jnp.concatenate(on), jnp.concatenate(mine), 0.0)
    bias_grad = (jnp.sum(pre_grad, axis=0) / TILE)[None]
    enc_grad = lax.dot_general(
        jnp.concatenate(inputs),
        pre_grad.astype(BF),
        (((0,), (0,)), ((), ())),
        preferred_element_type=F32,
    )
    enc_grad = (enc_grad / TILE).astype(BF)[None]
    return (total, enc_grad, bias_grad, dec_grad)


def solution(mesh):
    in_specs = (
        P("layer", "latent", None),
        P("layer", "latent", None),
        P("layer", None, "latent"),
        P("layer", "latent"),
        P(None, "layer", "latent", None),
        P(),
    )
    out_specs = (
        P(),
        P("layer", None, "latent"),
        P("layer", "latent"),
        P(None, "layer", "latent", None),
    )
    return jax.shard_map(shards, mesh=mesh, in_specs=in_specs, out_specs=out_specs, check_vma=False)
```

time: 161 us -> 165 us (1.025)
  starting transfers between devices: 74.2 us -> 83.2 us
  waiting for transfers between devices: 51.4 us -> 43.1 us
  matrix products: 13.7 us -> 19.6 us
  local copies, waits for them, and re-layouts: 4.1 us -> 7.2 us
  other arithmetic: 10.6 us -> 7.99 us
  between operations: 5.08 us -> 3.29 us
    ppermute x6 -> x18, starting transfers between devices: 12.2 us -> 33.2 us  [send_layer(): return lax.ppermute(value, 'layer', [(s, s + steps) for s in sources])]
    ppermute x36 -> x30, starting transfers between devices: 58.6 us -> 48 us  [send(): return lax.ppermute(value, 'latent', pairs(move, cores))]
    ppermute x3, waiting for transfers between devices: 8.51 us -> 0.01 us  [shards(): moved = lax.ppermute(square, 'layer', ring) if k else square]
    ppermute x6 -> x18, waiting for transfers between devices: 8.21 us -> 15.7 us  [send_layer(): return lax.ppermute(value, 'layer', [(s, s + steps) for s in sources])]
    ppermute x36 -> x30, waiting for transfers between devices: 34.6 us -> 27.5 us  [send(): return lax.ppermute(value, 'latent', pairs(move, cores))]
    dot_general x10 -> x17, matrix products: 12.3 us -> 18.6 us  [the longest x12 8.73 us: shards(): lax.dot_general(part, weight, (((1,), (1,)), ((), ())), preferred_element...]
    squeeze x1, local copies, waits for them, and re-layouts: 0.27 us -> 3.48 us  [shards(): lax.dynamic_index_in_dim(dec, (layer - k) % layers, 0, keepdims=False)]
    convert_element_type x4, other arithmetic: 3.06 us -> 0.26 us  [the longest x1 0.11 us: collect(): (beside[:count].astype(F32) + swap(beside[count:]).astype(F32)).astype(BF)]
  transfers between devices with their start and end apart: 45 -> 51, of which waited for: 21 -> 25; matrix products, arithmetic and copies ran while one was open for 7% -> 15% of each run, Pallas kernels for 0% -> 0%
where the time goes in v2:
time: 165 us; the launch traced here: 164 us
  starting transfers between devices  83.2 us (50%)
  waiting for transfers between devices  43.1 us (26%)
  matrix products  19.6 us (12%)
  other arithmetic  7.99 us (5%)
  local copies, waits for them, and re-layouts  7.2 us (4%)
  between operations  3.29 us (2%)
    ppermute x30, starting transfers between devices, send(): return lax.ppermute(value, 'latent', pairs(move, cores))  48 us
    ppermute x18, starting transfers between devices, send_layer(): return lax.ppermute(value, 'layer', [(s, s + steps) for s in sources])  33.2 us
    ppermute x30, waiting for transfers between devices, send(): return lax.ppermute(value, 'latent', pairs(move, cores))  27.5 us
    ppermute x18, waiting for transfers between devices, send_layer(): return lax.ppermute(value, 'layer', [(s, s + steps) for s in sources])  15.7 us
    dot_general x12, matrix products, shards(): lax.dot_general(part, weight, (((1,), (1,)), ((), ())), preferred_element...  8.73 us
    dot_general x1, matrix products, shards(): lax.dot_general(jnp.concatenate(placed, axis=1), full, (((0,), (0,)), (()...  5.82 us
    squeeze x1, local copies, waits for them, and re-layouts, shards(): lax.dynamic_index_in_dim(dec, (layer - k) % layers, 0, keepdims=False)  3.48 us
  transfers between devices with their start and end apart: 51, of which 25 were waited for; matrix products, arithmetic and copies ran while one was open for 15% of the time, Pallas kernels for 0%

profile of v2, /device:TPU:1, one launch (start us, length us, event | category | flops | bytes accessed | tf_op | source)
XLA Modules:
  0.0 164.5 jit_solution(11308478743365663342)
XLA Ops:
  0.6 3.3 %collective-permute-start = (bf16[8,1792]{1,0:T(8,128)(2,1)}, bf16[8,1792]{1,0:T(8,128)(2,1)S(1)}, u32[]{:S(2)}, u32[]{:S(2)}) collective-permute-start(bf16[8,1792]{1,0:T(8,128)(2,1)} %bitcast.66), channel_id=1, source_target_pairs={{0,1},{1,0},{2,3},{3,2},{4,5},{5,4},{6,7},{7,6},{8,9},{9,8},{10,11... | collective-permute-start | bytes 86024 | tf_op jit(solution)/shard_map/ppermute | solution.py:27
  5.4 3.5 %dynamic-slice_bitcast_fusion.3 = (bf16[256,1792]{1,0:T(8,128)(2,1)S(1)}, bf16[256,1792]{1,0:T(8,128)(2,1)S(1)}, bf16[256,1792]{1,0:T(8,128)(2,1)}, bf16[256,1792]{1,0:T(8,128)(2,1)}) fusion(bf16[4,1,256,1792]{3,2,1,0:T(8,128)(2,1)} %param.10, s32[]{:T(128)S(6)} %select_n.426, s32[]{:T(128)S(6)} %select_n.428, s32[]{:T(128)S(6)} %select_n.432, s32[]{:T(128)S(6)} %select_n.430), kind=kLoop, calls=%fused_computation.49 | loop fusion | bytes 7340048 | tf_op jit(solution)/shard_map/jit(dynamic_index_in_dim)/squeeze | solution.py:103
  9.0 7.1 %collective-permute-start.1 = (bf16[16,1792]{1,0:T(8,128)(2,1)S(1)}, bf16[16,1792]{1,0:T(8,128)(2,1)S(1)}, u32[]{:S(2)}, u32[]{:S(2)}) collective-permute-start(bf16[16,1792]{1,0:T(8,128)(2,1)S(1)} %maximum_select_fusion.2), channel_id=1, source_target_pairs={{1,9},{3,11},{5,13},{7,15},{9,1},{11,3},{13,5},{15,7},{17,25},{19,... | collective-permute-start | bytes 172040 | tf_op jit(solution)/shard_map/ppermute | solution.py:27
  16.9 4.7 %collective-permute-start.4 = (bf16[16,1792]{1,0:T(8,128)(2,1)S(1)}, bf16[16,1792]{1,0:T(8,128)(2,1)S(1)}, u32[]{:S(2)}, u32[]{:S(2)}) collective-permute-start(bf16[16,1792]{1,0:T(8,128)(2,1)S(1)} %maximum_select_fusion.2), channel_id=1, source_target_pairs={{0,6},{1,11},{2,8},{3,13},{4,10},{5,15},{6,12},{7,1},{8,14},{9,3},... | collective-permute-start | bytes 172040 | tf_op jit(solution)/shard_map/ppermute | solution.py:27
  21.6 1.9 %collective-permute-done.4 = bf16[16,1792]{1,0:T(8,128)(2,1)S(1)} collective-permute-done((bf16[16,1792]{1,0:T(8,128)(2,1)S(1)}, bf16[16,1792]{1,0:T(8,128)(2,1)S(1)}, u32[]{:S(2)}, u32[]{:S(2)}) %collective-permute-start.4) | collective-permute-done | bytes 57376 | tf_op jit(solution)/shard_map/ppermute | solution.py:27
  23.5 3.0 %collective-permute-start.17 = (bf16[64,1792]{1,0:T(8,128)(2,1)S(1)}, bf16[64,1792]{1,0:T(8,128)(2,1)S(1)}, u32[]{:S(2)}, u32[]{:S(2)}) collective-permute-start(bf16[64,1792]{1,0:T(8,128)(2,1)S(1)} %pad_maximum_fusion.2), channel_id=1, source_target_pairs={{0,32},{1,33},{2,34},{3,35},{4,36},{5,37},{6,38},{7,39},{8,40},{9,... | collective-permute-start | bytes 688136 | tf_op jit(solution)/shard_map/ppermute | solution.py:27
  26.6 1.4 collective-permute-done.5
  28.4 4.5 %collective-permute-start.8 = (bf16[128,256]{1,0:T(8,128)(2,1)S(1)}, bf16[128,256]{1,0:T(8,128)(2,1)S(1)}, u32[]{:S(2)}, u32[]{:S(2)}) collective-permute-start(bf16[128,256]{1,0:T(8,128)(2,1)S(1)} %get-tuple-element.62), channel_id=1, source_target_pairs={{0,192},{1,193},{2,194},{3,195},{4,196},{5,197},{6,198},{7,199},{8... | collective-permute-start | bytes 196616 | tf_op jit(solution)/shard_map/ppermute | solution.py:37
  32.9 1.3 collective-permute-start.7
  34.2 2.5 %collective-permute-start.6 = (bf16[128,256]{1,0:T(8,128)(2,1)S(1)}, bf16[128,256]{1,0:T(8,128)(2,1)S(1)}, u32[]{:S(2)}, u32[]{:S(2)}) collective-permute-start(bf16[128,256]{1,0:T(8,128)(2,1)S(1)} %get-tuple-element.62), channel_id=1, source_target_pairs={{0,64},{64,128},{128,192},{1,65},{65,129},{129,193},{2,66},{66,130... | collective-permute-start | bytes 196616 | tf_op jit(solution)/shard_map/ppermute | solution.py:37
  38.0 1.3 collective-permute-start.18
  40.7 2.6 %collective-permute-start.21 = (bf16[128,256]{1,0:T(8,128)(2,1)S(1)}, bf16[128,256]{1,0:T(8,128)(2,1)S(1)}, u32[]{:S(2)}, u32[]{:S(2)}) collective-permute-start(bf16[128,256]{1,0:T(8,128)(2,1)S(1)} %get-tuple-element.64), channel_id=1, source_target_pairs={{0,192},{1,193},{2,194},{3,195},{4,196},{5,197},{6,198},{7,199},{8... | collective-permute-start | bytes 196616 | tf_op jit(solution)/shard_map/ppermute | solution.py:37
  43.4 2.3 %collective-permute-start.20 = (bf16[128,256]{1,0:T(8,128)(2,1)S(1)}, bf16[128,256]{1,0:T(8,128)(2,1)S(1)}, u32[]{:S(2)}, u32[]{:S(2)}) collective-permute-start(bf16[128,256]{1,0:T(8,128)(2,1)S(1)} %get-tuple-element.64), channel_id=1, source_target_pairs={{0,128},{64,192},{1,129},{65,193},{2,130},{66,194},{3,131},{67,195... | collective-permute-start | bytes 196616 | tf_op jit(solution)/shard_map/ppermute | solution.py:37
  45.6 1.5 collective-permute-start.19
  49.1 1.6 collective-permute-start.22
  51.2 2.7 %collective-permute-start.13 = (bf16[256,256]{1,0:T(8,128)(2,1)S(1)}, bf16[256,256]{1,0:T(8,128)(2,1)S(1)}, u32[]{:S(2)}, u32[]{:S(2)}) collective-permute-start(bf16[256,256]{1,0:T(8,128)(2,1)S(1)} %get-tuple-element.60), channel_id=1, source_target_pairs={{0,192},{1,193},{2,194},{3,195},{4,196},{5,197},{6,198},{7,199},{8... | collective-permute-start | bytes 393224 | tf_op jit(solution)/shard_map/ppermute | solution.py:37
  53.9 2.9 %collective-permute-start.12 = (bf16[256,256]{1,0:T(8,128)(2,1)S(1)}, bf16[256,256]{1,0:T(8,128)(2,1)S(1)}, u32[]{:S(2)}, u32[]{:S(2)}) collective-permute-start(bf16[256,256]{1,0:T(8,128)(2,1)S(1)} %get-tuple-element.60), channel_id=1, source_target_pairs={{0,128},{64,192},{1,129},{65,193},{2,130},{66,194},{3,131},{67,195... | collective-permute-start | bytes 393224 | tf_op jit(solution)/shard_map/ppermute | solution.py:37
  56.9 1.3 collective-permute-start.11
  59.8 2.8 %collective-permute-done.11 = bf16[256,256]{1,0:T(8,128)(2,1)S(1)} collective-permute-done((bf16[256,256]{1,0:T(8,128)(2,1)S(1)}, bf16[256,256]{1,0:T(8,128)(2,1)S(1)}, u32[]{:S(2)}, u32[]{:S(2)}) %collective-permute-start.11) | collective-permute-done | bytes 131104 | tf_op jit(solution)/shard_map/ppermute | solution.py:37
  64.9 1.4 collective-permute-done.14
  67.0 8.0 %collective-permute-done.15 = bf16[128,1792]{1,0:T(8,128)(2,1)S(1)} collective-permute-done((bf16[128,1792]{1,0:T(8,128)(2,1)S(1)}, bf16[128,1792]{1,0:T(8,128)(2,1)S(1)}, u32[]{:S(2)}, u32[]{:S(2)}) %collective-permute-start.15) | collective-permute-done | bytes 458784 | tf_op jit(solution)/shard_map/ppermute | solution.py:27
  77.4 5.4 %collective-permute-start.24 = (bf16[16,1792]{1,0:T(8,128)(2,1)S(1)}, bf16[16,1792]{1,0:T(8,128)(2,1)S(1)}, u32[]{:S(2)}, u32[]{:S(2)}) collective-permute-start(bf16[16,1792]{1,0:T(8,128)(2,1)S(1)} %get-tuple-element.42), channel_id=1, source_target_pairs={{1,9},{3,11},{5,13},{7,15},{9,1},{11,3},{13,5},{15,7},{17,25},{19,... | collective-permute-start | bytes 172040 | tf_op jit(solution)/shard_map/ppermute | solution.py:27
  82.8 1.7 %collective-permute-start.27 = (bf16[16,1792]{1,0:T(8,128)(2,1)S(1)}, bf16[16,1792]{1,0:T(8,128)(2,1)S(1)}, u32[]{:S(2)}, u32[]{:S(2)}) collective-permute-start(bf16[16,1792]{1,0:T(8,128)(2,1)S(1)} %get-tuple-element.43), channel_id=1, source_target_pairs={{0,10},{1,7},{2,12},{3,9},{4,14},{5,11},{6,0},{7,13},{8,2},{9,15},... | collective-permute-start | bytes 172040 | tf_op jit(solution)/shard_map/ppermute | solution.py:27
  84.5 2.4 %collective-permute-start.26 = (bf16[16,1792]{1,0:T(8,128)(2,1)S(1)}, bf16[16,1792]{1,0:T(8,128)(2,1)S(1)}, u32[]{:S(2)}, u32[]{:S(2)}) collective-permute-start(bf16[16,1792]{1,0:T(8,128)(2,1)S(1)} %get-tuple-element.44), channel_id=1, source_target_pairs={{0,12},{1,5},{2,14},{3,7},{4,0},{5,9},{6,2},{7,11},{8,4},{9,13},{1... | collective-permute-start | bytes 172040 | tf_op jit(solution)/shard_map/ppermute | solution.py:27
  87.0 2.0 %collective-permute-done.27 = bf16[16,1792]{1,0:T(8,128)(2,1)S(1)} collective-permute-done((bf16[16,1792]{1,0:T(8,128)(2,1)S(1)}, bf16[16,1792]{1,0:T(8,128)(2,1)S(1)}, u32[]{:S(2)}, u32[]{:S(2)}) %collective-permute-start.27) | collective-permute-done | bytes 57376 | tf_op jit(solution)/shard_map/ppermute | solution.py:27
  88.9 3.0 %collective-permute-done.26 = bf16[16,1792]{1,0:T(8,128)(2,1)S(1)} collective-permute-done((bf16[16,1792]{1,0:T(8,128)(2,1)S(1)}, bf16[16,1792]{1,0:T(8,128)(2,1)S(1)}, u32[]{:S(2)}, u32[]{:S(2)}) %collective-permute-start.26) | collective-permute-done | bytes 57376 | tf_op jit(solution)/shard_map/ppermute | solution.py:27
  93.4 5.1 %collective-permute-start.30 = (bf16[16,1792]{1,0:T(8,128)(2,1)S(1)}, bf16[16,1792]{1,0:T(8,128)(2,1)S(1)}, u32[]{:S(2)}, u32[]{:S(2)}) collective-permute-start(bf16[16,1792]{1,0:T(8,128)(2,1)S(1)} %subtract_convert_fusion), channel_id=1, source_target_pairs={{1,9},{3,11},{5,13},{7,15},{9,1},{11,3},{13,5},{15,7},{17,25},{19,... | collective-permute-start | bytes 172040 | tf_op jit(solution)/shard_map/ppermute | solution.py:27
  99.6 1.5 collective-permute-start.33
  101.0 1.6 collective-permute-start.32
  104.4 1.7 %collective-permute-done.32 = bf16[16,1792]{1,0:T(8,128)(2,1)S(1)} collective-permute-done((bf16[16,1792]{1,0:T(8,128)(2,1)S(1)}, bf16[16,1792]{1,0:T(8,128)(2,1)S(1)}, u32[]{:S(2)}, u32[]{:S(2)}) %collective-permute-start.32) | collective-permute-done | bytes 57376 | tf_op jit(solution)/shard_map/ppermute | solution.py:27
  106.6 1.4 collective-permute-done.34
  108.9 2.6 %collective-permute-start.35 = (bf16[128,1792]{1,0:T(8,128)(2,1)S(1)}, bf16[128,1792]{1,0:T(8,128)(2,1)S(1)}, u32[]{:S(2)}, u32[]{:S(2)}) collective-permute-start(bf16[128,1792]{1,0:T(8,128)(2,1)S(1)} %get-tuple-element.40), channel_id=1, source_target_pairs={{0,16},{1,49},{2,18},{3,51},{4,20},{5,53},{6,22},{7,55},{8,24},{9,... | collective-permute-start | bytes 1376264 | tf_op jit(solution)/shard_map/ppermute | solution.py:27
  111.6 1.3 collective-permute-start.42
  112.9 1.3 collective-permute-start.43
  114.6 1.3 collective-permute-start.44
  117.3 2.5 %collective-permute-done.35 = bf16[128,1792]{1,0:T(8,128)(2,1)S(1)} collective-permute-done((bf16[128,1792]{1,0:T(8,128)(2,1)S(1)}, bf16[128,1792]{1,0:T(8,128)(2,1)S(1)}, u32[]{:S(2)}, u32[]{:S(2)}) %collective-permute-start.35) | collective-permute-done | bytes 458784 | tf_op jit(solution)/shard_map/ppermute | solution.py:27
  120.8 3.0 %collective-permute-done.44 = bf16[128,256]{1,0:T(8,128)(2,1)S(1)} collective-permute-done((bf16[128,256]{1,0:T(8,128)(2,1)S(1)}, bf16[128,256]{1,0:T(8,128)(2,1)S(1)}, u32[]{:S(2)}, u32[]{:S(2)}) %collective-permute-start.44) | collective-permute-done | bytes 65568 | tf_op jit(solution)/shard_map/ppermute | solution.py:37
  132.9 1.3 select_reduce_fusion
  138.1 1.3 collective-permute-start.46
  139.5 5.8 %multiply_convert_fusion = bf16[1024,1792]{1,0:T(8,128)(2,1)} fusion(bf16[512,1792]{1,0:T(8,128)(2,1)} %copy-done.5, bf16[512,256]{1,0:T(8,128)(2,1)} %get-tuple-element.27, bf16[512,256]{1,0:T(8,128)(2,1)} %get-tuple-element.29, bf16[512,256]{1,0:T(8,128)(2,1)} %get-tuple-element.28, bf16[512,256]{1,0:T(8,128)(2,1)} %get-tuple-element.26), kind=kOutput, calls=%fused_computation | convolution fusion | flops 1886912512 | bytes 6553600 | tf_op jit(solution)/shard_map/dot_general | solution.py:147
  145.9 1.3 collective-permute-start.48
  147.2 1.3 collective-permute-start.49
  148.5 1.3 collective-permute-start.50
  151.6 1.3 collective-permute-start.47
  152.9 1.8 %collective-permute-done.49 = bf16[128,256]{1,0:T(8,128)(2,1)S(1)} collective-permute-done((bf16[128,256]{1,0:T(8,128)(2,1)S(1)}, bf16[128,256]{1,0:T(8,128)(2,1)S(1)}, u32[]{:S(2)}, u32[]{:S(2)}) %collective-permute-start.49) | collective-permute-done | bytes 65568 | tf_op jit(solution)/shard_map/ppermute | solution.py:37
  154.7 2.6 %collective-permute-done.50 = bf16[128,256]{1,0:T(8,128)(2,1)S(1)} collective-permute-done((bf16[128,256]{1,0:T(8,128)(2,1)S(1)}, bf16[128,256]{1,0:T(8,128)(2,1)S(1)}, u32[]{:S(2)}, u32[]{:S(2)}) %collective-permute-start.50) | collective-permute-done | bytes 65568 | tf_op jit(solution)/shard_map/ppermute | solution.py:37
  157.8 2.8 %collective-permute-done.47 = bf16[256,256]{1,0:T(8,128)(2,1)S(1)} collective-permute-done((bf16[256,256]{1,0:T(8,128)(2,1)S(1)}, bf16[256,256]{1,0:T(8,128)(2,1)S(1)}, u32[]{:S(2)}, u32[]{:S(2)}) %collective-permute-start.47) | collective-permute-done | bytes 131104 | tf_op jit(solution)/shard_map/ppermute | solution.py:37
  161.2 1.6 fusion.1
  (174 shorter events, 39.7 us)
Async XLA Ops:
  0.6 8.3 %collective-permute-start = (bf16[8,1792]{1,0:T(8,128)(2,1)}, bf16[8,1792]{1,0:T(8,128)(2,1)S(1)}, u32[]{:S(2)}, u32[]{:S(2)}) collective-permute-start(bf16[8,1792]{1,0:T(8,128)(2,1)} %bitcast.66), channel_id=1, source_target_pairs={{0,1},{1,0},{2,3},{3,2},{4,5},{5,4},{6,7},{7,6},{8,9},{9,8},{10,11... | collective-permute-start | bytes 86024 | tf_op jit(solution)/shard_map/ppermute | solution.py:27
  4.0 88.1 %collective-permute-start.29 = (bf16[8,1792]{1,0:T(8,128)(2,1)}, bf16[8,1792]{1,0:T(8,128)(2,1)S(1)}, u32[]{:S(2)}, u32[]{:S(2)}) collective-permute-start(bf16[8,1792]{1,0:T(8,128)(2,1)} %bitcast.69), channel_id=1, source_target_pairs={{0,1},{1,0},{2,3},{3,2},{4,5},{5,4},{6,7},{7,6},{8,9},{9,8},{10,11... | collective-permute-start | bytes 86024 | tf_op jit(solution)/shard_map/ppermute | solution.py:27
  9.0 12.5 %collective-permute-start.1 = (bf16[16,1792]{1,0:T(8,128)(2,1)S(1)}, bf16[16,1792]{1,0:T(8,128)(2,1)S(1)}, u32[]{:S(2)}, u32[]{:S(2)}) collective-permute-start(bf16[16,1792]{1,0:T(8,128)(2,1)S(1)} %maximum_select_fusion.2), channel_id=1, source_target_pairs={{1,9},{3,11},{5,13},{7,15},{9,1},{11,3},{13,5},{15,7},{17,25},{19,... | collective-permute-start | bytes 172040 | tf_op jit(solution)/shard_map/ppermute | solution.py:27
  16.7 4.8 %collective-permute-start.3 = (bf16[16,1792]{1,0:T(8,128)(2,1)S(1)}, bf16[16,1792]{1,0:T(8,128)(2,1)S(1)}, u32[]{:S(2)}, u32[]{:S(2)}) collective-permute-start(bf16[16,1792]{1,0:T(8,128)(2,1)S(1)} %maximum_select_fusion.2), channel_id=1, source_target_pairs={{0,4},{1,13},{2,6},{3,15},{4,8},{5,1},{6,10},{7,3},{8,12},{9,5},{1... | collective-permute-start | bytes 172040 | tf_op jit(solution)/shard_map/ppermute | solution.py:27
  16.8 4.8 %collective-permute-start.2 = (bf16[16,1792]{1,0:T(8,128)(2,1)S(1)}, bf16[16,1792]{1,0:T(8,128)(2,1)S(1)}, u32[]{:S(2)}, u32[]{:S(2)}) collective-permute-start(bf16[16,1792]{1,0:T(8,128)(2,1)S(1)} %maximum_select_fusion.2), channel_id=1, source_target_pairs={{0,2},{1,15},{2,4},{3,1},{4,6},{5,3},{6,8},{7,5},{8,10},{9,7},{10,... | collective-permute-start | bytes 172040 | tf_op jit(solution)/shard_map/ppermute | solution.py:27
  16.9 6.6 %collective-permute-start.4 = (bf16[16,1792]{1,0:T(8,128)(2,1)S(1)}, bf16[16,1792]{1,0:T(8,128)(2,1)S(1)}, u32[]{:S(2)}, u32[]{:S(2)}) collective-permute-start(bf16[16,1792]{1,0:T(8,128)(2,1)S(1)} %maximum_select_fusion.2), channel_id=1, source_target_pairs={{0,6},{1,11},{2,8},{3,13},{4,10},{5,15},{6,12},{7,1},{8,14},{9,3},... | collective-permute-start | bytes 172040 | tf_op jit(solution)/shard_map/ppermute | solution.py:27
  23.5 13.3 %collective-permute-start.17 = (bf16[64,1792]{1,0:T(8,128)(2,1)S(1)}, bf16[64,1792]{1,0:T(8,128)(2,1)S(1)}, u32[]{:S(2)}, u32[]{:S(2)}) collective-permute-start(bf16[64,1792]{1,0:T(8,128)(2,1)S(1)} %pad_maximum_fusion.2), channel_id=1, source_target_pairs={{0,32},{1,33},{2,34},{3,35},{4,36},{5,37},{6,38},{7,39},{8,40},{9,... | collective-permute-start | bytes 688136 | tf_op jit(solution)/shard_map/ppermute | solution.py:27
  28.4 10.9 %collective-permute-start.8 = (bf16[128,256]{1,0:T(8,128)(2,1)S(1)}, bf16[128,256]{1,0:T(8,128)(2,1)S(1)}, u32[]{:S(2)}, u32[]{:S(2)}) collective-permute-start(bf16[128,256]{1,0:T(8,128)(2,1)S(1)} %get-tuple-element.62), channel_id=1, source_target_pairs={{0,192},{1,193},{2,194},{3,195},{4,196},{5,197},{6,198},{7,199},{8... | collective-permute-start | bytes 196616 | tf_op jit(solution)/shard_map/ppermute | solution.py:37
  32.9 6.4 %collective-permute-start.7 = (bf16[128,256]{1,0:T(8,128)(2,1)S(1)}, bf16[128,256]{1,0:T(8,128)(2,1)S(1)}, u32[]{:S(2)}, u32[]{:S(2)}) collective-permute-start(bf16[128,256]{1,0:T(8,128)(2,1)S(1)} %get-tuple-element.62), channel_id=1, source_target_pairs={{0,128},{64,192},{1,129},{65,193},{2,130},{66,194},{3,131},{67,195... | collective-permute-start | bytes 196616 | tf_op jit(solution)/shard_map/ppermute | solution.py:37
  34.2 3.8 %collective-permute-start.6 = (bf16[128,256]{1,0:T(8,128)(2,1)S(1)}, bf16[128,256]{1,0:T(8,128)(2,1)S(1)}, u32[]{:S(2)}, u32[]{:S(2)}) collective-permute-start(bf16[128,256]{1,0:T(8,128)(2,1)S(1)} %get-tuple-element.62), channel_id=1, source_target_pairs={{0,64},{64,128},{128,192},{1,65},{65,129},{129,193},{2,66},{66,130... | collective-permute-start | bytes 196616 | tf_op jit(solution)/shard_map/ppermute | solution.py:37
  36.8 10.4 %collective-permute-start.9 = (bf16[128,1792]{1,0:T(8,128)(2,1)S(1)}, bf16[128,1792]{1,0:T(8,128)(2,1)S(1)}, u32[]{:S(2)}, u32[]{:S(2)}) collective-permute-start(bf16[128,1792]{1,0:T(8,128)(2,1)S(1)} %get-tuple-element.39), channel_id=1, source_target_pairs={{0,16},{1,49},{2,18},{3,51},{4,20},{5,53},{6,22},{7,55},{8,24},{9,... | collective-permute-start | bytes 1376264 | tf_op jit(solution)/shard_map/ppermute | solution.py:27
  38.0 2.4 %collective-permute-start.18 = (bf16[64,1792]{1,0:T(8,128)(2,1)S(1)}, bf16[64,1792]{1,0:T(8,128)(2,1)S(1)}, u32[]{:S(2)}, u32[]{:S(2)}) collective-permute-start(bf16[64,1792]{1,0:T(8,128)(2,1)S(1)} %collective-permute-done.17), channel_id=1, source_target_pairs={{0,1},{1,0},{2,3},{3,2},{4,5},{5,4},{6,7},{7,6},{8,9},{9,8},{10,11... | collective-permute-start | bytes 688136 | tf_op jit(solution)/shard_map/ppermute | solution.py:27
  40.7 7.5 %collective-permute-start.21 = (bf16[128,256]{1,0:T(8,128)(2,1)S(1)}, bf16[128,256]{1,0:T(8,128)(2,1)S(1)}, u32[]{:S(2)}, u32[]{:S(2)}) collective-permute-start(bf16[128,256]{1,0:T(8,128)(2,1)S(1)} %get-tuple-element.64), channel_id=1, source_target_pairs={{0,192},{1,193},{2,194},{3,195},{4,196},{5,197},{6,198},{7,199},{8... | collective-permute-start | bytes 196616 | tf_op jit(solution)/shard_map/ppermute | solution.py:37
  43.4 4.9 %collective-permute-start.20 = (bf16[128,256]{1,0:T(8,128)(2,1)S(1)}, bf16[128,256]{1,0:T(8,128)(2,1)S(1)}, u32[]{:S(2)}, u32[]{:S(2)}) collective-permute-start(bf16[128,256]{1,0:T(8,128)(2,1)S(1)} %get-tuple-element.64), channel_id=1, source_target_pairs={{0,128},{64,192},{1,129},{65,193},{2,130},{66,194},{3,131},{67,195... | collective-permute-start | bytes 196616 | tf_op jit(solution)/shard_map/ppermute | solution.py:37
  45.6 2.8 %collective-permute-start.19 = (bf16[128,256]{1,0:T(8,128)(2,1)S(1)}, bf16[128,256]{1,0:T(8,128)(2,1)S(1)}, u32[]{:S(2)}, u32[]{:S(2)}) collective-permute-start(bf16[128,256]{1,0:T(8,128)(2,1)S(1)} %get-tuple-element.64), channel_id=1, source_target_pairs={{0,64},{64,128},{128,192},{1,65},{65,129},{129,193},{2,66},{66,130... | collective-permute-start | bytes 196616 | tf_op jit(solution)/shard_map/ppermute | solution.py:37
  47.3 3.5 %collective-permute-start.10 = (bf16[128,1792]{1,0:T(8,128)(2,1)S(1)}, bf16[128,1792]{1,0:T(8,128)(2,1)S(1)}, u32[]{:S(2)}, u32[]{:S(2)}) collective-permute-start(bf16[128,1792]{1,0:T(8,128)(2,1)S(1)} %collective-permute-done.9), channel_id=1, source_target_pairs={{0,1},{1,0},{2,3},{3,2},{4,5},{5,4},{6,7},{7,6},{8,9},{9,8},{10,11... | collective-permute-start | bytes 1376264 | tf_op jit(solution)/shard_map/ppermute | solution.py:27
  49.1 9.0 %collective-permute-start.22 = (bf16[64,1792]{1,0:T(8,128)(2,1)S(1)}, bf16[64,1792]{1,0:T(8,128)(2,1)S(1)}, u32[]{:S(2)}, u32[]{:S(2)}) collective-permute-start(bf16[64,1792]{1,0:T(8,128)(2,1)S(1)} %slice.89), channel_id=1, source_target_pairs={{0,1},{1,0},{2,3},{3,2},{4,5},{5,4},{6,7},{7,6},{8,9},{9,8},{10,11... | collective-permute-start | bytes 688136 | tf_op jit(solution)/shard_map/ppermute | solution.py:27
  51.2 8.3 %collective-permute-start.13 = (bf16[256,256]{1,0:T(8,128)(2,1)S(1)}, bf16[256,256]{1,0:T(8,128)(2,1)S(1)}, u32[]{:S(2)}, u32[]{:S(2)}) collective-permute-start(bf16[256,256]{1,0:T(8,128)(2,1)S(1)} %get-tuple-element.60), channel_id=1, source_target_pairs={{0,192},{1,193},{2,194},{3,195},{4,196},{5,197},{6,198},{7,199},{8... | collective-permute-start | bytes 393224 | tf_op jit(solution)/shard_map/ppermute | solution.py:37
  53.9 5.9 %collective-permute-start.12 = (bf16[256,256]{1,0:T(8,128)(2,1)S(1)}, bf16[256,256]{1,0:T(8,128)(2,1)S(1)}, u32[]{:S(2)}, u32[]{:S(2)}) collective-permute-start(bf16[256,256]{1,0:T(8,128)(2,1)S(1)} %get-tuple-element.60), channel_id=1, source_target_pairs={{0,128},{64,192},{1,129},{65,193},{2,130},{66,194},{3,131},{67,195... | collective-permute-start | bytes 393224 | tf_op jit(solution)/shard_map/ppermute | solution.py:37
  56.9 5.7 %collective-permute-start.11 = (bf16[256,256]{1,0:T(8,128)(2,1)S(1)}, bf16[256,256]{1,0:T(8,128)(2,1)S(1)}, u32[]{:S(2)}, u32[]{:S(2)}) collective-permute-start(bf16[256,256]{1,0:T(8,128)(2,1)S(1)} %get-tuple-element.60), channel_id=1, source_target_pairs={{0,64},{64,128},{128,192},{1,65},{65,129},{129,193},{2,66},{66,130... | collective-permute-start | bytes 393224 | tf_op jit(solution)/shard_map/ppermute | solution.py:37
  58.3 17.9 %collective-permute-start.23 = (bf16[64,1792]{1,0:T(8,128)(2,1)S(1)}, bf16[64,1792]{1,0:T(8,128)(2,1)S(1)}, u32[]{:S(2)}, u32[]{:S(2)}) collective-permute-start(bf16[64,1792]{1,0:T(8,128)(2,1)S(1)} %add_convert_fusion.1), channel_id=1, source_target_pairs={{0,32},{1,33},{2,34},{3,35},{4,36},{5,37},{6,38},{7,39},{8,40},{9,... | collective-permute-start | bytes 688136 | tf_op jit(solution)/shard_map/ppermute | solution.py:27
  63.8 2.5 %collective-permute-start.14 = (bf16[128,1792]{1,0:T(8,128)(2,1)S(1)}, bf16[128,1792]{1,0:T(8,128)(2,1)S(1)}, u32[]{:S(2)}, u32[]{:S(2)}) collective-permute-start(bf16[128,1792]{1,0:T(8,128)(2,1)S(1)} %slice.85), channel_id=1, source_target_pairs={{0,1},{1,0},{2,3},{3,2},{4,5},{5,4},{6,7},{7,6},{8,9},{9,8},{10,11... | collective-permute-start | bytes 1376264 | tf_op jit(solution)/shard_map/ppermute | solution.py:27
  66.4 8.6 %collective-permute-start.15 = (bf16[128,1792]{1,0:T(8,128)(2,1)S(1)}, bf16[128,1792]{1,0:T(8,128)(2,1)S(1)}, u32[]{:S(2)}, u32[]{:S(2)}) collective-permute-start(bf16[128,1792]{1,0:T(8,128)(2,1)S(1)} %add_convert_fusion), channel_id=1, source_target_pairs={{0,48},{1,17},{2,50},{3,19},{4,52},{5,21},{6,54},{7,23},{8,56},{9,... | collective-permute-start | bytes 1376264 | tf_op jit(solution)/shard_map/ppermute | solution.py:27
  75.7 1.6 collective-permute-start.16
  77.4 9.6 %collective-permute-start.24 = (bf16[16,1792]{1,0:T(8,128)(2,1)S(1)}, bf16[16,1792]{1,0:T(8,128)(2,1)S(1)}, u32[]{:S(2)}, u32[]{:S(2)}) collective-permute-start(bf16[16,1792]{1,0:T(8,128)(2,1)S(1)} %get-tuple-element.42), channel_id=1, source_target_pairs={{1,9},{3,11},{5,13},{7,15},{9,1},{11,3},{13,5},{15,7},{17,25},{19,... | collective-permute-start | bytes 172040 | tf_op jit(solution)/shard_map/ppermute | solution.py:27
  82.8 6.2 %collective-permute-start.27 = (bf16[16,1792]{1,0:T(8,128)(2,1)S(1)}, bf16[16,1792]{1,0:T(8,128)(2,1)S(1)}, u32[]{:S(2)}, u32[]{:S(2)}) collective-permute-start(bf16[16,1792]{1,0:T(8,128)(2,1)S(1)} %get-tuple-element.43), channel_id=1, source_target_pairs={{0,10},{1,7},{2,12},{3,9},{4,14},{5,11},{6,0},{7,13},{8,2},{9,15},... | collective-permute-start | bytes 172040 | tf_op jit(solution)/shard_map/ppermute | solution.py:27
  84.5 7.5 %collective-permute-start.26 = (bf16[16,1792]{1,0:T(8,128)(2,1)S(1)}, bf16[16,1792]{1,0:T(8,128)(2,1)S(1)}, u32[]{:S(2)}, u32[]{:S(2)}) collective-permute-start(bf16[16,1792]{1,0:T(8,128)(2,1)S(1)} %get-tuple-element.44), channel_id=1, source_target_pairs={{0,12},{1,5},{2,14},{3,7},{4,0},{5,9},{6,2},{7,11},{8,4},{9,13},{1... | collective-permute-start | bytes 172040 | tf_op jit(solution)/shard_map/ppermute | solution.py:27
  86.9 5.1 %collective-permute-start.25 = (bf16[16,1792]{1,0:T(8,128)(2,1)S(1)}, bf16[16,1792]{1,0:T(8,128)(2,1)S(1)}, u32[]{:S(2)}, u32[]{:S(2)}) collective-permute-start(bf16[16,1792]{1,0:T(8,128)(2,1)S(1)} %get-tuple-element.45), channel_id=1, source_target_pairs={{0,14},{1,3},{2,0},{3,5},{4,2},{5,7},{6,4},{7,9},{8,6},{9,11},{10,... | collective-permute-start | bytes 172040 | tf_op jit(solution)/shard_map/ppermute | solution.py:27
  93.4 10.4 %collective-permute-start.30 = (bf16[16,1792]{1,0:T(8,128)(2,1)S(1)}, bf16[16,1792]{1,0:T(8,128)(2,1)S(1)}, u32[]{:S(2)}, u32[]{:S(2)}) collective-permute-start(bf16[16,1792]{1,0:T(8,128)(2,1)S(1)} %subtract_convert_fusion), channel_id=1, source_target_pairs={{1,9},{3,11},{5,13},{7,15},{9,1},{11,3},{13,5},{15,7},{17,25},{19,... | collective-permute-start | bytes 172040 | tf_op jit(solution)/shard_map/ppermute | solution.py:27
  99.6 4.8 %collective-permute-start.33 = (bf16[16,1792]{1,0:T(8,128)(2,1)S(1)}, bf16[16,1792]{1,0:T(8,128)(2,1)S(1)}, u32[]{:S(2)}, u32[]{:S(2)}) collective-permute-start(bf16[16,1792]{1,0:T(8,128)(2,1)S(1)} %subtract_convert_fusion), channel_id=1, source_target_pairs={{0,6},{1,11},{2,8},{3,13},{4,10},{5,15},{6,12},{7,1},{8,14},{9,3},... | collective-permute-start | bytes 172040 | tf_op jit(solution)/shard_map/ppermute | solution.py:27
  101.0 5.0 %collective-permute-start.32 = (bf16[16,1792]{1,0:T(8,128)(2,1)S(1)}, bf16[16,1792]{1,0:T(8,128)(2,1)S(1)}, u32[]{:S(2)}, u32[]{:S(2)}) collective-permute-start(bf16[16,1792]{1,0:T(8,128)(2,1)S(1)} %subtract_convert_fusion), channel_id=1, source_target_pairs={{0,4},{1,13},{2,6},{3,15},{4,8},{5,1},{6,10},{7,3},{8,12},{9,5},{1... | collective-permute-start | bytes 172040 | tf_op jit(solution)/shard_map/ppermute | solution.py:27
  102.6 3.6 %collective-permute-start.31 = (bf16[16,1792]{1,0:T(8,128)(2,1)S(1)}, bf16[16,1792]{1,0:T(8,128)(2,1)S(1)}, u32[]{:S(2)}, u32[]{:S(2)}) collective-permute-start(bf16[16,1792]{1,0:T(8,128)(2,1)S(1)} %subtract_convert_fusion), channel_id=1, source_target_pairs={{0,2},{1,15},{2,4},{3,1},{4,6},{5,3},{6,8},{7,5},{8,10},{9,7},{10,... | collective-permute-start | bytes 172040 | tf_op jit(solution)/shard_map/ppermute | solution.py:27
  106.2 10.8 %collective-permute-start.37 = (bf16[64,1792]{1,0:T(8,128)(2,1)S(1)}, bf16[64,1792]{1,0:T(8,128)(2,1)S(1)}, u32[]{:S(2)}, u32[]{:S(2)}) collective-permute-start(bf16[64,1792]{1,0:T(8,128)(2,1)S(1)} %pad_maximum_fusion.3), channel_id=1, source_target_pairs={{0,32},{1,33},{2,34},{3,35},{4,36},{5,37},{6,38},{7,39},{8,40},{9,... | collective-permute-start | bytes 688136 | tf_op jit(solution)/shard_map/ppermute | solution.py:27
  108.9 10.8 %collective-permute-start.35 = (bf16[128,1792]{1,0:T(8,128)(2,1)S(1)}, bf16[128,1792]{1,0:T(8,128)(2,1)S(1)}, u32[]{:S(2)}, u32[]{:S(2)}) collective-permute-start(bf16[128,1792]{1,0:T(8,128)(2,1)S(1)} %get-tuple-element.40), channel_id=1, source_target_pairs={{0,16},{1,49},{2,18},{3,51},{4,20},{5,53},{6,22},{7,55},{8,24},{9,... | collective-permute-start | bytes 1376264 | tf_op jit(solution)/shard_map/ppermute | solution.py:27
  111.6 9.0 %collective-permute-start.42 = (bf16[128,256]{1,0:T(8,128)(2,1)S(1)}, bf16[128,256]{1,0:T(8,128)(2,1)S(1)}, u32[]{:S(2)}, u32[]{:S(2)}) collective-permute-start(bf16[128,256]{1,0:T(8,128)(2,1)S(1)} %convolution_convert_fusion.11), channel_id=1, source_target_pairs={{64,0},{128,64},{192,128},{65,1},{129,65},{193,129},{66,2},{130,66... | collective-permute-start | bytes 196616 | tf_op jit(solution)/shard_map/ppermute | solution.py:37
  112.9 8.0 %collective-permute-start.43 = (bf16[128,256]{1,0:T(8,128)(2,1)S(1)}, bf16[128,256]{1,0:T(8,128)(2,1)S(1)}, u32[]{:S(2)}, u32[]{:S(2)}) collective-permute-start(bf16[128,256]{1,0:T(8,128)(2,1)S(1)} %convolution_convert_fusion.10), channel_id=1, source_target_pairs={{128,0},{192,64},{129,1},{193,65},{130,2},{194,66},{131,3},{195,67... | collective-permute-start | bytes 196616 | tf_op jit(solution)/shard_map/ppermute | solution.py:37
  114.6 9.2 %collective-permute-start.44 = (bf16[128,256]{1,0:T(8,128)(2,1)S(1)}, bf16[128,256]{1,0:T(8,128)(2,1)S(1)}, u32[]{:S(2)}, u32[]{:S(2)}) collective-permute-start(bf16[128,256]{1,0:T(8,128)(2,1)S(1)} %convolution_convert_fusion.9), channel_id=1, source_target_pairs={{192,0},{193,1},{194,2},{195,3},{196,4},{197,5},{198,6},{199,7},{2... | collective-permute-start | bytes 196616 | tf_op jit(solution)/shard_map/ppermute | solution.py:37
  117.1 10.7 %collective-permute-start.38 = (bf16[64,1792]{1,0:T(8,128)(2,1)S(1)}, bf16[64,1792]{1,0:T(8,128)(2,1)S(1)}, u32[]{:S(2)}, u32[]{:S(2)}) collective-permute-start(bf16[64,1792]{1,0:T(8,128)(2,1)S(1)} %collective-permute-done.37), channel_id=1, source_target_pairs={{0,1},{1,0},{2,3},{3,2},{4,5},{5,4},{6,7},{7,6},{8,9},{9,8},{10,11... | collective-permute-start | bytes 688136 | tf_op jit(solution)/shard_map/ppermute | solution.py:27
  119.7 4.6 %collective-permute-start.36 = (bf16[128,1792]{1,0:T(8,128)(2,1)S(1)}, bf16[128,1792]{1,0:T(8,128)(2,1)S(1)}, u32[]{:S(2)}, u32[]{:S(2)}) collective-permute-start(bf16[128,1792]{1,0:T(8,128)(2,1)S(1)} %collective-permute-done.35), channel_id=1, source_target_pairs={{0,1},{1,0},{2,3},{3,2},{4,5},{5,4},{6,7},{7,6},{8,9},{9,8},{10,11... | collective-permute-start | bytes 1376264 | tf_op jit(solution)/shard_map/ppermute | solution.py:27
  134.8 13.8 %collective-permute-start.41 = (f32[8,128]{1,0:T(8,128)S(1)}, f32[8,128]{1,0:T(8,128)S(1)}, u32[]{:S(2)}, u32[]{:S(2)}) collective-permute-start(f32[8,128]{1,0:T(8,128)S(1)} %broadcast_in_dim.82), channel_id=1, source_target_pairs={{0,192},{64,0},{128,64},{192,128},{1,193},{65,1},{129,65},{193,129... | collective-permute-start | bytes 12296 | tf_op jit(solution)/shard_map/ppermute | solution.py:163
  135.7 11.5 %collective-permute-start.40 = (f32[8,128]{1,0:T(8,128)S(1)}, f32[8,128]{1,0:T(8,128)S(1)}, u32[]{:S(2)}, u32[]{:S(2)}) collective-permute-start(f32[8,128]{1,0:T(8,128)S(1)} %broadcast_in_dim.82), channel_id=1, source_target_pairs={{0,128},{64,192},{128,0},{192,64},{1,129},{65,193},{129,1},{193,65... | collective-permute-start | bytes 12296 | tf_op jit(solution)/shard_map/ppermute | solution.py:163
  136.5 9.3 %collective-permute-start.39 = (f32[8,128]{1,0:T(8,128)S(1)}, f32[8,128]{1,0:T(8,128)S(1)}, u32[]{:S(2)}, u32[]{:S(2)}) collective-permute-start(f32[8,128]{1,0:T(8,128)S(1)} %broadcast_in_dim.82), channel_id=1, source_target_pairs={{0,64},{64,128},{128,192},{192,0},{1,65},{65,129},{129,193},{193,1... | collective-permute-start | bytes 12296 | tf_op jit(solution)/shard_map/ppermute | solution.py:163
  136.8 20.9 %collective-permute-start.45 = (bf16[256,256]{1,0:T(8,128)(2,1)}, bf16[256,256]{1,0:T(8,128)(2,1)S(1)}, u32[]{:S(2)}, u32[]{:S(2)}) collective-permute-start(bf16[256,256]{1,0:T(8,128)(2,1)} %convolution_convert_fusion.5), channel_id=1, source_target_pairs={{64,0},{128,64},{192,128},{65,1},{129,65},{193,129},{66,2},{130,66... | collective-permute-start | bytes 393224 | tf_op jit(solution)/shard_map/ppermute | solution.py:37
  138.1 19.6 %collective-permute-start.46 = (bf16[256,256]{1,0:T(8,128)(2,1)}, bf16[256,256]{1,0:T(8,128)(2,1)S(1)}, u32[]{:S(2)}, u32[]{:S(2)}) collective-permute-start(bf16[256,256]{1,0:T(8,128)(2,1)} %convolution_convert_fusion.4), channel_id=1, source_target_pairs={{128,0},{192,64},{129,1},{193,65},{130,2},{194,66},{131,3},{195,67... | collective-permute-start | bytes 393224 | tf_op jit(solution)/shard_map/ppermute | solution.py:37
  145.9 5.7 %collective-permute-start.48 = (bf16[128,256]{1,0:T(8,128)(2,1)S(1)}, bf16[128,256]{1,0:T(8,128)(2,1)S(1)}, u32[]{:S(2)}, u32[]{:S(2)}) collective-permute-start(bf16[128,256]{1,0:T(8,128)(2,1)S(1)} %copy-done.9), channel_id=1, source_target_pairs={{64,0},{128,64},{192,128},{65,1},{129,65},{193,129},{66,2},{130,66... | collective-permute-start | bytes 196616 | tf_op jit(solution)/shard_map/ppermute | solution.py:37
  147.2 7.5 %collective-permute-start.49 = (bf16[128,256]{1,0:T(8,128)(2,1)S(1)}, bf16[128,256]{1,0:T(8,128)(2,1)S(1)}, u32[]{:S(2)}, u32[]{:S(2)}) collective-permute-start(bf16[128,256]{1,0:T(8,128)(2,1)S(1)} %copy-done.8), channel_id=1, source_target_pairs={{128,0},{192,64},{129,1},{193,65},{130,2},{194,66},{131,3},{195,67... | collective-permute-start | bytes 196616 | tf_op jit(solution)/shard_map/ppermute | solution.py:37
  148.5 8.7 %collective-permute-start.50 = (bf16[128,256]{1,0:T(8,128)(2,1)S(1)}, bf16[128,256]{1,0:T(8,128)(2,1)S(1)}, u32[]{:S(2)}, u32[]{:S(2)}) collective-permute-start(bf16[128,256]{1,0:T(8,128)(2,1)S(1)} %convolution_convert_fusion.6), channel_id=1, source_target_pairs={{192,0},{193,1},{194,2},{195,3},{196,4},{197,5},{198,6},{199,7},{2... | collective-permute-start | bytes 196616 | tf_op jit(solution)/shard_map/ppermute | solution.py:37
  151.6 9.0 %collective-permute-start.47 = (bf16[256,256]{1,0:T(8,128)(2,1)S(1)}, bf16[256,256]{1,0:T(8,128)(2,1)S(1)}, u32[]{:S(2)}, u32[]{:S(2)}) collective-permute-start(bf16[256,256]{1,0:T(8,128)(2,1)S(1)} %copy-done.6), channel_id=1, source_target_pairs={{192,0},{193,1},{194,2},{195,3},{196,4},{197,5},{198,6},{199,7},{2... | collective-permute-start | bytes 393224 | tf_op jit(solution)/shard_map/ppermute | solution.py:37
  (17 other events, 255.9 us)

commit v3 on v1

v3 whole, which is shorter than its diff:
```python
import functools

import jax
import jax.numpy as jnp
from jax import lax
from jax.experimental import pallas as pl
from jax.experimental.pallas import tpu as pltpu
from jax.sharding import PartitionSpec as P

TILE = 64
NTILE = 8
CAP = 6
Y, Z, C = 4, 8, 2
BF = jnp.bfloat16
F32 = jnp.float32
STEPS = (0, 1, 3, 2)


def index_of(y, z, c):
    return ((y % Y) * Z + z % Z) * C + c


def pairs(move, cores=(0, 1)):
    return [
        (index_of(y, z, c), index_of(*move(y, z, c)))
        for y in range(Y)
        for z in range(Z)
        for c in cores
    ]


def send(value, move, cores=(0, 1)):
    return lax.ppermute(value, "latent", pairs(move, cores))


def swap(value):
    return send(value, lambda y, z, c: (y, z, 1 - c))


def send_layer(value, steps):
    count = lax.axis_size("layer")
    sources = [s for s in range(count) if 0 <= s + steps < count]
    return lax.ppermute(value, "layer", [(s, s + steps) for s in sources])


def chip_rows(value, core):
    other = swap(value)
    return jnp.where(core == 0, jnp.concatenate([value, other]), jnp.concatenate([other, value]))


def spread_z(chip, core):
    near = [
        send(chip, lambda y, z, c, k=k: (y, z + k if c == 0 else z - k, c)) for k in (1, 2, 3)
    ]
    far = send(chip, lambda y, z, c: (y, z + 4, c), (1,))
    return jnp.concatenate([jnp.where(core == 0, chip, far)] + near)


def spread_y(half):
    parts = [half] + [send(half, lambda y, z, c, k=k: (y ^ k, z, c)) for k in STEPS[1:]]
    return parts, [swap(part) for part in parts]


def collect(halves, core):
    width = halves[0].shape[-1]
    halves = [half.reshape(Y, 4 * 2 * 8, width) for half in halves]
    own = [
        (halves[0][k].astype(F32) + swap(halves[1][k]).astype(F32)).astype(BF) for k in range(Y)
    ]
    row = own[0].astype(F32)
    for part, k in zip(own[1:], STEPS[1:]):
        row = row + send(part, lambda y, z, c, k=k: (y ^ k, z, c)).astype(F32)
    row = row.astype(BF).reshape(4, 16, width)
    far = send(row[0], lambda y, z, c: (y, z + 4, c), (1,))
    total = jnp.where(core == 0, row[0], far).astype(F32)
    for k in (1, 2, 3):
        piece = send(row[k], lambda y, z, c, k=k: (y, z - k if c == 0 else z + k, c))
        total = total + piece.astype(F32)
    total = total.astype(BF)
    return total.astype(F32) + swap(total).astype(F32)


def shard_chips(latent):
    y, z, c = latent // (Z * C), latent // C % Z, latent % C
    p = jnp.arange(Y * Z, dtype=jnp.int32)
    half, step, j = p // 16, p // 4 % 4, p % 4
    step = jnp.where(step < 2, step, 5 - step)
    side = (half + c) % 2
    from_z = jnp.where(side == 0, z - j, jnp.where(j == 0, z + 4, z + j)) % Z
    return (y ^ step) * Z + from_z


SMALL = pl.CostEstimate(flops=1000, bytes_accessed=1000, transcendentals=0)


def params(mib):
    return pltpu.CompilerParams(vmem_limit_bytes=mib * 1024 * 1024)


def join(parts, out_ref):
    at = 0
    for part in parts:
        out_ref[at : at + part.shape[0]] = part[...]
        at += part.shape[0]


def picked(slot, rows):
    at = lax.broadcasted_iota(jnp.int32, (CAP * TILE, rows), 0)
    return (at == slot).astype(F32).astype(BF)


def unpack(slot, packed):
    at = lax.broadcasted_iota(jnp.int32, (slot.shape[1], packed.shape[0]), 1)
    pick = (at == column(slot)).astype(F32).astype(BF)
    return jnp.dot(pick, packed, preferred_element_type=F32)


def column(row):
    return jnp.broadcast_to(row, (128, row.shape[1])).T[:, :1]


def early(halves):
    return [*halves[0][:-1], *halves[1][:-1]]


def late(halves):
    return [halves[0][-1], halves[1][-1]]


def early_late(row, rows_each):
    cut = 2 * rows_each - rows_each // 2
    return jnp.concatenate(
        [row[:, :cut], row[:, 2 * rows_each :][:, :cut], row[:, cut : 2 * rows_each]]
        + [row[:, 2 * rows_each + cut :]],
        axis=1,
    )


def encode_early_kernel(weight_ref, bias_ref, *refs):
    parts, (out_ref, rows_ref) = refs[:-2], refs[-2:]
    join(parts, rows_ref)
    out_ref[...] = (
        jnp.dot(rows_ref[...], weight_ref[...], preferred_element_type=F32) + bias_ref[...]
    )


def encode_early(weight, bias, parts):
    count = sum(part.shape[0] for part in parts)
    width, feats = weight.shape
    return pl.pallas_call(
        encode_early_kernel,
        out_shape=jax.ShapeDtypeStruct((count, feats), F32),
        scratch_shapes=[pltpu.VMEM((count, width), BF)],
        compiler_params=params(10),
        cost_estimate=SMALL,
        name="encode_early",
    )(weight, bias, *parts)


def encode_late_kernel(slot_ref, weight_ref, bias_ref, preact_ref, *refs):
    parts, (packed_ref, codes_ref, on_ref, rows_ref) = refs[:-4], refs[-4:]
    join(parts, rows_ref)
    last = jnp.dot(rows_ref[...], weight_ref[...], preferred_element_type=F32) + bias_ref[...]
    count = preact_ref.shape[0]
    slot = slot_ref[:1, :]
    live = column(slot) >= 0
    packed = None
    each, rest = count // 2, last.shape[0] // 2
    for preact, at, size in ((preact_ref[...], 0, each), (last, count, rest)):
        end = at + preact.shape[0]
        on = jnp.where(live[at:end] & (preact > 0), 1.0, 0.0)
        codes = jnp.where(on > 0, preact, 0.0).astype(BF)
        on = on.astype(BF)
        term = jnp.dot(picked(slot[:, at:end], end - at), codes, preferred_element_type=F32)
        packed = term if packed is None else packed + term
        for half in range(2):
            to = half * (each + rest) + (each if at else 0)
            codes_ref[to : to + size] = codes[half * size : half * size + size]
            on_ref[to : to + size] = on[half * size : half * size + size]
    packed_ref[...] = packed.astype(BF)


def encode_late(slot, weight, bias, preact, parts):
    count = sum(part.shape[0] for part in parts)
    width, feats = weight.shape
    total = preact.shape[0] + count
    return pl.pallas_call(
        encode_late_kernel,
        out_shape=[
            jax.ShapeDtypeStruct((CAP * TILE, feats), BF),
            jax.ShapeDtypeStruct((total, feats), BF),
            jax.ShapeDtypeStruct((total, feats), BF),
        ],
        scratch_shapes=[pltpu.VMEM((count, width), BF)],
        compiler_params=params(10),
        cost_estimate=SMALL,
        name="encode_late",
    )(slot, weight, bias, preact, *parts)


def turn_kernel(after_ref, *refs):
    parts, (out_ref, token_ref) = refs[:-2], refs[-2:]
    at = 0
    for first, second in zip(parts[0::2], parts[1::2]):
        both = jnp.concatenate([first[...], second[...]])
        out_ref[:, at : at + both.shape[0]] = both.T
        at += both.shape[0]
    token_ref[...] = after_ref[:16, :128]


def turn(parts, after):
    count = sum(part.shape[0] for part in parts)
    return pl.pallas_call(
        turn_kernel,
        out_shape=[
            jax.ShapeDtypeStruct((parts[0].shape[1], count), BF),
            jax.ShapeDtypeStruct((16, 128), BF),
        ],
        compiler_params=params(10),
        cost_estimate=SMALL,
        name="turn",
    )(after, *parts)


def dec_gradient_kernel(layer_ref, codes_ref, first_ref, second_ref, weight_ref, *refs):
    del layer_ref
    parts, (out_ref, own_ref, errors_ref) = refs[:-3], refs[-3:]
    over_rows = (((0,), (0,)), ((), ()))

    @pl.when(pl.program_id(0) == 0)
    def _():
        join(parts, errors_ref)
        own_ref[...] = lax.dot_general(
            errors_ref[...], weight_ref[...], (((1,), (1,)), ((), ())), preferred_element_type=F32
        )
        grad = lax.dot_general(
            codes_ref[...], errors_ref[...], over_rows, preferred_element_type=F32
        )
        out_ref[0] = (grad * (1.0 / TILE)).astype(BF)

    @pl.when(pl.program_id(0) > 0)
    def _():
        count = first_ref.shape[1]
        grad = lax.dot_general(
            first_ref[0], errors_ref[:count], over_rows, preferred_element_type=F32
        ) + lax.dot_general(
            second_ref[0], errors_ref[count:], over_rows, preferred_element_type=F32
        )
        out_ref[0] = (grad * (1.0 / TILE)).astype(BF)


def dec_gradient(layer, codes, first, second, weight, parts):
    layers = first.shape[0] + 1
    feats, width = weight.shape
    count = codes.shape[0]
    other = lambda k, at: (lax.max(k - 1, 0), 0, 0)
    whole = lambda array: pl.BlockSpec(array.shape, lambda k, at: (0,) * array.ndim)
    return pl.pallas_call(
        dec_gradient_kernel,
        grid_spec=pltpu.PrefetchScalarGridSpec(
            num_scalar_prefetch=1,
            grid=(layers,),
            in_specs=[
                whole(codes),
                pl.BlockSpec((1, *first.shape[1:]), other),
                pl.BlockSpec((1, *second.shape[1:]), other),
                whole(weight),
                *[whole(part) for part in parts],
            ],
            out_specs=[
                pl.BlockSpec(
                    (1, feats, width), lambda k, at: (lax.rem(at[0] - k + layers, layers), 0, 0)
                ),
                pl.BlockSpec((count, feats), lambda k, at: (0, 0)),
            ],
            scratch_shapes=[pltpu.VMEM((count, width), BF)],
        ),
        out_shape=[
            jax.ShapeDtypeStruct((layers, feats, width), BF),
            jax.ShapeDtypeStruct((count, feats), F32),
        ],
        compiler_params=params(20),
        cost_estimate=SMALL,
        name="dec_gradient",
    )(layer.reshape(1), codes, first, second, weight, *parts)


def add_squares(parts, out_ref, start):
    for part in parts:
        count, width = part.shape
        for at in range(0, count, 16):
            value = part[at : at + 16, :].astype(F32)
            value = value * value
            value = value[:8] + value[8:]
            total = value[:, :128]
            for lane in range(128, width, 128):
                total = total + value[:, lane : lane + 128]
            out_ref[start] = total
            start += 1


def back_early_kernel(layers, *refs):
    weights, parts = refs[: layers - 1], refs[layers - 1 : -3]
    out_ref, squares_ref, errors_ref = refs[-3:]
    join(parts, errors_ref)
    add_squares(parts, squares_ref, 0)
    for k in range(layers - 1):
        back = lax.dot_general(
            errors_ref[...],
            weights[k][...],
            (((1,), (1,)), ((), ())),
            preferred_element_type=F32,
        )
        out_ref[k] = back.astype(BF)


def back_early(weights, parts):
    count = sum(part.shape[0] for part in parts)
    feats, width = weights[0].shape
    return pl.pallas_call(
        functools.partial(back_early_kernel, len(weights) + 1),
        out_shape=[
            jax.ShapeDtypeStruct((len(weights), count, feats), BF),
            jax.ShapeDtypeStruct((count // 16, 8, 128), F32),
        ],
        scratch_shapes=[pltpu.VMEM((count, width), BF)],
        compiler_params=params(12),
        cost_estimate=SMALL,
        name="back_early",
    )(*weights, *parts)


def back_late_kernel(layers, place_ref, slot_ref, squares_ref, backs_ref, *refs):
    weights, refs = refs[: layers - 1], refs[layers - 1 :]
    parts, away = refs[: -layers - 1], refs[-layers - 1 : -2]
    errors_ref, sums_ref = refs[-2:]
    join(parts, errors_ref)
    count = squares_ref.shape[0]
    sums_ref[:count] = squares_ref[...]
    add_squares(parts, sums_ref, count)
    total = jnp.zeros((8, 128), F32)
    for chip in range(Y * Z):
        total = total + sums_ref[place_ref[chip]]
    left = jnp.broadcast_to(jnp.sum(total), (16, weights[0].shape[0]))
    row = lax.broadcasted_iota(jnp.int32, left.shape, 0)
    split = jnp.zeros(left.shape, F32)
    for k in range(3):
        piece = left.astype(BF).astype(F32)
        split = jnp.where(row == k, piece, split)
        left = left - piece
    packed = CAP * TILE
    before = backs_ref.shape[1]
    for k in range(1, layers):
        back = lax.dot_general(
            errors_ref[...],
            weights[k - 1][...],
            (((1,), (1,)), ((), ())),
            preferred_element_type=F32,
        )
        slot = slot_ref[k : k + 1, :]
        pick = picked(slot, slot.shape[1])
        here = jnp.dot(pick[:, :before], backs_ref[k - 1], preferred_element_type=F32)
        here = here + jnp.dot(pick[:, before:], back.astype(BF), preferred_element_type=F32)
        away[k - 1][:packed] = here.astype(BF)
        away[k - 1][packed:] = split.astype(BF)


def back_late(place, slot, squares, backs, weights, parts):
    layers = len(weights) + 1
    feats, width = weights[0].shape
    count = sum(part.shape[0] for part in parts)
    vmem = pl.BlockSpec(memory_space=pltpu.VMEM)
    return pl.pallas_call(
        functools.partial(back_late_kernel, layers),
        in_specs=[pl.BlockSpec(memory_space=pltpu.SMEM)]
        + [vmem] * (3 + len(weights) + len(parts)),
        out_specs=[vmem] * (layers - 1),
        out_shape=[jax.ShapeDtypeStruct((CAP * TILE + 16, feats), BF)] * (layers - 1),
        scratch_shapes=[pltpu.VMEM((count, width), BF), pltpu.VMEM((Y * Z, 8, 128), F32)],
        compiler_params=params(12),
        cost_estimate=SMALL,
        name="back_late",
    )(place, slot, squares, backs, *weights, *parts)


def decode_kernel(slot_ref, token_ref, codes_ref, *refs):
    del token_ref
    layers = (len(refs) - 1) // 2
    came, weights, out_ref, sources_ref = (
        refs[: layers - 1],
        refs[layers - 1 : 2 * layers - 1],
        refs[-2],
        refs[-1],
    )
    total = jnp.dot(codes_ref[...], weights[0][...], preferred_element_type=F32)
    for k in range(1, layers):
        source = unpack(slot_ref[k : k + 1, :], came[k - 1][...]).astype(BF)
        sources_ref[k - 1] = source
        total = total + jnp.dot(source, weights[k][...], preferred_element_type=F32)
    out_ref[...] = total.astype(BF)


def decode(slot, token, codes, came, weights):
    count, feats = codes.shape
    width = weights[0].shape[1]
    return pl.pallas_call(
        decode_kernel,
        out_shape=[
            jax.ShapeDtypeStruct((count, width), BF),
            jax.ShapeDtypeStruct((len(came), count, feats), BF),
        ],
        compiler_params=params(14),
        cost_estimate=SMALL,
        name="decode",
    )(slot, token, codes, *came, *weights)


def code_gradient_kernel(slot_ref, errors_ref, weight_ref, square_ref, out_ref):
    back = lax.dot_general(
        errors_ref[...], weight_ref[...], (((1,), (1,)), ((), ())), preferred_element_type=F32
    )
    count = CAP * TILE
    at = lax.broadcasted_iota(jnp.int32, (count, back.shape[0]), 0)
    pick = (at == slot_ref[...]).astype(F32).astype(BF)
    out_ref[:count] = jnp.dot(pick, back.astype(BF), preferred_element_type=F32).astype(BF)
    out_ref[count:] = square_ref[...]


def code_gradient(slot, errors, weight, square):
    return pl.pallas_call(
        code_gradient_kernel,
        out_shape=jax.ShapeDtypeStruct((CAP * TILE + 16, weight.shape[0]), BF),
        compiler_params=params(10),
        cost_estimate=SMALL,
        name="code_gradient",
    )(slot[None], errors, weight, square)


def enc_gradient_kernel(count, layer_ref, slot_ref, rows_ref, on_ref, own_ref, away_ref, *refs):
    came, (enc_ref, bias_ref, loss_ref, pre_ref) = refs[:-4], refs[-4:]
    packed = CAP * TILE
    layers = len(came) + 1

    @pl.when(pl.program_id(0) == 0)
    def _():
        total = own_ref[...]
        for k, ref in enumerate(came, 1):
            part = unpack(slot_ref[:1, :], ref[:packed])
            total = total + jnp.where(layer_ref[0] + k < layers, part, 0.0)
        total = jnp.where(on_ref[...] > 0, total, 0.0)
        bias_ref[...] = jnp.sum(total, axis=0, keepdims=True) * (1.0 / TILE)
        pre_ref[...] = total.astype(BF)
        sums = []
        for block in [ref[packed:] for ref in (away_ref, *came)]:
            block = block.astype(F32)
            sums.append(block[0:1] + block[1:2] + block[2:3])
        loss = jnp.zeros_like(sums[0])
        for s in range(layers):
            for k in range(layers):
                mine = lax.rem(layer_ref[0] + k, layers) == s
                loss = loss + jnp.where(mine, sums[k], 0.0)
        loss_ref[...] = loss[:, :1] * (0.5 / count)

    grad = jnp.dot(rows_ref[...], pre_ref[...], preferred_element_type=F32)
    enc_ref[...] = (grad * (1.0 / TILE)).astype(BF)


def enc_gradient(layer, slot, rows, on, own, away, came):
    width, count = rows.shape
    feats = own.shape[1]
    whole = lambda array: pl.BlockSpec(array.shape, lambda i: (0,) * array.ndim)
    part = width // 2
    return pl.pallas_call(
        functools.partial(enc_gradient_kernel, (len(came) + 1) * count * width),
        grid=(width // part,),
        in_specs=[
            pl.BlockSpec(memory_space=pltpu.SMEM),
            whole(slot),
            pl.BlockSpec((part, count), lambda i: (i, 0)),
            whole(on),
            whole(own),
            whole(away),
            *[whole(array) for array in came],
        ],
        out_specs=[
            pl.BlockSpec((part, feats), lambda i: (i, 0)),
            pl.BlockSpec((1, feats), lambda i: (0, 0)),
            pl.BlockSpec((1, 1), lambda i: (0, 0)),
        ],
        out_shape=[
            jax.ShapeDtypeStruct((width, feats), BF),
            jax.ShapeDtypeStruct((1, feats), F32),
            jax.ShapeDtypeStruct((1, 1), F32),
        ],
        scratch_shapes=[pltpu.VMEM((count, feats), BF)],
        compiler_params=params(12),
        cost_estimate=SMALL,
        name="enc_gradient",
    )(layer.reshape(1), slot, rows, on, own, away, *came)


def shards(residual, target, enc_weight, enc_bias, dec_weight, active):
    layers = dec_weight.shape[0]
    width = residual.shape[-1]
    layer = lax.axis_index("layer")
    latent = lax.axis_index("latent")
    core = latent % C

    half = spread_z(chip_rows(residual[0], core), core)
    half, target, dec, active = lax.optimization_barrier((half, target, dec_weight, active))
    rows = spread_y(half)

    chips = shard_chips(latent)
    hit = jnp.any(active == latent, axis=2)
    hit = jnp.stack(
        [
            lax.dynamic_index_in_dim(hit, (layer - k) % layers, 0, keepdims=False)
            for k in range(layers)
        ]
    )
    live = jnp.any(
        (chips[:, None] // 4 == jnp.arange(NTILE)[None, :])[None] & hit[:, None, :], axis=2
    )
    before = jnp.arange(Y * Z)[None, :] <= jnp.arange(Y * Z)[:, None]
    slot = jnp.sum(jnp.where(before[None] & live[:, None, :], 1, 0), axis=2) - 1
    slot = jnp.where(live, slot * 16, -TILE * NTILE)
    slot = jnp.repeat(slot, 16, axis=1) + jnp.tile(jnp.arange(16), Y * Z)[None, :]
    ordered = early_late(slot, TILE * NTILE // 4)
    place = jnp.sum(
        jnp.where(
            early_late(jnp.repeat(chips, 16)[None], TILE * NTILE // 4)[:, ::16]
            == jnp.arange(Y * Z)[:, None],
            jnp.arange(Y * Z)[None, :],
            0,
        ),
        axis=1,
        dtype=jnp.int32,
    )
    weights = [
        lax.dynamic_index_in_dim(dec[:, 0], (layer - k) % layers, 0, keepdims=False)
        for k in range(layers)
    ]
    goal = chip_rows(target[0], core)

    preact = encode_early(enc_weight[0], enc_bias, early(rows))
    packed, codes, on = encode_late(ordered, enc_weight[0], enc_bias, preact, late(rows))
    came = [send_layer(packed, k) for k in range(1, layers)]
    turned, token = turn([*rows[0], *rows[1]], packed)
    count = codes.shape[0] // 2
    partial, sources = zip(
        *[
            decode(slot[:, at : at + count], token, codes[at : at + count], came, weights)
            for at in (0, count)
        ]
    )
    errors = (collect(partial, core) - goal.astype(F32)).astype(BF)
    errors = spread_y(spread_z(errors, core))
    backs, squares = back_early(weights[1:], early(errors))
    away = back_late(place, ordered, squares, backs, weights[1:], late(errors))
    came = []
    for k in range(1, layers):
        ring = [(s, (s - k) % layers) for s in range(layers)]
        came.append(lax.ppermute(away[k - 1], "layer", ring))
    dec_grad, own = dec_gradient(layer, codes, *sources, weights[0], [*errors[0], *errors[1]])
    enc_grad, bias_grad, loss = enc_gradient(layer, slot, turned, on, own, away[0], came)
    loss = loss[0, 0]
    return (loss, enc_grad[None], bias_grad, dec_grad[:, None])


def solution(mesh):
    in_specs = (
        P("layer", "latent", None),
        P("layer", "latent", None),
        P("layer", None, "latent"),
        P("layer", "latent"),
        P(None, "layer", "latent", None),
        P(),
    )
    out_specs = (
        P(),
        P("layer", None, "latent"),
        P("layer", "latent"),
        P(None, "layer", "latent", None),
    )
    return jax.shard_map(shards, mesh=mesh, in_specs=in_specs, out_specs=out_specs, check_vma=False)
```

time: 161 us -> 143 us (0.89); the launches traced: 159 us -> 143 us
  Pallas kernels: 0 us -> 23.3 us
  matrix products: 13.7 us -> 0 us
  starting transfers between devices: 74.2 us -> 64.6 us
  waiting for transfers between devices: 51.4 us -> 44.2 us
  other arithmetic: 10.6 us -> 3.56 us
  between operations: 5.08 us -> 1.19 us
  local copies, waits for them, and re-layouts: 4.1 us -> 6.07 us
    pallas_call x0 -> x9, Pallas kernels: none -> 23.3 us  [the longest x1 5.86 us: dec_gradient(): pl.pallas_call(dec_gradient_kernel, grid_spec=pltpu.PrefetchScalarGridSpe...]
    dot_general x11 -> x0, matrix products: 13.7 us -> none  [the longest x4 4.91 us: shards(): lax.dot_general(full, weight, (((1,), (1,)), ((), ())), preferred_element...]
    ppermute x36, starting transfers between devices: 58.6 us -> 50.7 us  [send(): return lax.ppermute(value, 'latent', pairs(move, cores))]
    ppermute x3, waiting for transfers between devices: 8.51 us -> 1.38 us  [shards(): came.append(lax.ppermute(away[k - 1], 'layer', ring))]
    ppermute x6 -> x3, waiting for transfers between devices: 8.21 us -> 1.91 us  [send_layer(): return lax.ppermute(value, 'layer', [(s, s + steps) for s in sources])]
    ppermute x36, waiting for transfers between devices: 34.6 us -> 40.9 us  [send(): return lax.ppermute(value, 'latent', pairs(move, cores))]
    ppermute x6 -> x3, starting transfers between devices: 12.2 us -> 7.4 us  [send_layer(): return lax.ppermute(value, 'layer', [(s, s + steps) for s in sources])]
    ppermute x3, starting transfers between devices: 3.5 us -> 6.43 us  [shards(): came.append(lax.ppermute(away[k - 1], 'layer', ring))]
  transfers between devices with their start and end apart: 45 -> 42, of which waited for: 21 -> 23; matrix products, arithmetic and copies ran while one was open for 7% -> 4% of each run, Pallas kernels for 0% -> 9%
where the time goes in v3:
time: 143 us
  starting transfers between devices  64.6 us (45%)
  waiting for transfers between devices  44.2 us (31%)
  Pallas kernels  23.3 us (16%)
  local copies, waits for them, and re-layouts  6.07 us (4%)
  other arithmetic  3.56 us (2%)
    ppermute x36, starting transfers between devices, send(): return lax.ppermute(value, 'latent', pairs(move, cores))  50.7 us
    ppermute x36, waiting for transfers between devices, send(): return lax.ppermute(value, 'latent', pairs(move, cores))  40.9 us
    ppermute x3, starting transfers between devices, send_layer(): return lax.ppermute(value, 'layer', [(s, s + steps) for s in sources])  7.4 us
    ppermute x3, starting transfers between devices, shards(): came.append(lax.ppermute(away[k - 1], 'layer', ring))  6.43 us
    pallas_call x1, Pallas kernels, dec_gradient(): pl.pallas_call(dec_gradient_kernel, grid_spec=pltpu.PrefetchScalarGridSpe...  5.86 us
    pallas_call x2, Pallas kernels, decode(): pl.pallas_call(decode_kernel, out_shape=[jax.ShapeDtypeStruct((count, wid...  3.99 us
    pallas_call x1, Pallas kernels, back_late(): pl.pallas_call(functools.partial(back_late_kernel, layers), in_specs=[pl....  3.52 us
    unnamed x30, local copies, waits for them, and re-layouts  2.93 us
  transfers between devices with their start and end apart: 42, of which 23 were waited for; matrix products, arithmetic and copies ran while one was open for 4% of the time, Pallas kernels for 9%

profile of v3, /device:TPU:1, one launch (start us, length us, event | category | flops | bytes accessed | tf_op | source)
XLA Modules:
  0.0 142.9 jit_solution(7589466222561843193)
XLA Ops:
  0.6 3.3 %collective-permute-start = (bf16[8,1792]{1,0:T(8,128)(2,1)}, bf16[8,1792]{1,0:T(8,128)(2,1)S(1)}, u32[]{:S(2)}, u32[]{:S(2)}) collective-permute-start(bf16[8,1792]{1,0:T(8,128)(2,1)} %bitcast.20), channel_id=1, source_target_pairs={{0,1},{1,0},{2,3},{3,2},{4,5},{5,4},{6,7},{7,6},{8,9},{9,8},{10,11... | collective-permute-start | bytes 86024 | tf_op jit(solution)/shard_map/ppermute | solution.py:33
  5.9 7.1 %collective-permute-start.1 = (bf16[16,1792]{1,0:T(8,128)(2,1)S(1)}, bf16[16,1792]{1,0:T(8,128)(2,1)S(1)}, u32[]{:S(2)}, u32[]{:S(2)}) collective-permute-start(bf16[16,1792]{1,0:T(8,128)(2,1)S(1)} %maximum_select_fusion), channel_id=1, source_target_pairs={{1,9},{3,11},{5,13},{7,15},{9,1},{11,3},{13,5},{15,7},{17,25},{19,... | collective-permute-start | bytes 172040 | tf_op jit(solution)/shard_map/ppermute | solution.py:33
  13.2 4.7 %collective-permute-start.4 = (bf16[16,1792]{1,0:T(8,128)(2,1)S(1)}, bf16[16,1792]{1,0:T(8,128)(2,1)S(1)}, u32[]{:S(2)}, u32[]{:S(2)}) collective-permute-start(bf16[16,1792]{1,0:T(8,128)(2,1)S(1)} %maximum_select_fusion), channel_id=1, source_target_pairs={{0,6},{1,11},{2,8},{3,13},{4,10},{5,15},{6,12},{7,1},{8,14},{9,3},... | collective-permute-start | bytes 172040 | tf_op jit(solution)/shard_map/ppermute | solution.py:33
  18.7 1.1 collective-permute-done.4
  19.8 3.0 %collective-permute-start.10 = (bf16[64,1792]{1,0:T(8,128)(2,1)S(1)}, bf16[64,1792]{1,0:T(8,128)(2,1)}, u32[]{:S(2)}, u32[]{:S(2)}) collective-permute-start(bf16[64,1792]{1,0:T(8,128)(2,1)S(1)} %pad_maximum_fusion.refs_0_), channel_id=1, source_target_pairs={{0,32},{1,33},{2,34},{3,35},{4,36},{5,37},{6,38},{7,39},{8,40},{9,... | collective-permute-start | bytes 688136 | tf_op jit(solution)/shard_map/ppermute | solution.py:33
  23.5 0.9 compare_reduce_fusion
  24.9 2.3 %dynamic-slice_bitcast_fusion = (bf16[256,1792]{1,0:T(8,128)(2,1)S(1)}, bf16[256,1792]{1,0:T(8,128)(2,1)S(1)}, bf16[256,1792]{1,0:T(8,128)(2,1)S(1)}, bf16[256,1792]{1,0:T(8,128)(2,1)S(1)}) fusion(bf16[4,1,256,1792]{3,2,1,0:T(8,128)(2,1)} %param.10, s32[]{:T(128)S(6)} %select_n.208, s32[]{:T(128)S(6)} %select_n.206, s32[]{:T(128)S(6)} %select_n.204, ...), kind=kLoop, calls=%fused_computation | loop fusion | bytes 7340048 | tf_op jit(solution)/shard_map/jit(dynamic_index_in_dim)/squeeze | solution.py:540
  27.4 0.9 collective-permute-done.10.refs_0_.refs_3_
  28.3 4.8 %collective-permute-done.6.refs_2_ = bf16[64,1792]{1,0:T(8,128)(2,1)S(1)} collective-permute-done((bf16[64,1792]{1,0:T(8,128)(2,1)S(1)}, bf16[64,1792]{1,0:T(8,128)(2,1)S(1)}, u32[]{:S(2)}, u32[]{:S(2)}) %collective-permute-start.6) | collective-permute-done | bytes 229408 | tf_op jit(solution)/shard_map/ppermute | solution.py:33
  33.7 0.9 collective-permute-done.9.refs_5_.refs_6_
  35.3 1.5 %encode_early.1.preact_ref = f32[384,256]{1,0:T(8,128)S(1)} custom-call(bf16[1792,256]{1,0:T(8,128)(2,1)S(1)} %bitcast.18, f32[1,256]{1,0:T(1,128)S(1)} %copy-done.13, bf16[64,1792]{1,0:T(8,128)(2,1)S(1)} %pad_maximum_fusion.refs_0_, bf16[64,1792]{1,0:T(8,128)(2,1)} %collective-permute-done.5.refs_1_, bf16[64,1792]{1,0:T(8,128)(2,1)S(1)} %collective-permute-done.6.refs_2_, ...), custom_call_target="tpu_custom_call" | custom-call | flops 1000 | bytes 1000 | tf_op jit(solution)/shard_map/encode_early/pallas_call | solution.py:150
  36.8 1.7 %encode_late.1 = (bf16[384,256]{1,0:T(8,128)(2,1)S(1)}, bf16[512,256]{1,0:T(8,128)(2,1)S(1)}, bf16[512,256]{1,0:T(8,128)(2,1)S(1)}) custom-call(s32[4,512]{1,0:T(4,128)S(1)} %pad_add_fusion.slot_ref, bf16[1792,256]{1,0:T(8,128)(2,1)S(1)} %bitcast.19, f32[1,256]{1,0:T(1,128)S(1)} %copy-done.13, f32[384,256]{1,0:T(8,128)S(1)} %encode_early.1.preact_ref, ...), custom_call_target="tpu_custom_call" | custom-call | flops 1000 | bytes 1000 | tf_op jit(solution)/shard_map/encode_late/pallas_call | solution.py:187
  39.2 3.6 %collective-permute-start.14 = (bf16[384,256]{1,0:T(8,128)(2,1)S(1)}, bf16[384,256]{1,0:T(8,128)(2,1)S(1)}, u32[]{:S(2)}, u32[]{:S(2)}) collective-permute-start(bf16[384,256]{1,0:T(8,128)(2,1)S(1)} %get-tuple-element.29.after_ref), channel_id=1, source_target_pairs={{0,192},{1,193},{2,194},{3,195},{4,196},{5,197},{6,198},{7,199},{8... | collective-permute-start | bytes 589832 | tf_op jit(solution)/shard_map/ppermute | solution.py:43
  42.8 1.3 collective-permute-start.13
  44.1 2.5 %collective-permute-start.12 = (bf16[384,256]{1,0:T(8,128)(2,1)S(1)}, bf16[384,256]{1,0:T(8,128)(2,1)S(1)}, u32[]{:S(2)}, u32[]{:S(2)}) collective-permute-start(bf16[384,256]{1,0:T(8,128)(2,1)S(1)} %get-tuple-element.29.after_ref), channel_id=1, source_target_pairs={{0,64},{64,128},{128,192},{1,65},{65,129},{129,193},{2,66},{66,130... | collective-permute-start | bytes 589832 | tf_op jit(solution)/shard_map/ppermute | solution.py:43
  46.7 0.9 copy-done.6
  47.6 1.6 %turn.1 = (bf16[1792,512]{1,0:T(8,128)(2,1)S(1)}, bf16[16,128]{1,0:T(8,128)(2,1)S(1)}) custom-call(bf16[384,256]{1,0:T(8,128)(2,1)S(1)} %get-tuple-element.29.after_ref, bf16[64,1792]{1,0:T(8,128)(2,1)S(1)} %pad_maximum_fusion.refs_0_, bf16[64,1792]{1,0:T(8,128)(2,1)} %collective-permute-done.5.refs_1_, bf16[64,1792]{1,0:T(8,128)(2,1)S(1)} %copy-done.6, ...), custom_call_target="tpu_custom_call" | custom-call | flops 1000 | bytes 1000 | tf_op jit(solution)/shard_map/turn/pallas_call | solution.py:213
  49.2 1.2 copy-done.3
  51.0 1.3 collective-permute-done.12.refs_0_
  52.3 2.0 %decode.3 = (bf16[256,1792]{1,0:T(8,128)(2,1)S(1)}, bf16[3,256,256]{2,1,0:T(8,128)(2,1)S(1)}) custom-call(s32[4,256]{1,0:T(4,128)S(1)} %get-tuple-element.81.slot_ref, bf16[16,128]{1,0:T(8,128)(2,1)S(1)} %get-tuple-element.33.token_ref, bf16[256,256]{1,0:T(8,128)(2,1)S(1)} %get-tuple-element.75.codes_ref, ...), custom_call_target="tpu_custom_call" | custom-call | flops 1000 | bytes 1000 | tf_op jit(solution)/shard_map/decode/pallas_call | solution.py:406
  54.4 1.3 collective-permute-start.20
  56.5 2.0 %decode.2 = (bf16[256,1792]{1,0:T(8,128)(2,1)S(1)}, bf16[3,256,256]{2,1,0:T(8,128)(2,1)S(1)}) custom-call(s32[4,256]{1,0:T(4,128)S(1)} %get-tuple-element.82.slot_ref, bf16[16,128]{1,0:T(8,128)(2,1)S(1)} %get-tuple-element.33.token_ref, bf16[256,256]{1,0:T(8,128)(2,1)S(1)} %get-tuple-element.76.codes_ref, ...), custom_call_target="tpu_custom_call" | custom-call | flops 1000 | bytes 1000 | tf_op jit(solution)/shard_map/decode/pallas_call | solution.py:406
  58.7 1.4 collective-permute-start.17
  60.1 2.6 %collective-permute-start.21 = (bf16[64,1792]{1,0:T(8,128)(2,1)S(1)}, bf16[64,1792]{1,0:T(8,128)(2,1)S(1)}, u32[]{:S(2)}, u32[]{:S(2)}) collective-permute-start(bf16[64,1792]{1,0:T(8,128)(2,1)S(1)} %get-tuple-element.73), channel_id=1, source_target_pairs={{0,32},{1,33},{2,34},{3,35},{4,36},{5,37},{6,38},{7,39},{8,40},{9,... | collective-permute-start | bytes 688136 | tf_op jit(solution)/shard_map/ppermute | solution.py:33
  62.7 3.1 %collective-permute-done.17 = bf16[64,1792]{1,0:T(8,128)(2,1)S(1)} collective-permute-done((bf16[64,1792]{1,0:T(8,128)(2,1)S(1)}, bf16[64,1792]{1,0:T(8,128)(2,1)S(1)}, u32[]{:S(2)}, u32[]{:S(2)}) %collective-permute-start.17) | collective-permute-done | bytes 229408 | tf_op jit(solution)/shard_map/ppermute | solution.py:33
  65.8 7.4 %collective-permute-done.21 = bf16[64,1792]{1,0:T(8,128)(2,1)S(1)} collective-permute-done((bf16[64,1792]{1,0:T(8,128)(2,1)S(1)}, bf16[64,1792]{1,0:T(8,128)(2,1)S(1)}, u32[]{:S(2)}, u32[]{:S(2)}) %collective-permute-start.21) | collective-permute-done | bytes 229408 | tf_op jit(solution)/shard_map/ppermute | solution.py:33
  73.2 2.0 %collective-permute-done.19 = bf16[64,1792]{1,0:T(8,128)(2,1)S(1)} collective-permute-done((bf16[64,1792]{1,0:T(8,128)(2,1)S(1)}, bf16[64,1792]{1,0:T(8,128)(2,1)S(1)}, u32[]{:S(2)}, u32[]{:S(2)}) %collective-permute-start.19) | collective-permute-done | bytes 229408 | tf_op jit(solution)/shard_map/ppermute | solution.py:33
  75.3 6.6 %collective-permute-start.22 = (bf16[16,1792]{1,0:T(8,128)(2,1)S(1)}, bf16[16,1792]{1,0:T(8,128)(2,1)S(1)}, u32[]{:S(2)}, u32[]{:S(2)}) collective-permute-start(bf16[16,1792]{1,0:T(8,128)(2,1)S(1)} %get-tuple-element.77), channel_id=1, source_target_pairs={{1,9},{3,11},{5,13},{7,15},{9,1},{11,3},{13,5},{15,7},{17,25},{19,... | collective-permute-start | bytes 172040 | tf_op jit(solution)/shard_map/ppermute | solution.py:33
  82.1 3.4 %collective-permute-start.24 = (bf16[16,1792]{1,0:T(8,128)(2,1)S(1)}, bf16[16,1792]{1,0:T(8,128)(2,1)S(1)}, u32[]{:S(2)}, u32[]{:S(2)}) collective-permute-start(bf16[16,1792]{1,0:T(8,128)(2,1)S(1)} %get-tuple-element.79), channel_id=1, source_target_pairs={{0,12},{1,5},{2,14},{3,7},{4,0},{5,9},{6,2},{7,11},{8,4},{9,13},{1... | collective-permute-start | bytes 172040 | tf_op jit(solution)/shard_map/ppermute | solution.py:33
  86.2 2.2 %collective-permute-done.25 = bf16[16,1792]{1,0:T(8,128)(2,1)S(1)} collective-permute-done((bf16[16,1792]{1,0:T(8,128)(2,1)S(1)}, bf16[16,1792]{1,0:T(8,128)(2,1)S(1)}, u32[]{:S(2)}, u32[]{:S(2)}) %collective-permute-start.25) | collective-permute-done | bytes 57376 | tf_op jit(solution)/shard_map/ppermute | solution.py:33
  88.8 1.7 %collective-permute-done.23 = bf16[16,1792]{1,0:T(8,128)(2,1)S(1)} collective-permute-done((bf16[16,1792]{1,0:T(8,128)(2,1)S(1)}, bf16[16,1792]{1,0:T(8,128)(2,1)S(1)}, u32[]{:S(2)}, u32[]{:S(2)}) %collective-permute-start.23) | collective-permute-done | bytes 57376 | tf_op jit(solution)/shard_map/ppermute | solution.py:33
  92.0 4.5 %collective-permute-start.28 = (bf16[16,1792]{1,0:T(8,128)(2,1)S(1)}, bf16[16,1792]{1,0:T(8,128)(2,1)S(1)}, u32[]{:S(2)}, u32[]{:S(2)}) collective-permute-start(bf16[16,1792]{1,0:T(8,128)(2,1)S(1)} %subtract_convert_fusion), channel_id=1, source_target_pairs={{1,9},{3,11},{5,13},{7,15},{9,1},{11,3},{13,5},{15,7},{17,25},{19,... | collective-permute-start | bytes 172040 | tf_op jit(solution)/shard_map/ppermute | solution.py:33
  96.5 2.3 %collective-permute-start.31 = (bf16[16,1792]{1,0:T(8,128)(2,1)S(1)}, bf16[16,1792]{1,0:T(8,128)(2,1)S(1)}, u32[]{:S(2)}, u32[]{:S(2)}) collective-permute-start(bf16[16,1792]{1,0:T(8,128)(2,1)S(1)} %subtract_convert_fusion), channel_id=1, source_target_pairs={{0,6},{1,11},{2,8},{3,13},{4,10},{5,15},{6,12},{7,1},{8,14},{9,3},... | collective-permute-start | bytes 172040 | tf_op jit(solution)/shard_map/ppermute | solution.py:33
  98.8 1.3 collective-permute-start.30
  100.1 1.0 collective-permute-start.29
  101.1 2.0 %collective-permute-done.28 = bf16[16,1792]{1,0:T(8,128)(2,1)S(1)} collective-permute-done((bf16[16,1792]{1,0:T(8,128)(2,1)S(1)}, bf16[16,1792]{1,0:T(8,128)(2,1)S(1)}, u32[]{:S(2)}, u32[]{:S(2)}) %collective-permute-start.28) | collective-permute-done | bytes 57376 | tf_op jit(solution)/shard_map/ppermute | solution.py:33
  104.3 1.1 collective-permute-start.33
  105.3 1.6 %collective-permute-start.32 = (bf16[64,1792]{1,0:T(8,128)(2,1)S(1)}, bf16[64,1792]{1,0:T(8,128)(2,1)}, u32[]{:S(2)}, u32[]{:S(2)}) collective-permute-start(bf16[64,1792]{1,0:T(8,128)(2,1)S(1)} %pad_maximum_fusion.1.refs_0_.refs_3_), channel_id=1, source_target_pairs={{0,16},{1,17},{2,18},{3,19},{4,20},{5,21},{6,22},{7,23},{8,24},{9,... | collective-permute-start | bytes 688136 | tf_op jit(solution)/shard_map/ppermute | solution.py:33
  107.8 5.5 %collective-permute-done.34.refs_3_ = bf16[64,1792]{1,0:T(8,128)(2,1)S(1)} collective-permute-done((bf16[64,1792]{1,0:T(8,128)(2,1)S(1)}, bf16[64,1792]{1,0:T(8,128)(2,1)S(1)}, u32[]{:S(2)}, u32[]{:S(2)}) %collective-permute-start.34) | collective-permute-done | bytes 229408 | tf_op jit(solution)/shard_map/ppermute | solution.py:33
  113.9 4.2 %collective-permute-done.33.refs_2_.refs_5_ = bf16[64,1792]{1,0:T(8,128)(2,1)} collective-permute-done((bf16[64,1792]{1,0:T(8,128)(2,1)S(1)}, bf16[64,1792]{1,0:T(8,128)(2,1)}, u32[]{:S(2)}, u32[]{:S(2)}) %collective-permute-start.33) | collective-permute-done | bytes 229408 | tf_op jit(solution)/shard_map/ppermute | solution.py:33
  119.1 1.0 collective-permute-done.37.refs_6_.refs_8_
  120.4 2.7 %back_early.1 = (bf16[3,384,256]{2,1,0:T(8,128)(2,1)S(1)}, f32[24,8,128]{2,1,0:T(8,128)S(1)}) custom-call(bf16[256,1792]{1,0:T(8,128)(2,1)S(1)} %get-tuple-element.66.refs_4_.refs_0_, bf16[256,1792]{1,0:T(8,128)(2,1)S(1)} %get-tuple-element.65.refs_5_.refs_1_, bf16[256,1792]{1,0:T(8,128)(2,1)S(1)} %get-tuple-element.64.refs_6_.refs_2_, ...), custom_call_target="tpu_custom_call" | custom-call | flops 1000 | bytes 1000 | tf_op jit(solution)/shard_map/back_early/pallas_call | solution.py:320
  123.2 3.5 %back_late.1 = (bf16[400,256]{1,0:T(8,128)(2,1)S(1)}, bf16[400,256]{1,0:T(8,128)(2,1)S(1)}, bf16[400,256]{1,0:T(8,128)(2,1)S(1)}) custom-call(s32[32]{0:T(128)S(1)} %select_reduce_fusion.1.place_ref, s32[4,512]{1,0:T(4,128)S(1)} %pad_add_fusion.slot_ref, f32[24,8,128]{2,1,0:T(8,128)S(1)} %get-tuple-element.41.squares_ref, ...), custom_call_target="tpu_custom_call" | custom-call | flops 1000 | bytes 1000 | tf_op jit(solution)/shard_map/back_late/pallas_call | solution.py:373
  126.7 3.8 %collective-permute-start.40 = (bf16[400,256]{1,0:T(8,128)(2,1)S(1)}, bf16[400,256]{1,0:T(8,128)(2,1)S(1)}, u32[]{:S(2)}, u32[]{:S(2)}) collective-permute-start(bf16[400,256]{1,0:T(8,128)(2,1)S(1)} %get-tuple-element.44), channel_id=1, source_target_pairs={{0,128},{64,192},{128,0},{192,64},{1,129},{65,193},{129,1},{193,65... | collective-permute-start | bytes 614408 | tf_op jit(solution)/shard_map/ppermute | solution.py:563
  130.4 2.7 %collective-permute-start.39 = (bf16[400,256]{1,0:T(8,128)(2,1)S(1)}, bf16[400,256]{1,0:T(8,128)(2,1)S(1)}, u32[]{:S(2)}, u32[]{:S(2)}) collective-permute-start(bf16[400,256]{1,0:T(8,128)(2,1)S(1)} %get-tuple-element.43.away_ref), channel_id=1, source_target_pairs={{0,192},{64,0},{128,64},{192,128},{1,193},{65,1},{129,65},{193,129... | collective-permute-start | bytes 614408 | tf_op jit(solution)/shard_map/ppermute | solution.py:563
  133.1 5.9 %dec_gradient.1 = (bf16[4,256,1792]{2,1,0:T(8,128)(2,1)}, f32[512,256]{1,0:T(8,128)S(1)}) custom-call(s32[1]{0:T(128)} %bitcast.layer_ref, bf16[512,256]{1,0:T(8,128)(2,1)S(1)} %get-tuple-element.32.codes_ref, bf16[3,256,256]{2,1,0:T(8,128)(2,1)S(1)} %copy-done.10, bf16[3,256,256]{2,1,0:T(8,128)(2,1)S(1)} %copy-done.8, bf16[256,1792]{1,0:T(8,128)(2,1)S(1)} %copy-done.1, ...), custom_call_target="tpu_custom_call" | custom-call | flops 1000 | bytes 1000 | tf_op jit(solution)/shard_map/dec_gradient/pallas_call | solution.py:258
  139.0 1.4 collective-permute-done.41.refs_2_
  140.4 2.5 %enc_gradient.1 = (bf16[1792,256]{1,0:T(8,128)(2,1)}, f32[1,256]{1,0:T(1,128)}, f32[1,1]{1,0:T(1,128)}) custom-call(s32[1]{0:T(128)} %bitcast.layer_ref, s32[4,512]{1,0:T(4,128)S(1)} %broadcast_add_fusion.slot_ref, bf16[1792,512]{1,0:T(8,128)(2,1)S(1)} %copy-done.4, bf16[512,256]{1,0:T(8,128)(2,1)S(1)} %copy-done.12, ...), custom_call_target="tpu_custom_call" | custom-call | flops 1000 | bytes 1000 | tf_op jit(solution)/shard_map/enc_gradient/pallas_call | solution.py:473
  (113 shorter events, 14.6 us)
Async XLA Ops:
  0.6 4.4 %collective-permute-start = (bf16[8,1792]{1,0:T(8,128)(2,1)}, bf16[8,1792]{1,0:T(8,128)(2,1)S(1)}, u32[]{:S(2)}, u32[]{:S(2)}) collective-permute-start(bf16[8,1792]{1,0:T(8,128)(2,1)} %bitcast.20), channel_id=1, source_target_pairs={{0,1},{1,0},{2,3},{3,2},{4,5},{5,4},{6,7},{7,6},{8,9},{9,8},{10,11... | collective-permute-start | bytes 86024 | tf_op jit(solution)/shard_map/ppermute | solution.py:33
  5.9 12.0 %collective-permute-start.1 = (bf16[16,1792]{1,0:T(8,128)(2,1)S(1)}, bf16[16,1792]{1,0:T(8,128)(2,1)S(1)}, u32[]{:S(2)}, u32[]{:S(2)}) collective-permute-start(bf16[16,1792]{1,0:T(8,128)(2,1)S(1)} %maximum_select_fusion), channel_id=1, source_target_pairs={{1,9},{3,11},{5,13},{7,15},{9,1},{11,3},{13,5},{15,7},{17,25},{19,... | collective-permute-start | bytes 172040 | tf_op jit(solution)/shard_map/ppermute | solution.py:33
  13.0 5.7 %collective-permute-start.3 = (bf16[16,1792]{1,0:T(8,128)(2,1)S(1)}, bf16[16,1792]{1,0:T(8,128)(2,1)S(1)}, u32[]{:S(2)}, u32[]{:S(2)}) collective-permute-start(bf16[16,1792]{1,0:T(8,128)(2,1)S(1)} %maximum_select_fusion), channel_id=1, source_target_pairs={{0,4},{1,13},{2,6},{3,15},{4,8},{5,1},{6,10},{7,3},{8,12},{9,5},{1... | collective-permute-start | bytes 172040 | tf_op jit(solution)/shard_map/ppermute | solution.py:33
  13.1 5.6 %collective-permute-start.2 = (bf16[16,1792]{1,0:T(8,128)(2,1)S(1)}, bf16[16,1792]{1,0:T(8,128)(2,1)S(1)}, u32[]{:S(2)}, u32[]{:S(2)}) collective-permute-start(bf16[16,1792]{1,0:T(8,128)(2,1)S(1)} %maximum_select_fusion), channel_id=1, source_target_pairs={{0,2},{1,15},{2,4},{3,1},{4,6},{5,3},{6,8},{7,5},{8,10},{9,7},{10,... | collective-permute-start | bytes 172040 | tf_op jit(solution)/shard_map/ppermute | solution.py:33
  13.2 6.6 %collective-permute-start.4 = (bf16[16,1792]{1,0:T(8,128)(2,1)S(1)}, bf16[16,1792]{1,0:T(8,128)(2,1)S(1)}, u32[]{:S(2)}, u32[]{:S(2)}) collective-permute-start(bf16[16,1792]{1,0:T(8,128)(2,1)S(1)} %maximum_select_fusion), channel_id=1, source_target_pairs={{0,6},{1,11},{2,8},{3,13},{4,10},{5,15},{6,12},{7,1},{8,14},{9,3},... | collective-permute-start | bytes 172040 | tf_op jit(solution)/shard_map/ppermute | solution.py:33
  19.8 8.5 %collective-permute-start.10 = (bf16[64,1792]{1,0:T(8,128)(2,1)S(1)}, bf16[64,1792]{1,0:T(8,128)(2,1)}, u32[]{:S(2)}, u32[]{:S(2)}) collective-permute-start(bf16[64,1792]{1,0:T(8,128)(2,1)S(1)} %pad_maximum_fusion.refs_0_), channel_id=1, source_target_pairs={{0,32},{1,33},{2,34},{3,35},{4,36},{5,37},{6,38},{7,39},{8,40},{9,... | collective-permute-start | bytes 688136 | tf_op jit(solution)/shard_map/ppermute | solution.py:33
  22.8 11.0 %collective-permute-start.7 = (bf16[64,1792]{1,0:T(8,128)(2,1)S(1)}, bf16[64,1792]{1,0:T(8,128)(2,1)S(1)}, u32[]{:S(2)}, u32[]{:S(2)}) collective-permute-start(bf16[64,1792]{1,0:T(8,128)(2,1)S(1)} %pad_maximum_fusion.refs_0_), channel_id=1, source_target_pairs={{0,1},{1,0},{2,3},{3,2},{4,5},{5,4},{6,7},{7,6},{8,9},{9,8},{10,11... | collective-permute-start | bytes 688136 | tf_op jit(solution)/shard_map/ppermute | solution.py:33
  22.8 10.3 %collective-permute-start.6 = (bf16[64,1792]{1,0:T(8,128)(2,1)S(1)}, bf16[64,1792]{1,0:T(8,128)(2,1)S(1)}, u32[]{:S(2)}, u32[]{:S(2)}) collective-permute-start(bf16[64,1792]{1,0:T(8,128)(2,1)S(1)} %pad_maximum_fusion.refs_0_), channel_id=1, source_target_pairs={{0,48},{1,49},{2,50},{3,51},{4,52},{5,53},{6,54},{7,55},{8,56},{9,... | collective-permute-start | bytes 688136 | tf_op jit(solution)/shard_map/ppermute | solution.py:33
  23.5 10.0 %collective-permute-start.5 = (bf16[64,1792]{1,0:T(8,128)(2,1)S(1)}, bf16[64,1792]{1,0:T(8,128)(2,1)}, u32[]{:S(2)}, u32[]{:S(2)}) collective-permute-start(bf16[64,1792]{1,0:T(8,128)(2,1)S(1)} %pad_maximum_fusion.refs_0_), channel_id=1, source_target_pairs={{0,16},{1,17},{2,18},{3,19},{4,20},{5,21},{6,22},{7,23},{8,24},{9,... | collective-permute-start | bytes 688136 | tf_op jit(solution)/shard_map/ppermute | solution.py:33
  27.3 29.2 %copy-start = (bf16[256,1792]{1,0:T(8,128)(2,1)}, bf16[256,1792]{1,0:T(8,128)(2,1)S(1)}, u32[]{:S(2)}) copy-start(bf16[256,1792]{1,0:T(8,128)(2,1)S(1)} %get-tuple-element.67.refs_3_.weight_ref) | copy-start | bytes 2752516
  28.3 8.5 %collective-permute-start.11 = (bf16[64,1792]{1,0:T(8,128)(2,1)}, bf16[64,1792]{1,0:T(8,128)(2,1)S(1)}, u32[]{:S(2)}, u32[]{:S(2)}) collective-permute-start(bf16[64,1792]{1,0:T(8,128)(2,1)} %collective-permute-done.10.refs_0_.refs_3_), channel_id=1, source_target_pairs={{0,1},{1,0},{2,3},{3,2},{4,5},{5,4},{6,7},{7,6},{8,9},{9,8},{10,11... | collective-permute-start | bytes 688136 | tf_op jit(solution)/shard_map/ppermute | solution.py:33
  33.1 1.6 %collective-permute-start.9 = (bf16[64,1792]{1,0:T(8,128)(2,1)S(1)}, bf16[64,1792]{1,0:T(8,128)(2,1)S(1)}, u32[]{:S(2)}, u32[]{:S(2)}) collective-permute-start(bf16[64,1792]{1,0:T(8,128)(2,1)S(1)} %collective-permute-done.6.refs_2_), channel_id=1, source_target_pairs={{0,1},{1,0},{2,3},{3,2},{4,5},{5,4},{6,7},{7,6},{8,9},{9,8},{10,11... | collective-permute-start | bytes 688136 | tf_op jit(solution)/shard_map/ppermute | solution.py:33
  33.6 1.7 %collective-permute-start.8 = (bf16[64,1792]{1,0:T(8,128)(2,1)}, bf16[64,1792]{1,0:T(8,128)(2,1)S(1)}, u32[]{:S(2)}, u32[]{:S(2)}) collective-permute-start(bf16[64,1792]{1,0:T(8,128)(2,1)} %collective-permute-done.5.refs_1_), channel_id=1, source_target_pairs={{0,1},{1,0},{2,3},{3,2},{4,5},{5,4},{6,7},{7,6},{8,9},{9,8},{10,11... | collective-permute-start | bytes 688136 | tf_op jit(solution)/shard_map/ppermute | solution.py:33
  39.2 11.8 %collective-permute-start.14 = (bf16[384,256]{1,0:T(8,128)(2,1)S(1)}, bf16[384,256]{1,0:T(8,128)(2,1)S(1)}, u32[]{:S(2)}, u32[]{:S(2)}) collective-permute-start(bf16[384,256]{1,0:T(8,128)(2,1)S(1)} %get-tuple-element.29.after_ref), channel_id=1, source_target_pairs={{0,192},{1,193},{2,194},{3,195},{4,196},{5,197},{6,198},{7,199},{8... | collective-permute-start | bytes 589832 | tf_op jit(solution)/shard_map/ppermute | solution.py:43
  42.8 8.2 %collective-permute-start.13 = (bf16[384,256]{1,0:T(8,128)(2,1)S(1)}, bf16[384,256]{1,0:T(8,128)(2,1)S(1)}, u32[]{:S(2)}, u32[]{:S(2)}) collective-permute-start(bf16[384,256]{1,0:T(8,128)(2,1)S(1)} %get-tuple-element.29.after_ref), channel_id=1, source_target_pairs={{0,128},{64,192},{1,129},{65,193},{2,130},{66,194},{3,131},{67,195... | collective-permute-start | bytes 589832 | tf_op jit(solution)/shard_map/ppermute | solution.py:43
  44.1 8.2 %collective-permute-start.12 = (bf16[384,256]{1,0:T(8,128)(2,1)S(1)}, bf16[384,256]{1,0:T(8,128)(2,1)S(1)}, u32[]{:S(2)}, u32[]{:S(2)}) collective-permute-start(bf16[384,256]{1,0:T(8,128)(2,1)S(1)} %get-tuple-element.29.after_ref), channel_id=1, source_target_pairs={{0,64},{64,128},{128,192},{1,65},{65,129},{129,193},{2,66},{66,130... | collective-permute-start | bytes 589832 | tf_op jit(solution)/shard_map/ppermute | solution.py:43
  54.4 4.1 %collective-permute-start.20 = (bf16[64,1792]{1,0:T(8,128)(2,1)S(1)}, bf16[64,1792]{1,0:T(8,128)(2,1)S(1)}, u32[]{:S(2)}, u32[]{:S(2)}) collective-permute-start(bf16[64,1792]{1,0:T(8,128)(2,1)S(1)} %get-tuple-element.69), channel_id=1, source_target_pairs={{0,1},{1,0},{2,3},{3,2},{4,5},{5,4},{6,7},{7,6},{8,9},{9,8},{10,11... | collective-permute-start | bytes 688136 | tf_op jit(solution)/shard_map/ppermute | solution.py:33
  55.7 2.8 %collective-permute-start.18 = (bf16[64,1792]{1,0:T(8,128)(2,1)S(1)}, bf16[64,1792]{1,0:T(8,128)(2,1)S(1)}, u32[]{:S(2)}, u32[]{:S(2)}) collective-permute-start(bf16[64,1792]{1,0:T(8,128)(2,1)S(1)} %get-tuple-element.70), channel_id=1, source_target_pairs={{0,1},{1,0},{2,3},{3,2},{4,5},{5,4},{6,7},{7,6},{8,9},{9,8},{10,11... | collective-permute-start | bytes 688136 | tf_op jit(solution)/shard_map/ppermute | solution.py:33
  55.9 2.6 %collective-permute-start.16 = (bf16[64,1792]{1,0:T(8,128)(2,1)S(1)}, bf16[64,1792]{1,0:T(8,128)(2,1)S(1)}, u32[]{:S(2)}, u32[]{:S(2)}) collective-permute-start(bf16[64,1792]{1,0:T(8,128)(2,1)S(1)} %get-tuple-element.71), channel_id=1, source_target_pairs={{0,1},{1,0},{2,3},{3,2},{4,5},{5,4},{6,7},{7,6},{8,9},{9,8},{10,11... | collective-permute-start | bytes 688136 | tf_op jit(solution)/shard_map/ppermute | solution.py:33
  56.2 6.5 %collective-permute-start.15 = (bf16[64,1792]{1,0:T(8,128)(2,1)S(1)}, bf16[64,1792]{1,0:T(8,128)(2,1)S(1)}, u32[]{:S(2)}, u32[]{:S(2)}) collective-permute-start(bf16[64,1792]{1,0:T(8,128)(2,1)S(1)} %get-tuple-element.68), channel_id=1, source_target_pairs={{0,1},{1,0},{2,3},{3,2},{4,5},{5,4},{6,7},{7,6},{8,9},{9,8},{10,11... | collective-permute-start | bytes 688136 | tf_op jit(solution)/shard_map/ppermute | solution.py:33
  56.5 34.2 %copy-start.14 = (bf16[1,8,1792]{2,1,0:T(8,128)(2,1)S(1)}, bf16[1,8,1792]{2,1,0:T(8,128)(2,1)}, u32[]{:S(2)}) copy-start(bf16[1,8,1792]{2,1,0:T(8,128)(2,1)} %param.7) | copy-start | bytes 86020
  58.5 45.8 %copy-start.9 = (bf16[3,256,256]{2,1,0:T(8,128)(2,1)}, bf16[3,256,256]{2,1,0:T(8,128)(2,1)S(1)}, u32[]{:S(2)}) copy-start(bf16[3,256,256]{2,1,0:T(8,128)(2,1)S(1)} %get-tuple-element.35.first_ref) | copy-start | bytes 1179652
  58.7 7.1 %collective-permute-start.17 = (bf16[64,1792]{1,0:T(8,128)(2,1)S(1)}, bf16[64,1792]{1,0:T(8,128)(2,1)S(1)}, u32[]{:S(2)}, u32[]{:S(2)}) collective-permute-start(bf16[64,1792]{1,0:T(8,128)(2,1)S(1)} %get-tuple-element.72), channel_id=1, source_target_pairs={{0,16},{1,17},{2,18},{3,19},{4,20},{5,21},{6,22},{7,23},{8,24},{9,... | collective-permute-start | bytes 688136 | tf_op jit(solution)/shard_map/ppermute | solution.py:33
  60.1 13.1 %collective-permute-start.21 = (bf16[64,1792]{1,0:T(8,128)(2,1)S(1)}, bf16[64,1792]{1,0:T(8,128)(2,1)S(1)}, u32[]{:S(2)}, u32[]{:S(2)}) collective-permute-start(bf16[64,1792]{1,0:T(8,128)(2,1)S(1)} %get-tuple-element.73), channel_id=1, source_target_pairs={{0,32},{1,33},{2,34},{3,35},{4,36},{5,37},{6,38},{7,39},{8,40},{9,... | collective-permute-start | bytes 688136 | tf_op jit(solution)/shard_map/ppermute | solution.py:33
  62.7 12.5 %collective-permute-start.19 = (bf16[64,1792]{1,0:T(8,128)(2,1)S(1)}, bf16[64,1792]{1,0:T(8,128)(2,1)S(1)}, u32[]{:S(2)}, u32[]{:S(2)}) collective-permute-start(bf16[64,1792]{1,0:T(8,128)(2,1)S(1)} %get-tuple-element.74), channel_id=1, source_target_pairs={{0,48},{1,49},{2,50},{3,51},{4,52},{5,53},{6,54},{7,55},{8,56},{9,... | collective-permute-start | bytes 688136 | tf_op jit(solution)/shard_map/ppermute | solution.py:33
  75.3 10.9 %collective-permute-start.22 = (bf16[16,1792]{1,0:T(8,128)(2,1)S(1)}, bf16[16,1792]{1,0:T(8,128)(2,1)S(1)}, u32[]{:S(2)}, u32[]{:S(2)}) collective-permute-start(bf16[16,1792]{1,0:T(8,128)(2,1)S(1)} %get-tuple-element.77), channel_id=1, source_target_pairs={{1,9},{3,11},{5,13},{7,15},{9,1},{11,3},{13,5},{15,7},{17,25},{19,... | collective-permute-start | bytes 172040 | tf_op jit(solution)/shard_map/ppermute | solution.py:33
  82.0 6.5 %collective-permute-start.25 = (bf16[16,1792]{1,0:T(8,128)(2,1)S(1)}, bf16[16,1792]{1,0:T(8,128)(2,1)S(1)}, u32[]{:S(2)}, u32[]{:S(2)}) collective-permute-start(bf16[16,1792]{1,0:T(8,128)(2,1)S(1)} %get-tuple-element.78), channel_id=1, source_target_pairs={{0,10},{1,7},{2,12},{3,9},{4,14},{5,11},{6,0},{7,13},{8,2},{9,15},... | collective-permute-start | bytes 172040 | tf_op jit(solution)/shard_map/ppermute | solution.py:33
  82.1 6.7 %collective-permute-start.24 = (bf16[16,1792]{1,0:T(8,128)(2,1)S(1)}, bf16[16,1792]{1,0:T(8,128)(2,1)S(1)}, u32[]{:S(2)}, u32[]{:S(2)}) collective-permute-start(bf16[16,1792]{1,0:T(8,128)(2,1)S(1)} %get-tuple-element.79), channel_id=1, source_target_pairs={{0,12},{1,5},{2,14},{3,7},{4,0},{5,9},{6,2},{7,11},{8,4},{9,13},{1... | collective-permute-start | bytes 172040 | tf_op jit(solution)/shard_map/ppermute | solution.py:33
  85.5 5.0 %collective-permute-start.23 = (bf16[16,1792]{1,0:T(8,128)(2,1)S(1)}, bf16[16,1792]{1,0:T(8,128)(2,1)S(1)}, u32[]{:S(2)}, u32[]{:S(2)}) collective-permute-start(bf16[16,1792]{1,0:T(8,128)(2,1)S(1)} %get-tuple-element.80), channel_id=1, source_target_pairs={{0,14},{1,3},{2,0},{3,5},{4,2},{5,7},{6,4},{7,9},{8,6},{9,11},{10,... | collective-permute-start | bytes 172040 | tf_op jit(solution)/shard_map/ppermute | solution.py:33
  90.5 1.5 %collective-permute-start.26 = (bf16[16,1792]{1,0:T(8,128)(2,1)S(1)}, bf16[16,1792]{1,0:T(8,128)(2,1)S(1)}, u32[]{:S(2)}, u32[]{:S(2)}) collective-permute-start(bf16[16,1792]{1,0:T(8,128)(2,1)S(1)} %add_convert_fusion.5), channel_id=1, source_target_pairs={{0,1},{1,0},{2,3},{3,2},{4,5},{5,4},{6,7},{7,6},{8,9},{9,8},{10,11... | collective-permute-start | bytes 172040 | tf_op jit(solution)/shard_map/ppermute | solution.py:33
  90.7 1.3 collective-permute-start.27
  92.0 11.1 %collective-permute-start.28 = (bf16[16,1792]{1,0:T(8,128)(2,1)S(1)}, bf16[16,1792]{1,0:T(8,128)(2,1)S(1)}, u32[]{:S(2)}, u32[]{:S(2)}) collective-permute-start(bf16[16,1792]{1,0:T(8,128)(2,1)S(1)} %subtract_convert_fusion), channel_id=1, source_target_pairs={{1,9},{3,11},{5,13},{7,15},{9,1},{11,3},{13,5},{15,7},{17,25},{19,... | collective-permute-start | bytes 172040 | tf_op jit(solution)/shard_map/ppermute | solution.py:33
  96.5 6.6 %collective-permute-start.31 = (bf16[16,1792]{1,0:T(8,128)(2,1)S(1)}, bf16[16,1792]{1,0:T(8,128)(2,1)S(1)}, u32[]{:S(2)}, u32[]{:S(2)}) collective-permute-start(bf16[16,1792]{1,0:T(8,128)(2,1)S(1)} %subtract_convert_fusion), channel_id=1, source_target_pairs={{0,6},{1,11},{2,8},{3,13},{4,10},{5,15},{6,12},{7,1},{8,14},{9,3},... | collective-permute-start | bytes 172040 | tf_op jit(solution)/shard_map/ppermute | solution.py:33
  98.8 4.7 %collective-permute-start.30 = (bf16[16,1792]{1,0:T(8,128)(2,1)S(1)}, bf16[16,1792]{1,0:T(8,128)(2,1)S(1)}, u32[]{:S(2)}, u32[]{:S(2)}) collective-permute-start(bf16[16,1792]{1,0:T(8,128)(2,1)S(1)} %subtract_convert_fusion), channel_id=1, source_target_pairs={{0,4},{1,13},{2,6},{3,15},{4,8},{5,1},{6,10},{7,3},{8,12},{9,5},{1... | collective-permute-start | bytes 172040 | tf_op jit(solution)/shard_map/ppermute | solution.py:33
  100.1 4.1 %collective-permute-start.29 = (bf16[16,1792]{1,0:T(8,128)(2,1)S(1)}, bf16[16,1792]{1,0:T(8,128)(2,1)S(1)}, u32[]{:S(2)}, u32[]{:S(2)}) collective-permute-start(bf16[16,1792]{1,0:T(8,128)(2,1)S(1)} %subtract_convert_fusion), channel_id=1, source_target_pairs={{0,2},{1,15},{2,4},{3,1},{4,6},{5,3},{6,8},{7,5},{8,10},{9,7},{10,... | collective-permute-start | bytes 172040 | tf_op jit(solution)/shard_map/ppermute | solution.py:33
  104.2 9.2 %collective-permute-start.34 = (bf16[64,1792]{1,0:T(8,128)(2,1)S(1)}, bf16[64,1792]{1,0:T(8,128)(2,1)S(1)}, u32[]{:S(2)}, u32[]{:S(2)}) collective-permute-start(bf16[64,1792]{1,0:T(8,128)(2,1)S(1)} %pad_maximum_fusion.1.refs_0_.refs_3_), channel_id=1, source_target_pairs={{0,32},{1,33},{2,34},{3,35},{4,36},{5,37},{6,38},{7,39},{8,40},{9,... | collective-permute-start | bytes 688136 | tf_op jit(solution)/shard_map/ppermute | solution.py:33
  104.3 13.8 %collective-permute-start.33 = (bf16[64,1792]{1,0:T(8,128)(2,1)S(1)}, bf16[64,1792]{1,0:T(8,128)(2,1)}, u32[]{:S(2)}, u32[]{:S(2)}) collective-permute-start(bf16[64,1792]{1,0:T(8,128)(2,1)S(1)} %pad_maximum_fusion.1.refs_0_.refs_3_), channel_id=1, source_target_pairs={{0,48},{1,49},{2,50},{3,51},{4,52},{5,53},{6,54},{7,55},{8,56},{9,... | collective-permute-start | bytes 688136 | tf_op jit(solution)/shard_map/ppermute | solution.py:33
  105.3 13.3 %collective-permute-start.32 = (bf16[64,1792]{1,0:T(8,128)(2,1)S(1)}, bf16[64,1792]{1,0:T(8,128)(2,1)}, u32[]{:S(2)}, u32[]{:S(2)}) collective-permute-start(bf16[64,1792]{1,0:T(8,128)(2,1)S(1)} %pad_maximum_fusion.1.refs_0_.refs_3_), channel_id=1, source_target_pairs={{0,16},{1,17},{2,18},{3,19},{4,20},{5,21},{6,22},{7,23},{8,24},{9,... | collective-permute-start | bytes 688136 | tf_op jit(solution)/shard_map/ppermute | solution.py:33
  107.1 12.0 %collective-permute-start.35 = (bf16[64,1792]{1,0:T(8,128)(2,1)S(1)}, bf16[64,1792]{1,0:T(8,128)(2,1)}, u32[]{:S(2)}, u32[]{:S(2)}) collective-permute-start(bf16[64,1792]{1,0:T(8,128)(2,1)S(1)} %pad_maximum_fusion.1.refs_0_.refs_3_), channel_id=1, source_target_pairs={{0,1},{1,0},{2,3},{3,2},{4,5},{5,4},{6,7},{7,6},{8,9},{9,8},{10,11... | collective-permute-start | bytes 688136 | tf_op jit(solution)/shard_map/ppermute | solution.py:33
  113.3 9.8 %collective-permute-start.38 = (bf16[64,1792]{1,0:T(8,128)(2,1)S(1)}, bf16[64,1792]{1,0:T(8,128)(2,1)}, u32[]{:S(2)}, u32[]{:S(2)}) collective-permute-start(bf16[64,1792]{1,0:T(8,128)(2,1)S(1)} %collective-permute-done.34.refs_3_), channel_id=1, source_target_pairs={{0,1},{1,0},{2,3},{3,2},{4,5},{5,4},{6,7},{7,6},{8,9},{9,8},{10,11... | collective-permute-start | bytes 688136 | tf_op jit(solution)/shard_map/ppermute | solution.py:33
  118.1 2.0 %collective-permute-start.37 = (bf16[64,1792]{1,0:T(8,128)(2,1)}, bf16[64,1792]{1,0:T(8,128)(2,1)}, u32[]{:S(2)}, u32[]{:S(2)}) collective-permute-start(bf16[64,1792]{1,0:T(8,128)(2,1)} %collective-permute-done.33.refs_2_.refs_5_), channel_id=1, source_target_pairs={{0,1},{1,0},{2,3},{3,2},{4,5},{5,4},{6,7},{7,6},{8,9},{9,8},{10,11... | collective-permute-start | bytes 688136 | tf_op jit(solution)/shard_map/ppermute | solution.py:33
  118.6 1.8 %collective-permute-start.36 = (bf16[64,1792]{1,0:T(8,128)(2,1)}, bf16[64,1792]{1,0:T(8,128)(2,1)}, u32[]{:S(2)}, u32[]{:S(2)}) collective-permute-start(bf16[64,1792]{1,0:T(8,128)(2,1)} %collective-permute-done.32.refs_1_.refs_4_), channel_id=1, source_target_pairs={{0,1},{1,0},{2,3},{3,2},{4,5},{5,4},{6,7},{7,6},{8,9},{9,8},{10,11... | collective-permute-start | bytes 688136 | tf_op jit(solution)/shard_map/ppermute | solution.py:33
  119.0 14.1 %copy-start.1 = (bf16[256,1792]{1,0:T(8,128)(2,1)S(1)}, bf16[256,1792]{1,0:T(8,128)(2,1)}, u32[]{:S(2)}) copy-start(bf16[256,1792]{1,0:T(8,128)(2,1)} %copy-done) | copy-start | bytes 2752516
  123.1 17.2 %copy-start.4 = (bf16[1792,512]{1,0:T(8,128)(2,1)S(1)}, bf16[1792,512]{1,0:T(8,128)(2,1)}, u32[]{:S(2)}) copy-start(bf16[1792,512]{1,0:T(8,128)(2,1)} %copy-done.3) | copy-start | bytes 5505028
  123.1 17.2 %copy-start.12 = (bf16[512,256]{1,0:T(8,128)(2,1)S(1)}, bf16[512,256]{1,0:T(8,128)(2,1)}, u32[]{:S(2)}) copy-start(bf16[512,256]{1,0:T(8,128)(2,1)} %copy-done.11) | copy-start | bytes 786436
  126.7 12.3 %collective-permute-start.40 = (bf16[400,256]{1,0:T(8,128)(2,1)S(1)}, bf16[400,256]{1,0:T(8,128)(2,1)S(1)}, u32[]{:S(2)}, u32[]{:S(2)}) collective-permute-start(bf16[400,256]{1,0:T(8,128)(2,1)S(1)} %get-tuple-element.44), channel_id=1, source_target_pairs={{0,128},{64,192},{128,0},{192,64},{1,129},{65,193},{129,1},{193,65... | collective-permute-start | bytes 614408 | tf_op jit(solution)/shard_map/ppermute | solution.py:563
  130.4 9.9 %collective-permute-start.41 = (bf16[400,256]{1,0:T(8,128)(2,1)S(1)}, bf16[400,256]{1,0:T(8,128)(2,1)S(1)}, u32[]{:S(2)}, u32[]{:S(2)}) collective-permute-start(bf16[400,256]{1,0:T(8,128)(2,1)S(1)} %get-tuple-element.45), channel_id=1, source_target_pairs={{0,64},{64,128},{128,192},{192,0},{1,65},{65,129},{129,193},{193,1... | collective-permute-start | bytes 614408 | tf_op jit(solution)/shard_map/ppermute | solution.py:563
  130.4 9.9 %collective-permute-start.39 = (bf16[400,256]{1,0:T(8,128)(2,1)S(1)}, bf16[400,256]{1,0:T(8,128)(2,1)S(1)}, u32[]{:S(2)}, u32[]{:S(2)}) collective-permute-start(bf16[400,256]{1,0:T(8,128)(2,1)S(1)} %get-tuple-element.43.away_ref), channel_id=1, source_target_pairs={{0,192},{64,0},{128,64},{192,128},{1,193},{65,1},{129,65},{193,129... | collective-permute-start | bytes 614408 | tf_op jit(solution)/shard_map/ppermute | solution.py:563
  (9 other events, 57.6 us)

commit v4 on v3

v4 whole, which is shorter than its diff:
```python
import functools

import jax
import jax.numpy as jnp
from jax import lax
from jax.experimental import pallas as pl
from jax.experimental.pallas import tpu as pltpu
from jax.sharding import PartitionSpec as P

TILE = 64
NTILE = 8
CAP = 6
Y, Z, C = 4, 8, 2
BF = jnp.bfloat16
F32 = jnp.float32
STEPS = (0, 1, 3, 2)


def index_of(y, z, c):
    return ((y % Y) * Z + z % Z) * C + c


def pairs(move, cores=(0, 1)):
    return [
        (index_of(y, z, c), index_of(*move(y, z, c)))
        for y in range(Y)
        for z in range(Z)
        for c in cores
    ]


def send(value, move, cores=(0, 1)):
    return lax.ppermute(value, "latent", pairs(move, cores))


def swap(value):
    return send(value, lambda y, z, c: (y, z, 1 - c))


def send_layer(value, steps):
    count = lax.axis_size("layer")
    sources = [s for s in range(count) if 0 <= s + steps < count]
    return lax.ppermute(value, "layer", [(s, s + steps) for s in sources])


def chip_rows(value, core):
    other = swap(value)
    return jnp.where(core == 0, jnp.concatenate([value, other]), jnp.concatenate([other, value]))


def spread_z(chip, core):
    near = [
        send(chip, lambda y, z, c, k=k: (y, z ^ (k + 4 * c), c)) for k in (1, 2, 3)
    ]
    far = send(chip, lambda y, z, c: (y, z ^ 4, c), (1,))
    return jnp.concatenate([jnp.where(core == 0, chip, far)] + near)


def spread_y(half):
    parts = [half] + [send(half, lambda y, z, c, k=k: (y ^ k, z, c)) for k in STEPS[1:]]
    return parts + [swap(part) for part in parts]


def collect(halves, core):
    width = halves[0].shape[-1]
    halves = [half.reshape(Y, 4 * 2 * 8, width) for half in halves]
    own = [
        (halves[0][k].astype(F32) + swap(halves[1][k]).astype(F32)).astype(BF) for k in range(Y)
    ]
    row = own[0].astype(F32)
    for part, k in zip(own[1:], STEPS[1:]):
        row = row + send(part, lambda y, z, c, k=k: (y ^ k, z, c)).astype(F32)
    row = row.astype(BF).reshape(4, 16, width)
    far = send(row[0], lambda y, z, c: (y, z ^ 4, c), (1,))
    total = jnp.where(core == 0, row[0], far).astype(F32)
    for k in (1, 2, 3):
        piece = send(row[k], lambda y, z, c, k=k: (y, z ^ (k + 4 * c), c))
        total = total + piece.astype(F32)
    total = total.astype(BF)
    return total.astype(F32) + swap(total).astype(F32)


def shard_chips(latent):
    y, z, c = latent // (Z * C), latent // C % Z, latent % C
    p = jnp.arange(Y * Z, dtype=jnp.int32)
    half, step, j = p // 16, p // 4 % 4, p % 4
    step = jnp.where(step < 2, step, 5 - step)
    side = (half + c) % 2
    from_z = z ^ (j + 4 * side)
    return (y ^ step) * Z + from_z


SMALL = pl.CostEstimate(flops=1000, bytes_accessed=1000, transcendentals=0)


def params(mib):
    return pltpu.CompilerParams(vmem_limit_bytes=mib * 1024 * 1024)


def join(parts, out_ref):
    at = 0
    for part in parts:
        out_ref[at : at + part.shape[0]] = part[...]
        at += part.shape[0]


def pack(source_ref, k, value_ref, out_ref):
    for place in range(CAP * TILE // 16):
        start = pl.multiple_of(source_ref[k, place] * 16, 16)
        out_ref[place * 16 : place * 16 + 16, :] = value_ref[pl.ds(start, 16), :]


def unpacked(slot_ref, k, shard, packed_ref):
    slot = slot_ref[k, shard]
    start = pl.multiple_of(lax.max(slot, 0) * 16, 16)
    value = packed_ref[pl.ds(start, 16), :]
    return jnp.where(slot >= 0, value, jnp.zeros_like(value))


def encode_kernel(slot_ref, source_ref, weight_ref, bias_ref, *refs):
    parts, (packed_ref, codes_ref, on_ref, rows_ref) = refs[:-4], refs[-4:]
    join(parts, rows_ref)
    preact = jnp.dot(rows_ref[...], weight_ref[...], preferred_element_type=F32) + bias_ref[...]
    for shard in range(Y * Z):
        at = slice(shard * 16, shard * 16 + 16)
        on = jnp.where((preact[at] > 0) & (slot_ref[0, shard] >= 0), 1.0, 0.0)
        codes_ref[at, :] = jnp.where(on > 0, preact[at], 0.0).astype(BF)
        on_ref[at, :] = on.astype(BF)
    pack(source_ref, 0, codes_ref, packed_ref)


def specs(scalars, arrays):
    return [pl.BlockSpec(memory_space=pltpu.SMEM)] * scalars + [
        pl.BlockSpec(memory_space=pltpu.VMEM)
    ] * arrays


def encode(slot, source, weight, bias, parts):
    count = sum(part.shape[0] for part in parts)
    width, feats = weight.shape
    return pl.pallas_call(
        encode_kernel,
        in_specs=specs(2, 2 + len(parts)),
        out_shape=[
            jax.ShapeDtypeStruct((CAP * TILE, feats), BF),
            jax.ShapeDtypeStruct((count, feats), BF),
            jax.ShapeDtypeStruct((count, feats), BF),
        ],
        scratch_shapes=[pltpu.VMEM((count, width), BF)],
        compiler_params=params(10),
        cost_estimate=SMALL,
        name="encode",
    )(slot, source, weight, bias, *parts)


def turn_kernel(after_ref, *refs):
    parts, (out_ref, token_ref) = refs[:-2], refs[-2:]
    at = 0
    for first, second in zip(parts[0::2], parts[1::2]):
        both = jnp.concatenate([first[...], second[...]])
        out_ref[:, at : at + both.shape[0]] = both.T
        at += both.shape[0]
    token_ref[...] = after_ref[:16, :128]


def turn(parts, after):
    count = sum(part.shape[0] for part in parts)
    return pl.pallas_call(
        turn_kernel,
        out_shape=[
            jax.ShapeDtypeStruct((parts[0].shape[1], count), BF),
            jax.ShapeDtypeStruct((16, 128), BF),
        ],
        compiler_params=params(10),
        cost_estimate=SMALL,
        name="turn",
    )(after, *parts)


def dec_gradient_kernel(layer_ref, codes_ref, first_ref, second_ref, weight_ref, *refs):
    del layer_ref
    parts, (out_ref, own_ref, errors_ref) = refs[:-3], refs[-3:]
    over_rows = (((0,), (0,)), ((), ()))

    @pl.when(pl.program_id(0) == 0)
    def _():
        join(parts, errors_ref)
        own_ref[...] = lax.dot_general(
            errors_ref[...], weight_ref[...], (((1,), (1,)), ((), ())), preferred_element_type=F32
        )
        grad = lax.dot_general(
            codes_ref[...], errors_ref[...], over_rows, preferred_element_type=F32
        )
        out_ref[0] = (grad * (1.0 / TILE)).astype(BF)

    @pl.when(pl.program_id(0) > 0)
    def _():
        count = first_ref.shape[1]
        grad = lax.dot_general(
            first_ref[0], errors_ref[:count], over_rows, preferred_element_type=F32
        ) + lax.dot_general(
            second_ref[0], errors_ref[count:], over_rows, preferred_element_type=F32
        )
        out_ref[0] = (grad * (1.0 / TILE)).astype(BF)


def dec_gradient(layer, codes, first, second, weight, parts):
    layers = first.shape[0] + 1
    feats, width = weight.shape
    count = codes.shape[0]
    other = lambda k, at: (lax.max(k - 1, 0), 0, 0)
    whole = lambda array: pl.BlockSpec(array.shape, lambda k, at: (0,) * array.ndim)
    return pl.pallas_call(
        dec_gradient_kernel,
        grid_spec=pltpu.PrefetchScalarGridSpec(
            num_scalar_prefetch=1,
            grid=(layers,),
            in_specs=[
                whole(codes),
                pl.BlockSpec((1, *first.shape[1:]), other),
                pl.BlockSpec((1, *second.shape[1:]), other),
                whole(weight),
                *[whole(part) for part in parts],
            ],
            out_specs=[
                pl.BlockSpec(
                    (1, feats, width), lambda k, at: (lax.rem(at[0] - k + layers, layers), 0, 0)
                ),
                pl.BlockSpec((count, feats), lambda k, at: (0, 0)),
            ],
            scratch_shapes=[pltpu.VMEM((count, width), BF)],
        ),
        out_shape=[
            jax.ShapeDtypeStruct((layers, feats, width), BF),
            jax.ShapeDtypeStruct((count, feats), F32),
        ],
        compiler_params=params(20),
        cost_estimate=SMALL,
        name="dec_gradient",
    )(layer.reshape(1), codes, first, second, weight, *parts)


def add_squares(parts, out_ref, start):
    for part in parts:
        count, width = part.shape
        for at in range(0, count, 16):
            value = part[at : at + 16, :].astype(F32)
            value = value * value
            value = value[:8] + value[8:]
            total = value[:, :128]
            for lane in range(128, width, 128):
                total = total + value[:, lane : lane + 128]
            out_ref[start] = total
            start += 1


def back_kernel(layers, place_ref, source_ref, *refs):
    weights, refs = refs[: layers - 1], refs[layers - 1 :]
    away, errors_ref, back_ref, sums_ref = refs[-layers - 2 : -3], refs[-3], refs[-2], refs[-1]
    parts = refs[: -layers - 2]
    join(parts, errors_ref)
    packed = CAP * TILE
    for k in range(1, layers):
        back_ref[k - 1] = lax.dot_general(
            errors_ref[...],
            weights[k - 1][...],
            (((1,), (1,)), ((), ())),
            preferred_element_type=F32,
        ).astype(BF)
        pack(source_ref, k, back_ref.at[k - 1], away[k - 1])
    add_squares(parts, sums_ref, 0)
    total = jnp.zeros((8, 128), F32)
    for chip in range(Y * Z):
        total = total + sums_ref[place_ref[chip]]
    left = jnp.broadcast_to(jnp.sum(total), (16, weights[0].shape[0]))
    row = lax.broadcasted_iota(jnp.int32, left.shape, 0)
    split = jnp.zeros(left.shape, F32)
    for k in range(3):
        piece = left.astype(BF).astype(F32)
        split = jnp.where(row == k, piece, split)
        left = left - piece
    for ref in away:
        ref[packed:, :] = split.astype(BF)


def back(place, source, weights, parts):
    layers = len(weights) + 1
    feats, width = weights[0].shape
    count = sum(part.shape[0] for part in parts)
    return pl.pallas_call(
        functools.partial(back_kernel, layers),
        in_specs=specs(2, len(weights) + len(parts)),
        out_shape=[jax.ShapeDtypeStruct((CAP * TILE + 16, feats), BF)] * (layers - 1),
        scratch_shapes=[
            pltpu.VMEM((count, width), BF),
            pltpu.VMEM((layers - 1, count, feats), BF),
            pltpu.VMEM((Y * Z, 8, 128), F32),
        ],
        compiler_params=params(14),
        cost_estimate=SMALL,
        name="back",
    )(place, source, *weights, *parts)


def decode_kernel(half, slot_ref, token_ref, codes_ref, *refs):
    del token_ref
    layers = (len(refs) - 1) // 2
    came, weights = refs[: layers - 1], refs[layers - 1 : 2 * layers - 1]
    out_ref, sources_ref = refs[-2:]
    count = out_ref.shape[0]
    total = jnp.dot(
        codes_ref[half * count : half * count + count, :],
        weights[0][...],
        preferred_element_type=F32,
    )
    shards_of = count // 16
    for k in range(1, layers):
        for shard in range(shards_of):
            sources_ref[k - 1, shard * 16 : shard * 16 + 16, :] = unpacked(
                slot_ref, k, half * shards_of + shard, came[k - 1]
            )
        total = total + jnp.dot(
            sources_ref[k - 1], weights[k][...], preferred_element_type=F32
        )
    out_ref[...] = total.astype(BF)


def decode(half, slot, token, codes, came, weights):
    count, feats = codes.shape[0] // 2, codes.shape[1]
    width = weights[0].shape[1]
    return pl.pallas_call(
        functools.partial(decode_kernel, half),
        in_specs=specs(1, 2 + len(came) + len(weights)),
        out_shape=[
            jax.ShapeDtypeStruct((count, width), BF),
            jax.ShapeDtypeStruct((len(came), count, feats), BF),
        ],
        compiler_params=params(14),
        cost_estimate=SMALL,
        name="decode",
    )(slot, token, codes, *came, *weights)


def enc_gradient_kernel(count, layer_ref, slot_ref, rows_ref, on_ref, own_ref, away_ref, *refs):
    came, (enc_ref, bias_ref, loss_ref, pre_ref) = refs[:-4], refs[-4:]
    packed = CAP * TILE
    layers = len(came) + 1

    @pl.when(pl.program_id(0) == 0)
    def _():
        pieces = []
        for shard in range(own_ref.shape[0] // 16):
            piece = own_ref[shard * 16 : shard * 16 + 16, :]
            for k, ref in enumerate(came, 1):
                part = unpacked(slot_ref, 0, shard, ref).astype(F32)
                piece = piece + jnp.where(layer_ref[0] + k < layers, part, 0.0)
            pieces.append(piece)
        total = jnp.concatenate(pieces)
        total = jnp.where(on_ref[...] > 0, total, 0.0)
        bias_ref[...] = jnp.sum(total, axis=0, keepdims=True) * (1.0 / TILE)
        pre_ref[...] = total.astype(BF)
        sums = []
        for block in [ref[packed:] for ref in (away_ref, *came)]:
            block = block.astype(F32)
            sums.append(block[0:1] + block[1:2] + block[2:3])
        loss = jnp.zeros_like(sums[0])
        for s in range(layers):
            for k in range(layers):
                mine = lax.rem(layer_ref[0] + k, layers) == s
                loss = loss + jnp.where(mine, sums[k], 0.0)
        loss_ref[...] = loss[:, :1] * (0.5 / count)

    grad = jnp.dot(rows_ref[...], pre_ref[...], preferred_element_type=F32)
    enc_ref[...] = (grad * (1.0 / TILE)).astype(BF)


def enc_gradient(layer, slot, rows, on, own, away, came):
    width, count = rows.shape
    feats = own.shape[1]
    whole = lambda array: pl.BlockSpec(array.shape, lambda i: (0,) * array.ndim)
    part = width // 2
    return pl.pallas_call(
        functools.partial(enc_gradient_kernel, (len(came) + 1) * count * width),
        grid=(width // part,),
        in_specs=[
            pl.BlockSpec(memory_space=pltpu.SMEM),
            pl.BlockSpec(memory_space=pltpu.SMEM),
            pl.BlockSpec((part, count), lambda i: (i, 0)),
            whole(on),
            whole(own),
            whole(away),
            *[whole(array) for array in came],
        ],
        out_specs=[
            pl.BlockSpec((part, feats), lambda i: (i, 0)),
            pl.BlockSpec((1, feats), lambda i: (0, 0)),
            pl.BlockSpec((1, 1), lambda i: (0, 0)),
        ],
        out_shape=[
            jax.ShapeDtypeStruct((width, feats), BF),
            jax.ShapeDtypeStruct((1, feats), F32),
            jax.ShapeDtypeStruct((1, 1), F32),
        ],
        scratch_shapes=[pltpu.VMEM((count, feats), BF)],
        compiler_params=params(12),
        cost_estimate=SMALL,
        name="enc_gradient",
    )(layer.reshape(1), slot, rows, on, own, away, *came)


def shards(residual, target, enc_weight, enc_bias, dec_weight, active):
    layers = dec_weight.shape[0]
    width = residual.shape[-1]
    layer = lax.axis_index("layer")
    latent = lax.axis_index("latent")
    core = latent % C

    half = spread_z(chip_rows(residual[0], core), core)
    half, target, dec, active = lax.optimization_barrier((half, target, dec_weight, active))
    rows = spread_y(half)

    chips = shard_chips(latent)
    hit = jnp.any(active == latent, axis=2)
    hit = jnp.stack(
        [
            lax.dynamic_index_in_dim(hit, (layer - k) % layers, 0, keepdims=False)
            for k in range(layers)
        ]
    )
    live = jnp.any(
        (chips[:, None] // 4 == jnp.arange(NTILE)[None, :])[None] & hit[:, None, :], axis=2
    )
    every = jnp.arange(Y * Z)
    before = every[None, :] <= every[:, None]
    slot = jnp.sum(jnp.where(before[None] & live[:, None, :], 1, 0), axis=2, dtype=jnp.int32) - 1
    slot = jnp.where(live, jnp.minimum(slot, CAP * 4 - 1), -1)
    source = jnp.sum(
        jnp.where(slot[:, None, :] == jnp.arange(CAP * 4)[None, :, None], every, 0),
        axis=2,
        dtype=jnp.int32,
    )
    source = jnp.minimum(source, Y * Z - 1)
    place = jnp.sum(
        jnp.where(chips[None, :] == every[:, None], every[None, :], 0), axis=1, dtype=jnp.int32
    )
    weights = [
        lax.dynamic_index_in_dim(dec[:, 0], (layer - k) % layers, 0, keepdims=False)
        for k in range(layers)
    ]
    goal = chip_rows(target[0], core)

    packed, codes, on = encode(slot, source, enc_weight[0], enc_bias, rows)
    came = [send_layer(packed, k) for k in range(1, layers)]
    turned, token = turn(rows, packed)
    goal, token = lax.optimization_barrier((goal, token))
    partial, sources = zip(
        *[decode(half, slot, token, codes, came, weights) for half in range(2)]
    )
    errors = (collect(partial, core) - goal.astype(F32)).astype(BF)
    errors = spread_y(spread_z(errors, core))
    away = back(place, source, weights[1:], errors)
    came = []
    for k in range(1, layers):
        ring = [(s, (s - k) % layers) for s in range(layers)]
        came.append(lax.ppermute(away[k - 1], "layer", ring))
    dec_grad, own = dec_gradient(layer, codes, *sources, weights[0], errors)
    enc_grad, bias_grad, loss = enc_gradient(layer, slot, turned, on, own, away[0], came)
    loss = loss[0, 0]
    return (loss, enc_grad[None], bias_grad, dec_grad[:, None])


def solution(mesh):
    in_specs = (
        P("layer", "latent", None),
        P("layer", "latent", None),
        P("layer", None, "latent"),
        P("layer", "latent"),
        P(None, "layer", "latent", None),
        P(),
    )
    out_specs = (
        P(),
        P("layer", None, "latent"),
        P("layer", "latent"),
        P(None, "layer", "latent", None),
    )
    return jax.shard_map(shards, mesh=mesh, in_specs=in_specs, out_specs=out_specs, check_vma=False)
```

time: 143 us -> 135 us (0.944)
  Pallas kernels: 23.3 us -> 14.5 us
  local copies, waits for them, and re-layouts: 6.07 us -> 2.44 us
  waiting for transfers between devices: 44.2 us -> 46.6 us
  starting transfers between devices: 64.6 us -> 66.7 us
    pallas_call x6 -> x4, Pallas kernels: 13.4 us -> 7.1 us  [the longest x2 3.37 us: decode(): pl.pallas_call(functools.partial(decode_kernel, half), in_specs=specs(1,...]
    ppermute x3, waiting for transfers between devices: 1.91 us -> 5.08 us  [send_layer(): return lax.ppermute(value, 'layer', [(s, s + steps) for s in sources])]
    unnamed x30 -> x6, local copies, waits for them, and re-layouts: 2.93 us -> 0.02 us
    ppermute x36, waiting for transfers between devices: 40.9 us -> 38.7 us  [send(): return lax.ppermute(value, 'latent', pairs(move, cores))]
    ppermute x3, waiting for transfers between devices: 1.38 us -> 2.89 us  [shards(): came.append(lax.ppermute(away[k - 1], 'layer', ring))]
    pallas_call x1, Pallas kernels: 5.86 us -> 4.37 us  [dec_gradient(): pl.pallas_call(dec_gradient_kernel, grid_spec=pltpu.PrefetchScalarGridSpe...]
  transfers between devices with their start and end apart: 42 -> 42, of which waited for: 23 -> 23; matrix products, arithmetic and copies ran while one was open for 4% -> 4% of each run, Pallas kernels for 9% -> 6%
where the time goes in v4:
time: 135 us
  starting transfers between devices  66.7 us (49%)
  waiting for transfers between devices  46.6 us (35%)
  Pallas kernels  14.5 us (11%)
  other arithmetic  3.56 us (3%)
  local copies, waits for them, and re-layouts  2.44 us (2%)
    ppermute x36, starting transfers between devices, send(): return lax.ppermute(value, 'latent', pairs(move, cores))  52.1 us
    ppermute x36, waiting for transfers between devices, send(): return lax.ppermute(value, 'latent', pairs(move, cores))  38.7 us
    ppermute x3, starting transfers between devices, send_layer(): return lax.ppermute(value, 'layer', [(s, s + steps) for s in sources])  8.18 us
    ppermute x3, starting transfers between devices, shards(): came.append(lax.ppermute(away[k - 1], 'layer', ring))  6.43 us
    ppermute x3, waiting for transfers between devices, send_layer(): return lax.ppermute(value, 'layer', [(s, s + steps) for s in sources])  5.08 us
    pallas_call x1, Pallas kernels, dec_gradient(): pl.pallas_call(dec_gradient_kernel, grid_spec=pltpu.PrefetchScalarGridSpe...  4.37 us
    pallas_call x2, Pallas kernels, decode(): pl.pallas_call(functools.partial(decode_kernel, half), in_specs=specs(1,...  3.37 us
    ppermute x3, waiting for transfers between devices, shards(): came.append(lax.ppermute(away[k - 1], 'layer', ring))  2.89 us
  transfers between devices with their start and end apart: 42, of which 23 were waited for; matrix products, arithmetic and copies ran while one was open for 4% of the time, Pallas kernels for 6%

profile of v4, /device:TPU:1, one launch (start us, length us, event | category | flops | bytes accessed | tf_op | source)
XLA Modules:
  0.0 134.9 jit_solution(2228153777682538451)
XLA Ops:
  0.6 3.3 %collective-permute-start = (bf16[8,1792]{1,0:T(8,128)(2,1)}, bf16[8,1792]{1,0:T(8,128)(2,1)S(1)}, u32[]{:S(2)}, u32[]{:S(2)}) collective-permute-start(bf16[8,1792]{1,0:T(8,128)(2,1)} %bitcast.18), channel_id=1, source_target_pairs={{0,1},{1,0},{2,3},{3,2},{4,5},{5,4},{6,7},{7,6},{8,9},{9,8},{10,11... | collective-permute-start | bytes 86024 | tf_op jit(solution)/shard_map/ppermute | solution.py:33
  4.1 0.9 collective-permute-done
  5.9 7.1 %collective-permute-start.1 = (bf16[16,1792]{1,0:T(8,128)(2,1)S(1)}, bf16[16,1792]{1,0:T(8,128)(2,1)S(1)}, u32[]{:S(2)}, u32[]{:S(2)}) collective-permute-start(bf16[16,1792]{1,0:T(8,128)(2,1)S(1)} %maximum_select_fusion), channel_id=1, source_target_pairs={{1,9},{3,11},{5,13},{7,15},{9,1},{11,3},{13,5},{15,7},{17,25},{19,... | collective-permute-start | bytes 172040 | tf_op jit(solution)/shard_map/ppermute | solution.py:33
  13.1 4.0 %collective-permute-start.2 = (bf16[16,1792]{1,0:T(8,128)(2,1)S(1)}, bf16[16,1792]{1,0:T(8,128)(2,1)S(1)}, u32[]{:S(2)}, u32[]{:S(2)}) collective-permute-start(bf16[16,1792]{1,0:T(8,128)(2,1)S(1)} %maximum_select_fusion), channel_id=1, source_target_pairs={{0,2},{1,11},{2,0},{3,9},{4,6},{5,15},{6,4},{7,13},{8,10},{9,3},{1... | collective-permute-start | bytes 172040 | tf_op jit(solution)/shard_map/ppermute | solution.py:33
  17.1 0.8 broadcast_select_fusion.1
  18.4 1.6 %collective-permute-done.2 = bf16[16,1792]{1,0:T(8,128)(2,1)S(1)} collective-permute-done((bf16[16,1792]{1,0:T(8,128)(2,1)S(1)}, bf16[16,1792]{1,0:T(8,128)(2,1)S(1)}, u32[]{:S(2)}, u32[]{:S(2)}) %collective-permute-start.2) | collective-permute-done | bytes 57376 | tf_op jit(solution)/shard_map/ppermute | solution.py:33
  20.0 1.3 collective-permute-done.4
  21.5 3.0 %collective-permute-start.7 = (bf16[64,1792]{1,0:T(8,128)(2,1)S(1)}, bf16[64,1792]{1,0:T(8,128)(2,1)S(1)}, u32[]{:S(2)}, u32[]{:S(2)}) collective-permute-start(bf16[64,1792]{1,0:T(8,128)(2,1)S(1)} %pad_maximum_fusion.refs_0_), channel_id=1, source_target_pairs={{0,32},{1,33},{2,34},{3,35},{4,36},{5,37},{6,38},{7,39},{8,40},{9,... | collective-permute-start | bytes 688136 | tf_op jit(solution)/shard_map/ppermute | solution.py:33
  25.2 0.9 compare_reduce_fusion
  26.1 1.1 collective-permute-start.12
  27.2 2.3 %dynamic-slice_bitcast_fusion = (bf16[256,1792]{1,0:T(8,128)(2,1)S(1)}, bf16[256,1792]{1,0:T(8,128)(2,1)S(1)}, bf16[256,1792]{1,0:T(8,128)(2,1)S(1)}, bf16[256,1792]{1,0:T(8,128)(2,1)S(1)}) fusion(bf16[4,1,256,1792]{3,2,1,0:T(8,128)(2,1)} %param.10, s32[]{:T(128)S(6)} %select_n.206, s32[]{:T(128)S(6)} %select_n.204, s32[]{:T(128)S(6)} %select_n.202, ...), kind=kLoop, calls=%fused_computation | loop fusion | bytes 7340048 | tf_op jit(solution)/shard_map/jit(dynamic_index_in_dim)/squeeze | solution.py:447
  29.8 2.1 %collective-permute-start.11 = (bf16[64,1792]{1,0:T(8,128)(2,1)S(1)}, bf16[64,1792]{1,0:T(8,128)(2,1)S(1)}, u32[]{:S(2)}, u32[]{:S(2)}) collective-permute-start(bf16[64,1792]{1,0:T(8,128)(2,1)S(1)} %collective-permute-done.7.refs_3_), channel_id=1, source_target_pairs={{0,1},{1,0},{2,3},{3,2},{4,5},{5,4},{6,7},{7,6},{8,9},{9,8},{10,11... | collective-permute-start | bytes 688136 | tf_op jit(solution)/shard_map/ppermute | solution.py:33
  31.9 3.6 %collective-permute-done.6.refs_2_ = bf16[64,1792]{1,0:T(8,128)(2,1)S(1)} collective-permute-done((bf16[64,1792]{1,0:T(8,128)(2,1)S(1)}, bf16[64,1792]{1,0:T(8,128)(2,1)S(1)}, u32[]{:S(2)}, u32[]{:S(2)}) %collective-permute-start.6) | collective-permute-done | bytes 229408 | tf_op jit(solution)/shard_map/ppermute | solution.py:33
  37.5 1.3 encode.1
  38.7 4.4 %collective-permute-start.15 = (bf16[384,256]{1,0:T(8,128)(2,1)S(1)}, bf16[384,256]{1,0:T(8,128)(2,1)S(1)}, u32[]{:S(2)}, u32[]{:S(2)}) collective-permute-start(bf16[384,256]{1,0:T(8,128)(2,1)S(1)} %get-tuple-element.29.after_ref), channel_id=1, source_target_pairs={{0,192},{1,193},{2,194},{3,195},{4,196},{5,197},{6,198},{7,199},{8... | collective-permute-start | bytes 589832 | tf_op jit(solution)/shard_map/ppermute | solution.py:43
  43.1 1.3 collective-permute-start.14
  44.5 2.5 %collective-permute-start.13 = (bf16[384,256]{1,0:T(8,128)(2,1)S(1)}, bf16[384,256]{1,0:T(8,128)(2,1)S(1)}, u32[]{:S(2)}, u32[]{:S(2)}) collective-permute-start(bf16[384,256]{1,0:T(8,128)(2,1)S(1)} %get-tuple-element.29.after_ref), channel_id=1, source_target_pairs={{0,64},{64,128},{128,192},{1,65},{65,129},{129,193},{2,66},{66,130... | collective-permute-start | bytes 589832 | tf_op jit(solution)/shard_map/ppermute | solution.py:43
  47.5 3.7 %collective-permute-done.15.refs_2_ = bf16[384,256]{1,0:T(8,128)(2,1)S(1)} collective-permute-done((bf16[384,256]{1,0:T(8,128)(2,1)S(1)}, bf16[384,256]{1,0:T(8,128)(2,1)S(1)}, u32[]{:S(2)}, u32[]{:S(2)}) %collective-permute-start.15) | collective-permute-done | bytes 196640 | tf_op jit(solution)/shard_map/ppermute | solution.py:43
  51.3 1.3 %collective-permute-done.13.refs_0_ = bf16[384,256]{1,0:T(8,128)(2,1)S(1)} collective-permute-done((bf16[384,256]{1,0:T(8,128)(2,1)S(1)}, bf16[384,256]{1,0:T(8,128)(2,1)S(1)}, u32[]{:S(2)}, u32[]{:S(2)}) %collective-permute-start.13) | collective-permute-done | bytes 196640 | tf_op jit(solution)/shard_map/ppermute | solution.py:43
  52.6 1.7 %decode.3 = (bf16[256,1792]{1,0:T(8,128)(2,1)S(1)}, bf16[3,256,256]{2,1,0:T(8,128)(2,1)S(1)}) custom-call(s32[4,32]{1,0:T(4,128)S(1)} %minimum_select_fusion.slot_ref, bf16[16,128]{1,0:T(8,128)(2,1)S(1)} %get-tuple-element.35.token_ref, bf16[512,256]{1,0:T(8,128)(2,1)S(1)} %get-tuple-element.32.codes_ref, ...), custom_call_target="tpu_custom_call" | custom-call | flops 1000 | bytes 1000 | tf_op jit(solution)/shard_map/decode/pallas_call | solution.py:331
  54.4 1.3 collective-permute-start.21
  56.3 1.7 %decode.2 = (bf16[256,1792]{1,0:T(8,128)(2,1)S(1)}, bf16[3,256,256]{2,1,0:T(8,128)(2,1)S(1)}) custom-call(s32[4,32]{1,0:T(4,128)S(1)} %minimum_select_fusion.slot_ref, bf16[16,128]{1,0:T(8,128)(2,1)S(1)} %get-tuple-element.35.token_ref, bf16[512,256]{1,0:T(8,128)(2,1)S(1)} %get-tuple-element.32.codes_ref, ...), custom_call_target="tpu_custom_call" | custom-call | flops 1000 | bytes 1000 | tf_op jit(solution)/shard_map/decode/pallas_call | solution.py:331
  58.2 1.4 %collective-permute-start.18 = (bf16[64,1792]{1,0:T(8,128)(2,1)S(1)}, bf16[64,1792]{1,0:T(8,128)(2,1)S(1)}, u32[]{:S(2)}, u32[]{:S(2)}) collective-permute-start(bf16[64,1792]{1,0:T(8,128)(2,1)S(1)} %get-tuple-element.68), channel_id=1, source_target_pairs={{0,16},{1,17},{2,18},{3,19},{4,20},{5,21},{6,22},{7,23},{8,24},{9,... | collective-permute-start | bytes 688136 | tf_op jit(solution)/shard_map/ppermute | solution.py:33
  59.5 2.6 %collective-permute-start.22 = (bf16[64,1792]{1,0:T(8,128)(2,1)S(1)}, bf16[64,1792]{1,0:T(8,128)(2,1)S(1)}, u32[]{:S(2)}, u32[]{:S(2)}) collective-permute-start(bf16[64,1792]{1,0:T(8,128)(2,1)S(1)} %get-tuple-element.69), channel_id=1, source_target_pairs={{0,32},{1,33},{2,34},{3,35},{4,36},{5,37},{6,38},{7,39},{8,40},{9,... | collective-permute-start | bytes 688136 | tf_op jit(solution)/shard_map/ppermute | solution.py:33
  62.2 2.9 %collective-permute-done.18 = bf16[64,1792]{1,0:T(8,128)(2,1)S(1)} collective-permute-done((bf16[64,1792]{1,0:T(8,128)(2,1)S(1)}, bf16[64,1792]{1,0:T(8,128)(2,1)S(1)}, u32[]{:S(2)}, u32[]{:S(2)}) %collective-permute-start.18) | collective-permute-done | bytes 229408 | tf_op jit(solution)/shard_map/ppermute | solution.py:33
  65.0 7.4 %collective-permute-done.22 = bf16[64,1792]{1,0:T(8,128)(2,1)S(1)} collective-permute-done((bf16[64,1792]{1,0:T(8,128)(2,1)S(1)}, bf16[64,1792]{1,0:T(8,128)(2,1)S(1)}, u32[]{:S(2)}, u32[]{:S(2)}) %collective-permute-start.22) | collective-permute-done | bytes 229408 | tf_op jit(solution)/shard_map/ppermute | solution.py:33
  72.4 2.0 %collective-permute-done.20 = bf16[64,1792]{1,0:T(8,128)(2,1)S(1)} collective-permute-done((bf16[64,1792]{1,0:T(8,128)(2,1)S(1)}, bf16[64,1792]{1,0:T(8,128)(2,1)S(1)}, u32[]{:S(2)}, u32[]{:S(2)}) %collective-permute-start.20) | collective-permute-done | bytes 229408 | tf_op jit(solution)/shard_map/ppermute | solution.py:33
  74.6 5.1 %collective-permute-start.23 = (bf16[16,1792]{1,0:T(8,128)(2,1)S(1)}, bf16[16,1792]{1,0:T(8,128)(2,1)S(1)}, u32[]{:S(2)}, u32[]{:S(2)}) collective-permute-start(bf16[16,1792]{1,0:T(8,128)(2,1)S(1)} %get-tuple-element.71), channel_id=1, source_target_pairs={{1,9},{3,11},{5,13},{7,15},{9,1},{11,3},{13,5},{15,7},{17,25},{19,... | collective-permute-start | bytes 172040 | tf_op jit(solution)/shard_map/ppermute | solution.py:33
  79.7 0.9 collective-permute-start.26
  80.6 3.4 %collective-permute-start.25 = (bf16[16,1792]{1,0:T(8,128)(2,1)S(1)}, bf16[16,1792]{1,0:T(8,128)(2,1)S(1)}, u32[]{:S(2)}, u32[]{:S(2)}) collective-permute-start(bf16[16,1792]{1,0:T(8,128)(2,1)S(1)} %get-tuple-element.73), channel_id=1, source_target_pairs={{0,4},{1,13},{2,6},{3,15},{4,0},{5,9},{6,2},{7,11},{8,12},{9,5},{1... | collective-permute-start | bytes 172040 | tf_op jit(solution)/shard_map/ppermute | solution.py:33
  84.7 2.6 %collective-permute-done.25 = bf16[16,1792]{1,0:T(8,128)(2,1)S(1)} collective-permute-done((bf16[16,1792]{1,0:T(8,128)(2,1)S(1)}, bf16[16,1792]{1,0:T(8,128)(2,1)S(1)}, u32[]{:S(2)}, u32[]{:S(2)}) %collective-permute-start.25) | collective-permute-done | bytes 57376 | tf_op jit(solution)/shard_map/ppermute | solution.py:33
  87.2 2.9 %collective-permute-done.24 = bf16[16,1792]{1,0:T(8,128)(2,1)S(1)} collective-permute-done((bf16[16,1792]{1,0:T(8,128)(2,1)S(1)}, bf16[16,1792]{1,0:T(8,128)(2,1)S(1)}, u32[]{:S(2)}, u32[]{:S(2)}) %collective-permute-start.24) | collective-permute-done | bytes 57376 | tf_op jit(solution)/shard_map/ppermute | solution.py:33
  90.2 1.2 collective-permute-done.27
  91.5 6.2 %collective-permute-start.28 = (bf16[16,1792]{1,0:T(8,128)(2,1)S(1)}, bf16[16,1792]{1,0:T(8,128)(2,1)S(1)}, u32[]{:S(2)}, u32[]{:S(2)}) collective-permute-start(bf16[16,1792]{1,0:T(8,128)(2,1)S(1)} %subtract_convert_fusion), channel_id=1, source_target_pairs={{1,9},{3,11},{5,13},{7,15},{9,1},{11,3},{13,5},{15,7},{17,25},{19,... | collective-permute-start | bytes 172040 | tf_op jit(solution)/shard_map/ppermute | solution.py:33
  97.8 1.8 %collective-permute-start.30 = (bf16[16,1792]{1,0:T(8,128)(2,1)S(1)}, bf16[16,1792]{1,0:T(8,128)(2,1)S(1)}, u32[]{:S(2)}, u32[]{:S(2)}) collective-permute-start(bf16[16,1792]{1,0:T(8,128)(2,1)S(1)} %subtract_convert_fusion), channel_id=1, source_target_pairs={{0,4},{1,13},{2,6},{3,15},{4,0},{5,9},{6,2},{7,11},{8,12},{9,5},{1... | collective-permute-start | bytes 172040 | tf_op jit(solution)/shard_map/ppermute | solution.py:33
  99.5 2.3 %collective-permute-start.29 = (bf16[16,1792]{1,0:T(8,128)(2,1)S(1)}, bf16[16,1792]{1,0:T(8,128)(2,1)S(1)}, u32[]{:S(2)}, u32[]{:S(2)}) collective-permute-start(bf16[16,1792]{1,0:T(8,128)(2,1)S(1)} %subtract_convert_fusion), channel_id=1, source_target_pairs={{0,2},{1,11},{2,0},{3,9},{4,6},{5,15},{6,4},{7,13},{8,10},{9,3},{1... | collective-permute-start | bytes 172040 | tf_op jit(solution)/shard_map/ppermute | solution.py:33
  102.3 1.2 collective-permute-done.30
  103.5 2.1 %collective-permute-done.29 = bf16[16,1792]{1,0:T(8,128)(2,1)S(1)} collective-permute-done((bf16[16,1792]{1,0:T(8,128)(2,1)S(1)}, bf16[16,1792]{1,0:T(8,128)(2,1)S(1)}, u32[]{:S(2)}, u32[]{:S(2)}) %collective-permute-start.29) | collective-permute-done | bytes 57376 | tf_op jit(solution)/shard_map/ppermute | solution.py:33
  105.7 1.0 collective-permute-start.33
  106.7 1.7 %collective-permute-start.32 = (bf16[64,1792]{1,0:T(8,128)(2,1)S(1)}, bf16[64,1792]{1,0:T(8,128)(2,1)S(1)}, u32[]{:S(2)}, u32[]{:S(2)}) collective-permute-start(bf16[64,1792]{1,0:T(8,128)(2,1)S(1)} %pad_maximum_fusion.1.refs_0_.refs_3_), channel_id=1, source_target_pairs={{0,16},{1,17},{2,18},{3,19},{4,20},{5,21},{6,22},{7,23},{8,24},{9,... | collective-permute-start | bytes 688136 | tf_op jit(solution)/shard_map/ppermute | solution.py:33
  108.4 3.9 %collective-permute-done.34.refs_3_.refs_6_ = bf16[64,1792]{1,0:T(8,128)(2,1)S(1)} collective-permute-done((bf16[64,1792]{1,0:T(8,128)(2,1)S(1)}, bf16[64,1792]{1,0:T(8,128)(2,1)S(1)}, u32[]{:S(2)}, u32[]{:S(2)}) %collective-permute-start.34) | collective-permute-done | bytes 229408 | tf_op jit(solution)/shard_map/ppermute | solution.py:33
  112.2 2.1 %collective-permute-done.33.refs_2_.refs_5_ = bf16[64,1792]{1,0:T(8,128)(2,1)S(1)} collective-permute-done((bf16[64,1792]{1,0:T(8,128)(2,1)S(1)}, bf16[64,1792]{1,0:T(8,128)(2,1)S(1)}, u32[]{:S(2)}, u32[]{:S(2)}) %collective-permute-start.33) | collective-permute-done | bytes 229408 | tf_op jit(solution)/shard_map/ppermute | solution.py:33
  116.2 2.5 %back.1 = (bf16[400,256]{1,0:T(8,128)(2,1)S(1)}, bf16[400,256]{1,0:T(8,128)(2,1)S(1)}, bf16[400,256]{1,0:T(8,128)(2,1)S(1)}) custom-call(s32[32]{0:T(128)S(1)} %select_reduce_fusion.2.place_ref, s32[4,24]{1,0:T(4,128)S(1)} %broadcast_minimum_fusion.source_ref, bf16[256,1792]{1,0:T(8,128)(2,1)S(1)} %get-tuple-element.62.refs_4_.refs_0_, ...), custom_call_target="tpu_custom_call" | custom-call | flops 1000 | bytes 1000 | tf_op jit(solution)/shard_map/back/pallas_call | solution.py:290
  118.7 3.8 %collective-permute-start.40 = (bf16[400,256]{1,0:T(8,128)(2,1)S(1)}, bf16[400,256]{1,0:T(8,128)(2,1)S(1)}, u32[]{:S(2)}, u32[]{:S(2)}) collective-permute-start(bf16[400,256]{1,0:T(8,128)(2,1)S(1)} %get-tuple-element.44), channel_id=1, source_target_pairs={{0,128},{64,192},{128,0},{192,64},{1,129},{65,193},{129,1},{193,65... | collective-permute-start | bytes 614408 | tf_op jit(solution)/shard_map/ppermute | solution.py:465
  122.4 2.7 %collective-permute-start.39 = (bf16[400,256]{1,0:T(8,128)(2,1)S(1)}, bf16[400,256]{1,0:T(8,128)(2,1)S(1)}, u32[]{:S(2)}, u32[]{:S(2)}) collective-permute-start(bf16[400,256]{1,0:T(8,128)(2,1)S(1)} %get-tuple-element.43.away_ref), channel_id=1, source_target_pairs={{0,192},{64,0},{128,64},{192,128},{1,193},{65,1},{129,65},{193,129... | collective-permute-start | bytes 614408 | tf_op jit(solution)/shard_map/ppermute | solution.py:465
  125.1 4.4 %dec_gradient.1 = (bf16[4,256,1792]{2,1,0:T(8,128)(2,1)}, f32[512,256]{1,0:T(8,128)S(1)}) custom-call(s32[1]{0:T(128)} %bitcast.layer_ref, bf16[512,256]{1,0:T(8,128)(2,1)S(1)} %get-tuple-element.32.codes_ref, bf16[3,256,256]{2,1,0:T(8,128)(2,1)S(1)} %get-tuple-element.37.first_ref, bf16[3,256,256]{2,1,0:T(8,128)(2,1)S(1)} %get-tuple-element.38.second_ref, ...), custom_call_target="tpu_custom_call" | custom-call | flops 1000 | bytes 1000 | tf_op jit(solution)/shard_map/dec_gradient/pallas_call | solution.py:213
  129.5 2.9 %collective-permute-done.41.refs_2_ = bf16[400,256]{1,0:T(8,128)(2,1)S(1)} collective-permute-done((bf16[400,256]{1,0:T(8,128)(2,1)S(1)}, bf16[400,256]{1,0:T(8,128)(2,1)S(1)}, u32[]{:S(2)}, u32[]{:S(2)}) %collective-permute-start.41) | collective-permute-done | bytes 204832 | tf_op jit(solution)/shard_map/ppermute | solution.py:465
  132.4 2.5 %enc_gradient.1 = (bf16[1792,256]{1,0:T(8,128)(2,1)}, f32[1,256]{1,0:T(1,128)}, f32[1,1]{1,0:T(1,128)}) custom-call(s32[1]{0:T(128)} %bitcast.layer_ref, s32[4,32]{1,0:T(4,128)S(1)} %minimum_select_fusion.slot_ref, bf16[1792,512]{1,0:T(8,128)(2,1)S(1)} %get-tuple-element.30.rows_ref, bf16[512,256]{1,0:T(8,128)(2,1)S(1)} %get-tuple-element.31.on_ref, ...), custom_call_target="tpu_custom_call" | custom-call | flops 1000 | bytes 1000 | tf_op jit(solution)/shard_map/enc_gradient/pallas_call | solution.py:382
  (74 shorter events, 9.3 us)
Async XLA Ops:
  0.6 4.4 %collective-permute-start = (bf16[8,1792]{1,0:T(8,128)(2,1)}, bf16[8,1792]{1,0:T(8,128)(2,1)S(1)}, u32[]{:S(2)}, u32[]{:S(2)}) collective-permute-start(bf16[8,1792]{1,0:T(8,128)(2,1)} %bitcast.18), channel_id=1, source_target_pairs={{0,1},{1,0},{2,3},{3,2},{4,5},{5,4},{6,7},{7,6},{8,9},{9,8},{10,11... | collective-permute-start | bytes 86024 | tf_op jit(solution)/shard_map/ppermute | solution.py:33
  5.9 11.2 %collective-permute-start.1 = (bf16[16,1792]{1,0:T(8,128)(2,1)S(1)}, bf16[16,1792]{1,0:T(8,128)(2,1)S(1)}, u32[]{:S(2)}, u32[]{:S(2)}) collective-permute-start(bf16[16,1792]{1,0:T(8,128)(2,1)S(1)} %maximum_select_fusion), channel_id=1, source_target_pairs={{1,9},{3,11},{5,13},{7,15},{9,1},{11,3},{13,5},{15,7},{17,25},{19,... | collective-permute-start | bytes 172040 | tf_op jit(solution)/shard_map/ppermute | solution.py:33
  13.0 5.4 %collective-permute-start.3 = (bf16[16,1792]{1,0:T(8,128)(2,1)S(1)}, bf16[16,1792]{1,0:T(8,128)(2,1)S(1)}, u32[]{:S(2)}, u32[]{:S(2)}) collective-permute-start(bf16[16,1792]{1,0:T(8,128)(2,1)S(1)} %maximum_select_fusion), channel_id=1, source_target_pairs={{0,4},{1,13},{2,6},{3,15},{4,0},{5,9},{6,2},{7,11},{8,12},{9,5},{1... | collective-permute-start | bytes 172040 | tf_op jit(solution)/shard_map/ppermute | solution.py:33
  13.1 7.0 %collective-permute-start.2 = (bf16[16,1792]{1,0:T(8,128)(2,1)S(1)}, bf16[16,1792]{1,0:T(8,128)(2,1)S(1)}, u32[]{:S(2)}, u32[]{:S(2)}) collective-permute-start(bf16[16,1792]{1,0:T(8,128)(2,1)S(1)} %maximum_select_fusion), channel_id=1, source_target_pairs={{0,2},{1,11},{2,0},{3,9},{4,6},{5,15},{6,4},{7,13},{8,10},{9,3},{1... | collective-permute-start | bytes 172040 | tf_op jit(solution)/shard_map/ppermute | solution.py:33
  17.1 4.2 %collective-permute-start.4 = (bf16[16,1792]{1,0:T(8,128)(2,1)S(1)}, bf16[16,1792]{1,0:T(8,128)(2,1)S(1)}, u32[]{:S(2)}, u32[]{:S(2)}) collective-permute-start(bf16[16,1792]{1,0:T(8,128)(2,1)S(1)} %maximum_select_fusion), channel_id=1, source_target_pairs={{0,6},{1,15},{2,4},{3,13},{4,2},{5,11},{6,0},{7,9},{8,14},{9,7},{1... | collective-permute-start | bytes 172040 | tf_op jit(solution)/shard_map/ppermute | solution.py:33
  21.4 15.2 %collective-permute-start.8 = (bf16[64,1792]{1,0:T(8,128)(2,1)S(1)}, bf16[64,1792]{1,0:T(8,128)(2,1)S(1)}, u32[]{:S(2)}, u32[]{:S(2)}) collective-permute-start(bf16[64,1792]{1,0:T(8,128)(2,1)S(1)} %pad_maximum_fusion.refs_0_), channel_id=1, source_target_pairs={{0,1},{1,0},{2,3},{3,2},{4,5},{5,4},{6,7},{7,6},{8,9},{9,8},{10,11... | collective-permute-start | bytes 688136 | tf_op jit(solution)/shard_map/ppermute | solution.py:33
  21.5 8.4 %collective-permute-start.7 = (bf16[64,1792]{1,0:T(8,128)(2,1)S(1)}, bf16[64,1792]{1,0:T(8,128)(2,1)S(1)}, u32[]{:S(2)}, u32[]{:S(2)}) collective-permute-start(bf16[64,1792]{1,0:T(8,128)(2,1)S(1)} %pad_maximum_fusion.refs_0_), channel_id=1, source_target_pairs={{0,32},{1,33},{2,34},{3,35},{4,36},{5,37},{6,38},{7,39},{8,40},{9,... | collective-permute-start | bytes 688136 | tf_op jit(solution)/shard_map/ppermute | solution.py:33
  24.5 11.0 %collective-permute-start.6 = (bf16[64,1792]{1,0:T(8,128)(2,1)S(1)}, bf16[64,1792]{1,0:T(8,128)(2,1)S(1)}, u32[]{:S(2)}, u32[]{:S(2)}) collective-permute-start(bf16[64,1792]{1,0:T(8,128)(2,1)S(1)} %pad_maximum_fusion.refs_0_), channel_id=1, source_target_pairs={{0,48},{1,49},{2,50},{3,51},{4,52},{5,53},{6,54},{7,55},{8,56},{9,... | collective-permute-start | bytes 688136 | tf_op jit(solution)/shard_map/ppermute | solution.py:33
  25.2 10.8 %collective-permute-start.5 = (bf16[64,1792]{1,0:T(8,128)(2,1)S(1)}, bf16[64,1792]{1,0:T(8,128)(2,1)S(1)}, u32[]{:S(2)}, u32[]{:S(2)}) collective-permute-start(bf16[64,1792]{1,0:T(8,128)(2,1)S(1)} %pad_maximum_fusion.refs_0_), channel_id=1, source_target_pairs={{0,16},{1,17},{2,18},{3,19},{4,20},{5,21},{6,22},{7,23},{8,24},{9,... | collective-permute-start | bytes 688136 | tf_op jit(solution)/shard_map/ppermute | solution.py:33
  26.1 20.9 %collective-permute-start.12 = (bf16[8,1792]{1,0:T(8,128)(2,1)}, bf16[8,1792]{1,0:T(8,128)(2,1)S(1)}, u32[]{:S(2)}, u32[]{:S(2)}) collective-permute-start(bf16[8,1792]{1,0:T(8,128)(2,1)} %bitcast.21), channel_id=1, source_target_pairs={{0,1},{1,0},{2,3},{3,2},{4,5},{5,4},{6,7},{7,6},{8,9},{9,8},{10,11... | collective-permute-start | bytes 86024 | tf_op jit(solution)/shard_map/ppermute | solution.py:33
  27.2 10.3 %copy-start = (bf16[1,1792,256]{2,1,0:T(8,128)(2,1)S(1)}, bf16[1,1792,256]{2,1,0:T(8,128)(2,1)}, u32[]{:S(2)}) copy-start(bf16[1,1792,256]{2,1,0:T(8,128)(2,1)} %param.8) | copy-start | bytes 2752516
  27.2 10.3 %copy-start.1 = (f32[1,256]{1,0:T(1,128)S(1)}, f32[1,256]{1,0:T(1,128)}, u32[]{:S(2)}) copy-start(f32[1,256]{1,0:T(1,128)} %bias_ref.1) | copy-start | bytes 3076
  27.2 19.8 %copy-start.2 = (bf16[1,8,1792]{2,1,0:T(8,128)(2,1)S(1)}, bf16[1,8,1792]{2,1,0:T(8,128)(2,1)}, u32[]{:S(2)}) copy-start(bf16[1,8,1792]{2,1,0:T(8,128)(2,1)} %param.7) | copy-start | bytes 86020
  29.8 6.7 %collective-permute-start.11 = (bf16[64,1792]{1,0:T(8,128)(2,1)S(1)}, bf16[64,1792]{1,0:T(8,128)(2,1)S(1)}, u32[]{:S(2)}, u32[]{:S(2)}) collective-permute-start(bf16[64,1792]{1,0:T(8,128)(2,1)S(1)} %collective-permute-done.7.refs_3_), channel_id=1, source_target_pairs={{0,1},{1,0},{2,3},{3,2},{4,5},{5,4},{6,7},{7,6},{8,9},{9,8},{10,11... | collective-permute-start | bytes 688136 | tf_op jit(solution)/shard_map/ppermute | solution.py:33
  35.5 1.6 %collective-permute-start.10 = (bf16[64,1792]{1,0:T(8,128)(2,1)S(1)}, bf16[64,1792]{1,0:T(8,128)(2,1)S(1)}, u32[]{:S(2)}, u32[]{:S(2)}) collective-permute-start(bf16[64,1792]{1,0:T(8,128)(2,1)S(1)} %collective-permute-done.6.refs_2_), channel_id=1, source_target_pairs={{0,1},{1,0},{2,3},{3,2},{4,5},{5,4},{6,7},{7,6},{8,9},{9,8},{10,11... | collective-permute-start | bytes 688136 | tf_op jit(solution)/shard_map/ppermute | solution.py:33
  36.0 1.5 %collective-permute-start.9 = (bf16[64,1792]{1,0:T(8,128)(2,1)S(1)}, bf16[64,1792]{1,0:T(8,128)(2,1)S(1)}, u32[]{:S(2)}, u32[]{:S(2)}) collective-permute-start(bf16[64,1792]{1,0:T(8,128)(2,1)S(1)} %collective-permute-done.5.refs_1_), channel_id=1, source_target_pairs={{0,1},{1,0},{2,3},{3,2},{4,5},{5,4},{6,7},{7,6},{8,9},{9,8},{10,11... | collective-permute-start | bytes 688136 | tf_op jit(solution)/shard_map/ppermute | solution.py:33
  38.7 12.5 %collective-permute-start.15 = (bf16[384,256]{1,0:T(8,128)(2,1)S(1)}, bf16[384,256]{1,0:T(8,128)(2,1)S(1)}, u32[]{:S(2)}, u32[]{:S(2)}) collective-permute-start(bf16[384,256]{1,0:T(8,128)(2,1)S(1)} %get-tuple-element.29.after_ref), channel_id=1, source_target_pairs={{0,192},{1,193},{2,194},{3,195},{4,196},{5,197},{6,198},{7,199},{8... | collective-permute-start | bytes 589832 | tf_op jit(solution)/shard_map/ppermute | solution.py:43
  43.1 8.1 %collective-permute-start.14 = (bf16[384,256]{1,0:T(8,128)(2,1)S(1)}, bf16[384,256]{1,0:T(8,128)(2,1)S(1)}, u32[]{:S(2)}, u32[]{:S(2)}) collective-permute-start(bf16[384,256]{1,0:T(8,128)(2,1)S(1)} %get-tuple-element.29.after_ref), channel_id=1, source_target_pairs={{0,128},{64,192},{1,129},{65,193},{2,130},{66,194},{3,131},{67,195... | collective-permute-start | bytes 589832 | tf_op jit(solution)/shard_map/ppermute | solution.py:43
  44.5 8.1 %collective-permute-start.13 = (bf16[384,256]{1,0:T(8,128)(2,1)S(1)}, bf16[384,256]{1,0:T(8,128)(2,1)S(1)}, u32[]{:S(2)}, u32[]{:S(2)}) collective-permute-start(bf16[384,256]{1,0:T(8,128)(2,1)S(1)} %get-tuple-element.29.after_ref), channel_id=1, source_target_pairs={{0,64},{64,128},{128,192},{1,65},{65,129},{129,193},{2,66},{66,130... | collective-permute-start | bytes 589832 | tf_op jit(solution)/shard_map/ppermute | solution.py:43
  54.4 3.6 %collective-permute-start.21 = (bf16[64,1792]{1,0:T(8,128)(2,1)S(1)}, bf16[64,1792]{1,0:T(8,128)(2,1)S(1)}, u32[]{:S(2)}, u32[]{:S(2)}) collective-permute-start(bf16[64,1792]{1,0:T(8,128)(2,1)S(1)} %get-tuple-element.65), channel_id=1, source_target_pairs={{0,1},{1,0},{2,3},{3,2},{4,5},{5,4},{6,7},{7,6},{8,9},{9,8},{10,11... | collective-permute-start | bytes 688136 | tf_op jit(solution)/shard_map/ppermute | solution.py:33
  55.6 2.3 %collective-permute-start.19 = (bf16[64,1792]{1,0:T(8,128)(2,1)S(1)}, bf16[64,1792]{1,0:T(8,128)(2,1)S(1)}, u32[]{:S(2)}, u32[]{:S(2)}) collective-permute-start(bf16[64,1792]{1,0:T(8,128)(2,1)S(1)} %get-tuple-element.66), channel_id=1, source_target_pairs={{0,1},{1,0},{2,3},{3,2},{4,5},{5,4},{6,7},{7,6},{8,9},{9,8},{10,11... | collective-permute-start | bytes 688136 | tf_op jit(solution)/shard_map/ppermute | solution.py:33
  55.8 2.2 %collective-permute-start.17 = (bf16[64,1792]{1,0:T(8,128)(2,1)S(1)}, bf16[64,1792]{1,0:T(8,128)(2,1)S(1)}, u32[]{:S(2)}, u32[]{:S(2)}) collective-permute-start(bf16[64,1792]{1,0:T(8,128)(2,1)S(1)} %get-tuple-element.67), channel_id=1, source_target_pairs={{0,1},{1,0},{2,3},{3,2},{4,5},{5,4},{6,7},{7,6},{8,9},{9,8},{10,11... | collective-permute-start | bytes 688136 | tf_op jit(solution)/shard_map/ppermute | solution.py:33
  56.2 6.0 %collective-permute-start.16 = (bf16[64,1792]{1,0:T(8,128)(2,1)S(1)}, bf16[64,1792]{1,0:T(8,128)(2,1)S(1)}, u32[]{:S(2)}, u32[]{:S(2)}) collective-permute-start(bf16[64,1792]{1,0:T(8,128)(2,1)S(1)} %get-tuple-element.64), channel_id=1, source_target_pairs={{0,1},{1,0},{2,3},{3,2},{4,5},{5,4},{6,7},{7,6},{8,9},{9,8},{10,11... | collective-permute-start | bytes 688136 | tf_op jit(solution)/shard_map/ppermute | solution.py:33
  58.2 6.9 %collective-permute-start.18 = (bf16[64,1792]{1,0:T(8,128)(2,1)S(1)}, bf16[64,1792]{1,0:T(8,128)(2,1)S(1)}, u32[]{:S(2)}, u32[]{:S(2)}) collective-permute-start(bf16[64,1792]{1,0:T(8,128)(2,1)S(1)} %get-tuple-element.68), channel_id=1, source_target_pairs={{0,16},{1,17},{2,18},{3,19},{4,20},{5,21},{6,22},{7,23},{8,24},{9,... | collective-permute-start | bytes 688136 | tf_op jit(solution)/shard_map/ppermute | solution.py:33
  59.5 12.9 %collective-permute-start.22 = (bf16[64,1792]{1,0:T(8,128)(2,1)S(1)}, bf16[64,1792]{1,0:T(8,128)(2,1)S(1)}, u32[]{:S(2)}, u32[]{:S(2)}) collective-permute-start(bf16[64,1792]{1,0:T(8,128)(2,1)S(1)} %get-tuple-element.69), channel_id=1, source_target_pairs={{0,32},{1,33},{2,34},{3,35},{4,36},{5,37},{6,38},{7,39},{8,40},{9,... | collective-permute-start | bytes 688136 | tf_op jit(solution)/shard_map/ppermute | solution.py:33
  62.2 12.3 %collective-permute-start.20 = (bf16[64,1792]{1,0:T(8,128)(2,1)S(1)}, bf16[64,1792]{1,0:T(8,128)(2,1)S(1)}, u32[]{:S(2)}, u32[]{:S(2)}) collective-permute-start(bf16[64,1792]{1,0:T(8,128)(2,1)S(1)} %get-tuple-element.70), channel_id=1, source_target_pairs={{0,48},{1,49},{2,50},{3,51},{4,52},{5,53},{6,54},{7,55},{8,56},{9,... | collective-permute-start | bytes 688136 | tf_op jit(solution)/shard_map/ppermute | solution.py:33
  74.6 10.1 %collective-permute-start.23 = (bf16[16,1792]{1,0:T(8,128)(2,1)S(1)}, bf16[16,1792]{1,0:T(8,128)(2,1)S(1)}, u32[]{:S(2)}, u32[]{:S(2)}) collective-permute-start(bf16[16,1792]{1,0:T(8,128)(2,1)S(1)} %get-tuple-element.71), channel_id=1, source_target_pairs={{1,9},{3,11},{5,13},{7,15},{9,1},{11,3},{13,5},{15,7},{17,25},{19,... | collective-permute-start | bytes 172040 | tf_op jit(solution)/shard_map/ppermute | solution.py:33
  79.7 5.0 %collective-permute-start.26 = (bf16[16,1792]{1,0:T(8,128)(2,1)S(1)}, bf16[16,1792]{1,0:T(8,128)(2,1)S(1)}, u32[]{:S(2)}, u32[]{:S(2)}) collective-permute-start(bf16[16,1792]{1,0:T(8,128)(2,1)S(1)} %get-tuple-element.72), channel_id=1, source_target_pairs={{0,6},{1,15},{2,4},{3,13},{4,2},{5,11},{6,0},{7,9},{8,14},{9,7},{1... | collective-permute-start | bytes 172040 | tf_op jit(solution)/shard_map/ppermute | solution.py:33
  80.6 6.6 %collective-permute-start.25 = (bf16[16,1792]{1,0:T(8,128)(2,1)S(1)}, bf16[16,1792]{1,0:T(8,128)(2,1)S(1)}, u32[]{:S(2)}, u32[]{:S(2)}) collective-permute-start(bf16[16,1792]{1,0:T(8,128)(2,1)S(1)} %get-tuple-element.73), channel_id=1, source_target_pairs={{0,4},{1,13},{2,6},{3,15},{4,0},{5,9},{6,2},{7,11},{8,12},{9,5},{1... | collective-permute-start | bytes 172040 | tf_op jit(solution)/shard_map/ppermute | solution.py:33
  84.1 6.0 %collective-permute-start.24 = (bf16[16,1792]{1,0:T(8,128)(2,1)S(1)}, bf16[16,1792]{1,0:T(8,128)(2,1)S(1)}, u32[]{:S(2)}, u32[]{:S(2)}) collective-permute-start(bf16[16,1792]{1,0:T(8,128)(2,1)S(1)} %get-tuple-element.74), channel_id=1, source_target_pairs={{0,2},{1,11},{2,0},{3,9},{4,6},{5,15},{6,4},{7,13},{8,10},{9,3},{1... | collective-permute-start | bytes 172040 | tf_op jit(solution)/shard_map/ppermute | solution.py:33
  90.1 1.3 collective-permute-start.27
  91.5 10.4 %collective-permute-start.28 = (bf16[16,1792]{1,0:T(8,128)(2,1)S(1)}, bf16[16,1792]{1,0:T(8,128)(2,1)S(1)}, u32[]{:S(2)}, u32[]{:S(2)}) collective-permute-start(bf16[16,1792]{1,0:T(8,128)(2,1)S(1)} %subtract_convert_fusion), channel_id=1, source_target_pairs={{1,9},{3,11},{5,13},{7,15},{9,1},{11,3},{13,5},{15,7},{17,25},{19,... | collective-permute-start | bytes 172040 | tf_op jit(solution)/shard_map/ppermute | solution.py:33
  97.7 4.6 %collective-permute-start.31 = (bf16[16,1792]{1,0:T(8,128)(2,1)S(1)}, bf16[16,1792]{1,0:T(8,128)(2,1)S(1)}, u32[]{:S(2)}, u32[]{:S(2)}) collective-permute-start(bf16[16,1792]{1,0:T(8,128)(2,1)S(1)} %subtract_convert_fusion), channel_id=1, source_target_pairs={{0,6},{1,15},{2,4},{3,13},{4,2},{5,11},{6,0},{7,9},{8,14},{9,7},{1... | collective-permute-start | bytes 172040 | tf_op jit(solution)/shard_map/ppermute | solution.py:33
  97.8 5.7 %collective-permute-start.30 = (bf16[16,1792]{1,0:T(8,128)(2,1)S(1)}, bf16[16,1792]{1,0:T(8,128)(2,1)S(1)}, u32[]{:S(2)}, u32[]{:S(2)}) collective-permute-start(bf16[16,1792]{1,0:T(8,128)(2,1)S(1)} %subtract_convert_fusion), channel_id=1, source_target_pairs={{0,4},{1,13},{2,6},{3,15},{4,0},{5,9},{6,2},{7,11},{8,12},{9,5},{1... | collective-permute-start | bytes 172040 | tf_op jit(solution)/shard_map/ppermute | solution.py:33
  99.5 6.1 %collective-permute-start.29 = (bf16[16,1792]{1,0:T(8,128)(2,1)S(1)}, bf16[16,1792]{1,0:T(8,128)(2,1)S(1)}, u32[]{:S(2)}, u32[]{:S(2)}) collective-permute-start(bf16[16,1792]{1,0:T(8,128)(2,1)S(1)} %subtract_convert_fusion), channel_id=1, source_target_pairs={{0,2},{1,11},{2,0},{3,9},{4,6},{5,15},{6,4},{7,13},{8,10},{9,3},{1... | collective-permute-start | bytes 172040 | tf_op jit(solution)/shard_map/ppermute | solution.py:33
  105.6 6.6 %collective-permute-start.34 = (bf16[64,1792]{1,0:T(8,128)(2,1)S(1)}, bf16[64,1792]{1,0:T(8,128)(2,1)S(1)}, u32[]{:S(2)}, u32[]{:S(2)}) collective-permute-start(bf16[64,1792]{1,0:T(8,128)(2,1)S(1)} %pad_maximum_fusion.1.refs_0_.refs_3_), channel_id=1, source_target_pairs={{0,32},{1,33},{2,34},{3,35},{4,36},{5,37},{6,38},{7,39},{8,40},{9,... | collective-permute-start | bytes 688136 | tf_op jit(solution)/shard_map/ppermute | solution.py:33
  105.7 8.6 %collective-permute-start.33 = (bf16[64,1792]{1,0:T(8,128)(2,1)S(1)}, bf16[64,1792]{1,0:T(8,128)(2,1)S(1)}, u32[]{:S(2)}, u32[]{:S(2)}) collective-permute-start(bf16[64,1792]{1,0:T(8,128)(2,1)S(1)} %pad_maximum_fusion.1.refs_0_.refs_3_), channel_id=1, source_target_pairs={{0,48},{1,49},{2,50},{3,51},{4,52},{5,53},{6,54},{7,55},{8,56},{9,... | collective-permute-start | bytes 688136 | tf_op jit(solution)/shard_map/ppermute | solution.py:33
  106.7 7.7 %collective-permute-start.32 = (bf16[64,1792]{1,0:T(8,128)(2,1)S(1)}, bf16[64,1792]{1,0:T(8,128)(2,1)S(1)}, u32[]{:S(2)}, u32[]{:S(2)}) collective-permute-start(bf16[64,1792]{1,0:T(8,128)(2,1)S(1)} %pad_maximum_fusion.1.refs_0_.refs_3_), channel_id=1, source_target_pairs={{0,16},{1,17},{2,18},{3,19},{4,20},{5,21},{6,22},{7,23},{8,24},{9,... | collective-permute-start | bytes 688136 | tf_op jit(solution)/shard_map/ppermute | solution.py:33
  108.4 6.6 %collective-permute-start.35 = (bf16[64,1792]{1,0:T(8,128)(2,1)S(1)}, bf16[64,1792]{1,0:T(8,128)(2,1)S(1)}, u32[]{:S(2)}, u32[]{:S(2)}) collective-permute-start(bf16[64,1792]{1,0:T(8,128)(2,1)S(1)} %pad_maximum_fusion.1.refs_0_.refs_3_), channel_id=1, source_target_pairs={{0,1},{1,0},{2,3},{3,2},{4,5},{5,4},{6,7},{7,6},{8,9},{9,8},{10,11... | collective-permute-start | bytes 688136 | tf_op jit(solution)/shard_map/ppermute | solution.py:33
  112.2 2.7 %collective-permute-start.38 = (bf16[64,1792]{1,0:T(8,128)(2,1)S(1)}, bf16[64,1792]{1,0:T(8,128)(2,1)S(1)}, u32[]{:S(2)}, u32[]{:S(2)}) collective-permute-start(bf16[64,1792]{1,0:T(8,128)(2,1)S(1)} %collective-permute-done.34.refs_3_.refs_6_), channel_id=1, source_target_pairs={{0,1},{1,0},{2,3},{3,2},{4,5},{5,4},{6,7},{7,6},{8,9},{9,8},{10,11... | collective-permute-start | bytes 688136 | tf_op jit(solution)/shard_map/ppermute | solution.py:33
  114.4 1.5 %collective-permute-start.37 = (bf16[64,1792]{1,0:T(8,128)(2,1)S(1)}, bf16[64,1792]{1,0:T(8,128)(2,1)S(1)}, u32[]{:S(2)}, u32[]{:S(2)}) collective-permute-start(bf16[64,1792]{1,0:T(8,128)(2,1)S(1)} %collective-permute-done.33.refs_2_.refs_5_), channel_id=1, source_target_pairs={{0,1},{1,0},{2,3},{3,2},{4,5},{5,4},{6,7},{7,6},{8,9},{9,8},{10,11... | collective-permute-start | bytes 688136 | tf_op jit(solution)/shard_map/ppermute | solution.py:33
  114.4 1.8 %collective-permute-start.36 = (bf16[64,1792]{1,0:T(8,128)(2,1)S(1)}, bf16[64,1792]{1,0:T(8,128)(2,1)S(1)}, u32[]{:S(2)}, u32[]{:S(2)}) collective-permute-start(bf16[64,1792]{1,0:T(8,128)(2,1)S(1)} %collective-permute-done.32.refs_1_.refs_4_), channel_id=1, source_target_pairs={{0,1},{1,0},{2,3},{3,2},{4,5},{5,4},{6,7},{7,6},{8,9},{9,8},{10,11... | collective-permute-start | bytes 688136 | tf_op jit(solution)/shard_map/ppermute | solution.py:33
  118.7 10.8 %collective-permute-start.40 = (bf16[400,256]{1,0:T(8,128)(2,1)S(1)}, bf16[400,256]{1,0:T(8,128)(2,1)S(1)}, u32[]{:S(2)}, u32[]{:S(2)}) collective-permute-start(bf16[400,256]{1,0:T(8,128)(2,1)S(1)} %get-tuple-element.44), channel_id=1, source_target_pairs={{0,128},{64,192},{128,0},{192,64},{1,129},{65,193},{129,1},{193,65... | collective-permute-start | bytes 614408 | tf_op jit(solution)/shard_map/ppermute | solution.py:465
  122.4 9.9 %collective-permute-start.41 = (bf16[400,256]{1,0:T(8,128)(2,1)S(1)}, bf16[400,256]{1,0:T(8,128)(2,1)S(1)}, u32[]{:S(2)}, u32[]{:S(2)}) collective-permute-start(bf16[400,256]{1,0:T(8,128)(2,1)S(1)} %get-tuple-element.45), channel_id=1, source_target_pairs={{0,64},{64,128},{128,192},{192,0},{1,65},{65,129},{129,193},{193,1... | collective-permute-start | bytes 614408 | tf_op jit(solution)/shard_map/ppermute | solution.py:465
  122.4 9.9 %collective-permute-start.39 = (bf16[400,256]{1,0:T(8,128)(2,1)S(1)}, bf16[400,256]{1,0:T(8,128)(2,1)S(1)}, u32[]{:S(2)}, u32[]{:S(2)}) collective-permute-start(bf16[400,256]{1,0:T(8,128)(2,1)S(1)} %get-tuple-element.43.away_ref), channel_id=1, source_target_pairs={{0,192},{64,0},{128,64},{192,128},{1,193},{65,1},{129,65},{193,129... | collective-permute-start | bytes 614408 | tf_op jit(solution)/shard_map/ppermute | solution.py:465

commit v5 on v4

--- a/solution.py
+++ b/solution.py
@@ -13,7 +13,8 @@
 Y, Z, C = 4, 8, 2
 BF = jnp.bfloat16
 F32 = jnp.float32
-STEPS = (0, 1, 3, 2)
+STEPS = (0, 2, 1, 3)
+ORDER = (2, 1, 3)
 
 
 def index_of(y, z, c):
@@ -84,7 +85,7 @@
     y, z, c = latent // (Z * C), latent // C % Z, latent % C
     p = jnp.arange(Y * Z, dtype=jnp.int32)
     half, step, j = p // 16, p // 4 % 4, p % 4
-    step = jnp.where(step < 2, step, 5 - step)
+    step = sum(jnp.where(step == i, to, 0) for i, to in enumerate(STEPS))
     side = (half + c) % 2
     from_z = z ^ (j + 4 * side)
     return (y ^ step) * Z + from_z
@@ -177,10 +178,9 @@
     )(after, *parts)
 
 
-def dec_gradient_kernel(layer_ref, codes_ref, first_ref, second_ref, weight_ref, *refs):
+def dec_gradient_kernel(layer_ref, first_ref, second_ref, weight_ref, *refs):
     del layer_ref
     parts, (out_ref, own_ref, errors_ref) = refs[:-3], refs[-3:]
-    over_rows = (((0,), (0,)), ((), ()))
 
     @pl.when(pl.program_id(0) == 0)
     def _():
@@ -188,27 +188,18 @@
         own_ref[...] = lax.dot_general(
             errors_ref[...], weight_ref[...], (((1,), (1,)), ((), ())), preferred_element_type=F32
         )
-        grad = lax.dot_general(
-            codes_ref[...], errors_ref[...], over_rows, preferred_element_type=F32
-        )
-        out_ref[0] = (grad * (1.0 / TILE)).astype(BF)
-
-    @pl.when(pl.program_id(0) > 0)
-    def _():
-        count = first_ref.shape[1]
-        grad = lax.dot_general(
-            first_ref[0], errors_ref[:count], over_rows, preferred_element_type=F32
-        ) + lax.dot_general(
-            second_ref[0], errors_ref[count:], over_rows, preferred_element_type=F32
-        )
-        out_ref[0] = (grad * (1.0 / TILE)).astype(BF)
-
-
-def dec_gradient(layer, codes, first, second, weight, parts):
-    layers = first.shape[0] + 1
-    feats, width = weight.shape
-    count = codes.shape[0]
-    other = lambda k, at: (lax.max(k - 1, 0), 0, 0)
+
+    codes = jnp.concatenate([first_ref[...], second_ref[...]])
+    grad = lax.dot_general(
+        codes, errors_ref[...], (((0,), (0,)), ((), ())), preferred_element_type=F32
+    )
+    out_ref[0] = (grad * (1.0 / TILE)).astype(BF)
+
+
+def dec_gradient(layer, layers, first, second, weight, parts):
+    depth, width = weight.shape
+    feats = depth // layers
+    count = first.shape[0] + second.shape[0]
     whole = lambda array: pl.BlockSpec(array.shape, lambda k, at: (0,) * array.ndim)
     return pl.pallas_call(
         dec_gradient_kernel,
@@ -216,10 +207,9 @@
             num_scalar_prefetch=1,
             grid=(layers,),
             in_specs=[
-                whole(codes),
-                pl.BlockSpec((1, *first.shape[1:]), other),
-                pl.BlockSpec((1, *second.shape[1:]), other),
-                whole(weight),
+                pl.BlockSpec((first.shape[0], feats), lambda k, at: (0, k)),
+                pl.BlockSpec((second.shape[0], feats), lambda k, at: (0, k)),
+                pl.BlockSpec((feats, width), lambda k, at: (0, 0)),
                 *[whole(part) for part in parts],
             ],
             out_specs=[
@@ -237,7 +227,7 @@
         compiler_params=params(20),
         cost_estimate=SMALL,
         name="dec_gradient",
-    )(layer.reshape(1), codes, first, second, weight, *parts)
+    )(layer.reshape(1), first, second, weight, *parts)
 
 
 def add_squares(parts, out_ref, start):
@@ -254,25 +244,25 @@
             start += 1
 
 
-def back_kernel(layers, place_ref, source_ref, *refs):
-    weights, refs = refs[: layers - 1], refs[layers - 1 :]
+def back_kernel(layers, place_ref, source_ref, weight_ref, *refs):
+    feats = weight_ref.shape[0] // layers
     away, errors_ref, back_ref, sums_ref = refs[-layers - 2 : -3], refs[-3], refs[-2], refs[-1]
     parts = refs[: -layers - 2]
     join(parts, errors_ref)
     packed = CAP * TILE
-    for k in range(1, layers):
-        back_ref[k - 1] = lax.dot_general(
+    for at, k in enumerate(ORDER):
+        back_ref[at] = lax.dot_general(
             errors_ref[...],
-            weights[k - 1][...],
+            weight_ref[k * feats : (k + 1) * feats, :],
             (((1,), (1,)), ((), ())),
             preferred_element_type=F32,
         ).astype(BF)
-        pack(source_ref, k, back_ref.at[k - 1], away[k - 1])
+        pack(source_ref, k, back_ref.at[at], away[at])
     add_squares(parts, sums_ref, 0)
     total = jnp.zeros((8, 128), F32)
     for chip in range(Y * Z):
         total = total + sums_ref[place_ref[chip]]
-    left = jnp.broadcast_to(jnp.sum(total), (16, weights[0].shape[0]))
+    left = jnp.broadcast_to(jnp.sum(total), (16, feats))
     row = lax.broadcasted_iota(jnp.int32, left.shape, 0)
     split = jnp.zeros(left.shape, F32)
     for k in range(3):
@@ -283,13 +273,12 @@
         ref[packed:, :] = split.astype(BF)
 
 
-def back(place, source, weights, parts):
-    layers = len(weights) + 1
-    feats, width = weights[0].shape
+def back(place, source, layers, weight, parts):
+    feats, width = weight.shape[0] // layers, weight.shape[1]
     count = sum(part.shape[0] for part in parts)
     return pl.pallas_call(
         functools.partial(back_kernel, layers),
-        in_specs=specs(2, len(weights) + len(parts)),
+        in_specs=specs(2, 1 + len(parts)),
         out_shape=[jax.ShapeDtypeStruct((CAP * TILE + 16, feats), BF)] * (layers - 1),
         scratch_shapes=[
             pltpu.VMEM((count, width), BF),
@@ -299,46 +288,39 @@
         compiler_params=params(14),
         cost_estimate=SMALL,
         name="back",
-    )(place, source, *weights, *parts)
-
-
-def decode_kernel(half, slot_ref, token_ref, codes_ref, *refs):
+    )(place, source, weight, *parts)
+
+
+def decode_kernel(half, slot_ref, token_ref, codes_ref, weight_ref, *refs):
     del token_ref
-    layers = (len(refs) - 1) // 2
-    came, weights = refs[: layers - 1], refs[layers - 1 : 2 * layers - 1]
-    out_ref, sources_ref = refs[-2:]
-    count = out_ref.shape[0]
-    total = jnp.dot(
-        codes_ref[half * count : half * count + count, :],
-        weights[0][...],
-        preferred_element_type=F32,
-    )
+    came, (out_ref, sources_ref) = refs[:-2], refs[-2:]
+    count, feats = out_ref.shape[0], codes_ref.shape[1]
+    sources_ref[:, :feats] = codes_ref[half * count : half * count + count, :]
     shards_of = count // 16
-    for k in range(1, layers):
+    for k, ref in zip(ORDER, came):
         for shard in range(shards_of):
-            sources_ref[k - 1, shard * 16 : shard * 16 + 16, :] = unpacked(
-                slot_ref, k, half * shards_of + shard, came[k - 1]
+            sources_ref[shard * 16 : shard * 16 + 16, k * feats : (k + 1) * feats] = unpacked(
+                slot_ref, k, half * shards_of + shard, ref
             )
-        total = total + jnp.dot(
-            sources_ref[k - 1], weights[k][...], preferred_element_type=F32
-        )
-    out_ref[...] = total.astype(BF)
-
-
-def decode(half, slot, token, codes, came, weights):
-    count, feats = codes.shape[0] // 2, codes.shape[1]
-    width = weights[0].shape[1]
+    out_ref[...] = jnp.dot(
+        sources_ref[...], weight_ref[...], preferred_element_type=F32
+    ).astype(BF)
+
+
+def decode(half, slot, token, codes, came, weight):
+    count = codes.shape[0] // 2
+    depth, width = weight.shape
     return pl.pallas_call(
         functools.partial(decode_kernel, half),
-        in_specs=specs(1, 2 + len(came) + len(weights)),
+        in_specs=specs(1, 3 + len(came)),
         out_shape=[
             jax.ShapeDtypeStruct((count, width), BF),
-            jax.ShapeDtypeStruct((len(came), count, feats), BF),
+            jax.ShapeDtypeStruct((count, depth), BF),
         ],
         compiler_params=params(14),
         cost_estimate=SMALL,
         name="decode",
-    )(slot, token, codes, *came, *weights)
+    )(slot, token, codes, weight, *came)
 
 
 def enc_gradient_kernel(count, layer_ref, slot_ref, rows_ref, on_ref, own_ref, away_ref, *refs):
@@ -351,7 +333,7 @@
         pieces = []
         for shard in range(own_ref.shape[0] // 16):
             piece = own_ref[shard * 16 : shard * 16 + 16, :]
-            for k, ref in enumerate(came, 1):
+            for k, ref in zip(ORDER, came):
                 part = unpacked(slot_ref, 0, shard, ref).astype(F32)
                 piece = piece + jnp.where(layer_ref[0] + k < layers, part, 0.0)
             pieces.append(piece)
@@ -366,7 +348,7 @@
         loss = jnp.zeros_like(sums[0])
         for s in range(layers):
             for k in range(layers):
-                mine = lax.rem(layer_ref[0] + k, layers) == s
+                mine = lax.rem(layer_ref[0] + (0, *ORDER)[k], layers) == s
                 loss = loss + jnp.where(mine, sums[k], 0.0)
         loss_ref[...] = loss[:, :1] * (0.5 / count)
 
@@ -443,27 +425,29 @@
     place = jnp.sum(
         jnp.where(chips[None, :] == every[:, None], every[None, :], 0), axis=1, dtype=jnp.int32
     )
-    weights = [
-        lax.dynamic_index_in_dim(dec[:, 0], (layer - k) % layers, 0, keepdims=False)
-        for k in range(layers)
-    ]
+    decoder = jnp.concatenate(
+        [
+            lax.dynamic_index_in_dim(dec[:, 0], (layer - k) % layers, 0, keepdims=False)
+            for k in range(layers)
+        ]
+    )
     goal = chip_rows(target[0], core)
 
     packed, codes, on = encode(slot, source, enc_weight[0], enc_bias, rows)
-    came = [send_layer(packed, k) for k in range(1, layers)]
+    came = [send_layer(packed, k) for k in ORDER]
     turned, token = turn(rows, packed)
     goal, token = lax.optimization_barrier((goal, token))
     partial, sources = zip(
-        *[decode(half, slot, token, codes, came, weights) for half in range(2)]
+        *[decode(half, slot, token, codes, came, decoder) for half in range(2)]
     )
     errors = (collect(partial, core) - goal.astype(F32)).astype(BF)
     errors = spread_y(spread_z(errors, core))
-    away = back(place, source, weights[1:], errors)
+    away = back(place, source, layers, decoder, errors)
     came = []
-    for k in range(1, layers):
+    for k, message in zip(ORDER, away):
         ring = [(s, (s - k) % layers) for s in range(layers)]
-        came.append(lax.ppermute(away[k - 1], "layer", ring))
-    dec_grad, own = dec_gradient(layer, codes, *sources, weights[0], errors)
+        came.append(lax.ppermute(message, "layer", ring))
+    dec_grad, own = dec_gradient(layer, layers, *sources, decoder, errors)
     enc_grad, bias_grad, loss = enc_gradient(layer, slot, turned, on, own, away[0], came)
     loss = loss[0, 0]
     return (loss, enc_grad[None], bias_grad, dec_grad[:, None])

time: 135 us -> 128 us (0.948)
  starting transfers between devices: 66.7 us -> 62 us
  waiting for transfers between devices: 46.6 us -> 43.5 us
    ppermute x36, starting transfers between devices: 52.1 us -> 48.6 us  [send(): return lax.ppermute(value, 'latent', pairs(move, cores))]
    ppermute x36, waiting for transfers between devices: 38.7 us -> 35.4 us  [send(): return lax.ppermute(value, 'latent', pairs(move, cores))]
where the time goes in v5:
time: 128 us
  starting transfers between devices  62 us (48%)
  waiting for transfers between devices  43.5 us (34%)
  Pallas kernels  15 us (12%)
  other arithmetic  3.91 us (3%)
  local copies, waits for them, and re-layouts  2.36 us (2%)
    ppermute x36, starting transfers between devices, send(): return lax.ppermute(value, 'latent', pairs(move, cores))  48.6 us
    ppermute x36, waiting for transfers between devices, send(): return lax.ppermute(value, 'latent', pairs(move, cores))  35.4 us
    ppermute x3, starting transfers between devices, send_layer(): return lax.ppermute(value, 'layer', [(s, s + steps) for s in sources])  8.19 us
    ppermute x3, starting transfers between devices, shards(): came.append(lax.ppermute(message, 'layer', ring))  5.22 us
    pallas_call x1, Pallas kernels, dec_gradient(): pl.pallas_call(dec_gradient_kernel, grid_spec=pltpu.PrefetchScalarGridSpe...  4.77 us
    ppermute x3, waiting for transfers between devices, send_layer(): return lax.ppermute(value, 'layer', [(s, s + steps) for s in sources])  4.58 us
    ppermute x3, waiting for transfers between devices, shards(): came.append(lax.ppermute(message, 'layer', ring))  3.58 us
    pallas_call x2, Pallas kernels, decode(): pl.pallas_call(functools.partial(decode_kernel, half), in_specs=specs(1,...  3.4 us
  transfers between devices with their start and end apart: 42, of which 23 were waited for; matrix products, arithmetic and copies ran while one was open for 4% of the time, Pallas kernels for 6%

profile of v5, /device:TPU:1, one launch (start us, length us, event | category | flops | bytes accessed | tf_op | source)
XLA Modules:
  0.0 127.8 jit_solution(10705474909296719057)
XLA Ops:
  0.6 3.3 %collective-permute-start = (bf16[8,1792]{1,0:T(8,128)(2,1)}, bf16[8,1792]{1,0:T(8,128)(2,1)S(1)}, u32[]{:S(2)}, u32[]{:S(2)}) collective-permute-start(bf16[8,1792]{1,0:T(8,128)(2,1)} %bitcast.18), channel_id=1, source_target_pairs={{0,1},{1,0},{2,3},{3,2},{4,5},{5,4},{6,7},{7,6},{8,9},{9,8},{10,11... | collective-permute-start | bytes 86024 | tf_op jit(solution)/shard_map/ppermute | solution.py:34
  4.1 0.9 collective-permute-done
  5.0 0.8 maximum_select_fusion
  5.9 7.1 %collective-permute-start.1 = (bf16[16,1792]{1,0:T(8,128)(2,1)S(1)}, bf16[16,1792]{1,0:T(8,128)(2,1)S(1)}, u32[]{:S(2)}, u32[]{:S(2)}) collective-permute-start(bf16[16,1792]{1,0:T(8,128)(2,1)S(1)} %maximum_select_fusion), channel_id=1, source_target_pairs={{1,9},{3,11},{5,13},{7,15},{9,1},{11,3},{13,5},{15,7},{17,25},{19,... | collective-permute-start | bytes 172040 | tf_op jit(solution)/shard_map/ppermute | solution.py:34
  13.1 4.0 %collective-permute-start.3 = (bf16[16,1792]{1,0:T(8,128)(2,1)S(1)}, bf16[16,1792]{1,0:T(8,128)(2,1)S(1)}, u32[]{:S(2)}, u32[]{:S(2)}) collective-permute-start(bf16[16,1792]{1,0:T(8,128)(2,1)S(1)} %maximum_select_fusion), channel_id=1, source_target_pairs={{0,4},{1,13},{2,6},{3,15},{4,0},{5,9},{6,2},{7,11},{8,12},{9,5},{1... | collective-permute-start | bytes 172040 | tf_op jit(solution)/shard_map/ppermute | solution.py:34
  17.5 0.8 broadcast_select_fusion.1
  18.4 0.9 collective-permute-done.3
  19.3 4.1 %collective-permute-done.2 = bf16[16,1792]{1,0:T(8,128)(2,1)S(1)} collective-permute-done((bf16[16,1792]{1,0:T(8,128)(2,1)S(1)}, bf16[16,1792]{1,0:T(8,128)(2,1)S(1)}, u32[]{:S(2)}, u32[]{:S(2)}) %collective-permute-start.2) | collective-permute-done | bytes 57376 | tf_op jit(solution)/shard_map/ppermute | solution.py:34
  23.4 3.0 %collective-permute-start.5 = (bf16[64,1792]{1,0:T(8,128)(2,1)S(1)}, bf16[64,1792]{1,0:T(8,128)(2,1)S(1)}, u32[]{:S(2)}, u32[]{:S(2)}) collective-permute-start(bf16[64,1792]{1,0:T(8,128)(2,1)S(1)} %pad_maximum_fusion.1.refs_0_), channel_id=1, source_target_pairs={{0,32},{1,33},{2,34},{3,35},{4,36},{5,37},{6,38},{7,39},{8,40},{9,... | collective-permute-start | bytes 688136 | tf_op jit(solution)/shard_map/ppermute | solution.py:34
  27.1 0.9 compare_reduce_fusion
  28.6 2.3 %dynamic-slice_bitcast_fusion.3 = (bf16[256,1792]{1,0:T(8,128)(2,1)S(1)}, bf16[256,1792]{1,0:T(8,128)(2,1)S(1)}, bf16[256,1792]{1,0:T(8,128)(2,1)S(1)}, bf16[256,1792]{1,0:T(8,128)(2,1)S(1)}) fusion(bf16[4,1,256,1792]{3,2,1,0:T(8,128)(2,1)} %param.10, s32[]{:T(128)S(6)} %select_n.226, s32[]{:T(128)S(6)} %select_n.232, s32[]{:T(128)S(6)} %select_n.230, ...), kind=kLoop, calls=%fused_computation.4 | loop fusion | bytes 7340048 | tf_op jit(solution)/shard_map/jit(dynamic_index_in_dim)/squeeze | solution.py:430
  31.7 1.0 collective-permute-done.6.refs_2_
  33.3 0.8 collective-permute-done.10.refs_6_
  34.5 1.3 encode.1
  35.7 4.7 %collective-permute-start.13 = (bf16[384,256]{1,0:T(8,128)(2,1)S(1)}, bf16[384,256]{1,0:T(8,128)(2,1)S(1)}, u32[]{:S(2)}, u32[]{:S(2)}) collective-permute-start(bf16[384,256]{1,0:T(8,128)(2,1)S(1)} %get-tuple-element.29.after_ref), channel_id=1, source_target_pairs={{0,128},{64,192},{1,129},{65,193},{2,130},{66,194},{3,131},{67,195... | collective-permute-start | bytes 589832 | tf_op jit(solution)/shard_map/ppermute | solution.py:44
  40.4 2.2 %collective-permute-start.14 = (bf16[384,256]{1,0:T(8,128)(2,1)S(1)}, bf16[384,256]{1,0:T(8,128)(2,1)S(1)}, u32[]{:S(2)}, u32[]{:S(2)}) collective-permute-start(bf16[384,256]{1,0:T(8,128)(2,1)S(1)} %get-tuple-element.29.after_ref), channel_id=1, source_target_pairs={{0,64},{64,128},{128,192},{1,65},{65,129},{129,193},{2,66},{66,130... | collective-permute-start | bytes 589832 | tf_op jit(solution)/shard_map/ppermute | solution.py:44
  42.6 1.3 %collective-permute-start.15 = (bf16[384,256]{1,0:T(8,128)(2,1)S(1)}, bf16[384,256]{1,0:T(8,128)(2,1)S(1)}, u32[]{:S(2)}, u32[]{:S(2)}) collective-permute-start(bf16[384,256]{1,0:T(8,128)(2,1)S(1)} %get-tuple-element.29.after_ref), channel_id=1, source_target_pairs={{0,192},{1,193},{2,194},{3,195},{4,196},{5,197},{6,198},{7,199},{8... | collective-permute-start | bytes 589832 | tf_op jit(solution)/shard_map/ppermute | solution.py:44
  44.5 4.2 %collective-permute-done.14.refs_1_ = bf16[384,256]{1,0:T(8,128)(2,1)S(1)} collective-permute-done((bf16[384,256]{1,0:T(8,128)(2,1)S(1)}, bf16[384,256]{1,0:T(8,128)(2,1)S(1)}, u32[]{:S(2)}, u32[]{:S(2)}) %collective-permute-start.14) | collective-permute-done | bytes 196640 | tf_op jit(solution)/shard_map/ppermute | solution.py:44
  49.1 1.7 %decode.3 = (bf16[256,1792]{1,0:T(8,128)(2,1)S(1)}, bf16[256,1024]{1,0:T(8,128)(2,1)S(1)}) custom-call(s32[4,32]{1,0:T(4,128)S(1)} %minimum_select_fusion.slot_ref, bf16[16,128]{1,0:T(8,128)(2,1)S(1)} %get-tuple-element.34.token_ref, bf16[512,256]{1,0:T(8,128)(2,1)S(1)} %get-tuple-element.35.codes_ref, bf16[1024,1792]{1,0:T(8,128)(2,1)S(1)} %pad_maximum_fusion.weight_ref, ...), custom_call_target="tpu_custom_call" | custom-call | flops 1000 | bytes 1000 | tf_op jit(solution)/shard_map/decode/pallas_call | solution.py:313
  50.9 0.7 collective-permute-start.17
  52.2 1.7 %decode.2 = (bf16[256,1792]{1,0:T(8,128)(2,1)S(1)}, bf16[256,1024]{1,0:T(8,128)(2,1)S(1)}) custom-call(s32[4,32]{1,0:T(4,128)S(1)} %minimum_select_fusion.slot_ref, bf16[16,128]{1,0:T(8,128)(2,1)S(1)} %get-tuple-element.34.token_ref, bf16[512,256]{1,0:T(8,128)(2,1)S(1)} %get-tuple-element.35.codes_ref, bf16[1024,1792]{1,0:T(8,128)(2,1)S(1)} %pad_maximum_fusion.weight_ref, ...), custom_call_target="tpu_custom_call" | custom-call | flops 1000 | bytes 1000 | tf_op jit(solution)/shard_map/decode/pallas_call | solution.py:313
  54.1 2.1 %collective-permute-start.22 = (bf16[64,1792]{1,0:T(8,128)(2,1)S(1)}, bf16[64,1792]{1,0:T(8,128)(2,1)S(1)}, u32[]{:S(2)}, u32[]{:S(2)}) collective-permute-start(bf16[64,1792]{1,0:T(8,128)(2,1)S(1)} %get-tuple-element.69), channel_id=1, source_target_pairs={{0,48},{1,49},{2,50},{3,51},{4,52},{5,53},{6,54},{7,55},{8,56},{9,... | collective-permute-start | bytes 688136 | tf_op jit(solution)/shard_map/ppermute | solution.py:34
  56.3 1.8 %collective-permute-start.18 = (bf16[64,1792]{1,0:T(8,128)(2,1)S(1)}, bf16[64,1792]{1,0:T(8,128)(2,1)S(1)}, u32[]{:S(2)}, u32[]{:S(2)}) collective-permute-start(bf16[64,1792]{1,0:T(8,128)(2,1)S(1)} %get-tuple-element.68), channel_id=1, source_target_pairs={{0,32},{1,33},{2,34},{3,35},{4,36},{5,37},{6,38},{7,39},{8,40},{9,... | collective-permute-start | bytes 688136 | tf_op jit(solution)/shard_map/ppermute | solution.py:34
  58.1 4.1 %collective-permute-done.22 = bf16[64,1792]{1,0:T(8,128)(2,1)S(1)} collective-permute-done((bf16[64,1792]{1,0:T(8,128)(2,1)S(1)}, bf16[64,1792]{1,0:T(8,128)(2,1)S(1)}, u32[]{:S(2)}, u32[]{:S(2)}) %collective-permute-start.22) | collective-permute-done | bytes 229408 | tf_op jit(solution)/shard_map/ppermute | solution.py:34
  62.7 5.3 %collective-permute-done.18 = bf16[64,1792]{1,0:T(8,128)(2,1)S(1)} collective-permute-done((bf16[64,1792]{1,0:T(8,128)(2,1)S(1)}, bf16[64,1792]{1,0:T(8,128)(2,1)S(1)}, u32[]{:S(2)}, u32[]{:S(2)}) %collective-permute-start.18) | collective-permute-done | bytes 229408 | tf_op jit(solution)/shard_map/ppermute | solution.py:34
  68.8 2.4 %collective-permute-start.25 = (bf16[16,1792]{1,0:T(8,128)(2,1)S(1)}, bf16[16,1792]{1,0:T(8,128)(2,1)S(1)}, u32[]{:S(2)}, u32[]{:S(2)}) collective-permute-start(bf16[16,1792]{1,0:T(8,128)(2,1)S(1)} %get-tuple-element.73), channel_id=1, source_target_pairs={{0,4},{1,13},{2,6},{3,15},{4,0},{5,9},{6,2},{7,11},{8,12},{9,5},{1... | collective-permute-start | bytes 172040 | tf_op jit(solution)/shard_map/ppermute | solution.py:34
  71.2 2.0 %collective-permute-start.24 = (bf16[16,1792]{1,0:T(8,128)(2,1)S(1)}, bf16[16,1792]{1,0:T(8,128)(2,1)S(1)}, u32[]{:S(2)}, u32[]{:S(2)}) collective-permute-start(bf16[16,1792]{1,0:T(8,128)(2,1)S(1)} %get-tuple-element.74), channel_id=1, source_target_pairs={{0,2},{1,11},{2,0},{3,9},{4,6},{5,15},{6,4},{7,13},{8,10},{9,3},{1... | collective-permute-start | bytes 172040 | tf_op jit(solution)/shard_map/ppermute | solution.py:34
  73.2 5.0 %collective-permute-start.23 = (bf16[16,1792]{1,0:T(8,128)(2,1)S(1)}, bf16[16,1792]{1,0:T(8,128)(2,1)S(1)}, u32[]{:S(2)}, u32[]{:S(2)}) collective-permute-start(bf16[16,1792]{1,0:T(8,128)(2,1)S(1)} %get-tuple-element.71), channel_id=1, source_target_pairs={{1,9},{3,11},{5,13},{7,15},{9,1},{11,3},{13,5},{15,7},{17,25},{19,... | collective-permute-start | bytes 172040 | tf_op jit(solution)/shard_map/ppermute | solution.py:34
  78.6 3.4 %collective-permute-done.23 = bf16[16,1792]{1,0:T(8,128)(2,1)S(1)} collective-permute-done((bf16[16,1792]{1,0:T(8,128)(2,1)S(1)}, bf16[16,1792]{1,0:T(8,128)(2,1)S(1)}, u32[]{:S(2)}, u32[]{:S(2)}) %collective-permute-start.23) | collective-permute-done | bytes 57376 | tf_op jit(solution)/shard_map/ppermute | solution.py:34
  82.1 1.2 collective-permute-done.27
  83.4 5.1 %collective-permute-start.28 = (bf16[16,1792]{1,0:T(8,128)(2,1)S(1)}, bf16[16,1792]{1,0:T(8,128)(2,1)S(1)}, u32[]{:S(2)}, u32[]{:S(2)}) collective-permute-start(bf16[16,1792]{1,0:T(8,128)(2,1)S(1)} %subtract_convert_fusion), channel_id=1, source_target_pairs={{1,9},{3,11},{5,13},{7,15},{9,1},{11,3},{13,5},{15,7},{17,25},{19,... | collective-permute-start | bytes 172040 | tf_op jit(solution)/shard_map/ppermute | solution.py:34
  89.1 3.3 %collective-permute-start.30 = (bf16[16,1792]{1,0:T(8,128)(2,1)S(1)}, bf16[16,1792]{1,0:T(8,128)(2,1)S(1)}, u32[]{:S(2)}, u32[]{:S(2)}) collective-permute-start(bf16[16,1792]{1,0:T(8,128)(2,1)S(1)} %subtract_convert_fusion), channel_id=1, source_target_pairs={{0,4},{1,13},{2,6},{3,15},{4,0},{5,9},{6,2},{7,11},{8,12},{9,5},{1... | collective-permute-start | bytes 172040 | tf_op jit(solution)/shard_map/ppermute | solution.py:34
  92.3 1.1 collective-permute-start.29
  93.5 1.4 %collective-permute-done.31 = bf16[16,1792]{1,0:T(8,128)(2,1)S(1)} collective-permute-done((bf16[16,1792]{1,0:T(8,128)(2,1)S(1)}, bf16[16,1792]{1,0:T(8,128)(2,1)S(1)}, u32[]{:S(2)}, u32[]{:S(2)}) %collective-permute-start.31) | collective-permute-done | bytes 57376 | tf_op jit(solution)/shard_map/ppermute | solution.py:34
  94.9 3.5 %collective-permute-done.29 = bf16[16,1792]{1,0:T(8,128)(2,1)S(1)} collective-permute-done((bf16[16,1792]{1,0:T(8,128)(2,1)S(1)}, bf16[16,1792]{1,0:T(8,128)(2,1)S(1)}, u32[]{:S(2)}, u32[]{:S(2)}) %collective-permute-start.29) | collective-permute-done | bytes 57376 | tf_op jit(solution)/shard_map/ppermute | solution.py:34
  98.4 1.4 %collective-permute-start.32 = (bf16[64,1792]{1,0:T(8,128)(2,1)S(1)}, bf16[64,1792]{1,0:T(8,128)(2,1)S(1)}, u32[]{:S(2)}, u32[]{:S(2)}) collective-permute-start(bf16[64,1792]{1,0:T(8,128)(2,1)S(1)} %pad_maximum_fusion.2.refs_0_), channel_id=1, source_target_pairs={{0,32},{1,33},{2,34},{3,35},{4,36},{5,37},{6,38},{7,39},{8,40},{9,... | collective-permute-start | bytes 688136 | tf_op jit(solution)/shard_map/ppermute | solution.py:34
  99.8 1.3 %collective-permute-start.33 = (bf16[64,1792]{1,0:T(8,128)(2,1)S(1)}, bf16[64,1792]{1,0:T(8,128)(2,1)S(1)}, u32[]{:S(2)}, u32[]{:S(2)}) collective-permute-start(bf16[64,1792]{1,0:T(8,128)(2,1)S(1)} %pad_maximum_fusion.2.refs_0_), channel_id=1, source_target_pairs={{0,16},{1,17},{2,18},{3,19},{4,20},{5,21},{6,22},{7,23},{8,24},{9,... | collective-permute-start | bytes 688136 | tf_op jit(solution)/shard_map/ppermute | solution.py:34
  101.1 0.6 collective-permute-start.34
  101.7 3.3 %collective-permute-done.32.refs_1_ = bf16[64,1792]{1,0:T(8,128)(2,1)S(1)} collective-permute-done((bf16[64,1792]{1,0:T(8,128)(2,1)S(1)}, bf16[64,1792]{1,0:T(8,128)(2,1)S(1)}, u32[]{:S(2)}, u32[]{:S(2)}) %collective-permute-start.32) | collective-permute-done | bytes 229408 | tf_op jit(solution)/shard_map/ppermute | solution.py:34
  105.0 2.0 %collective-permute-done.33.refs_2_ = bf16[64,1792]{1,0:T(8,128)(2,1)S(1)} collective-permute-done((bf16[64,1792]{1,0:T(8,128)(2,1)S(1)}, bf16[64,1792]{1,0:T(8,128)(2,1)S(1)}, u32[]{:S(2)}, u32[]{:S(2)}) %collective-permute-start.33) | collective-permute-done | bytes 229408 | tf_op jit(solution)/shard_map/ppermute | solution.py:34
  107.0 0.8 collective-permute-done.34.refs_3_
  108.5 0.8 collective-permute-done.38.refs_7_
  109.2 2.5 %back.1 = (bf16[400,256]{1,0:T(8,128)(2,1)S(1)}, bf16[400,256]{1,0:T(8,128)(2,1)S(1)}, bf16[400,256]{1,0:T(8,128)(2,1)S(1)}) custom-call(s32[32]{0:T(128)S(1)} %select_reduce_fusion.2.place_ref, s32[4,24]{1,0:T(4,128)S(1)} %broadcast_minimum_fusion.source_ref, bf16[1024,1792]{1,0:T(8,128)(2,1)S(1)} %pad_maximum_fusion.weight_ref, ...), custom_call_target="tpu_custom_call" | custom-call | flops 1000 | bytes 1000 | tf_op jit(solution)/shard_map/back/pallas_call | solution.py:279
  111.7 3.8 %collective-permute-start.39 = (bf16[400,256]{1,0:T(8,128)(2,1)S(1)}, bf16[400,256]{1,0:T(8,128)(2,1)S(1)}, u32[]{:S(2)}, u32[]{:S(2)}) collective-permute-start(bf16[400,256]{1,0:T(8,128)(2,1)S(1)} %get-tuple-element.43.away_ref), channel_id=1, source_target_pairs={{0,128},{64,192},{128,0},{192,64},{1,129},{65,193},{129,1},{193,65... | collective-permute-start | bytes 614408 | tf_op jit(solution)/shard_map/ppermute | solution.py:449
  115.5 0.9 collective-permute-start.40
  116.9 4.8 %dec_gradient.1 = (bf16[4,256,1792]{2,1,0:T(8,128)(2,1)}, f32[512,256]{1,0:T(8,128)S(1)}) custom-call(s32[1]{0:T(128)} %bitcast.layer_ref, bf16[256,1024]{1,0:T(8,128)(2,1)S(1)} %get-tuple-element.37.first_ref, bf16[256,1024]{1,0:T(8,128)(2,1)S(1)} %get-tuple-element.38.second_ref, bf16[1024,1792]{1,0:T(8,128)(2,1)S(1)} %pad_maximum_fusion.weight_ref, ...), custom_call_target="tpu_custom_call" | custom-call | flops 1000 | bytes 1000 | tf_op jit(solution)/shard_map/dec_gradient/pallas_call | solution.py:204
  121.7 3.6 %collective-permute-done.40.refs_1_ = bf16[400,256]{1,0:T(8,128)(2,1)S(1)} collective-permute-done((bf16[400,256]{1,0:T(8,128)(2,1)S(1)}, bf16[400,256]{1,0:T(8,128)(2,1)S(1)}, u32[]{:S(2)}, u32[]{:S(2)}) %collective-permute-start.40) | collective-permute-done | bytes 204832 | tf_op jit(solution)/shard_map/ppermute | solution.py:449
  125.3 2.5 %enc_gradient.1 = (bf16[1792,256]{1,0:T(8,128)(2,1)}, f32[1,256]{1,0:T(1,128)}, f32[1,1]{1,0:T(1,128)}) custom-call(s32[1]{0:T(128)} %bitcast.layer_ref, s32[4,32]{1,0:T(4,128)S(1)} %minimum_select_fusion.slot_ref, bf16[1792,512]{1,0:T(8,128)(2,1)S(1)} %get-tuple-element.30.rows_ref, bf16[512,256]{1,0:T(8,128)(2,1)S(1)} %get-tuple-element.31.on_ref, ...), custom_call_target="tpu_custom_call" | custom-call | flops 1000 | bytes 1000 | tf_op jit(solution)/shard_map/enc_gradient/pallas_call | solution.py:364
  (75 shorter events, 9.2 us)
Async XLA Ops:
  0.6 4.4 %collective-permute-start = (bf16[8,1792]{1,0:T(8,128)(2,1)}, bf16[8,1792]{1,0:T(8,128)(2,1)S(1)}, u32[]{:S(2)}, u32[]{:S(2)}) collective-permute-start(bf16[8,1792]{1,0:T(8,128)(2,1)} %bitcast.18), channel_id=1, source_target_pairs={{0,1},{1,0},{2,3},{3,2},{4,5},{5,4},{6,7},{7,6},{8,9},{9,8},{10,11... | collective-permute-start | bytes 86024 | tf_op jit(solution)/shard_map/ppermute | solution.py:34
  5.9 11.7 %collective-permute-start.1 = (bf16[16,1792]{1,0:T(8,128)(2,1)S(1)}, bf16[16,1792]{1,0:T(8,128)(2,1)S(1)}, u32[]{:S(2)}, u32[]{:S(2)}) collective-permute-start(bf16[16,1792]{1,0:T(8,128)(2,1)S(1)} %maximum_select_fusion), channel_id=1, source_target_pairs={{1,9},{3,11},{5,13},{7,15},{9,1},{11,3},{13,5},{15,7},{17,25},{19,... | collective-permute-start | bytes 172040 | tf_op jit(solution)/shard_map/ppermute | solution.py:34
  13.0 5.4 %collective-permute-start.4 = (bf16[16,1792]{1,0:T(8,128)(2,1)S(1)}, bf16[16,1792]{1,0:T(8,128)(2,1)S(1)}, u32[]{:S(2)}, u32[]{:S(2)}) collective-permute-start(bf16[16,1792]{1,0:T(8,128)(2,1)S(1)} %maximum_select_fusion), channel_id=1, source_target_pairs={{0,6},{1,15},{2,4},{3,13},{4,2},{5,11},{6,0},{7,9},{8,14},{9,7},{1... | collective-permute-start | bytes 172040 | tf_op jit(solution)/shard_map/ppermute | solution.py:34
  13.1 6.2 %collective-permute-start.3 = (bf16[16,1792]{1,0:T(8,128)(2,1)S(1)}, bf16[16,1792]{1,0:T(8,128)(2,1)S(1)}, u32[]{:S(2)}, u32[]{:S(2)}) collective-permute-start(bf16[16,1792]{1,0:T(8,128)(2,1)S(1)} %maximum_select_fusion), channel_id=1, source_target_pairs={{0,4},{1,13},{2,6},{3,15},{4,0},{5,9},{6,2},{7,11},{8,12},{9,5},{1... | collective-permute-start | bytes 172040 | tf_op jit(solution)/shard_map/ppermute | solution.py:34
  17.1 6.3 %collective-permute-start.2 = (bf16[16,1792]{1,0:T(8,128)(2,1)S(1)}, bf16[16,1792]{1,0:T(8,128)(2,1)S(1)}, u32[]{:S(2)}, u32[]{:S(2)}) collective-permute-start(bf16[16,1792]{1,0:T(8,128)(2,1)S(1)} %maximum_select_fusion), channel_id=1, source_target_pairs={{0,2},{1,11},{2,0},{3,9},{4,6},{5,15},{6,4},{7,13},{8,10},{9,3},{1... | collective-permute-start | bytes 172040 | tf_op jit(solution)/shard_map/ppermute | solution.py:34
  23.4 8.2 %collective-permute-start.5 = (bf16[64,1792]{1,0:T(8,128)(2,1)S(1)}, bf16[64,1792]{1,0:T(8,128)(2,1)S(1)}, u32[]{:S(2)}, u32[]{:S(2)}) collective-permute-start(bf16[64,1792]{1,0:T(8,128)(2,1)S(1)} %pad_maximum_fusion.1.refs_0_), channel_id=1, source_target_pairs={{0,32},{1,33},{2,34},{3,35},{4,36},{5,37},{6,38},{7,39},{8,40},{9,... | collective-permute-start | bytes 688136 | tf_op jit(solution)/shard_map/ppermute | solution.py:34
  26.4 6.3 %collective-permute-start.6 = (bf16[64,1792]{1,0:T(8,128)(2,1)S(1)}, bf16[64,1792]{1,0:T(8,128)(2,1)S(1)}, u32[]{:S(2)}, u32[]{:S(2)}) collective-permute-start(bf16[64,1792]{1,0:T(8,128)(2,1)S(1)} %pad_maximum_fusion.1.refs_0_), channel_id=1, source_target_pairs={{0,16},{1,17},{2,18},{3,19},{4,20},{5,21},{6,22},{7,23},{8,24},{9,... | collective-permute-start | bytes 688136 | tf_op jit(solution)/shard_map/ppermute | solution.py:34
  26.8 6.1 %collective-permute-start.7 = (bf16[64,1792]{1,0:T(8,128)(2,1)S(1)}, bf16[64,1792]{1,0:T(8,128)(2,1)S(1)}, u32[]{:S(2)}, u32[]{:S(2)}) collective-permute-start(bf16[64,1792]{1,0:T(8,128)(2,1)S(1)} %pad_maximum_fusion.1.refs_0_), channel_id=1, source_target_pairs={{0,48},{1,49},{2,50},{3,51},{4,52},{5,53},{6,54},{7,55},{8,56},{9,... | collective-permute-start | bytes 688136 | tf_op jit(solution)/shard_map/ppermute | solution.py:34
  27.1 6.2 %collective-permute-start.8 = (bf16[64,1792]{1,0:T(8,128)(2,1)S(1)}, bf16[64,1792]{1,0:T(8,128)(2,1)S(1)}, u32[]{:S(2)}, u32[]{:S(2)}) collective-permute-start(bf16[64,1792]{1,0:T(8,128)(2,1)S(1)} %pad_maximum_fusion.1.refs_0_), channel_id=1, source_target_pairs={{0,1},{1,0},{2,3},{3,2},{4,5},{5,4},{6,7},{7,6},{8,9},{9,8},{10,11... | collective-permute-start | bytes 688136 | tf_op jit(solution)/shard_map/ppermute | solution.py:34
  28.0 15.9 %collective-permute-start.12 = (bf16[8,1792]{1,0:T(8,128)(2,1)}, bf16[8,1792]{1,0:T(8,128)(2,1)S(1)}, u32[]{:S(2)}, u32[]{:S(2)}) collective-permute-start(bf16[8,1792]{1,0:T(8,128)(2,1)} %bitcast.21), channel_id=1, source_target_pairs={{0,1},{1,0},{2,3},{3,2},{4,5},{5,4},{6,7},{7,6},{8,9},{9,8},{10,11... | collective-permute-start | bytes 86024 | tf_op jit(solution)/shard_map/ppermute | solution.py:34
  31.0 3.5 %copy-start = (bf16[1,1792,256]{2,1,0:T(8,128)(2,1)S(1)}, bf16[1,1792,256]{2,1,0:T(8,128)(2,1)}, u32[]{:S(2)}) copy-start(bf16[1,1792,256]{2,1,0:T(8,128)(2,1)} %param.8) | copy-start | bytes 2752516
  31.0 3.5 %copy-start.1 = (f32[1,256]{1,0:T(1,128)S(1)}, f32[1,256]{1,0:T(1,128)}, u32[]{:S(2)}) copy-start(f32[1,256]{1,0:T(1,128)} %bias_ref.1) | copy-start | bytes 3076
  31.0 13.0 %copy-start.2 = (bf16[1,8,1792]{2,1,0:T(8,128)(2,1)S(1)}, bf16[1,8,1792]{2,1,0:T(8,128)(2,1)}, u32[]{:S(2)}) copy-start(bf16[1,8,1792]{2,1,0:T(8,128)(2,1)} %param.7) | copy-start | bytes 86020
  31.5 1.8 %collective-permute-start.9 = (bf16[64,1792]{1,0:T(8,128)(2,1)S(1)}, bf16[64,1792]{1,0:T(8,128)(2,1)S(1)}, u32[]{:S(2)}, u32[]{:S(2)}) collective-permute-start(bf16[64,1792]{1,0:T(8,128)(2,1)S(1)} %collective-permute-done.5.refs_1_), channel_id=1, source_target_pairs={{0,1},{1,0},{2,3},{3,2},{4,5},{5,4},{6,7},{7,6},{8,9},{9,8},{10,11... | collective-permute-start | bytes 688136 | tf_op jit(solution)/shard_map/ppermute | solution.py:34
  32.7 1.5 %collective-permute-start.10 = (bf16[64,1792]{1,0:T(8,128)(2,1)S(1)}, bf16[64,1792]{1,0:T(8,128)(2,1)S(1)}, u32[]{:S(2)}, u32[]{:S(2)}) collective-permute-start(bf16[64,1792]{1,0:T(8,128)(2,1)S(1)} %collective-permute-done.6.refs_2_), channel_id=1, source_target_pairs={{0,1},{1,0},{2,3},{3,2},{4,5},{5,4},{6,7},{7,6},{8,9},{9,8},{10,11... | collective-permute-start | bytes 688136 | tf_op jit(solution)/shard_map/ppermute | solution.py:34
  32.8 1.6 %collective-permute-start.11 = (bf16[64,1792]{1,0:T(8,128)(2,1)S(1)}, bf16[64,1792]{1,0:T(8,128)(2,1)S(1)}, u32[]{:S(2)}, u32[]{:S(2)}) collective-permute-start(bf16[64,1792]{1,0:T(8,128)(2,1)S(1)} %collective-permute-done.7.refs_3_), channel_id=1, source_target_pairs={{0,1},{1,0},{2,3},{3,2},{4,5},{5,4},{6,7},{7,6},{8,9},{9,8},{10,11... | collective-permute-start | bytes 688136 | tf_op jit(solution)/shard_map/ppermute | solution.py:34
  35.7 8.8 %collective-permute-start.13 = (bf16[384,256]{1,0:T(8,128)(2,1)S(1)}, bf16[384,256]{1,0:T(8,128)(2,1)S(1)}, u32[]{:S(2)}, u32[]{:S(2)}) collective-permute-start(bf16[384,256]{1,0:T(8,128)(2,1)S(1)} %get-tuple-element.29.after_ref), channel_id=1, source_target_pairs={{0,128},{64,192},{1,129},{65,193},{2,130},{66,194},{3,131},{67,195... | collective-permute-start | bytes 589832 | tf_op jit(solution)/shard_map/ppermute | solution.py:44
  40.4 8.4 %collective-permute-start.14 = (bf16[384,256]{1,0:T(8,128)(2,1)S(1)}, bf16[384,256]{1,0:T(8,128)(2,1)S(1)}, u32[]{:S(2)}, u32[]{:S(2)}) collective-permute-start(bf16[384,256]{1,0:T(8,128)(2,1)S(1)} %get-tuple-element.29.after_ref), channel_id=1, source_target_pairs={{0,64},{64,128},{128,192},{1,65},{65,129},{129,193},{2,66},{66,130... | collective-permute-start | bytes 589832 | tf_op jit(solution)/shard_map/ppermute | solution.py:44
  42.6 6.5 %collective-permute-start.15 = (bf16[384,256]{1,0:T(8,128)(2,1)S(1)}, bf16[384,256]{1,0:T(8,128)(2,1)S(1)}, u32[]{:S(2)}, u32[]{:S(2)}) collective-permute-start(bf16[384,256]{1,0:T(8,128)(2,1)S(1)} %get-tuple-element.29.after_ref), channel_id=1, source_target_pairs={{0,192},{1,193},{2,194},{3,195},{4,196},{5,197},{6,198},{7,199},{8... | collective-permute-start | bytes 589832 | tf_op jit(solution)/shard_map/ppermute | solution.py:44
  50.9 3.1 %collective-permute-start.17 = (bf16[64,1792]{1,0:T(8,128)(2,1)S(1)}, bf16[64,1792]{1,0:T(8,128)(2,1)S(1)}, u32[]{:S(2)}, u32[]{:S(2)}) collective-permute-start(bf16[64,1792]{1,0:T(8,128)(2,1)S(1)} %get-tuple-element.67), channel_id=1, source_target_pairs={{0,1},{1,0},{2,3},{3,2},{4,5},{5,4},{6,7},{7,6},{8,9},{9,8},{10,11... | collective-permute-start | bytes 688136 | tf_op jit(solution)/shard_map/ppermute | solution.py:34
  51.6 2.3 %collective-permute-start.21 = (bf16[64,1792]{1,0:T(8,128)(2,1)S(1)}, bf16[64,1792]{1,0:T(8,128)(2,1)S(1)}, u32[]{:S(2)}, u32[]{:S(2)}) collective-permute-start(bf16[64,1792]{1,0:T(8,128)(2,1)S(1)} %get-tuple-element.65), channel_id=1, source_target_pairs={{0,1},{1,0},{2,3},{3,2},{4,5},{5,4},{6,7},{7,6},{8,9},{9,8},{10,11... | collective-permute-start | bytes 688136 | tf_op jit(solution)/shard_map/ppermute | solution.py:34
  51.7 2.2 %collective-permute-start.19 = (bf16[64,1792]{1,0:T(8,128)(2,1)S(1)}, bf16[64,1792]{1,0:T(8,128)(2,1)S(1)}, u32[]{:S(2)}, u32[]{:S(2)}) collective-permute-start(bf16[64,1792]{1,0:T(8,128)(2,1)S(1)} %get-tuple-element.66), channel_id=1, source_target_pairs={{0,1},{1,0},{2,3},{3,2},{4,5},{5,4},{6,7},{7,6},{8,9},{9,8},{10,11... | collective-permute-start | bytes 688136 | tf_op jit(solution)/shard_map/ppermute | solution.py:34
  52.1 6.0 %collective-permute-start.16 = (bf16[64,1792]{1,0:T(8,128)(2,1)S(1)}, bf16[64,1792]{1,0:T(8,128)(2,1)S(1)}, u32[]{:S(2)}, u32[]{:S(2)}) collective-permute-start(bf16[64,1792]{1,0:T(8,128)(2,1)S(1)} %get-tuple-element.64), channel_id=1, source_target_pairs={{0,1},{1,0},{2,3},{3,2},{4,5},{5,4},{6,7},{7,6},{8,9},{9,8},{10,11... | collective-permute-start | bytes 688136 | tf_op jit(solution)/shard_map/ppermute | solution.py:34
  54.1 8.1 %collective-permute-start.22 = (bf16[64,1792]{1,0:T(8,128)(2,1)S(1)}, bf16[64,1792]{1,0:T(8,128)(2,1)S(1)}, u32[]{:S(2)}, u32[]{:S(2)}) collective-permute-start(bf16[64,1792]{1,0:T(8,128)(2,1)S(1)} %get-tuple-element.69), channel_id=1, source_target_pairs={{0,48},{1,49},{2,50},{3,51},{4,52},{5,53},{6,54},{7,55},{8,56},{9,... | collective-permute-start | bytes 688136 | tf_op jit(solution)/shard_map/ppermute | solution.py:34
  56.3 6.5 %collective-permute-start.20 = (bf16[64,1792]{1,0:T(8,128)(2,1)S(1)}, bf16[64,1792]{1,0:T(8,128)(2,1)S(1)}, u32[]{:S(2)}, u32[]{:S(2)}) collective-permute-start(bf16[64,1792]{1,0:T(8,128)(2,1)S(1)} %get-tuple-element.70), channel_id=1, source_target_pairs={{0,16},{1,17},{2,18},{3,19},{4,20},{5,21},{6,22},{7,23},{8,24},{9,... | collective-permute-start | bytes 688136 | tf_op jit(solution)/shard_map/ppermute | solution.py:34
  56.3 11.7 %collective-permute-start.18 = (bf16[64,1792]{1,0:T(8,128)(2,1)S(1)}, bf16[64,1792]{1,0:T(8,128)(2,1)S(1)}, u32[]{:S(2)}, u32[]{:S(2)}) collective-permute-start(bf16[64,1792]{1,0:T(8,128)(2,1)S(1)} %get-tuple-element.68), channel_id=1, source_target_pairs={{0,32},{1,33},{2,34},{3,35},{4,36},{5,37},{6,38},{7,39},{8,40},{9,... | collective-permute-start | bytes 688136 | tf_op jit(solution)/shard_map/ppermute | solution.py:34
  68.2 10.0 %collective-permute-start.26 = (bf16[16,1792]{1,0:T(8,128)(2,1)S(1)}, bf16[16,1792]{1,0:T(8,128)(2,1)S(1)}, u32[]{:S(2)}, u32[]{:S(2)}) collective-permute-start(bf16[16,1792]{1,0:T(8,128)(2,1)S(1)} %get-tuple-element.72), channel_id=1, source_target_pairs={{0,6},{1,15},{2,4},{3,13},{4,2},{5,11},{6,0},{7,9},{8,14},{9,7},{1... | collective-permute-start | bytes 172040 | tf_op jit(solution)/shard_map/ppermute | solution.py:34
  68.8 9.4 %collective-permute-start.25 = (bf16[16,1792]{1,0:T(8,128)(2,1)S(1)}, bf16[16,1792]{1,0:T(8,128)(2,1)S(1)}, u32[]{:S(2)}, u32[]{:S(2)}) collective-permute-start(bf16[16,1792]{1,0:T(8,128)(2,1)S(1)} %get-tuple-element.73), channel_id=1, source_target_pairs={{0,4},{1,13},{2,6},{3,15},{4,0},{5,9},{6,2},{7,11},{8,12},{9,5},{1... | collective-permute-start | bytes 172040 | tf_op jit(solution)/shard_map/ppermute | solution.py:34
  71.2 7.4 %collective-permute-start.24 = (bf16[16,1792]{1,0:T(8,128)(2,1)S(1)}, bf16[16,1792]{1,0:T(8,128)(2,1)S(1)}, u32[]{:S(2)}, u32[]{:S(2)}) collective-permute-start(bf16[16,1792]{1,0:T(8,128)(2,1)S(1)} %get-tuple-element.74), channel_id=1, source_target_pairs={{0,2},{1,11},{2,0},{3,9},{4,6},{5,15},{6,4},{7,13},{8,10},{9,3},{1... | collective-permute-start | bytes 172040 | tf_op jit(solution)/shard_map/ppermute | solution.py:34
  73.2 8.8 %collective-permute-start.23 = (bf16[16,1792]{1,0:T(8,128)(2,1)S(1)}, bf16[16,1792]{1,0:T(8,128)(2,1)S(1)}, u32[]{:S(2)}, u32[]{:S(2)}) collective-permute-start(bf16[16,1792]{1,0:T(8,128)(2,1)S(1)} %get-tuple-element.71), channel_id=1, source_target_pairs={{1,9},{3,11},{5,13},{7,15},{9,1},{11,3},{13,5},{15,7},{17,25},{19,... | collective-permute-start | bytes 172040 | tf_op jit(solution)/shard_map/ppermute | solution.py:34
  82.0 1.3 %collective-permute-start.27 = (bf16[16,1792]{1,0:T(8,128)(2,1)S(1)}, bf16[16,1792]{1,0:T(8,128)(2,1)S(1)}, u32[]{:S(2)}, u32[]{:S(2)}) collective-permute-start(bf16[16,1792]{1,0:T(8,128)(2,1)S(1)} %add_convert_fusion.5), channel_id=1, source_target_pairs={{0,1},{1,0},{2,3},{3,2},{4,5},{5,4},{6,7},{7,6},{8,9},{9,8},{10,11... | collective-permute-start | bytes 172040 | tf_op jit(solution)/shard_map/ppermute | solution.py:34
  83.4 10.1 %collective-permute-start.28 = (bf16[16,1792]{1,0:T(8,128)(2,1)S(1)}, bf16[16,1792]{1,0:T(8,128)(2,1)S(1)}, u32[]{:S(2)}, u32[]{:S(2)}) collective-permute-start(bf16[16,1792]{1,0:T(8,128)(2,1)S(1)} %subtract_convert_fusion), channel_id=1, source_target_pairs={{1,9},{3,11},{5,13},{7,15},{9,1},{11,3},{13,5},{15,7},{17,25},{19,... | collective-permute-start | bytes 172040 | tf_op jit(solution)/shard_map/ppermute | solution.py:34
  88.5 6.4 %collective-permute-start.31 = (bf16[16,1792]{1,0:T(8,128)(2,1)S(1)}, bf16[16,1792]{1,0:T(8,128)(2,1)S(1)}, u32[]{:S(2)}, u32[]{:S(2)}) collective-permute-start(bf16[16,1792]{1,0:T(8,128)(2,1)S(1)} %subtract_convert_fusion), channel_id=1, source_target_pairs={{0,6},{1,15},{2,4},{3,13},{4,2},{5,11},{6,0},{7,9},{8,14},{9,7},{1... | collective-permute-start | bytes 172040 | tf_op jit(solution)/shard_map/ppermute | solution.py:34
  89.1 5.8 %collective-permute-start.30 = (bf16[16,1792]{1,0:T(8,128)(2,1)S(1)}, bf16[16,1792]{1,0:T(8,128)(2,1)S(1)}, u32[]{:S(2)}, u32[]{:S(2)}) collective-permute-start(bf16[16,1792]{1,0:T(8,128)(2,1)S(1)} %subtract_convert_fusion), channel_id=1, source_target_pairs={{0,4},{1,13},{2,6},{3,15},{4,0},{5,9},{6,2},{7,11},{8,12},{9,5},{1... | collective-permute-start | bytes 172040 | tf_op jit(solution)/shard_map/ppermute | solution.py:34
  92.3 6.0 %collective-permute-start.29 = (bf16[16,1792]{1,0:T(8,128)(2,1)S(1)}, bf16[16,1792]{1,0:T(8,128)(2,1)S(1)}, u32[]{:S(2)}, u32[]{:S(2)}) collective-permute-start(bf16[16,1792]{1,0:T(8,128)(2,1)S(1)} %subtract_convert_fusion), channel_id=1, source_target_pairs={{0,2},{1,11},{2,0},{3,9},{4,6},{5,15},{6,4},{7,13},{8,10},{9,3},{1... | collective-permute-start | bytes 172040 | tf_op jit(solution)/shard_map/ppermute | solution.py:34
  98.4 6.6 %collective-permute-start.32 = (bf16[64,1792]{1,0:T(8,128)(2,1)S(1)}, bf16[64,1792]{1,0:T(8,128)(2,1)S(1)}, u32[]{:S(2)}, u32[]{:S(2)}) collective-permute-start(bf16[64,1792]{1,0:T(8,128)(2,1)S(1)} %pad_maximum_fusion.2.refs_0_), channel_id=1, source_target_pairs={{0,32},{1,33},{2,34},{3,35},{4,36},{5,37},{6,38},{7,39},{8,40},{9,... | collective-permute-start | bytes 688136 | tf_op jit(solution)/shard_map/ppermute | solution.py:34
  99.8 7.2 %collective-permute-start.33 = (bf16[64,1792]{1,0:T(8,128)(2,1)S(1)}, bf16[64,1792]{1,0:T(8,128)(2,1)S(1)}, u32[]{:S(2)}, u32[]{:S(2)}) collective-permute-start(bf16[64,1792]{1,0:T(8,128)(2,1)S(1)} %pad_maximum_fusion.2.refs_0_), channel_id=1, source_target_pairs={{0,16},{1,17},{2,18},{3,19},{4,20},{5,21},{6,22},{7,23},{8,24},{9,... | collective-permute-start | bytes 688136 | tf_op jit(solution)/shard_map/ppermute | solution.py:34
  101.1 6.6 %collective-permute-start.34 = (bf16[64,1792]{1,0:T(8,128)(2,1)S(1)}, bf16[64,1792]{1,0:T(8,128)(2,1)S(1)}, u32[]{:S(2)}, u32[]{:S(2)}) collective-permute-start(bf16[64,1792]{1,0:T(8,128)(2,1)S(1)} %pad_maximum_fusion.2.refs_0_), channel_id=1, source_target_pairs={{0,48},{1,49},{2,50},{3,51},{4,52},{5,53},{6,54},{7,55},{8,56},{9,... | collective-permute-start | bytes 688136 | tf_op jit(solution)/shard_map/ppermute | solution.py:34
  101.7 6.1 %collective-permute-start.35 = (bf16[64,1792]{1,0:T(8,128)(2,1)S(1)}, bf16[64,1792]{1,0:T(8,128)(2,1)S(1)}, u32[]{:S(2)}, u32[]{:S(2)}) collective-permute-start(bf16[64,1792]{1,0:T(8,128)(2,1)S(1)} %pad_maximum_fusion.2.refs_0_), channel_id=1, source_target_pairs={{0,1},{1,0},{2,3},{3,2},{4,5},{5,4},{6,7},{7,6},{8,9},{9,8},{10,11... | collective-permute-start | bytes 688136 | tf_op jit(solution)/shard_map/ppermute | solution.py:34
  105.0 2.9 %collective-permute-start.36 = (bf16[64,1792]{1,0:T(8,128)(2,1)S(1)}, bf16[64,1792]{1,0:T(8,128)(2,1)S(1)}, u32[]{:S(2)}, u32[]{:S(2)}) collective-permute-start(bf16[64,1792]{1,0:T(8,128)(2,1)S(1)} %collective-permute-done.32.refs_1_), channel_id=1, source_target_pairs={{0,1},{1,0},{2,3},{3,2},{4,5},{5,4},{6,7},{7,6},{8,9},{9,8},{10,11... | collective-permute-start | bytes 688136 | tf_op jit(solution)/shard_map/ppermute | solution.py:34
  107.0 1.5 %collective-permute-start.37 = (bf16[64,1792]{1,0:T(8,128)(2,1)S(1)}, bf16[64,1792]{1,0:T(8,128)(2,1)S(1)}, u32[]{:S(2)}, u32[]{:S(2)}) collective-permute-start(bf16[64,1792]{1,0:T(8,128)(2,1)S(1)} %collective-permute-done.33.refs_2_), channel_id=1, source_target_pairs={{0,1},{1,0},{2,3},{3,2},{4,5},{5,4},{6,7},{7,6},{8,9},{9,8},{10,11... | collective-permute-start | bytes 688136 | tf_op jit(solution)/shard_map/ppermute | solution.py:34
  107.7 1.5 %collective-permute-start.38 = (bf16[64,1792]{1,0:T(8,128)(2,1)S(1)}, bf16[64,1792]{1,0:T(8,128)(2,1)S(1)}, u32[]{:S(2)}, u32[]{:S(2)}) collective-permute-start(bf16[64,1792]{1,0:T(8,128)(2,1)S(1)} %collective-permute-done.34.refs_3_), channel_id=1, source_target_pairs={{0,1},{1,0},{2,3},{3,2},{4,5},{5,4},{6,7},{7,6},{8,9},{9,8},{10,11... | collective-permute-start | bytes 688136 | tf_op jit(solution)/shard_map/ppermute | solution.py:34
  111.7 10.0 %collective-permute-start.39 = (bf16[400,256]{1,0:T(8,128)(2,1)S(1)}, bf16[400,256]{1,0:T(8,128)(2,1)S(1)}, u32[]{:S(2)}, u32[]{:S(2)}) collective-permute-start(bf16[400,256]{1,0:T(8,128)(2,1)S(1)} %get-tuple-element.43.away_ref), channel_id=1, source_target_pairs={{0,128},{64,192},{128,0},{192,64},{1,129},{65,193},{129,1},{193,65... | collective-permute-start | bytes 614408 | tf_op jit(solution)/shard_map/ppermute | solution.py:449
  115.5 9.8 %collective-permute-start.40 = (bf16[400,256]{1,0:T(8,128)(2,1)S(1)}, bf16[400,256]{1,0:T(8,128)(2,1)S(1)}, u32[]{:S(2)}, u32[]{:S(2)}) collective-permute-start(bf16[400,256]{1,0:T(8,128)(2,1)S(1)} %get-tuple-element.44), channel_id=1, source_target_pairs={{0,192},{64,0},{128,64},{192,128},{1,193},{65,1},{129,65},{193,129... | collective-permute-start | bytes 614408 | tf_op jit(solution)/shard_map/ppermute | solution.py:449
  116.4 8.9 %collective-permute-start.41 = (bf16[400,256]{1,0:T(8,128)(2,1)S(1)}, bf16[400,256]{1,0:T(8,128)(2,1)S(1)}, u32[]{:S(2)}, u32[]{:S(2)}) collective-permute-start(bf16[400,256]{1,0:T(8,128)(2,1)S(1)} %get-tuple-element.45), channel_id=1, source_target_pairs={{0,64},{64,128},{128,192},{192,0},{1,65},{65,129},{129,193},{193,1... | collective-permute-start | bytes 614408 | tf_op jit(solution)/shard_map/ppermute | solution.py:449

commit v6 on v5

--- a/solution.py
+++ b/solution.py
@@ -14,7 +14,7 @@
 BF = jnp.bfloat16
 F32 = jnp.float32
 STEPS = (0, 2, 1, 3)
-ORDER = (2, 1, 3)
+ORDER = (2, 3, 1)
 
 
 def index_of(y, z, c):
@@ -40,8 +40,7 @@
 
 def send_layer(value, steps):
     count = lax.axis_size("layer")
-    sources = [s for s in range(count) if 0 <= s + steps < count]
-    return lax.ppermute(value, "layer", [(s, s + steps) for s in sources])
+    return lax.ppermute(value, "layer", [(s, (s + steps) % count) for s in range(count)])
 
 
 def chip_rows(value, core):
@@ -63,11 +62,13 @@
 
 
 def collect(halves, core):
-    width = halves[0].shape[-1]
-    halves = [half.reshape(Y, 4 * 2 * 8, width) for half in halves]
+    count, width = halves[0].shape
+    pairs_of = [slice(at, at + count // 2) for at in (0, count // 2)]
     own = [
-        (halves[0][k].astype(F32) + swap(halves[1][k]).astype(F32)).astype(BF) for k in range(Y)
+        (halves[0][at].astype(F32) + swap(halves[1][at]).astype(F32)).astype(BF)
+        for at in pairs_of
     ]
+    own = [part[at : at + count // Y] for part in own for at in (0, count // Y)]
     row = own[0].astype(F32)
     for part, k in zip(own[1:], STEPS[1:]):
         row = row + send(part, lambda y, z, c, k=k: (y ^ k, z, c)).astype(F32)
@@ -360,7 +361,7 @@
     width, count = rows.shape
     feats = own.shape[1]
     whole = lambda array: pl.BlockSpec(array.shape, lambda i: (0,) * array.ndim)
-    part = width // 2
+    part = width
     return pl.pallas_call(
         functools.partial(enc_gradient_kernel, (len(came) + 1) * count * width),
         grid=(width // part,),
@@ -415,7 +416,8 @@
     every = jnp.arange(Y * Z)
     before = every[None, :] <= every[:, None]
     slot = jnp.sum(jnp.where(before[None] & live[:, None, :], 1, 0), axis=2, dtype=jnp.int32) - 1
-    slot = jnp.where(live, jnp.minimum(slot, CAP * 4 - 1), -1)
+    known = live & (layer >= jnp.arange(layers))[:, None]
+    slot = jnp.where(known, jnp.minimum(slot, CAP * 4 - 1), -1)
     source = jnp.sum(
         jnp.where(slot[:, None, :] == jnp.arange(CAP * 4)[None, :, None], every, 0),
         axis=2,
@@ -443,10 +445,7 @@
     errors = (collect(partial, core) - goal.astype(F32)).astype(BF)
     errors = spread_y(spread_z(errors, core))
     away = back(place, source, layers, decoder, errors)
-    came = []
-    for k, message in zip(ORDER, away):
-        ring = [(s, (s - k) % layers) for s in range(layers)]
-        came.append(lax.ppermute(message, "layer", ring))
+    came = [send_layer(message, -k) for k, message in zip(ORDER, away)]
     dec_grad, own = dec_gradient(layer, layers, *sources, decoder, errors)
     enc_grad, bias_grad, loss = enc_gradient(layer, slot, turned, on, own, away[0], came)
     loss = loss[0, 0]

time: 128 us -> 127 us (level)
  starting transfers between devices: 62 us -> 58.3 us
  waiting for transfers between devices: 43.5 us -> 45.8 us
    ppermute x6, starting transfers between devices: 13.4 us -> 9.68 us  [send_layer(): lax.ppermute(value, 'layer', [(s, (s + steps) % count) for s in range(cou...]
    ppermute x6, waiting for transfers between devices: 8.16 us -> 10.3 us  [send_layer(): lax.ppermute(value, 'layer', [(s, (s + steps) % count) for s in range(cou...]
    ppermute x36 -> x34, waiting for transfers between devices: 35.4 us -> 35.6 us  [send(): return lax.ppermute(value, 'latent', pairs(move, cores))]
    ppermute x36 -> x34, starting transfers between devices: 48.6 us -> 48.7 us  [send(): return lax.ppermute(value, 'latent', pairs(move, cores))]
  transfers between devices with their start and end apart: 42 -> 40, of which waited for: 23 -> 24; matrix products, arithmetic and copies ran while one was open for 4% -> 4% of each run, Pallas kernels for 6% -> 7%
where the time goes in v6:
time: 127 us; the launch traced here: 126 us
  starting transfers between devices  58.3 us (46%)
  waiting for transfers between devices  45.8 us (36%)
  Pallas kernels  14.8 us (12%)
  other arithmetic  3.99 us (3%)
  local copies, waits for them, and re-layouts  2.41 us (2%)
    ppermute x34, starting transfers between devices, send(): return lax.ppermute(value, 'latent', pairs(move, cores))  48.7 us
    ppermute x34, waiting for transfers between devices, send(): return lax.ppermute(value, 'latent', pairs(move, cores))  35.6 us
    ppermute x6, waiting for transfers between devices, send_layer(): lax.ppermute(value, 'layer', [(s, (s + steps) % count) for s in range(cou...  10.3 us
    ppermute x6, starting transfers between devices, send_layer(): lax.ppermute(value, 'layer', [(s, (s + steps) % count) for s in range(cou...  9.68 us
    pallas_call x1, Pallas kernels, dec_gradient(): pl.pallas_call(dec_gradient_kernel, grid_spec=pltpu.PrefetchScalarGridSpe...  4.75 us
    pallas_call x2, Pallas kernels, decode(): pl.pallas_call(functools.partial(decode_kernel, half), in_specs=specs(1,...  3.39 us
  transfers between devices with their start and end apart: 40, of which 24 were waited for; matrix products, arithmetic and copies ran while one was open for 4% of the time, Pallas kernels for 7%

profile of v6, /device:TPU:1, one launch (start us, length us, event | category | flops | bytes accessed | tf_op | source)
XLA Modules:
  0.0 126.4 jit_solution(17893158447915041767)
XLA Ops:
  0.6 3.3 %collective-permute-start = (bf16[8,1792]{1,0:T(8,128)(2,1)}, bf16[8,1792]{1,0:T(8,128)(2,1)S(1)}, u32[]{:S(2)}, u32[]{:S(2)}) collective-permute-start(bf16[8,1792]{1,0:T(8,128)(2,1)} %bitcast.18), channel_id=1, source_target_pairs={{0,1},{1,0},{2,3},{3,2},{4,5},{5,4},{6,7},{7,6},{8,9},{9,8},{10,11... | collective-permute-start | bytes 86024 | tf_op jit(solution)/shard_map/ppermute | solution.py:34
  4.1 0.9 collective-permute-done
  5.0 0.8 maximum_select_fusion
  5.9 7.1 %collective-permute-start.1 = (bf16[16,1792]{1,0:T(8,128)(2,1)S(1)}, bf16[16,1792]{1,0:T(8,128)(2,1)S(1)}, u32[]{:S(2)}, u32[]{:S(2)}) collective-permute-start(bf16[16,1792]{1,0:T(8,128)(2,1)S(1)} %maximum_select_fusion), channel_id=1, source_target_pairs={{1,9},{3,11},{5,13},{7,15},{9,1},{11,3},{13,5},{15,7},{17,25},{19,... | collective-permute-start | bytes 172040 | tf_op jit(solution)/shard_map/ppermute | solution.py:34
  13.1 4.0 %collective-permute-start.3 = (bf16[16,1792]{1,0:T(8,128)(2,1)S(1)}, bf16[16,1792]{1,0:T(8,128)(2,1)S(1)}, u32[]{:S(2)}, u32[]{:S(2)}) collective-permute-start(bf16[16,1792]{1,0:T(8,128)(2,1)S(1)} %maximum_select_fusion), channel_id=1, source_target_pairs={{0,4},{1,13},{2,6},{3,15},{4,0},{5,9},{6,2},{7,11},{8,12},{9,5},{1... | collective-permute-start | bytes 172040 | tf_op jit(solution)/shard_map/ppermute | solution.py:34
  17.5 0.8 broadcast_select_fusion.1
  18.4 0.9 collective-permute-done.3
  19.3 4.1 %collective-permute-done.2 = bf16[16,1792]{1,0:T(8,128)(2,1)S(1)} collective-permute-done((bf16[16,1792]{1,0:T(8,128)(2,1)S(1)}, bf16[16,1792]{1,0:T(8,128)(2,1)S(1)}, u32[]{:S(2)}, u32[]{:S(2)}) %collective-permute-start.2) | collective-permute-done | bytes 57376 | tf_op jit(solution)/shard_map/ppermute | solution.py:34
  23.4 3.0 %collective-permute-start.5 = (bf16[64,1792]{1,0:T(8,128)(2,1)S(1)}, bf16[64,1792]{1,0:T(8,128)(2,1)S(1)}, u32[]{:S(2)}, u32[]{:S(2)}) collective-permute-start(bf16[64,1792]{1,0:T(8,128)(2,1)S(1)} %pad_maximum_fusion.1.refs_0_), channel_id=1, source_target_pairs={{0,32},{1,33},{2,34},{3,35},{4,36},{5,37},{6,38},{7,39},{8,40},{9,... | collective-permute-start | bytes 688136 | tf_op jit(solution)/shard_map/ppermute | solution.py:34
  27.1 0.9 compare_reduce_fusion
  28.6 2.3 %dynamic-slice_bitcast_fusion.3 = (bf16[256,1792]{1,0:T(8,128)(2,1)S(1)}, bf16[256,1792]{1,0:T(8,128)(2,1)S(1)}, bf16[256,1792]{1,0:T(8,128)(2,1)S(1)}, bf16[256,1792]{1,0:T(8,128)(2,1)S(1)}) fusion(bf16[4,1,256,1792]{3,2,1,0:T(8,128)(2,1)} %param.10, s32[]{:T(128)S(6)} %select_n.226, s32[]{:T(128)S(6)} %select_n.232, s32[]{:T(128)S(6)} %select_n.230, ...), kind=kLoop, calls=%fused_computation.6 | loop fusion | bytes 7340048 | tf_op jit(solution)/shard_map/jit(dynamic_index_in_dim)/squeeze | solution.py:432
  31.7 1.0 collective-permute-done.6.refs_2_
  33.3 0.8 collective-permute-done.10.refs_6_
  34.5 1.3 encode.1
  35.7 2.8 %collective-permute-start.13 = (bf16[384,256]{1,0:T(8,128)(2,1)S(1)}, bf16[384,256]{1,0:T(8,128)(2,1)S(1)}, u32[]{:S(2)}, u32[]{:S(2)}) collective-permute-start(bf16[384,256]{1,0:T(8,128)(2,1)S(1)} %get-tuple-element.29.after_ref), channel_id=1, source_target_pairs={{0,128},{64,192},{128,0},{192,64},{1,129},{65,193},{129,1},{193,65... | collective-permute-start | bytes 589832 | tf_op jit(solution)/shard_map/ppermute | solution.py:43
  38.6 0.9 collective-permute-start.14
  40.6 3.1 %collective-permute-done.13.refs_0_ = bf16[384,256]{1,0:T(8,128)(2,1)S(1)} collective-permute-done((bf16[384,256]{1,0:T(8,128)(2,1)S(1)}, bf16[384,256]{1,0:T(8,128)(2,1)S(1)}, u32[]{:S(2)}, u32[]{:S(2)}) %collective-permute-start.13) | collective-permute-done | bytes 196640 | tf_op jit(solution)/shard_map/ppermute | solution.py:43
  43.7 4.3 %collective-permute-done.14.refs_1_ = bf16[384,256]{1,0:T(8,128)(2,1)S(1)} collective-permute-done((bf16[384,256]{1,0:T(8,128)(2,1)S(1)}, bf16[384,256]{1,0:T(8,128)(2,1)S(1)}, u32[]{:S(2)}, u32[]{:S(2)}) %collective-permute-start.14) | collective-permute-done | bytes 196640 | tf_op jit(solution)/shard_map/ppermute | solution.py:43
  48.0 1.7 %decode.3 = (bf16[256,1792]{1,0:T(8,128)(2,1)S(1)}, bf16[256,1024]{1,0:T(8,128)(2,1)S(1)}) custom-call(s32[4,32]{1,0:T(4,128)S(1)} %minimum_select_fusion.slot_ref, bf16[16,128]{1,0:T(8,128)(2,1)S(1)} %get-tuple-element.34.token_ref, bf16[512,256]{1,0:T(8,128)(2,1)S(1)} %get-tuple-element.35.codes_ref, bf16[1024,1792]{1,0:T(8,128)(2,1)S(1)} %pad_maximum_fusion.weight_ref, ...), custom_call_target="tpu_custom_call" | custom-call | flops 1000 | bytes 1000 | tf_op jit(solution)/shard_map/decode/pallas_call | solution.py:314
  49.8 1.3 collective-permute-start.16
  51.1 1.7 %decode.2 = (bf16[256,1792]{1,0:T(8,128)(2,1)S(1)}, bf16[256,1024]{1,0:T(8,128)(2,1)S(1)}) custom-call(s32[4,32]{1,0:T(4,128)S(1)} %minimum_select_fusion.slot_ref, bf16[16,128]{1,0:T(8,128)(2,1)S(1)} %get-tuple-element.34.token_ref, bf16[512,256]{1,0:T(8,128)(2,1)S(1)} %get-tuple-element.35.codes_ref, bf16[1024,1792]{1,0:T(8,128)(2,1)S(1)} %pad_maximum_fusion.weight_ref, ...), custom_call_target="tpu_custom_call" | custom-call | flops 1000 | bytes 1000 | tf_op jit(solution)/shard_map/decode/pallas_call | solution.py:314
  53.4 2.1 %collective-permute-start.20 = (bf16[64,1792]{1,0:T(8,128)(2,1)S(1)}, bf16[64,1792]{1,0:T(8,128)(2,1)S(1)}, u32[]{:S(2)}, u32[]{:S(2)}) collective-permute-start(bf16[64,1792]{1,0:T(8,128)(2,1)S(1)} %get-tuple-element.69), channel_id=1, source_target_pairs={{0,48},{1,49},{2,50},{3,51},{4,52},{5,53},{6,54},{7,55},{8,56},{9,... | collective-permute-start | bytes 688136 | tf_op jit(solution)/shard_map/ppermute | solution.py:34
  55.5 1.9 %collective-permute-start.17 = (bf16[64,1792]{1,0:T(8,128)(2,1)S(1)}, bf16[64,1792]{1,0:T(8,128)(2,1)S(1)}, u32[]{:S(2)}, u32[]{:S(2)}) collective-permute-start(bf16[64,1792]{1,0:T(8,128)(2,1)S(1)} %slice.54), channel_id=1, source_target_pairs={{0,32},{1,33},{2,34},{3,35},{4,36},{5,37},{6,38},{7,39},{8,40},{9,... | collective-permute-start | bytes 688136 | tf_op jit(solution)/shard_map/ppermute | solution.py:34
  57.4 4.1 %collective-permute-done.20 = bf16[64,1792]{1,0:T(8,128)(2,1)S(1)} collective-permute-done((bf16[64,1792]{1,0:T(8,128)(2,1)S(1)}, bf16[64,1792]{1,0:T(8,128)(2,1)S(1)}, u32[]{:S(2)}, u32[]{:S(2)}) %collective-permute-start.20) | collective-permute-done | bytes 229408 | tf_op jit(solution)/shard_map/ppermute | solution.py:34
  62.0 5.3 %collective-permute-done.17 = bf16[64,1792]{1,0:T(8,128)(2,1)S(1)} collective-permute-done((bf16[64,1792]{1,0:T(8,128)(2,1)S(1)}, bf16[64,1792]{1,0:T(8,128)(2,1)S(1)}, u32[]{:S(2)}, u32[]{:S(2)}) %collective-permute-start.17) | collective-permute-done | bytes 229408 | tf_op jit(solution)/shard_map/ppermute | solution.py:34
  68.1 2.4 %collective-permute-start.23 = (bf16[16,1792]{1,0:T(8,128)(2,1)S(1)}, bf16[16,1792]{1,0:T(8,128)(2,1)S(1)}, u32[]{:S(2)}, u32[]{:S(2)}) collective-permute-start(bf16[16,1792]{1,0:T(8,128)(2,1)S(1)} %get-tuple-element.72), channel_id=1, source_target_pairs={{0,4},{1,13},{2,6},{3,15},{4,0},{5,9},{6,2},{7,11},{8,12},{9,5},{1... | collective-permute-start | bytes 172040 | tf_op jit(solution)/shard_map/ppermute | solution.py:34
  70.4 2.0 %collective-permute-start.22 = (bf16[16,1792]{1,0:T(8,128)(2,1)S(1)}, bf16[16,1792]{1,0:T(8,128)(2,1)S(1)}, u32[]{:S(2)}, u32[]{:S(2)}) collective-permute-start(bf16[16,1792]{1,0:T(8,128)(2,1)S(1)} %get-tuple-element.73), channel_id=1, source_target_pairs={{0,2},{1,11},{2,0},{3,9},{4,6},{5,15},{6,4},{7,13},{8,10},{9,3},{1... | collective-permute-start | bytes 172040 | tf_op jit(solution)/shard_map/ppermute | solution.py:34
  72.4 5.0 %collective-permute-start.21 = (bf16[16,1792]{1,0:T(8,128)(2,1)S(1)}, bf16[16,1792]{1,0:T(8,128)(2,1)S(1)}, u32[]{:S(2)}, u32[]{:S(2)}) collective-permute-start(bf16[16,1792]{1,0:T(8,128)(2,1)S(1)} %get-tuple-element.70), channel_id=1, source_target_pairs={{1,9},{3,11},{5,13},{7,15},{9,1},{11,3},{13,5},{15,7},{17,25},{19,... | collective-permute-start | bytes 172040 | tf_op jit(solution)/shard_map/ppermute | solution.py:34
  77.8 3.5 %collective-permute-done.21 = bf16[16,1792]{1,0:T(8,128)(2,1)S(1)} collective-permute-done((bf16[16,1792]{1,0:T(8,128)(2,1)S(1)}, bf16[16,1792]{1,0:T(8,128)(2,1)S(1)}, u32[]{:S(2)}, u32[]{:S(2)}) %collective-permute-start.21) | collective-permute-done | bytes 57376 | tf_op jit(solution)/shard_map/ppermute | solution.py:34
  81.4 1.2 collective-permute-done.25
  82.6 5.1 %collective-permute-start.26 = (bf16[16,1792]{1,0:T(8,128)(2,1)S(1)}, bf16[16,1792]{1,0:T(8,128)(2,1)S(1)}, u32[]{:S(2)}, u32[]{:S(2)}) collective-permute-start(bf16[16,1792]{1,0:T(8,128)(2,1)S(1)} %subtract_convert_fusion), channel_id=1, source_target_pairs={{1,9},{3,11},{5,13},{7,15},{9,1},{11,3},{13,5},{15,7},{17,25},{19,... | collective-permute-start | bytes 172040 | tf_op jit(solution)/shard_map/ppermute | solution.py:34
  88.3 3.3 %collective-permute-start.28 = (bf16[16,1792]{1,0:T(8,128)(2,1)S(1)}, bf16[16,1792]{1,0:T(8,128)(2,1)S(1)}, u32[]{:S(2)}, u32[]{:S(2)}) collective-permute-start(bf16[16,1792]{1,0:T(8,128)(2,1)S(1)} %subtract_convert_fusion), channel_id=1, source_target_pairs={{0,4},{1,13},{2,6},{3,15},{4,0},{5,9},{6,2},{7,11},{8,12},{9,5},{1... | collective-permute-start | bytes 172040 | tf_op jit(solution)/shard_map/ppermute | solution.py:34
  91.6 1.1 collective-permute-start.27
  92.7 1.4 %collective-permute-done.29 = bf16[16,1792]{1,0:T(8,128)(2,1)S(1)} collective-permute-done((bf16[16,1792]{1,0:T(8,128)(2,1)S(1)}, bf16[16,1792]{1,0:T(8,128)(2,1)S(1)}, u32[]{:S(2)}, u32[]{:S(2)}) %collective-permute-start.29) | collective-permute-done | bytes 57376 | tf_op jit(solution)/shard_map/ppermute | solution.py:34
  94.1 3.5 %collective-permute-done.27 = bf16[16,1792]{1,0:T(8,128)(2,1)S(1)} collective-permute-done((bf16[16,1792]{1,0:T(8,128)(2,1)S(1)}, bf16[16,1792]{1,0:T(8,128)(2,1)S(1)}, u32[]{:S(2)}, u32[]{:S(2)}) %collective-permute-start.27) | collective-permute-done | bytes 57376 | tf_op jit(solution)/shard_map/ppermute | solution.py:34
  97.6 1.4 %collective-permute-start.30 = (bf16[64,1792]{1,0:T(8,128)(2,1)S(1)}, bf16[64,1792]{1,0:T(8,128)(2,1)S(1)}, u32[]{:S(2)}, u32[]{:S(2)}) collective-permute-start(bf16[64,1792]{1,0:T(8,128)(2,1)S(1)} %pad_maximum_fusion.2.refs_0_), channel_id=1, source_target_pairs={{0,32},{1,33},{2,34},{3,35},{4,36},{5,37},{6,38},{7,39},{8,40},{9,... | collective-permute-start | bytes 688136 | tf_op jit(solution)/shard_map/ppermute | solution.py:34
  99.0 1.3 %collective-permute-start.31 = (bf16[64,1792]{1,0:T(8,128)(2,1)S(1)}, bf16[64,1792]{1,0:T(8,128)(2,1)S(1)}, u32[]{:S(2)}, u32[]{:S(2)}) collective-permute-start(bf16[64,1792]{1,0:T(8,128)(2,1)S(1)} %pad_maximum_fusion.2.refs_0_), channel_id=1, source_target_pairs={{0,16},{1,17},{2,18},{3,19},{4,20},{5,21},{6,22},{7,23},{8,24},{9,... | collective-permute-start | bytes 688136 | tf_op jit(solution)/shard_map/ppermute | solution.py:34
  100.3 0.6 collective-permute-start.32
  101.0 3.3 %collective-permute-done.30.refs_1_ = bf16[64,1792]{1,0:T(8,128)(2,1)S(1)} collective-permute-done((bf16[64,1792]{1,0:T(8,128)(2,1)S(1)}, bf16[64,1792]{1,0:T(8,128)(2,1)S(1)}, u32[]{:S(2)}, u32[]{:S(2)}) %collective-permute-start.30) | collective-permute-done | bytes 229408 | tf_op jit(solution)/shard_map/ppermute | solution.py:34
  104.3 2.0 %collective-permute-done.31.refs_2_ = bf16[64,1792]{1,0:T(8,128)(2,1)S(1)} collective-permute-done((bf16[64,1792]{1,0:T(8,128)(2,1)S(1)}, bf16[64,1792]{1,0:T(8,128)(2,1)S(1)}, u32[]{:S(2)}, u32[]{:S(2)}) %collective-permute-start.31) | collective-permute-done | bytes 229408 | tf_op jit(solution)/shard_map/ppermute | solution.py:34
  106.2 0.8 collective-permute-done.32.refs_3_
  107.7 0.8 collective-permute-done.36.refs_7_
  108.5 2.5 %back.1 = (bf16[400,256]{1,0:T(8,128)(2,1)S(1)}, bf16[400,256]{1,0:T(8,128)(2,1)S(1)}, bf16[400,256]{1,0:T(8,128)(2,1)S(1)}) custom-call(s32[32]{0:T(128)S(1)} %select_reduce_fusion.2.place_ref, s32[4,24]{1,0:T(4,128)S(1)} %broadcast_minimum_fusion.source_ref, bf16[1024,1792]{1,0:T(8,128)(2,1)S(1)} %pad_maximum_fusion.weight_ref, ...), custom_call_target="tpu_custom_call" | custom-call | flops 1000 | bytes 1000 | tf_op jit(solution)/shard_map/back/pallas_call | solution.py:280
  111.0 2.7 %collective-permute-start.37 = (bf16[400,256]{1,0:T(8,128)(2,1)S(1)}, bf16[400,256]{1,0:T(8,128)(2,1)S(1)}, u32[]{:S(2)}, u32[]{:S(2)}) collective-permute-start(bf16[400,256]{1,0:T(8,128)(2,1)S(1)} %get-tuple-element.43.away_ref), channel_id=1, source_target_pairs={{0,128},{64,192},{128,0},{192,64},{1,129},{65,193},{129,1},{193,65... | collective-permute-start | bytes 614408 | tf_op jit(solution)/shard_map/ppermute | solution.py:43
  114.0 2.4 %collective-permute-start.39 = (bf16[400,256]{1,0:T(8,128)(2,1)S(1)}, bf16[400,256]{1,0:T(8,128)(2,1)S(1)}, u32[]{:S(2)}, u32[]{:S(2)}) collective-permute-start(bf16[400,256]{1,0:T(8,128)(2,1)S(1)} %get-tuple-element.45), channel_id=1, source_target_pairs={{0,192},{64,0},{128,64},{192,128},{1,193},{65,1},{129,65},{193,129... | collective-permute-start | bytes 614408 | tf_op jit(solution)/shard_map/ppermute | solution.py:43
  116.4 4.8 %dec_gradient.1 = (bf16[4,256,1792]{2,1,0:T(8,128)(2,1)}, f32[512,256]{1,0:T(8,128)S(1)}) custom-call(s32[1]{0:T(128)} %bitcast.layer_ref, bf16[256,1024]{1,0:T(8,128)(2,1)S(1)} %get-tuple-element.37.first_ref, bf16[256,1024]{1,0:T(8,128)(2,1)S(1)} %get-tuple-element.38.second_ref, bf16[1024,1792]{1,0:T(8,128)(2,1)S(1)} %pad_maximum_fusion.weight_ref, ...), custom_call_target="tpu_custom_call" | custom-call | flops 1000 | bytes 1000 | tf_op jit(solution)/shard_map/dec_gradient/pallas_call | solution.py:205
  121.1 2.9 %collective-permute-done.38.refs_1_ = bf16[400,256]{1,0:T(8,128)(2,1)S(1)} collective-permute-done((bf16[400,256]{1,0:T(8,128)(2,1)S(1)}, bf16[400,256]{1,0:T(8,128)(2,1)S(1)}, u32[]{:S(2)}, u32[]{:S(2)}) %collective-permute-start.38) | collective-permute-done | bytes 204832 | tf_op jit(solution)/shard_map/ppermute | solution.py:43
  124.0 2.4 %enc_gradient.1 = (bf16[1792,256]{1,0:T(8,128)(2,1)}, f32[1,256]{1,0:T(1,128)}, f32[1,1]{1,0:T(1,128)}) custom-call(s32[1]{0:T(128)} %bitcast.layer_ref, s32[4,32]{1,0:T(4,128)S(1)} %minimum_select_fusion.slot_ref, bf16[1792,512]{1,0:T(8,128)(2,1)S(1)} %get-tuple-element.30.rows_ref, bf16[512,256]{1,0:T(8,128)(2,1)S(1)} %get-tuple-element.31.on_ref, ...), custom_call_target="tpu_custom_call" | custom-call | flops 1000 | bytes 1000 | tf_op jit(solution)/shard_map/enc_gradient/pallas_call | solution.py:365
  (74 shorter events, 9.0 us)
Async XLA Ops:
  0.6 4.4 %collective-permute-start = (bf16[8,1792]{1,0:T(8,128)(2,1)}, bf16[8,1792]{1,0:T(8,128)(2,1)S(1)}, u32[]{:S(2)}, u32[]{:S(2)}) collective-permute-start(bf16[8,1792]{1,0:T(8,128)(2,1)} %bitcast.18), channel_id=1, source_target_pairs={{0,1},{1,0},{2,3},{3,2},{4,5},{5,4},{6,7},{7,6},{8,9},{9,8},{10,11... | collective-permute-start | bytes 86024 | tf_op jit(solution)/shard_map/ppermute | solution.py:34
  5.9 11.7 %collective-permute-start.1 = (bf16[16,1792]{1,0:T(8,128)(2,1)S(1)}, bf16[16,1792]{1,0:T(8,128)(2,1)S(1)}, u32[]{:S(2)}, u32[]{:S(2)}) collective-permute-start(bf16[16,1792]{1,0:T(8,128)(2,1)S(1)} %maximum_select_fusion), channel_id=1, source_target_pairs={{1,9},{3,11},{5,13},{7,15},{9,1},{11,3},{13,5},{15,7},{17,25},{19,... | collective-permute-start | bytes 172040 | tf_op jit(solution)/shard_map/ppermute | solution.py:34
  13.0 5.4 %collective-permute-start.4 = (bf16[16,1792]{1,0:T(8,128)(2,1)S(1)}, bf16[16,1792]{1,0:T(8,128)(2,1)S(1)}, u32[]{:S(2)}, u32[]{:S(2)}) collective-permute-start(bf16[16,1792]{1,0:T(8,128)(2,1)S(1)} %maximum_select_fusion), channel_id=1, source_target_pairs={{0,6},{1,15},{2,4},{3,13},{4,2},{5,11},{6,0},{7,9},{8,14},{9,7},{1... | collective-permute-start | bytes 172040 | tf_op jit(solution)/shard_map/ppermute | solution.py:34
  13.1 6.2 %collective-permute-start.3 = (bf16[16,1792]{1,0:T(8,128)(2,1)S(1)}, bf16[16,1792]{1,0:T(8,128)(2,1)S(1)}, u32[]{:S(2)}, u32[]{:S(2)}) collective-permute-start(bf16[16,1792]{1,0:T(8,128)(2,1)S(1)} %maximum_select_fusion), channel_id=1, source_target_pairs={{0,4},{1,13},{2,6},{3,15},{4,0},{5,9},{6,2},{7,11},{8,12},{9,5},{1... | collective-permute-start | bytes 172040 | tf_op jit(solution)/shard_map/ppermute | solution.py:34
  17.1 6.3 %collective-permute-start.2 = (bf16[16,1792]{1,0:T(8,128)(2,1)S(1)}, bf16[16,1792]{1,0:T(8,128)(2,1)S(1)}, u32[]{:S(2)}, u32[]{:S(2)}) collective-permute-start(bf16[16,1792]{1,0:T(8,128)(2,1)S(1)} %maximum_select_fusion), channel_id=1, source_target_pairs={{0,2},{1,11},{2,0},{3,9},{4,6},{5,15},{6,4},{7,13},{8,10},{9,3},{1... | collective-permute-start | bytes 172040 | tf_op jit(solution)/shard_map/ppermute | solution.py:34
  23.4 8.2 %collective-permute-start.5 = (bf16[64,1792]{1,0:T(8,128)(2,1)S(1)}, bf16[64,1792]{1,0:T(8,128)(2,1)S(1)}, u32[]{:S(2)}, u32[]{:S(2)}) collective-permute-start(bf16[64,1792]{1,0:T(8,128)(2,1)S(1)} %pad_maximum_fusion.1.refs_0_), channel_id=1, source_target_pairs={{0,32},{1,33},{2,34},{3,35},{4,36},{5,37},{6,38},{7,39},{8,40},{9,... | collective-permute-start | bytes 688136 | tf_op jit(solution)/shard_map/ppermute | solution.py:34
  26.4 6.3 %collective-permute-start.6 = (bf16[64,1792]{1,0:T(8,128)(2,1)S(1)}, bf16[64,1792]{1,0:T(8,128)(2,1)S(1)}, u32[]{:S(2)}, u32[]{:S(2)}) collective-permute-start(bf16[64,1792]{1,0:T(8,128)(2,1)S(1)} %pad_maximum_fusion.1.refs_0_), channel_id=1, source_target_pairs={{0,16},{1,17},{2,18},{3,19},{4,20},{5,21},{6,22},{7,23},{8,24},{9,... | collective-permute-start | bytes 688136 | tf_op jit(solution)/shard_map/ppermute | solution.py:34
  26.8 6.1 %collective-permute-start.7 = (bf16[64,1792]{1,0:T(8,128)(2,1)S(1)}, bf16[64,1792]{1,0:T(8,128)(2,1)S(1)}, u32[]{:S(2)}, u32[]{:S(2)}) collective-permute-start(bf16[64,1792]{1,0:T(8,128)(2,1)S(1)} %pad_maximum_fusion.1.refs_0_), channel_id=1, source_target_pairs={{0,48},{1,49},{2,50},{3,51},{4,52},{5,53},{6,54},{7,55},{8,56},{9,... | collective-permute-start | bytes 688136 | tf_op jit(solution)/shard_map/ppermute | solution.py:34
  27.1 6.2 %collective-permute-start.8 = (bf16[64,1792]{1,0:T(8,128)(2,1)S(1)}, bf16[64,1792]{1,0:T(8,128)(2,1)S(1)}, u32[]{:S(2)}, u32[]{:S(2)}) collective-permute-start(bf16[64,1792]{1,0:T(8,128)(2,1)S(1)} %pad_maximum_fusion.1.refs_0_), channel_id=1, source_target_pairs={{0,1},{1,0},{2,3},{3,2},{4,5},{5,4},{6,7},{7,6},{8,9},{9,8},{10,11... | collective-permute-start | bytes 688136 | tf_op jit(solution)/shard_map/ppermute | solution.py:34
  28.0 12.0 %collective-permute-start.12 = (bf16[8,1792]{1,0:T(8,128)(2,1)}, bf16[8,1792]{1,0:T(8,128)(2,1)S(1)}, u32[]{:S(2)}, u32[]{:S(2)}) collective-permute-start(bf16[8,1792]{1,0:T(8,128)(2,1)} %bitcast.21), channel_id=1, source_target_pairs={{0,1},{1,0},{2,3},{3,2},{4,5},{5,4},{6,7},{7,6},{8,9},{9,8},{10,11... | collective-permute-start | bytes 86024 | tf_op jit(solution)/shard_map/ppermute | solution.py:34
  31.0 3.5 %copy-start = (bf16[1,1792,256]{2,1,0:T(8,128)(2,1)S(1)}, bf16[1,1792,256]{2,1,0:T(8,128)(2,1)}, u32[]{:S(2)}) copy-start(bf16[1,1792,256]{2,1,0:T(8,128)(2,1)} %param.8) | copy-start | bytes 2752516
  31.0 3.5 %copy-start.1 = (f32[1,256]{1,0:T(1,128)S(1)}, f32[1,256]{1,0:T(1,128)}, u32[]{:S(2)}) copy-start(f32[1,256]{1,0:T(1,128)} %bias_ref.1) | copy-start | bytes 3076
  31.0 9.0 %copy-start.2 = (bf16[1,8,1792]{2,1,0:T(8,128)(2,1)S(1)}, bf16[1,8,1792]{2,1,0:T(8,128)(2,1)}, u32[]{:S(2)}) copy-start(bf16[1,8,1792]{2,1,0:T(8,128)(2,1)} %param.7) | copy-start | bytes 86020
  31.6 1.7 %collective-permute-start.9 = (bf16[64,1792]{1,0:T(8,128)(2,1)S(1)}, bf16[64,1792]{1,0:T(8,128)(2,1)S(1)}, u32[]{:S(2)}, u32[]{:S(2)}) collective-permute-start(bf16[64,1792]{1,0:T(8,128)(2,1)S(1)} %collective-permute-done.5.refs_1_), channel_id=1, source_target_pairs={{0,1},{1,0},{2,3},{3,2},{4,5},{5,4},{6,7},{7,6},{8,9},{9,8},{10,11... | collective-permute-start | bytes 688136 | tf_op jit(solution)/shard_map/ppermute | solution.py:34
  32.7 1.5 %collective-permute-start.10 = (bf16[64,1792]{1,0:T(8,128)(2,1)S(1)}, bf16[64,1792]{1,0:T(8,128)(2,1)S(1)}, u32[]{:S(2)}, u32[]{:S(2)}) collective-permute-start(bf16[64,1792]{1,0:T(8,128)(2,1)S(1)} %collective-permute-done.6.refs_2_), channel_id=1, source_target_pairs={{0,1},{1,0},{2,3},{3,2},{4,5},{5,4},{6,7},{7,6},{8,9},{9,8},{10,11... | collective-permute-start | bytes 688136 | tf_op jit(solution)/shard_map/ppermute | solution.py:34
  32.8 1.6 %collective-permute-start.11 = (bf16[64,1792]{1,0:T(8,128)(2,1)S(1)}, bf16[64,1792]{1,0:T(8,128)(2,1)S(1)}, u32[]{:S(2)}, u32[]{:S(2)}) collective-permute-start(bf16[64,1792]{1,0:T(8,128)(2,1)S(1)} %collective-permute-done.7.refs_3_), channel_id=1, source_target_pairs={{0,1},{1,0},{2,3},{3,2},{4,5},{5,4},{6,7},{7,6},{8,9},{9,8},{10,11... | collective-permute-start | bytes 688136 | tf_op jit(solution)/shard_map/ppermute | solution.py:34
  35.7 7.9 %collective-permute-start.13 = (bf16[384,256]{1,0:T(8,128)(2,1)S(1)}, bf16[384,256]{1,0:T(8,128)(2,1)S(1)}, u32[]{:S(2)}, u32[]{:S(2)}) collective-permute-start(bf16[384,256]{1,0:T(8,128)(2,1)S(1)} %get-tuple-element.29.after_ref), channel_id=1, source_target_pairs={{0,128},{64,192},{128,0},{192,64},{1,129},{65,193},{129,1},{193,65... | collective-permute-start | bytes 589832 | tf_op jit(solution)/shard_map/ppermute | solution.py:43
  38.6 9.4 %collective-permute-start.14 = (bf16[384,256]{1,0:T(8,128)(2,1)S(1)}, bf16[384,256]{1,0:T(8,128)(2,1)S(1)}, u32[]{:S(2)}, u32[]{:S(2)}) collective-permute-start(bf16[384,256]{1,0:T(8,128)(2,1)S(1)} %get-tuple-element.29.after_ref), channel_id=1, source_target_pairs={{0,192},{64,0},{128,64},{192,128},{1,193},{65,1},{129,65},{193,129... | collective-permute-start | bytes 589832 | tf_op jit(solution)/shard_map/ppermute | solution.py:43
  39.4 8.6 %collective-permute-start.15 = (bf16[384,256]{1,0:T(8,128)(2,1)S(1)}, bf16[384,256]{1,0:T(8,128)(2,1)S(1)}, u32[]{:S(2)}, u32[]{:S(2)}) collective-permute-start(bf16[384,256]{1,0:T(8,128)(2,1)S(1)} %get-tuple-element.29.after_ref), channel_id=1, source_target_pairs={{0,64},{64,128},{128,192},{192,0},{1,65},{65,129},{129,193},{193,1... | collective-permute-start | bytes 589832 | tf_op jit(solution)/shard_map/ppermute | solution.py:43
  49.8 3.1 %collective-permute-start.16 = (bf16[128,1792]{1,0:T(8,128)(2,1)S(1)}, bf16[128,1792]{1,0:T(8,128)(2,1)S(1)}, u32[]{:S(2)}, u32[]{:S(2)}) collective-permute-start(bf16[128,1792]{1,0:T(8,128)(2,1)S(1)} %get-tuple-element.66), channel_id=1, source_target_pairs={{0,1},{1,0},{2,3},{3,2},{4,5},{5,4},{6,7},{7,6},{8,9},{9,8},{10,11... | collective-permute-start | bytes 1376264 | tf_op jit(solution)/shard_map/ppermute | solution.py:34
  51.0 2.1 %collective-permute-start.18 = (bf16[128,1792]{1,0:T(8,128)(2,1)S(1)}, bf16[128,1792]{1,0:T(8,128)(2,1)S(1)}, u32[]{:S(2)}, u32[]{:S(2)}) collective-permute-start(bf16[128,1792]{1,0:T(8,128)(2,1)S(1)} %get-tuple-element.67), channel_id=1, source_target_pairs={{0,1},{1,0},{2,3},{3,2},{4,5},{5,4},{6,7},{7,6},{8,9},{9,8},{10,11... | collective-permute-start | bytes 1376264 | tf_op jit(solution)/shard_map/ppermute | solution.py:34
  53.4 8.1 %collective-permute-start.20 = (bf16[64,1792]{1,0:T(8,128)(2,1)S(1)}, bf16[64,1792]{1,0:T(8,128)(2,1)S(1)}, u32[]{:S(2)}, u32[]{:S(2)}) collective-permute-start(bf16[64,1792]{1,0:T(8,128)(2,1)S(1)} %get-tuple-element.69), channel_id=1, source_target_pairs={{0,48},{1,49},{2,50},{3,51},{4,52},{5,53},{6,54},{7,55},{8,56},{9,... | collective-permute-start | bytes 688136 | tf_op jit(solution)/shard_map/ppermute | solution.py:34
  55.5 6.5 %collective-permute-start.19 = (bf16[64,1792]{1,0:T(8,128)(2,1)S(1)}, bf16[64,1792]{1,0:T(8,128)(2,1)S(1)}, u32[]{:S(2)}, u32[]{:S(2)}) collective-permute-start(bf16[64,1792]{1,0:T(8,128)(2,1)S(1)} %get-tuple-element.68), channel_id=1, source_target_pairs={{0,16},{1,17},{2,18},{3,19},{4,20},{5,21},{6,22},{7,23},{8,24},{9,... | collective-permute-start | bytes 688136 | tf_op jit(solution)/shard_map/ppermute | solution.py:34
  55.5 11.7 %collective-permute-start.17 = (bf16[64,1792]{1,0:T(8,128)(2,1)S(1)}, bf16[64,1792]{1,0:T(8,128)(2,1)S(1)}, u32[]{:S(2)}, u32[]{:S(2)}) collective-permute-start(bf16[64,1792]{1,0:T(8,128)(2,1)S(1)} %slice.54), channel_id=1, source_target_pairs={{0,32},{1,33},{2,34},{3,35},{4,36},{5,37},{6,38},{7,39},{8,40},{9,... | collective-permute-start | bytes 688136 | tf_op jit(solution)/shard_map/ppermute | solution.py:34
  67.4 10.0 %collective-permute-start.24 = (bf16[16,1792]{1,0:T(8,128)(2,1)S(1)}, bf16[16,1792]{1,0:T(8,128)(2,1)S(1)}, u32[]{:S(2)}, u32[]{:S(2)}) collective-permute-start(bf16[16,1792]{1,0:T(8,128)(2,1)S(1)} %get-tuple-element.71), channel_id=1, source_target_pairs={{0,6},{1,15},{2,4},{3,13},{4,2},{5,11},{6,0},{7,9},{8,14},{9,7},{1... | collective-permute-start | bytes 172040 | tf_op jit(solution)/shard_map/ppermute | solution.py:34
  68.1 9.4 %collective-permute-start.23 = (bf16[16,1792]{1,0:T(8,128)(2,1)S(1)}, bf16[16,1792]{1,0:T(8,128)(2,1)S(1)}, u32[]{:S(2)}, u32[]{:S(2)}) collective-permute-start(bf16[16,1792]{1,0:T(8,128)(2,1)S(1)} %get-tuple-element.72), channel_id=1, source_target_pairs={{0,4},{1,13},{2,6},{3,15},{4,0},{5,9},{6,2},{7,11},{8,12},{9,5},{1... | collective-permute-start | bytes 172040 | tf_op jit(solution)/shard_map/ppermute | solution.py:34
  70.4 7.4 %collective-permute-start.22 = (bf16[16,1792]{1,0:T(8,128)(2,1)S(1)}, bf16[16,1792]{1,0:T(8,128)(2,1)S(1)}, u32[]{:S(2)}, u32[]{:S(2)}) collective-permute-start(bf16[16,1792]{1,0:T(8,128)(2,1)S(1)} %get-tuple-element.73), channel_id=1, source_target_pairs={{0,2},{1,11},{2,0},{3,9},{4,6},{5,15},{6,4},{7,13},{8,10},{9,3},{1... | collective-permute-start | bytes 172040 | tf_op jit(solution)/shard_map/ppermute | solution.py:34
  72.4 8.8 %collective-permute-start.21 = (bf16[16,1792]{1,0:T(8,128)(2,1)S(1)}, bf16[16,1792]{1,0:T(8,128)(2,1)S(1)}, u32[]{:S(2)}, u32[]{:S(2)}) collective-permute-start(bf16[16,1792]{1,0:T(8,128)(2,1)S(1)} %get-tuple-element.70), channel_id=1, source_target_pairs={{1,9},{3,11},{5,13},{7,15},{9,1},{11,3},{13,5},{15,7},{17,25},{19,... | collective-permute-start | bytes 172040 | tf_op jit(solution)/shard_map/ppermute | solution.py:34
  81.3 1.3 %collective-permute-start.25 = (bf16[16,1792]{1,0:T(8,128)(2,1)S(1)}, bf16[16,1792]{1,0:T(8,128)(2,1)S(1)}, u32[]{:S(2)}, u32[]{:S(2)}) collective-permute-start(bf16[16,1792]{1,0:T(8,128)(2,1)S(1)} %add_convert_fusion.3), channel_id=1, source_target_pairs={{0,1},{1,0},{2,3},{3,2},{4,5},{5,4},{6,7},{7,6},{8,9},{9,8},{10,11... | collective-permute-start | bytes 172040 | tf_op jit(solution)/shard_map/ppermute | solution.py:34
  82.6 10.1 %collective-permute-start.26 = (bf16[16,1792]{1,0:T(8,128)(2,1)S(1)}, bf16[16,1792]{1,0:T(8,128)(2,1)S(1)}, u32[]{:S(2)}, u32[]{:S(2)}) collective-permute-start(bf16[16,1792]{1,0:T(8,128)(2,1)S(1)} %subtract_convert_fusion), channel_id=1, source_target_pairs={{1,9},{3,11},{5,13},{7,15},{9,1},{11,3},{13,5},{15,7},{17,25},{19,... | collective-permute-start | bytes 172040 | tf_op jit(solution)/shard_map/ppermute | solution.py:34
  87.7 6.4 %collective-permute-start.29 = (bf16[16,1792]{1,0:T(8,128)(2,1)S(1)}, bf16[16,1792]{1,0:T(8,128)(2,1)S(1)}, u32[]{:S(2)}, u32[]{:S(2)}) collective-permute-start(bf16[16,1792]{1,0:T(8,128)(2,1)S(1)} %subtract_convert_fusion), channel_id=1, source_target_pairs={{0,6},{1,15},{2,4},{3,13},{4,2},{5,11},{6,0},{7,9},{8,14},{9,7},{1... | collective-permute-start | bytes 172040 | tf_op jit(solution)/shard_map/ppermute | solution.py:34
  88.3 5.8 %collective-permute-start.28 = (bf16[16,1792]{1,0:T(8,128)(2,1)S(1)}, bf16[16,1792]{1,0:T(8,128)(2,1)S(1)}, u32[]{:S(2)}, u32[]{:S(2)}) collective-permute-start(bf16[16,1792]{1,0:T(8,128)(2,1)S(1)} %subtract_convert_fusion), channel_id=1, source_target_pairs={{0,4},{1,13},{2,6},{3,15},{4,0},{5,9},{6,2},{7,11},{8,12},{9,5},{1... | collective-permute-start | bytes 172040 | tf_op jit(solution)/shard_map/ppermute | solution.py:34
  91.6 6.0 %collective-permute-start.27 = (bf16[16,1792]{1,0:T(8,128)(2,1)S(1)}, bf16[16,1792]{1,0:T(8,128)(2,1)S(1)}, u32[]{:S(2)}, u32[]{:S(2)}) collective-permute-start(bf16[16,1792]{1,0:T(8,128)(2,1)S(1)} %subtract_convert_fusion), channel_id=1, source_target_pairs={{0,2},{1,11},{2,0},{3,9},{4,6},{5,15},{6,4},{7,13},{8,10},{9,3},{1... | collective-permute-start | bytes 172040 | tf_op jit(solution)/shard_map/ppermute | solution.py:34
  97.6 6.6 %collective-permute-start.30 = (bf16[64,1792]{1,0:T(8,128)(2,1)S(1)}, bf16[64,1792]{1,0:T(8,128)(2,1)S(1)}, u32[]{:S(2)}, u32[]{:S(2)}) collective-permute-start(bf16[64,1792]{1,0:T(8,128)(2,1)S(1)} %pad_maximum_fusion.2.refs_0_), channel_id=1, source_target_pairs={{0,32},{1,33},{2,34},{3,35},{4,36},{5,37},{6,38},{7,39},{8,40},{9,... | collective-permute-start | bytes 688136 | tf_op jit(solution)/shard_map/ppermute | solution.py:34
  99.0 7.2 %collective-permute-start.31 = (bf16[64,1792]{1,0:T(8,128)(2,1)S(1)}, bf16[64,1792]{1,0:T(8,128)(2,1)S(1)}, u32[]{:S(2)}, u32[]{:S(2)}) collective-permute-start(bf16[64,1792]{1,0:T(8,128)(2,1)S(1)} %pad_maximum_fusion.2.refs_0_), channel_id=1, source_target_pairs={{0,16},{1,17},{2,18},{3,19},{4,20},{5,21},{6,22},{7,23},{8,24},{9,... | collective-permute-start | bytes 688136 | tf_op jit(solution)/shard_map/ppermute | solution.py:34
  100.3 6.6 %collective-permute-start.32 = (bf16[64,1792]{1,0:T(8,128)(2,1)S(1)}, bf16[64,1792]{1,0:T(8,128)(2,1)S(1)}, u32[]{:S(2)}, u32[]{:S(2)}) collective-permute-start(bf16[64,1792]{1,0:T(8,128)(2,1)S(1)} %pad_maximum_fusion.2.refs_0_), channel_id=1, source_target_pairs={{0,48},{1,49},{2,50},{3,51},{4,52},{5,53},{6,54},{7,55},{8,56},{9,... | collective-permute-start | bytes 688136 | tf_op jit(solution)/shard_map/ppermute | solution.py:34
  101.0 6.1 %collective-permute-start.33 = (bf16[64,1792]{1,0:T(8,128)(2,1)S(1)}, bf16[64,1792]{1,0:T(8,128)(2,1)S(1)}, u32[]{:S(2)}, u32[]{:S(2)}) collective-permute-start(bf16[64,1792]{1,0:T(8,128)(2,1)S(1)} %pad_maximum_fusion.2.refs_0_), channel_id=1, source_target_pairs={{0,1},{1,0},{2,3},{3,2},{4,5},{5,4},{6,7},{7,6},{8,9},{9,8},{10,11... | collective-permute-start | bytes 688136 | tf_op jit(solution)/shard_map/ppermute | solution.py:34
  104.2 2.9 %collective-permute-start.34 = (bf16[64,1792]{1,0:T(8,128)(2,1)S(1)}, bf16[64,1792]{1,0:T(8,128)(2,1)S(1)}, u32[]{:S(2)}, u32[]{:S(2)}) collective-permute-start(bf16[64,1792]{1,0:T(8,128)(2,1)S(1)} %collective-permute-done.30.refs_1_), channel_id=1, source_target_pairs={{0,1},{1,0},{2,3},{3,2},{4,5},{5,4},{6,7},{7,6},{8,9},{9,8},{10,11... | collective-permute-start | bytes 688136 | tf_op jit(solution)/shard_map/ppermute | solution.py:34
  106.2 1.5 %collective-permute-start.35 = (bf16[64,1792]{1,0:T(8,128)(2,1)S(1)}, bf16[64,1792]{1,0:T(8,128)(2,1)S(1)}, u32[]{:S(2)}, u32[]{:S(2)}) collective-permute-start(bf16[64,1792]{1,0:T(8,128)(2,1)S(1)} %collective-permute-done.31.refs_2_), channel_id=1, source_target_pairs={{0,1},{1,0},{2,3},{3,2},{4,5},{5,4},{6,7},{7,6},{8,9},{9,8},{10,11... | collective-permute-start | bytes 688136 | tf_op jit(solution)/shard_map/ppermute | solution.py:34
  107.0 1.5 %collective-permute-start.36 = (bf16[64,1792]{1,0:T(8,128)(2,1)S(1)}, bf16[64,1792]{1,0:T(8,128)(2,1)S(1)}, u32[]{:S(2)}, u32[]{:S(2)}) collective-permute-start(bf16[64,1792]{1,0:T(8,128)(2,1)S(1)} %collective-permute-done.32.refs_3_), channel_id=1, source_target_pairs={{0,1},{1,0},{2,3},{3,2},{4,5},{5,4},{6,7},{7,6},{8,9},{9,8},{10,11... | collective-permute-start | bytes 688136 | tf_op jit(solution)/shard_map/ppermute | solution.py:34
  111.0 10.1 %collective-permute-start.37 = (bf16[400,256]{1,0:T(8,128)(2,1)S(1)}, bf16[400,256]{1,0:T(8,128)(2,1)S(1)}, u32[]{:S(2)}, u32[]{:S(2)}) collective-permute-start(bf16[400,256]{1,0:T(8,128)(2,1)S(1)} %get-tuple-element.43.away_ref), channel_id=1, source_target_pairs={{0,128},{64,192},{128,0},{192,64},{1,129},{65,193},{129,1},{193,65... | collective-permute-start | bytes 614408 | tf_op jit(solution)/shard_map/ppermute | solution.py:43
  113.7 10.3 %collective-permute-start.38 = (bf16[400,256]{1,0:T(8,128)(2,1)S(1)}, bf16[400,256]{1,0:T(8,128)(2,1)S(1)}, u32[]{:S(2)}, u32[]{:S(2)}) collective-permute-start(bf16[400,256]{1,0:T(8,128)(2,1)S(1)} %get-tuple-element.44), channel_id=1, source_target_pairs={{0,64},{64,128},{128,192},{192,0},{1,65},{65,129},{129,193},{193,1... | collective-permute-start | bytes 614408 | tf_op jit(solution)/shard_map/ppermute | solution.py:43
  114.0 10.0 %collective-permute-start.39 = (bf16[400,256]{1,0:T(8,128)(2,1)S(1)}, bf16[400,256]{1,0:T(8,128)(2,1)S(1)}, u32[]{:S(2)}, u32[]{:S(2)}) collective-permute-start(bf16[400,256]{1,0:T(8,128)(2,1)S(1)} %get-tuple-element.45), channel_id=1, source_target_pairs={{0,192},{64,0},{128,64},{192,128},{1,193},{65,1},{129,65},{193,129... | collective-permute-start | bytes 614408 | tf_op jit(solution)/shard_map/ppermute | solution.py:43

commit v7 on v6

--- a/solution.py
+++ b/solution.py
@@ -38,9 +38,8 @@
     return send(value, lambda y, z, c: (y, z, 1 - c))
 
 
-def send_layer(value, steps):
-    count = lax.axis_size("layer")
-    return lax.ppermute(value, "layer", [(s, (s + steps) % count) for s in range(count)])
+def trade(value, mask):
+    return lax.ppermute(value, "layer", [(s, s ^ mask) for s in range(lax.axis_size("layer"))])
 
 
 def chip_rows(value, core):
@@ -215,7 +214,7 @@
             ],
             out_specs=[
                 pl.BlockSpec(
-                    (1, feats, width), lambda k, at: (lax.rem(at[0] - k + layers, layers), 0, 0)
+                    (1, feats, width), lambda k, at: (at[0] ^ k, 0, 0)
                 ),
                 pl.BlockSpec((count, feats), lambda k, at: (0, 0)),
             ],
@@ -336,7 +335,7 @@
             piece = own_ref[shard * 16 : shard * 16 + 16, :]
             for k, ref in zip(ORDER, came):
                 part = unpacked(slot_ref, 0, shard, ref).astype(F32)
-                piece = piece + jnp.where(layer_ref[0] + k < layers, part, 0.0)
+                piece = piece + jnp.where((layer_ref[0] ^ k) > layer_ref[0], part, 0.0)
             pieces.append(piece)
         total = jnp.concatenate(pieces)
         total = jnp.where(on_ref[...] > 0, total, 0.0)
@@ -349,7 +348,7 @@
         loss = jnp.zeros_like(sums[0])
         for s in range(layers):
             for k in range(layers):
-                mine = lax.rem(layer_ref[0] + (0, *ORDER)[k], layers) == s
+                mine = (layer_ref[0] ^ (0, *ORDER)[k]) == s
                 loss = loss + jnp.where(mine, sums[k], 0.0)
         loss_ref[...] = loss[:, :1] * (0.5 / count)
 
@@ -406,7 +405,7 @@
     hit = jnp.any(active == latent, axis=2)
     hit = jnp.stack(
         [
-            lax.dynamic_index_in_dim(hit, (layer - k) % layers, 0, keepdims=False)
+            lax.dynamic_index_in_dim(hit, layer ^ k, 0, keepdims=False)
             for k in range(layers)
         ]
     )
@@ -416,7 +415,7 @@
     every = jnp.arange(Y * Z)
     before = every[None, :] <= every[:, None]
     slot = jnp.sum(jnp.where(before[None] & live[:, None, :], 1, 0), axis=2, dtype=jnp.int32) - 1
-    known = live & (layer >= jnp.arange(layers))[:, None]
+    known = live & (layer >= layer ^ jnp.arange(layers))[:, None]
     slot = jnp.where(known, jnp.minimum(slot, CAP * 4 - 1), -1)
     source = jnp.sum(
         jnp.where(slot[:, None, :] == jnp.arange(CAP * 4)[None, :, None], every, 0),
@@ -429,14 +428,14 @@
     )
     decoder = jnp.concatenate(
         [
-            lax.dynamic_index_in_dim(dec[:, 0], (layer - k) % layers, 0, keepdims=False)
+            lax.dynamic_index_in_dim(dec[:, 0], layer ^ k, 0, keepdims=False)
             for k in range(layers)
         ]
     )
     goal = chip_rows(target[0], core)
 
     packed, codes, on = encode(slot, source, enc_weight[0], enc_bias, rows)
-    came = [send_layer(packed, k) for k in ORDER]
+    came = [trade(packed, k) for k in ORDER]
     turned, token = turn(rows, packed)
     goal, token = lax.optimization_barrier((goal, token))
     partial, sources = zip(
@@ -445,7 +444,7 @@
     errors = (collect(partial, core) - goal.astype(F32)).astype(BF)
     errors = spread_y(spread_z(errors, core))
     away = back(place, source, layers, decoder, errors)
-    came = [send_layer(message, -k) for k, message in zip(ORDER, away)]
+    came = [trade(message, k) for k, message in zip(ORDER, away)]
     dec_grad, own = dec_gradient(layer, layers, *sources, decoder, errors)
     enc_grad, bias_grad, loss = enc_gradient(layer, slot, turned, on, own, away[0], came)
     loss = loss[0, 0]

time: 127 us -> 127 us (level)
  starting transfers between devices: 58.3 us -> 55.6 us
  waiting for transfers between devices: 45.8 us -> 48.4 us
    ppermute x6, waiting for transfers between devices: 10.3 us -> 13 us  [trade(): lax.ppermute(value, 'layer', [(s, s ^ mask) for s in range(lax.axis_size(...]
    ppermute x6, starting transfers between devices: 9.68 us -> 7.33 us  [trade(): lax.ppermute(value, 'layer', [(s, s ^ mask) for s in range(lax.axis_size(...]
where the time goes in v7:
time: 127 us; the launch traced here: 126 us
  starting transfers between devices  55.6 us (44%)
  waiting for transfers between devices  48.4 us (38%)
  Pallas kernels  14.8 us (12%)
  other arithmetic  3.99 us (3%)
  local copies, waits for them, and re-layouts  2.41 us (2%)
    ppermute x34, starting transfers between devices, send(): return lax.ppermute(value, 'latent', pairs(move, cores))  48.3 us
    ppermute x34, waiting for transfers between devices, send(): return lax.ppermute(value, 'latent', pairs(move, cores))  35.4 us
    ppermute x6, waiting for transfers between devices, trade(): lax.ppermute(value, 'layer', [(s, s ^ mask) for s in range(lax.axis_size(...  13 us
    ppermute x6, starting transfers between devices, trade(): lax.ppermute(value, 'layer', [(s, s ^ mask) for s in range(lax.axis_size(...  7.33 us
    pallas_call x1, Pallas kernels, dec_gradient(): pl.pallas_call(dec_gradient_kernel, grid_spec=pltpu.PrefetchScalarGridSpe...  4.76 us
    pallas_call x2, Pallas kernels, decode(): pl.pallas_call(functools.partial(decode_kernel, half), in_specs=specs(1,...  3.39 us
  transfers between devices with their start and end apart: 40, of which 24 were waited for; matrix products, arithmetic and copies ran while one was open for 4% of the time, Pallas kernels for 7%

profile of v7, /device:TPU:1, one launch (start us, length us, event | category | flops | bytes accessed | tf_op | source)
XLA Modules:
  0.0 126.2 jit_solution(3749962962316615551)
XLA Ops:
  0.6 3.3 %collective-permute-start = (bf16[8,1792]{1,0:T(8,128)(2,1)}, bf16[8,1792]{1,0:T(8,128)(2,1)S(1)}, u32[]{:S(2)}, u32[]{:S(2)}) collective-permute-start(bf16[8,1792]{1,0:T(8,128)(2,1)} %bitcast.18), channel_id=1, source_target_pairs={{0,1},{1,0},{2,3},{3,2},{4,5},{5,4},{6,7},{7,6},{8,9},{9,8},{10,11... | collective-permute-start | bytes 86024 | tf_op jit(solution)/shard_map/ppermute | solution.py:34
  4.0 1.0 collective-permute-done
  5.0 0.8 maximum_select_fusion
  5.9 7.1 %collective-permute-start.1 = (bf16[16,1792]{1,0:T(8,128)(2,1)S(1)}, bf16[16,1792]{1,0:T(8,128)(2,1)S(1)}, u32[]{:S(2)}, u32[]{:S(2)}) collective-permute-start(bf16[16,1792]{1,0:T(8,128)(2,1)S(1)} %maximum_select_fusion), channel_id=1, source_target_pairs={{1,9},{3,11},{5,13},{7,15},{9,1},{11,3},{13,5},{15,7},{17,25},{19,... | collective-permute-start | bytes 172040 | tf_op jit(solution)/shard_map/ppermute | solution.py:34
  13.1 4.0 %collective-permute-start.3 = (bf16[16,1792]{1,0:T(8,128)(2,1)S(1)}, bf16[16,1792]{1,0:T(8,128)(2,1)S(1)}, u32[]{:S(2)}, u32[]{:S(2)}) collective-permute-start(bf16[16,1792]{1,0:T(8,128)(2,1)S(1)} %maximum_select_fusion), channel_id=1, source_target_pairs={{0,4},{1,13},{2,6},{3,15},{4,0},{5,9},{6,2},{7,11},{8,12},{9,5},{1... | collective-permute-start | bytes 172040 | tf_op jit(solution)/shard_map/ppermute | solution.py:34
  17.5 0.8 broadcast_select_fusion.1
  18.4 0.9 collective-permute-done.3
  19.3 4.1 %collective-permute-done.2 = bf16[16,1792]{1,0:T(8,128)(2,1)S(1)} collective-permute-done((bf16[16,1792]{1,0:T(8,128)(2,1)S(1)}, bf16[16,1792]{1,0:T(8,128)(2,1)S(1)}, u32[]{:S(2)}, u32[]{:S(2)}) %collective-permute-start.2) | collective-permute-done | bytes 57376 | tf_op jit(solution)/shard_map/ppermute | solution.py:34
  23.4 3.0 %collective-permute-start.5 = (bf16[64,1792]{1,0:T(8,128)(2,1)S(1)}, bf16[64,1792]{1,0:T(8,128)(2,1)S(1)}, u32[]{:S(2)}, u32[]{:S(2)}) collective-permute-start(bf16[64,1792]{1,0:T(8,128)(2,1)S(1)} %pad_maximum_fusion.1.refs_0_), channel_id=1, source_target_pairs={{0,32},{1,33},{2,34},{3,35},{4,36},{5,37},{6,38},{7,39},{8,40},{9,... | collective-permute-start | bytes 688136 | tf_op jit(solution)/shard_map/ppermute | solution.py:34
  27.1 0.9 compare_reduce_fusion
  28.6 2.3 %dynamic-slice_bitcast_fusion.3 = (bf16[256,1792]{1,0:T(8,128)(2,1)S(1)}, bf16[256,1792]{1,0:T(8,128)(2,1)S(1)}, bf16[256,1792]{1,0:T(8,128)(2,1)S(1)}, bf16[256,1792]{1,0:T(8,128)(2,1)S(1)}) fusion(bf16[4,1,256,1792]{3,2,1,0:T(8,128)(2,1)} %param.10, s32[]{:T(128)S(6)} %select_n.201, s32[]{:T(128)S(6)} %select_n.204, s32[]{:T(128)S(6)} %select_n.203, ...), kind=kLoop, calls=%fused_computation.6 | loop fusion | bytes 7340048 | tf_op jit(solution)/shard_map/jit(dynamic_index_in_dim)/squeeze | solution.py:431
  31.7 1.0 collective-permute-done.6.refs_2_
  33.3 0.8 collective-permute-done.10.refs_6_
  34.5 1.3 encode.1
  35.7 2.8 %collective-permute-start.13 = (bf16[384,256]{1,0:T(8,128)(2,1)S(1)}, bf16[384,256]{1,0:T(8,128)(2,1)S(1)}, u32[]{:S(2)}, u32[]{:S(2)}) collective-permute-start(bf16[384,256]{1,0:T(8,128)(2,1)S(1)} %get-tuple-element.29.after_ref), channel_id=1, source_target_pairs={{0,128},{64,192},{128,0},{192,64},{1,129},{65,193},{129,1},{193,65... | collective-permute-start | bytes 589832 | tf_op jit(solution)/shard_map/ppermute | solution.py:42
  38.6 0.9 collective-permute-start.14
  40.0 3.7 %collective-permute-done.13.refs_0_ = bf16[384,256]{1,0:T(8,128)(2,1)S(1)} collective-permute-done((bf16[384,256]{1,0:T(8,128)(2,1)S(1)}, bf16[384,256]{1,0:T(8,128)(2,1)S(1)}, u32[]{:S(2)}, u32[]{:S(2)}) %collective-permute-start.13) | collective-permute-done | bytes 196640 | tf_op jit(solution)/shard_map/ppermute | solution.py:42
  43.7 4.7 %collective-permute-done.14.refs_1_ = bf16[384,256]{1,0:T(8,128)(2,1)S(1)} collective-permute-done((bf16[384,256]{1,0:T(8,128)(2,1)S(1)}, bf16[384,256]{1,0:T(8,128)(2,1)S(1)}, u32[]{:S(2)}, u32[]{:S(2)}) %collective-permute-start.14) | collective-permute-done | bytes 196640 | tf_op jit(solution)/shard_map/ppermute | solution.py:42
  48.4 1.7 %decode.3 = (bf16[256,1792]{1,0:T(8,128)(2,1)S(1)}, bf16[256,1024]{1,0:T(8,128)(2,1)S(1)}) custom-call(s32[4,32]{1,0:T(4,128)S(1)} %minimum_select_fusion.slot_ref, bf16[16,128]{1,0:T(8,128)(2,1)S(1)} %get-tuple-element.34.token_ref, bf16[512,256]{1,0:T(8,128)(2,1)S(1)} %get-tuple-element.35.codes_ref, bf16[1024,1792]{1,0:T(8,128)(2,1)S(1)} %pad_maximum_fusion.weight_ref, ...), custom_call_target="tpu_custom_call" | custom-call | flops 1000 | bytes 1000 | tf_op jit(solution)/shard_map/decode/pallas_call | solution.py:313
  50.2 0.7 collective-permute-start.16
  51.1 1.7 %decode.2 = (bf16[256,1792]{1,0:T(8,128)(2,1)S(1)}, bf16[256,1024]{1,0:T(8,128)(2,1)S(1)}) custom-call(s32[4,32]{1,0:T(4,128)S(1)} %minimum_select_fusion.slot_ref, bf16[16,128]{1,0:T(8,128)(2,1)S(1)} %get-tuple-element.34.token_ref, bf16[512,256]{1,0:T(8,128)(2,1)S(1)} %get-tuple-element.35.codes_ref, bf16[1024,1792]{1,0:T(8,128)(2,1)S(1)} %pad_maximum_fusion.weight_ref, ...), custom_call_target="tpu_custom_call" | custom-call | flops 1000 | bytes 1000 | tf_op jit(solution)/shard_map/decode/pallas_call | solution.py:313
  53.2 2.1 %collective-permute-start.20 = (bf16[64,1792]{1,0:T(8,128)(2,1)S(1)}, bf16[64,1792]{1,0:T(8,128)(2,1)S(1)}, u32[]{:S(2)}, u32[]{:S(2)}) collective-permute-start(bf16[64,1792]{1,0:T(8,128)(2,1)S(1)} %get-tuple-element.69), channel_id=1, source_target_pairs={{0,48},{1,49},{2,50},{3,51},{4,52},{5,53},{6,54},{7,55},{8,56},{9,... | collective-permute-start | bytes 688136 | tf_op jit(solution)/shard_map/ppermute | solution.py:34
  55.3 1.9 %collective-permute-start.17 = (bf16[64,1792]{1,0:T(8,128)(2,1)S(1)}, bf16[64,1792]{1,0:T(8,128)(2,1)S(1)}, u32[]{:S(2)}, u32[]{:S(2)}) collective-permute-start(bf16[64,1792]{1,0:T(8,128)(2,1)S(1)} %slice.54), channel_id=1, source_target_pairs={{0,32},{1,33},{2,34},{3,35},{4,36},{5,37},{6,38},{7,39},{8,40},{9,... | collective-permute-start | bytes 688136 | tf_op jit(solution)/shard_map/ppermute | solution.py:34
  57.3 4.1 %collective-permute-done.20 = bf16[64,1792]{1,0:T(8,128)(2,1)S(1)} collective-permute-done((bf16[64,1792]{1,0:T(8,128)(2,1)S(1)}, bf16[64,1792]{1,0:T(8,128)(2,1)S(1)}, u32[]{:S(2)}, u32[]{:S(2)}) %collective-permute-start.20) | collective-permute-done | bytes 229408 | tf_op jit(solution)/shard_map/ppermute | solution.py:34
  61.8 5.3 %collective-permute-done.17 = bf16[64,1792]{1,0:T(8,128)(2,1)S(1)} collective-permute-done((bf16[64,1792]{1,0:T(8,128)(2,1)S(1)}, bf16[64,1792]{1,0:T(8,128)(2,1)S(1)}, u32[]{:S(2)}, u32[]{:S(2)}) %collective-permute-start.17) | collective-permute-done | bytes 229408 | tf_op jit(solution)/shard_map/ppermute | solution.py:34
  67.9 2.4 %collective-permute-start.23 = (bf16[16,1792]{1,0:T(8,128)(2,1)S(1)}, bf16[16,1792]{1,0:T(8,128)(2,1)S(1)}, u32[]{:S(2)}, u32[]{:S(2)}) collective-permute-start(bf16[16,1792]{1,0:T(8,128)(2,1)S(1)} %get-tuple-element.72), channel_id=1, source_target_pairs={{0,4},{1,13},{2,6},{3,15},{4,0},{5,9},{6,2},{7,11},{8,12},{9,5},{1... | collective-permute-start | bytes 172040 | tf_op jit(solution)/shard_map/ppermute | solution.py:34
  70.2 2.0 %collective-permute-start.22 = (bf16[16,1792]{1,0:T(8,128)(2,1)S(1)}, bf16[16,1792]{1,0:T(8,128)(2,1)S(1)}, u32[]{:S(2)}, u32[]{:S(2)}) collective-permute-start(bf16[16,1792]{1,0:T(8,128)(2,1)S(1)} %get-tuple-element.73), channel_id=1, source_target_pairs={{0,2},{1,11},{2,0},{3,9},{4,6},{5,15},{6,4},{7,13},{8,10},{9,3},{1... | collective-permute-start | bytes 172040 | tf_op jit(solution)/shard_map/ppermute | solution.py:34
  72.2 5.0 %collective-permute-start.21 = (bf16[16,1792]{1,0:T(8,128)(2,1)S(1)}, bf16[16,1792]{1,0:T(8,128)(2,1)S(1)}, u32[]{:S(2)}, u32[]{:S(2)}) collective-permute-start(bf16[16,1792]{1,0:T(8,128)(2,1)S(1)} %get-tuple-element.70), channel_id=1, source_target_pairs={{1,9},{3,11},{5,13},{7,15},{9,1},{11,3},{13,5},{15,7},{17,25},{19,... | collective-permute-start | bytes 172040 | tf_op jit(solution)/shard_map/ppermute | solution.py:34
  77.6 3.5 %collective-permute-done.21 = bf16[16,1792]{1,0:T(8,128)(2,1)S(1)} collective-permute-done((bf16[16,1792]{1,0:T(8,128)(2,1)S(1)}, bf16[16,1792]{1,0:T(8,128)(2,1)S(1)}, u32[]{:S(2)}, u32[]{:S(2)}) %collective-permute-start.21) | collective-permute-done | bytes 57376 | tf_op jit(solution)/shard_map/ppermute | solution.py:34
  81.2 1.2 collective-permute-done.25
  82.5 5.1 %collective-permute-start.26 = (bf16[16,1792]{1,0:T(8,128)(2,1)S(1)}, bf16[16,1792]{1,0:T(8,128)(2,1)S(1)}, u32[]{:S(2)}, u32[]{:S(2)}) collective-permute-start(bf16[16,1792]{1,0:T(8,128)(2,1)S(1)} %subtract_convert_fusion), channel_id=1, source_target_pairs={{1,9},{3,11},{5,13},{7,15},{9,1},{11,3},{13,5},{15,7},{17,25},{19,... | collective-permute-start | bytes 172040 | tf_op jit(solution)/shard_map/ppermute | solution.py:34
  88.1 3.3 %collective-permute-start.28 = (bf16[16,1792]{1,0:T(8,128)(2,1)S(1)}, bf16[16,1792]{1,0:T(8,128)(2,1)S(1)}, u32[]{:S(2)}, u32[]{:S(2)}) collective-permute-start(bf16[16,1792]{1,0:T(8,128)(2,1)S(1)} %subtract_convert_fusion), channel_id=1, source_target_pairs={{0,4},{1,13},{2,6},{3,15},{4,0},{5,9},{6,2},{7,11},{8,12},{9,5},{1... | collective-permute-start | bytes 172040 | tf_op jit(solution)/shard_map/ppermute | solution.py:34
  91.4 1.1 collective-permute-start.27
  92.5 1.4 %collective-permute-done.29 = bf16[16,1792]{1,0:T(8,128)(2,1)S(1)} collective-permute-done((bf16[16,1792]{1,0:T(8,128)(2,1)S(1)}, bf16[16,1792]{1,0:T(8,128)(2,1)S(1)}, u32[]{:S(2)}, u32[]{:S(2)}) %collective-permute-start.29) | collective-permute-done | bytes 57376 | tf_op jit(solution)/shard_map/ppermute | solution.py:34
  93.9 3.5 %collective-permute-done.27 = bf16[16,1792]{1,0:T(8,128)(2,1)S(1)} collective-permute-done((bf16[16,1792]{1,0:T(8,128)(2,1)S(1)}, bf16[16,1792]{1,0:T(8,128)(2,1)S(1)}, u32[]{:S(2)}, u32[]{:S(2)}) %collective-permute-start.27) | collective-permute-done | bytes 57376 | tf_op jit(solution)/shard_map/ppermute | solution.py:34
  97.5 1.4 %collective-permute-start.30 = (bf16[64,1792]{1,0:T(8,128)(2,1)S(1)}, bf16[64,1792]{1,0:T(8,128)(2,1)S(1)}, u32[]{:S(2)}, u32[]{:S(2)}) collective-permute-start(bf16[64,1792]{1,0:T(8,128)(2,1)S(1)} %pad_maximum_fusion.2.refs_0_), channel_id=1, source_target_pairs={{0,32},{1,33},{2,34},{3,35},{4,36},{5,37},{6,38},{7,39},{8,40},{9,... | collective-permute-start | bytes 688136 | tf_op jit(solution)/shard_map/ppermute | solution.py:34
  98.9 1.3 %collective-permute-start.31 = (bf16[64,1792]{1,0:T(8,128)(2,1)S(1)}, bf16[64,1792]{1,0:T(8,128)(2,1)S(1)}, u32[]{:S(2)}, u32[]{:S(2)}) collective-permute-start(bf16[64,1792]{1,0:T(8,128)(2,1)S(1)} %pad_maximum_fusion.2.refs_0_), channel_id=1, source_target_pairs={{0,16},{1,17},{2,18},{3,19},{4,20},{5,21},{6,22},{7,23},{8,24},{9,... | collective-permute-start | bytes 688136 | tf_op jit(solution)/shard_map/ppermute | solution.py:34
  100.2 0.6 collective-permute-start.32
  100.8 3.3 %collective-permute-done.30.refs_1_ = bf16[64,1792]{1,0:T(8,128)(2,1)S(1)} collective-permute-done((bf16[64,1792]{1,0:T(8,128)(2,1)S(1)}, bf16[64,1792]{1,0:T(8,128)(2,1)S(1)}, u32[]{:S(2)}, u32[]{:S(2)}) %collective-permute-start.30) | collective-permute-done | bytes 229408 | tf_op jit(solution)/shard_map/ppermute | solution.py:34
  104.1 2.0 %collective-permute-done.31.refs_2_ = bf16[64,1792]{1,0:T(8,128)(2,1)S(1)} collective-permute-done((bf16[64,1792]{1,0:T(8,128)(2,1)S(1)}, bf16[64,1792]{1,0:T(8,128)(2,1)S(1)}, u32[]{:S(2)}, u32[]{:S(2)}) %collective-permute-start.31) | collective-permute-done | bytes 229408 | tf_op jit(solution)/shard_map/ppermute | solution.py:34
  106.0 0.8 collective-permute-done.32.refs_3_
  107.5 0.8 collective-permute-done.36.refs_7_
  108.3 2.5 %back.1 = (bf16[400,256]{1,0:T(8,128)(2,1)S(1)}, bf16[400,256]{1,0:T(8,128)(2,1)S(1)}, bf16[400,256]{1,0:T(8,128)(2,1)S(1)}) custom-call(s32[32]{0:T(128)S(1)} %select_reduce_fusion.2.place_ref, s32[4,24]{1,0:T(4,128)S(1)} %broadcast_minimum_fusion.source_ref, bf16[1024,1792]{1,0:T(8,128)(2,1)S(1)} %pad_maximum_fusion.weight_ref, ...), custom_call_target="tpu_custom_call" | custom-call | flops 1000 | bytes 1000 | tf_op jit(solution)/shard_map/back/pallas_call | solution.py:279
  110.8 1.8 %collective-permute-start.37 = (bf16[400,256]{1,0:T(8,128)(2,1)S(1)}, bf16[400,256]{1,0:T(8,128)(2,1)S(1)}, u32[]{:S(2)}, u32[]{:S(2)}) collective-permute-start(bf16[400,256]{1,0:T(8,128)(2,1)S(1)} %get-tuple-element.43.away_ref), channel_id=1, source_target_pairs={{0,128},{64,192},{128,0},{192,64},{1,129},{65,193},{129,1},{193,65... | collective-permute-start | bytes 614408 | tf_op jit(solution)/shard_map/ppermute | solution.py:42
  112.6 1.8 %collective-permute-start.38 = (bf16[400,256]{1,0:T(8,128)(2,1)S(1)}, bf16[400,256]{1,0:T(8,128)(2,1)S(1)}, u32[]{:S(2)}, u32[]{:S(2)}) collective-permute-start(bf16[400,256]{1,0:T(8,128)(2,1)S(1)} %get-tuple-element.44), channel_id=1, source_target_pairs={{0,192},{64,128},{128,64},{192,0},{1,193},{65,129},{129,65},{193,1... | collective-permute-start | bytes 614408 | tf_op jit(solution)/shard_map/ppermute | solution.py:42
  114.4 4.8 %dec_gradient.1 = (bf16[4,256,1792]{2,1,0:T(8,128)(2,1)}, f32[512,256]{1,0:T(8,128)S(1)}) custom-call(s32[1]{0:T(128)} %bitcast.layer_ref, bf16[256,1024]{1,0:T(8,128)(2,1)S(1)} %get-tuple-element.37.first_ref, bf16[256,1024]{1,0:T(8,128)(2,1)S(1)} %get-tuple-element.38.second_ref, bf16[1024,1792]{1,0:T(8,128)(2,1)S(1)} %pad_maximum_fusion.weight_ref, ...), custom_call_target="tpu_custom_call" | custom-call | flops 1000 | bytes 1000 | tf_op jit(solution)/shard_map/dec_gradient/pallas_call | solution.py:204
  119.2 4.6 %collective-permute-done.38.refs_1_ = bf16[400,256]{1,0:T(8,128)(2,1)S(1)} collective-permute-done((bf16[400,256]{1,0:T(8,128)(2,1)S(1)}, bf16[400,256]{1,0:T(8,128)(2,1)S(1)}, u32[]{:S(2)}, u32[]{:S(2)}) %collective-permute-start.38) | collective-permute-done | bytes 204832 | tf_op jit(solution)/shard_map/ppermute | solution.py:42
  123.8 2.4 %enc_gradient.1 = (bf16[1792,256]{1,0:T(8,128)(2,1)}, f32[1,256]{1,0:T(1,128)}, f32[1,1]{1,0:T(1,128)}) custom-call(s32[1]{0:T(128)} %bitcast.layer_ref, s32[4,32]{1,0:T(4,128)S(1)} %minimum_select_fusion.slot_ref, bf16[1792,512]{1,0:T(8,128)(2,1)S(1)} %get-tuple-element.30.rows_ref, bf16[512,256]{1,0:T(8,128)(2,1)S(1)} %get-tuple-element.31.on_ref, ...), custom_call_target="tpu_custom_call" | custom-call | flops 1000 | bytes 1000 | tf_op jit(solution)/shard_map/enc_gradient/pallas_call | solution.py:364
  (74 shorter events, 8.1 us)
Async XLA Ops:
  0.6 4.4 %collective-permute-start = (bf16[8,1792]{1,0:T(8,128)(2,1)}, bf16[8,1792]{1,0:T(8,128)(2,1)S(1)}, u32[]{:S(2)}, u32[]{:S(2)}) collective-permute-start(bf16[8,1792]{1,0:T(8,128)(2,1)} %bitcast.18), channel_id=1, source_target_pairs={{0,1},{1,0},{2,3},{3,2},{4,5},{5,4},{6,7},{7,6},{8,9},{9,8},{10,11... | collective-permute-start | bytes 86024 | tf_op jit(solution)/shard_map/ppermute | solution.py:34
  5.9 11.7 %collective-permute-start.1 = (bf16[16,1792]{1,0:T(8,128)(2,1)S(1)}, bf16[16,1792]{1,0:T(8,128)(2,1)S(1)}, u32[]{:S(2)}, u32[]{:S(2)}) collective-permute-start(bf16[16,1792]{1,0:T(8,128)(2,1)S(1)} %maximum_select_fusion), channel_id=1, source_target_pairs={{1,9},{3,11},{5,13},{7,15},{9,1},{11,3},{13,5},{15,7},{17,25},{19,... | collective-permute-start | bytes 172040 | tf_op jit(solution)/shard_map/ppermute | solution.py:34
  13.0 5.4 %collective-permute-start.4 = (bf16[16,1792]{1,0:T(8,128)(2,1)S(1)}, bf16[16,1792]{1,0:T(8,128)(2,1)S(1)}, u32[]{:S(2)}, u32[]{:S(2)}) collective-permute-start(bf16[16,1792]{1,0:T(8,128)(2,1)S(1)} %maximum_select_fusion), channel_id=1, source_target_pairs={{0,6},{1,15},{2,4},{3,13},{4,2},{5,11},{6,0},{7,9},{8,14},{9,7},{1... | collective-permute-start | bytes 172040 | tf_op jit(solution)/shard_map/ppermute | solution.py:34
  13.1 6.2 %collective-permute-start.3 = (bf16[16,1792]{1,0:T(8,128)(2,1)S(1)}, bf16[16,1792]{1,0:T(8,128)(2,1)S(1)}, u32[]{:S(2)}, u32[]{:S(2)}) collective-permute-start(bf16[16,1792]{1,0:T(8,128)(2,1)S(1)} %maximum_select_fusion), channel_id=1, source_target_pairs={{0,4},{1,13},{2,6},{3,15},{4,0},{5,9},{6,2},{7,11},{8,12},{9,5},{1... | collective-permute-start | bytes 172040 | tf_op jit(solution)/shard_map/ppermute | solution.py:34
  17.1 6.3 %collective-permute-start.2 = (bf16[16,1792]{1,0:T(8,128)(2,1)S(1)}, bf16[16,1792]{1,0:T(8,128)(2,1)S(1)}, u32[]{:S(2)}, u32[]{:S(2)}) collective-permute-start(bf16[16,1792]{1,0:T(8,128)(2,1)S(1)} %maximum_select_fusion), channel_id=1, source_target_pairs={{0,2},{1,11},{2,0},{3,9},{4,6},{5,15},{6,4},{7,13},{8,10},{9,3},{1... | collective-permute-start | bytes 172040 | tf_op jit(solution)/shard_map/ppermute | solution.py:34
  23.4 8.2 %collective-permute-start.5 = (bf16[64,1792]{1,0:T(8,128)(2,1)S(1)}, bf16[64,1792]{1,0:T(8,128)(2,1)S(1)}, u32[]{:S(2)}, u32[]{:S(2)}) collective-permute-start(bf16[64,1792]{1,0:T(8,128)(2,1)S(1)} %pad_maximum_fusion.1.refs_0_), channel_id=1, source_target_pairs={{0,32},{1,33},{2,34},{3,35},{4,36},{5,37},{6,38},{7,39},{8,40},{9,... | collective-permute-start | bytes 688136 | tf_op jit(solution)/shard_map/ppermute | solution.py:34
  26.4 6.3 %collective-permute-start.6 = (bf16[64,1792]{1,0:T(8,128)(2,1)S(1)}, bf16[64,1792]{1,0:T(8,128)(2,1)S(1)}, u32[]{:S(2)}, u32[]{:S(2)}) collective-permute-start(bf16[64,1792]{1,0:T(8,128)(2,1)S(1)} %pad_maximum_fusion.1.refs_0_), channel_id=1, source_target_pairs={{0,16},{1,17},{2,18},{3,19},{4,20},{5,21},{6,22},{7,23},{8,24},{9,... | collective-permute-start | bytes 688136 | tf_op jit(solution)/shard_map/ppermute | solution.py:34
  26.8 6.1 %collective-permute-start.7 = (bf16[64,1792]{1,0:T(8,128)(2,1)S(1)}, bf16[64,1792]{1,0:T(8,128)(2,1)S(1)}, u32[]{:S(2)}, u32[]{:S(2)}) collective-permute-start(bf16[64,1792]{1,0:T(8,128)(2,1)S(1)} %pad_maximum_fusion.1.refs_0_), channel_id=1, source_target_pairs={{0,48},{1,49},{2,50},{3,51},{4,52},{5,53},{6,54},{7,55},{8,56},{9,... | collective-permute-start | bytes 688136 | tf_op jit(solution)/shard_map/ppermute | solution.py:34
  27.1 6.2 %collective-permute-start.8 = (bf16[64,1792]{1,0:T(8,128)(2,1)S(1)}, bf16[64,1792]{1,0:T(8,128)(2,1)S(1)}, u32[]{:S(2)}, u32[]{:S(2)}) collective-permute-start(bf16[64,1792]{1,0:T(8,128)(2,1)S(1)} %pad_maximum_fusion.1.refs_0_), channel_id=1, source_target_pairs={{0,1},{1,0},{2,3},{3,2},{4,5},{5,4},{6,7},{7,6},{8,9},{9,8},{10,11... | collective-permute-start | bytes 688136 | tf_op jit(solution)/shard_map/ppermute | solution.py:34
  28.0 11.4 %collective-permute-start.12 = (bf16[8,1792]{1,0:T(8,128)(2,1)}, bf16[8,1792]{1,0:T(8,128)(2,1)S(1)}, u32[]{:S(2)}, u32[]{:S(2)}) collective-permute-start(bf16[8,1792]{1,0:T(8,128)(2,1)} %bitcast.21), channel_id=1, source_target_pairs={{0,1},{1,0},{2,3},{3,2},{4,5},{5,4},{6,7},{7,6},{8,9},{9,8},{10,11... | collective-permute-start | bytes 86024 | tf_op jit(solution)/shard_map/ppermute | solution.py:34
  31.0 3.5 %copy-start = (bf16[1,1792,256]{2,1,0:T(8,128)(2,1)S(1)}, bf16[1,1792,256]{2,1,0:T(8,128)(2,1)}, u32[]{:S(2)}) copy-start(bf16[1,1792,256]{2,1,0:T(8,128)(2,1)} %param.8) | copy-start | bytes 2752516
  31.0 3.5 %copy-start.1 = (f32[1,256]{1,0:T(1,128)S(1)}, f32[1,256]{1,0:T(1,128)}, u32[]{:S(2)}) copy-start(f32[1,256]{1,0:T(1,128)} %bias_ref.1) | copy-start | bytes 3076
  31.0 8.4 %copy-start.2 = (bf16[1,8,1792]{2,1,0:T(8,128)(2,1)S(1)}, bf16[1,8,1792]{2,1,0:T(8,128)(2,1)}, u32[]{:S(2)}) copy-start(bf16[1,8,1792]{2,1,0:T(8,128)(2,1)} %param.7) | copy-start | bytes 86020
  31.6 1.7 %collective-permute-start.9 = (bf16[64,1792]{1,0:T(8,128)(2,1)S(1)}, bf16[64,1792]{1,0:T(8,128)(2,1)S(1)}, u32[]{:S(2)}, u32[]{:S(2)}) collective-permute-start(bf16[64,1792]{1,0:T(8,128)(2,1)S(1)} %collective-permute-done.5.refs_1_), channel_id=1, source_target_pairs={{0,1},{1,0},{2,3},{3,2},{4,5},{5,4},{6,7},{7,6},{8,9},{9,8},{10,11... | collective-permute-start | bytes 688136 | tf_op jit(solution)/shard_map/ppermute | solution.py:34
  32.7 1.5 %collective-permute-start.10 = (bf16[64,1792]{1,0:T(8,128)(2,1)S(1)}, bf16[64,1792]{1,0:T(8,128)(2,1)S(1)}, u32[]{:S(2)}, u32[]{:S(2)}) collective-permute-start(bf16[64,1792]{1,0:T(8,128)(2,1)S(1)} %collective-permute-done.6.refs_2_), channel_id=1, source_target_pairs={{0,1},{1,0},{2,3},{3,2},{4,5},{5,4},{6,7},{7,6},{8,9},{9,8},{10,11... | collective-permute-start | bytes 688136 | tf_op jit(solution)/shard_map/ppermute | solution.py:34
  32.8 1.6 %collective-permute-start.11 = (bf16[64,1792]{1,0:T(8,128)(2,1)S(1)}, bf16[64,1792]{1,0:T(8,128)(2,1)S(1)}, u32[]{:S(2)}, u32[]{:S(2)}) collective-permute-start(bf16[64,1792]{1,0:T(8,128)(2,1)S(1)} %collective-permute-done.7.refs_3_), channel_id=1, source_target_pairs={{0,1},{1,0},{2,3},{3,2},{4,5},{5,4},{6,7},{7,6},{8,9},{9,8},{10,11... | collective-permute-start | bytes 688136 | tf_op jit(solution)/shard_map/ppermute | solution.py:34
  35.7 7.9 %collective-permute-start.13 = (bf16[384,256]{1,0:T(8,128)(2,1)S(1)}, bf16[384,256]{1,0:T(8,128)(2,1)S(1)}, u32[]{:S(2)}, u32[]{:S(2)}) collective-permute-start(bf16[384,256]{1,0:T(8,128)(2,1)S(1)} %get-tuple-element.29.after_ref), channel_id=1, source_target_pairs={{0,128},{64,192},{128,0},{192,64},{1,129},{65,193},{129,1},{193,65... | collective-permute-start | bytes 589832 | tf_op jit(solution)/shard_map/ppermute | solution.py:42
  38.6 9.8 %collective-permute-start.14 = (bf16[384,256]{1,0:T(8,128)(2,1)S(1)}, bf16[384,256]{1,0:T(8,128)(2,1)S(1)}, u32[]{:S(2)}, u32[]{:S(2)}) collective-permute-start(bf16[384,256]{1,0:T(8,128)(2,1)S(1)} %get-tuple-element.29.after_ref), channel_id=1, source_target_pairs={{0,192},{64,128},{128,64},{192,0},{1,193},{65,129},{129,65},{193,1... | collective-permute-start | bytes 589832 | tf_op jit(solution)/shard_map/ppermute | solution.py:42
  39.4 8.9 %collective-permute-start.15 = (bf16[384,256]{1,0:T(8,128)(2,1)S(1)}, bf16[384,256]{1,0:T(8,128)(2,1)S(1)}, u32[]{:S(2)}, u32[]{:S(2)}) collective-permute-start(bf16[384,256]{1,0:T(8,128)(2,1)S(1)} %get-tuple-element.29.after_ref), channel_id=1, source_target_pairs={{0,64},{64,0},{128,192},{192,128},{1,65},{65,1},{129,193},{193,129... | collective-permute-start | bytes 589832 | tf_op jit(solution)/shard_map/ppermute | solution.py:42
  50.2 2.7 %collective-permute-start.16 = (bf16[128,1792]{1,0:T(8,128)(2,1)S(1)}, bf16[128,1792]{1,0:T(8,128)(2,1)S(1)}, u32[]{:S(2)}, u32[]{:S(2)}) collective-permute-start(bf16[128,1792]{1,0:T(8,128)(2,1)S(1)} %get-tuple-element.66), channel_id=1, source_target_pairs={{0,1},{1,0},{2,3},{3,2},{4,5},{5,4},{6,7},{7,6},{8,9},{9,8},{10,11... | collective-permute-start | bytes 1376264 | tf_op jit(solution)/shard_map/ppermute | solution.py:34
  50.8 2.1 %collective-permute-start.18 = (bf16[128,1792]{1,0:T(8,128)(2,1)S(1)}, bf16[128,1792]{1,0:T(8,128)(2,1)S(1)}, u32[]{:S(2)}, u32[]{:S(2)}) collective-permute-start(bf16[128,1792]{1,0:T(8,128)(2,1)S(1)} %get-tuple-element.67), channel_id=1, source_target_pairs={{0,1},{1,0},{2,3},{3,2},{4,5},{5,4},{6,7},{7,6},{8,9},{9,8},{10,11... | collective-permute-start | bytes 1376264 | tf_op jit(solution)/shard_map/ppermute | solution.py:34
  53.2 8.1 %collective-permute-start.20 = (bf16[64,1792]{1,0:T(8,128)(2,1)S(1)}, bf16[64,1792]{1,0:T(8,128)(2,1)S(1)}, u32[]{:S(2)}, u32[]{:S(2)}) collective-permute-start(bf16[64,1792]{1,0:T(8,128)(2,1)S(1)} %get-tuple-element.69), channel_id=1, source_target_pairs={{0,48},{1,49},{2,50},{3,51},{4,52},{5,53},{6,54},{7,55},{8,56},{9,... | collective-permute-start | bytes 688136 | tf_op jit(solution)/shard_map/ppermute | solution.py:34
  55.3 6.5 %collective-permute-start.19 = (bf16[64,1792]{1,0:T(8,128)(2,1)S(1)}, bf16[64,1792]{1,0:T(8,128)(2,1)S(1)}, u32[]{:S(2)}, u32[]{:S(2)}) collective-permute-start(bf16[64,1792]{1,0:T(8,128)(2,1)S(1)} %get-tuple-element.68), channel_id=1, source_target_pairs={{0,16},{1,17},{2,18},{3,19},{4,20},{5,21},{6,22},{7,23},{8,24},{9,... | collective-permute-start | bytes 688136 | tf_op jit(solution)/shard_map/ppermute | solution.py:34
  55.3 11.7 %collective-permute-start.17 = (bf16[64,1792]{1,0:T(8,128)(2,1)S(1)}, bf16[64,1792]{1,0:T(8,128)(2,1)S(1)}, u32[]{:S(2)}, u32[]{:S(2)}) collective-permute-start(bf16[64,1792]{1,0:T(8,128)(2,1)S(1)} %slice.54), channel_id=1, source_target_pairs={{0,32},{1,33},{2,34},{3,35},{4,36},{5,37},{6,38},{7,39},{8,40},{9,... | collective-permute-start | bytes 688136 | tf_op jit(solution)/shard_map/ppermute | solution.py:34
  67.2 10.0 %collective-permute-start.24 = (bf16[16,1792]{1,0:T(8,128)(2,1)S(1)}, bf16[16,1792]{1,0:T(8,128)(2,1)S(1)}, u32[]{:S(2)}, u32[]{:S(2)}) collective-permute-start(bf16[16,1792]{1,0:T(8,128)(2,1)S(1)} %get-tuple-element.71), channel_id=1, source_target_pairs={{0,6},{1,15},{2,4},{3,13},{4,2},{5,11},{6,0},{7,9},{8,14},{9,7},{1... | collective-permute-start | bytes 172040 | tf_op jit(solution)/shard_map/ppermute | solution.py:34
  67.9 9.4 %collective-permute-start.23 = (bf16[16,1792]{1,0:T(8,128)(2,1)S(1)}, bf16[16,1792]{1,0:T(8,128)(2,1)S(1)}, u32[]{:S(2)}, u32[]{:S(2)}) collective-permute-start(bf16[16,1792]{1,0:T(8,128)(2,1)S(1)} %get-tuple-element.72), channel_id=1, source_target_pairs={{0,4},{1,13},{2,6},{3,15},{4,0},{5,9},{6,2},{7,11},{8,12},{9,5},{1... | collective-permute-start | bytes 172040 | tf_op jit(solution)/shard_map/ppermute | solution.py:34
  70.2 7.4 %collective-permute-start.22 = (bf16[16,1792]{1,0:T(8,128)(2,1)S(1)}, bf16[16,1792]{1,0:T(8,128)(2,1)S(1)}, u32[]{:S(2)}, u32[]{:S(2)}) collective-permute-start(bf16[16,1792]{1,0:T(8,128)(2,1)S(1)} %get-tuple-element.73), channel_id=1, source_target_pairs={{0,2},{1,11},{2,0},{3,9},{4,6},{5,15},{6,4},{7,13},{8,10},{9,3},{1... | collective-permute-start | bytes 172040 | tf_op jit(solution)/shard_map/ppermute | solution.py:34
  72.2 8.8 %collective-permute-start.21 = (bf16[16,1792]{1,0:T(8,128)(2,1)S(1)}, bf16[16,1792]{1,0:T(8,128)(2,1)S(1)}, u32[]{:S(2)}, u32[]{:S(2)}) collective-permute-start(bf16[16,1792]{1,0:T(8,128)(2,1)S(1)} %get-tuple-element.70), channel_id=1, source_target_pairs={{1,9},{3,11},{5,13},{7,15},{9,1},{11,3},{13,5},{15,7},{17,25},{19,... | collective-permute-start | bytes 172040 | tf_op jit(solution)/shard_map/ppermute | solution.py:34
  81.1 1.3 %collective-permute-start.25 = (bf16[16,1792]{1,0:T(8,128)(2,1)S(1)}, bf16[16,1792]{1,0:T(8,128)(2,1)S(1)}, u32[]{:S(2)}, u32[]{:S(2)}) collective-permute-start(bf16[16,1792]{1,0:T(8,128)(2,1)S(1)} %add_convert_fusion.3), channel_id=1, source_target_pairs={{0,1},{1,0},{2,3},{3,2},{4,5},{5,4},{6,7},{7,6},{8,9},{9,8},{10,11... | collective-permute-start | bytes 172040 | tf_op jit(solution)/shard_map/ppermute | solution.py:34
  82.5 10.1 %collective-permute-start.26 = (bf16[16,1792]{1,0:T(8,128)(2,1)S(1)}, bf16[16,1792]{1,0:T(8,128)(2,1)S(1)}, u32[]{:S(2)}, u32[]{:S(2)}) collective-permute-start(bf16[16,1792]{1,0:T(8,128)(2,1)S(1)} %subtract_convert_fusion), channel_id=1, source_target_pairs={{1,9},{3,11},{5,13},{7,15},{9,1},{11,3},{13,5},{15,7},{17,25},{19,... | collective-permute-start | bytes 172040 | tf_op jit(solution)/shard_map/ppermute | solution.py:34
  87.5 6.4 %collective-permute-start.29 = (bf16[16,1792]{1,0:T(8,128)(2,1)S(1)}, bf16[16,1792]{1,0:T(8,128)(2,1)S(1)}, u32[]{:S(2)}, u32[]{:S(2)}) collective-permute-start(bf16[16,1792]{1,0:T(8,128)(2,1)S(1)} %subtract_convert_fusion), channel_id=1, source_target_pairs={{0,6},{1,15},{2,4},{3,13},{4,2},{5,11},{6,0},{7,9},{8,14},{9,7},{1... | collective-permute-start | bytes 172040 | tf_op jit(solution)/shard_map/ppermute | solution.py:34
  88.1 5.8 %collective-permute-start.28 = (bf16[16,1792]{1,0:T(8,128)(2,1)S(1)}, bf16[16,1792]{1,0:T(8,128)(2,1)S(1)}, u32[]{:S(2)}, u32[]{:S(2)}) collective-permute-start(bf16[16,1792]{1,0:T(8,128)(2,1)S(1)} %subtract_convert_fusion), channel_id=1, source_target_pairs={{0,4},{1,13},{2,6},{3,15},{4,0},{5,9},{6,2},{7,11},{8,12},{9,5},{1... | collective-permute-start | bytes 172040 | tf_op jit(solution)/shard_map/ppermute | solution.py:34
  91.4 6.0 %collective-permute-start.27 = (bf16[16,1792]{1,0:T(8,128)(2,1)S(1)}, bf16[16,1792]{1,0:T(8,128)(2,1)S(1)}, u32[]{:S(2)}, u32[]{:S(2)}) collective-permute-start(bf16[16,1792]{1,0:T(8,128)(2,1)S(1)} %subtract_convert_fusion), channel_id=1, source_target_pairs={{0,2},{1,11},{2,0},{3,9},{4,6},{5,15},{6,4},{7,13},{8,10},{9,3},{1... | collective-permute-start | bytes 172040 | tf_op jit(solution)/shard_map/ppermute | solution.py:34
  97.5 6.6 %collective-permute-start.30 = (bf16[64,1792]{1,0:T(8,128)(2,1)S(1)}, bf16[64,1792]{1,0:T(8,128)(2,1)S(1)}, u32[]{:S(2)}, u32[]{:S(2)}) collective-permute-start(bf16[64,1792]{1,0:T(8,128)(2,1)S(1)} %pad_maximum_fusion.2.refs_0_), channel_id=1, source_target_pairs={{0,32},{1,33},{2,34},{3,35},{4,36},{5,37},{6,38},{7,39},{8,40},{9,... | collective-permute-start | bytes 688136 | tf_op jit(solution)/shard_map/ppermute | solution.py:34
  98.9 7.2 %collective-permute-start.31 = (bf16[64,1792]{1,0:T(8,128)(2,1)S(1)}, bf16[64,1792]{1,0:T(8,128)(2,1)S(1)}, u32[]{:S(2)}, u32[]{:S(2)}) collective-permute-start(bf16[64,1792]{1,0:T(8,128)(2,1)S(1)} %pad_maximum_fusion.2.refs_0_), channel_id=1, source_target_pairs={{0,16},{1,17},{2,18},{3,19},{4,20},{5,21},{6,22},{7,23},{8,24},{9,... | collective-permute-start | bytes 688136 | tf_op jit(solution)/shard_map/ppermute | solution.py:34
  100.2 6.6 %collective-permute-start.32 = (bf16[64,1792]{1,0:T(8,128)(2,1)S(1)}, bf16[64,1792]{1,0:T(8,128)(2,1)S(1)}, u32[]{:S(2)}, u32[]{:S(2)}) collective-permute-start(bf16[64,1792]{1,0:T(8,128)(2,1)S(1)} %pad_maximum_fusion.2.refs_0_), channel_id=1, source_target_pairs={{0,48},{1,49},{2,50},{3,51},{4,52},{5,53},{6,54},{7,55},{8,56},{9,... | collective-permute-start | bytes 688136 | tf_op jit(solution)/shard_map/ppermute | solution.py:34
  100.8 6.1 %collective-permute-start.33 = (bf16[64,1792]{1,0:T(8,128)(2,1)S(1)}, bf16[64,1792]{1,0:T(8,128)(2,1)S(1)}, u32[]{:S(2)}, u32[]{:S(2)}) collective-permute-start(bf16[64,1792]{1,0:T(8,128)(2,1)S(1)} %pad_maximum_fusion.2.refs_0_), channel_id=1, source_target_pairs={{0,1},{1,0},{2,3},{3,2},{4,5},{5,4},{6,7},{7,6},{8,9},{9,8},{10,11... | collective-permute-start | bytes 688136 | tf_op jit(solution)/shard_map/ppermute | solution.py:34
  104.1 2.9 %collective-permute-start.34 = (bf16[64,1792]{1,0:T(8,128)(2,1)S(1)}, bf16[64,1792]{1,0:T(8,128)(2,1)S(1)}, u32[]{:S(2)}, u32[]{:S(2)}) collective-permute-start(bf16[64,1792]{1,0:T(8,128)(2,1)S(1)} %collective-permute-done.30.refs_1_), channel_id=1, source_target_pairs={{0,1},{1,0},{2,3},{3,2},{4,5},{5,4},{6,7},{7,6},{8,9},{9,8},{10,11... | collective-permute-start | bytes 688136 | tf_op jit(solution)/shard_map/ppermute | solution.py:34
  106.0 1.5 %collective-permute-start.35 = (bf16[64,1792]{1,0:T(8,128)(2,1)S(1)}, bf16[64,1792]{1,0:T(8,128)(2,1)S(1)}, u32[]{:S(2)}, u32[]{:S(2)}) collective-permute-start(bf16[64,1792]{1,0:T(8,128)(2,1)S(1)} %collective-permute-done.31.refs_2_), channel_id=1, source_target_pairs={{0,1},{1,0},{2,3},{3,2},{4,5},{5,4},{6,7},{7,6},{8,9},{9,8},{10,11... | collective-permute-start | bytes 688136 | tf_op jit(solution)/shard_map/ppermute | solution.py:34
  106.8 1.5 %collective-permute-start.36 = (bf16[64,1792]{1,0:T(8,128)(2,1)S(1)}, bf16[64,1792]{1,0:T(8,128)(2,1)S(1)}, u32[]{:S(2)}, u32[]{:S(2)}) collective-permute-start(bf16[64,1792]{1,0:T(8,128)(2,1)S(1)} %collective-permute-done.32.refs_3_), channel_id=1, source_target_pairs={{0,1},{1,0},{2,3},{3,2},{4,5},{5,4},{6,7},{7,6},{8,9},{9,8},{10,11... | collective-permute-start | bytes 688136 | tf_op jit(solution)/shard_map/ppermute | solution.py:34
  110.8 8.4 %collective-permute-start.37 = (bf16[400,256]{1,0:T(8,128)(2,1)S(1)}, bf16[400,256]{1,0:T(8,128)(2,1)S(1)}, u32[]{:S(2)}, u32[]{:S(2)}) collective-permute-start(bf16[400,256]{1,0:T(8,128)(2,1)S(1)} %get-tuple-element.43.away_ref), channel_id=1, source_target_pairs={{0,128},{64,192},{128,0},{192,64},{1,129},{65,193},{129,1},{193,65... | collective-permute-start | bytes 614408 | tf_op jit(solution)/shard_map/ppermute | solution.py:42
  112.6 11.1 %collective-permute-start.38 = (bf16[400,256]{1,0:T(8,128)(2,1)S(1)}, bf16[400,256]{1,0:T(8,128)(2,1)S(1)}, u32[]{:S(2)}, u32[]{:S(2)}) collective-permute-start(bf16[400,256]{1,0:T(8,128)(2,1)S(1)} %get-tuple-element.44), channel_id=1, source_target_pairs={{0,192},{64,128},{128,64},{192,0},{1,193},{65,129},{129,65},{193,1... | collective-permute-start | bytes 614408 | tf_op jit(solution)/shard_map/ppermute | solution.py:42
  114.4 9.4 %collective-permute-start.39 = (bf16[400,256]{1,0:T(8,128)(2,1)S(1)}, bf16[400,256]{1,0:T(8,128)(2,1)S(1)}, u32[]{:S(2)}, u32[]{:S(2)}) collective-permute-start(bf16[400,256]{1,0:T(8,128)(2,1)S(1)} %get-tuple-element.45), channel_id=1, source_target_pairs={{0,64},{64,0},{128,192},{192,128},{1,65},{65,1},{129,193},{193,129... | collective-permute-start | bytes 614408 | tf_op jit(solution)/shard_map/ppermute | solution.py:42
